TPU v7x, 32 devices: a whole 2x2x4 slice. The times are simulated.
32 devices in a mesh: section: 4 (over y, x), dp: 8 (over z, core).
Axes of the slice: x: 2, y: 2, z: 4, core: 2. Of those that a mesh axis runs over, the one named last changes fastest.
Arguments:
- spikes: bfloat16 [32, 8, 4, 4, 1024], P('dp'), may hold values from 0 to 2
- labels: int32 [32], P('dp'), may hold values from 0 to 999
- readout: float32 [1024, 1000], replicated, may hold values from -0.1875 to 0.1875
- weights: float32 [4, 9216, 1024], P('section', 'dp'), may hold values from -6 to 6
- first_moment: float32 [4, 9216, 1024], P('section', 'dp'), may hold values from -4 to 4
- second_moment: float32 [4, 9216, 1024], P('section', 'dp'), may hold values from 1 to 16
Outputs:
- new_weights: float32 [4, 9216, 1024], P('section', 'dp')
- new_first: float32 [4, 9216, 1024], P('section', 'dp')
- new_second: float32 [4, 9216, 1024], P('section', 'dp')
All inputs are finite; a program needn't handle non-finite values.
Results may differ from a plain program's by a relative error of at most 0.015.
Values may be sent and summed in bfloat16 or wider, within the bound.
No kernel may reach another device: no remote copies, remote signals or barrier semaphores. Data moves between devices by JAX's collectives and lax.ppermute only.
A program may use at most 192 MiB of HBM per device.

v0:
```python
import functools
import jax
import jax.numpy as jnp
from jax import lax
from jax.experimental import pallas as pl
from jax.experimental.pallas import tpu as pltpu
from jax.sharding import PartitionSpec as P

leak_rate = 0.5
spike_slope = 4.0
threshold = 1.0
loss_scale = 4096.0
beta_first = 0.8
beta_second = 0.95
learn_rate = 0.5
adam_eps = 1e-08
HIGH = lax.Precision.HIGHEST
VMEM = pltpu.VMEM
LIMIT = 24 * 2**20


def slots_of(block, sections):
    return sorted({0, block, min(block + 1, sections - 1)})


def by_ring(slot):
    return slot > 0 and slot % 2 == 0


def fetch_weights(block, sections, scal, sources, weights, sems):
    s, z, core = scal[0], scal[1], scal[2]
    slot = jnp.where(block == s, 0, jnp.where(block < s, block + 1, block))
    slots = slots_of(block, sections)
    sources = list(sources)

    def copies(arrays):
        if len(arrays) == 1:
            return [pltpu.make_async_copy(arrays[0], weights, sems.at[0])]
        result = []
        for which, source in enumerate(arrays):
            ring, depth = source.shape[:2]
            owner_core = core if which == 0 else 1 - core
            for j in range(ring):
                place = lax.rem(z + j, ring)
                row = pl.multiple_of((place * 2 + owner_core) * depth, depth)
                result.append(
                    pltpu.make_async_copy(
                        source.at[j],
                        weights.at[pl.ds(row, depth), :],
                        sems.at[1 + which * ring + j],
                    )
                )
        return result

    choices = []
    for candidate in slots:
        count = 2 if by_ring(candidate) else 1
        choices.append((slot == candidate, sources[:count]))
        sources = sources[count:]

    for chosen, arrays in choices:

        @pl.when(chosen)
        def _():
            for copy in copies(arrays):
                copy.start()

    def wait():
        for chosen, arrays in choices:

            @pl.when(chosen)
            def _():
                for copy in copies(arrays):
                    copy.wait()

    return wait


def forward_kernel(dims, block, scal, *refs):
    last = block == dims[0] - 1
    sections, height, width, images, steps = dims
    slices = refs[:sections]
    refs = refs[sections:]
    count = sum(2 if by_ring(slot) else 1 for slot in slots_of(block, sections))
    sources = refs[:count]
    refs = refs[count:]
    if last:
        readout, out, fired_out, logits_out, weights, padded, work, sems = refs
    else:
        out, fired_out, weights, padded, work, sems = refs
    wait = fetch_weights(block, sections, scal, sources, weights, sems)
    rows, lanes = slices[0].shape
    group = images * steps
    channels = sections * lanes
    padded[...] = jnp.zeros_like(padded)
    for k in range(sections):
        padded[scal[0] ^ k, 1 : height + 1, 1 : width + 1] = slices[k][...].reshape(
            height, width, group, lanes
        )
    wait()
    total = jnp.zeros((rows, lanes), jnp.float32)
    for offset in range(9):
        r, c = divmod(offset, 3)
        lhs = jnp.concatenate(
            [
                padded[j, r : r + height, c : c + width].reshape(rows, lanes)
                for j in range(sections)
            ],
            axis=1,
        )
        total += jnp.dot(
            lhs,
            weights[offset * channels : (offset + 1) * channels, :],
            preferred_element_type=jnp.float32,
        )
    scale = float(9 * channels) ** (-0.5)
    current = total * scale
    count = rows // steps
    tiles = lanes // 128
    for tile in range(tiles):
        here, there = work.at[tile], fired_out.at[tile]
        here[...] = current[:, tile * 128 : (tile + 1) * 128]
        membrane = jnp.zeros((count, 128), jnp.float32)
        for t in range(steps):
            spot = pl.ds(t, count, stride=steps)
            h = leak_rate * membrane + here[spot, :]
            fired = jax.nn.sigmoid(spike_slope * (h - threshold))
            membrane = h - threshold * fired
            there[spot, :] = fired
    fired = jnp.concatenate([fired_out[tile] for tile in range(tiles)], axis=1)
    result = (slices[0][...].astype(jnp.float32) + fired).astype(jnp.bfloat16)
    out[...] = result
    if last:
        summed = jnp.sum(
            result.astype(jnp.float32).reshape(height * width, group, lanes), axis=0
        )
        pooled = jnp.sum(summed.reshape(images, steps, lanes), axis=1) / float(
            height * width * steps
        )
        logits_out[...] = jnp.dot(
            pooled, readout[...], precision=HIGH, preferred_element_type=jnp.float32
        )


def backward_kernel(dims, block, classes, scal, *refs):
    stage = 0 if block == dims[0] - 1 else (2 if block == 0 else 1)
    sections, height, width, images, steps = dims
    if stage == 0:
        logit_parts = refs[:sections]
        labels, readout = refs[sections : sections + 2]
        refs = refs[sections + 2 :]
    else:
        own_part = refs[0]
        arrived = refs[1:sections]
        refs = refs[sections:]
    fired = refs[0]
    refs = refs[1:]
    if stage < 2:
        count = sum(2 if by_ring(slot) else 1 for slot in slots_of(block, sections))
        sources = refs[:count]
        refs = refs[count:]
        raw_out, own_out = refs[:2]
        sends = refs[2 : 1 + sections]
        weights, padded, upstream, work, sems = refs[1 + sections :]
        wait = fetch_weights(block, sections, scal, sources, weights, sems)
        padded[...] = jnp.zeros_like(padded)
    else:
        raw_out, upstream, work = refs
    tiles, rows = fired.shape[:2]
    lanes = tiles * 128
    group = images * steps
    channels = sections * lanes
    cells = height * width
    count = rows // steps
    if stage == 0:
        logits = logit_parts[0][...]
        for part in logit_parts[1:]:
            logits = logits + part[...]
        lane = lax.broadcasted_iota(jnp.int32, logits.shape, 1)
        logits = jnp.where(lane < classes, logits, -jnp.inf)
        exponent = jnp.exp(logits - jnp.max(logits, axis=-1, keepdims=True))
        probability = exponent / jnp.sum(exponent, axis=-1, keepdims=True)
        onehot = (labels[...] == lane).astype(jnp.float32)
        dlogits = loss_scale * (probability - onehot)
        dpooled = lax.dot_general(
            dlogits,
            readout[...],
            (((1,), (1,)), ((), ())),
            precision=HIGH,
            preferred_element_type=jnp.float32,
        )
        spread = (dpooled / float(cells * steps)).astype(jnp.bfloat16).astype(jnp.float32)
        arriving = jnp.broadcast_to(
            spread[None, :, None, :], (cells, images, steps, lanes)
        ).reshape(rows, lanes)
    else:
        arriving = own_part[...]
        for part in arrived:
            arriving = arriving + part[...].astype(jnp.float32)
        arriving = arriving.astype(jnp.bfloat16).astype(jnp.float32)
    scale = float(9 * channels) ** (-0.5)
    for tile in range(tiles):
        upstream[tile] = arriving[:, tile * 128 : (tile + 1) * 128]
        here, there, fired_here = upstream.at[tile], work.at[tile], fired.at[tile]
        dmembrane = jnp.zeros((count, 128), jnp.float32)
        for t in reversed(range(steps)):
            spot = pl.ds(t, count, stride=steps)
            f = fired_here[spot, :]
            slope = spike_slope * (f * (1.0 - f))
            dh = dmembrane + (here[spot, :] - threshold * dmembrane) * slope
            there[spot, :] = dh * scale
            dmembrane = leak_rate * dh
    raw = jnp.concatenate([work[tile] for tile in range(tiles)], axis=1).astype(jnp.bfloat16)
    raw_out[...] = raw
    if stage == 2:
        return
    padded[1 : height + 1, 1 : width + 1] = raw.reshape(height, width, group, lanes)
    wait()
    for k in list(range(1, sections)) + [0]:
        total = jnp.zeros((rows, lanes), jnp.float32)
        for offset in range(9):
            r, c = divmod(offset, 3)
            lhs = padded[2 - r : 2 - r + height, 2 - c : 2 - c + width].reshape(rows, lanes)
            row = pl.multiple_of(offset * channels + (scal[0] ^ k) * lanes, lanes)
            total += lax.dot_general(
                lhs,
                weights[pl.ds(row, lanes), :],
                (((1,), (1,)), ((), ())),
                preferred_element_type=jnp.float32,
            )
        if k == 0:
            own_out[...] = total + jnp.concatenate([upstream[tile] for tile in range(tiles)], axis=1)
        else:
            sends[k - 1][...] = total.astype(jnp.bfloat16)


def vmem(count):
    return [pl.BlockSpec(memory_space=VMEM)] * count


def run_forward(dims, block, devices, scal, slices, sources, readout):
    sections, height, width, images, steps = dims
    rows, lanes = slices[0].shape
    depth = 9 * sections * lanes
    last = block == sections - 1
    shapes = [
        jax.ShapeDtypeStruct((rows, lanes), jnp.bfloat16),
        jax.ShapeDtypeStruct((lanes // 128, rows, 128), jnp.float32),
    ]
    operands = [scal, *slices, *sources]
    extra = []
    if last:
        shapes.append(jax.ShapeDtypeStruct((images, readout.shape[1]), jnp.float32))
        operands.append(readout)
        extra = vmem(1)
    return pl.pallas_call(
        functools.partial(forward_kernel, dims, block),
        out_shape=shapes,
        in_specs=[pl.BlockSpec(memory_space=pltpu.SMEM)]
        + vmem(sections)
        + [pl.BlockSpec(memory_space=pltpu.HBM)] * len(sources)
        + extra,
        out_specs=vmem(len(shapes)),
        scratch_shapes=[
            VMEM((depth, lanes), jnp.bfloat16),
            VMEM((sections, height + 2, width + 2, images * steps, lanes), jnp.bfloat16),
            VMEM((lanes // 128, rows, 128), jnp.float32),
            pltpu.SemaphoreType.DMA((1 + devices,)),
        ],
        compiler_params=pltpu.CompilerParams(vmem_limit_bytes=LIMIT),
        cost_estimate=pl.CostEstimate(
            flops=2 * rows * lanes * depth,
            bytes_accessed=2 * depth * lanes,
            transcendentals=rows * lanes,
        ),
        name="forward_block",
    )(*operands)


def run_backward(dims, block, devices, classes, scal, heads, fired, sources):
    sections, height, width, images, steps = dims
    stage = 0 if block == sections - 1 else (2 if block == 0 else 1)
    tiles, rows = fired.shape[:2]
    lanes = tiles * 128
    half = jax.ShapeDtypeStruct((rows, lanes), jnp.bfloat16)
    full = jax.ShapeDtypeStruct((rows, lanes), jnp.float32)
    operands = [scal, *heads, fired]
    specs = [pl.BlockSpec(memory_space=pltpu.SMEM)] + vmem(len(heads) + 1)
    work = [VMEM(fired.shape, jnp.float32), VMEM(fired.shape, jnp.float32)]
    cost = 0
    if stage < 2:
        depth = 9 * sections * lanes
        operands += list(sources)
        specs += [pl.BlockSpec(memory_space=pltpu.HBM)] * len(sources)
        shapes = [half, full] + [half] * (sections - 1)
        work = (
            [
                VMEM((depth, lanes), jnp.bfloat16),
                VMEM((height + 2, width + 2, images * steps, lanes), jnp.bfloat16),
            ]
            + work
            + [pltpu.SemaphoreType.DMA((1 + devices,))]
        )
        cost = depth
    else:
        shapes = [half]
    return pl.pallas_call(
        functools.partial(backward_kernel, dims, block, classes),
        out_shape=shapes,
        in_specs=specs,
        out_specs=vmem(len(shapes)),
        scratch_shapes=work,
        compiler_params=pltpu.CompilerParams(vmem_limit_bytes=LIMIT),
        cost_estimate=pl.CostEstimate(
            flops=2 * rows * lanes * cost + rows * lanes * 100,
            bytes_accessed=2 * cost * lanes + 8 * rows * lanes,
            transcendentals=0,
        ),
        name="backward_block",
    )(*operands)


def after(value, *earlier):
    return lax.optimization_barrier((value, *earlier))[0]


def hops(step, way, ring):
    if way > 0:
        pairs = [(i, i + 1) for i in range(step - 1, ring - 1)]
    else:
        pairs = [(i, i - 1) for i in range(1, ring - step + 1)]
    return [(2 * a + core, 2 * b + core) for a, b in pairs for core in range(2)]


def swap_core(value):
    count = lax.axis_size("dp")
    return lax.ppermute(value, "dp", [(i, i ^ 1) for i in range(count)])


def adam_update(weights, first_moment, second_moment, grad_total):
    new_first = beta_first * first_moment + (1.0 - beta_first) * grad_total
    new_second = beta_second * second_moment + (1.0 - beta_second) * grad_total * grad_total
    new_weights = weights - learn_rate * new_first / (jnp.sqrt(new_second) + adam_eps)
    return (new_weights, new_first, new_second)


def shards(spikes, labels, readout, weights, first_moment, second_moment):
    sections = lax.axis_size("section")
    devices = lax.axis_size("dp")
    ring = devices // 2
    s = lax.axis_index("section")
    d = lax.axis_index("dp")
    z, core = d // 2, d % 2
    images, steps, height, width, channels = spikes.shape
    group = images * steps
    rows = height * width * group
    lanes = channels // sections
    depth = weights.shape[1]
    classes = readout.shape[1]
    dims = (sections, height, width, images, steps)
    scal = jnp.stack([s, z, core]).astype(jnp.int32)

    def exchange(values):
        return [
            lax.ppermute(values[k], "section", [(i, i ^ (k + 1)) for i in range(sections)])
            for k in range(sections - 1)
        ]

    def columns(array, k):
        return lax.dynamic_slice_in_dim(array, (s ^ k) * lanes, lanes, 1)

    def pick(options, index):
        return lax.dynamic_index_in_dim(jnp.stack(options), index, 0, keepdims=False)

    pieces = [columns(weights[0], k).astype(jnp.bfloat16) for k in range(sections)]
    pieces = [pieces[0]] + exchange(pieces[1:])
    field = spikes.transpose(2, 3, 0, 1, 4).reshape(rows, channels)
    slices = [columns(field, k) for k in range(sections)]
    padded_classes = -(-classes // 128) * 128
    readout_own = lax.dynamic_slice_in_dim(readout, s * lanes, lanes, 0)
    readout_own = jnp.pad(readout_own, ((0, 0), (0, padded_classes - classes)))

    inputs, results, slots, done = [slices], [], {}, {}
    own_inputs = jnp.stack(slices)

    def holding(b):
        return [array for slot in slots_of(b, sections) for array in slots[slot]]

    def forward(b):
        nonlocal own_inputs
        results.append(run_forward(dims, b, devices, scal, inputs[b], holding(b), readout_own))
        if b < sections - 1:
            out = results[b][0]
            inputs.append([out] + exchange([out] * (sections - 1)))
            own_inputs = jnp.where(s == b + 1, jnp.stack(inputs[b + 1]), own_inputs)

    def piece_of(slot):
        if slot == 0:
            return pieces[0]
        return pick(pieces, jnp.where(slot - 1 < s, slot - 1, slot) ^ s)

    for slot in range(2, sections, 2):
        piece = piece_of(slot)
        gates = [readout_own, *slices] if slot == 2 else done[slot - 2, ring - 1]
        up = down = after(piece, *gates)
        for step in range(1, ring):
            up = lax.ppermute(up, "dp", hops(step, 1, ring))
            down = lax.ppermute(down, "dp", hops(step, -1, ring))
            done[slot, step] = [up, down]
        held = [piece]
        for j in range(1, ring):
            held.append(jnp.where(z + j < ring, done[slot, j][1], done[slot, ring - j][0]))
        held = jnp.stack(held)
        slots[slot] = [held, swap_core(held)]
    gates = []
    for slot in [0] + list(range(1, sections, 2)):
        piece = after(piece_of(slot), *gates) if gates else piece_of(slot)
        gathered = lax.all_gather(piece, "dp", axis=0, tiled=True)
        slots[slot] = [gathered]
        gates = [gathered] + done.get((2, 1) if slot == 0 else (slot + 1, ring - 1), [])
    for b in range(sections):
        forward(b)
    result = results[-1]
    logits = result[2]
    heads = [logits] + exchange([logits] * (sections - 1))
    heads += [labels[:, None], readout_own]

    def ordered(parts):
        return jnp.concatenate([pick(parts, s ^ j) for j in range(sections)], axis=1)

    own_x = jnp.concatenate(
        [
            lax.dynamic_index_in_dim(own_inputs, s ^ j, 0, keepdims=False)
            for j in range(sections)
        ],
        axis=1,
    )
    x_all = lax.all_gather(own_x, "dp")

    raws = [None] * sections
    for b in reversed(range(sections)):
        held = holding(b) if b > 0 else None
        result = run_backward(dims, b, devices, classes, scal, heads, results[b][1], held)
        raws[b] = result[0]
        if b > 0:
            heads = [result[1]] + exchange(result[2:])

    sent = [pick(raws, s ^ k) for k in range(sections)]
    own_raw = ordered([sent[0]] + exchange(sent[1:]))
    start = d * depth
    channel = start % channels
    step = 1
    while channels % (2 * step) == 0 and depth % (2 * step) == 0:
        step *= 2
    spans = -(-(channels - step + depth) // channels)

    fields = x_all.reshape(devices, height, width, group, channels)
    fields = jnp.pad(fields, ((0, 0), (1, 1), (1, 1), (0, 0), (0, 0)))
    shifted = []
    for i in range(spans):
        offset = jnp.minimum(start // channels + i, 8)
        shifted.append(
            lax.dynamic_slice(
                fields,
                (0, offset // 3, offset % 3, 0, 0),
                (devices, height, width, group, channels),
            ).reshape(devices * rows, channels)
        )
    cols = lax.dynamic_slice_in_dim(jnp.concatenate(shifted, axis=1), channel, depth, 1)

    raw_all = lax.all_gather(own_raw, "dp", axis=0, tiled=True)
    raw_all, cols = lax.optimization_barrier((raw_all, cols))
    grad = lax.dot_general(
        cols, raw_all, (((0,), (0,)), ((), ())), preferred_element_type=jnp.float32
    )
    return adam_update(weights, first_moment, second_moment, grad[None])


def solution(mesh):
    return jax.shard_map(
        shards,
        mesh=mesh,
        in_specs=(
            P("dp", None, None, None, None),
            P("dp"),
            P(),
            P("section", "dp", None),
            P("section", "dp", None),
            P("section", "dp", None),
        ),
        out_specs=(P("section", "dp", None), P("section", "dp", None), P("section", "dp", None)),
        check_vma=False,
    )
```

profile of v0, /device:TPU:0, one launch (start us, length us, event | category | flops | bytes accessed | tf_op | source)
XLA Modules:
  0.0 435.4 jit_solution(14232991201513709400)
XLA Ops:
  7.2 3.8 fusion.3
  11.1 3.0 collective-permute-start
  14.1 1.5 collective-permute-start.1
  15.7 1.3 constant_dynamic-slice_fusion.1
  17.4 1.8 copy.9
  21.2 7.4 %collective-permute-done = bf16[1152,256]{1,0:T(8,128)(2,1)} collective-permute-done((bf16[1152,256]{1,0:T(8,128)(2,1)}, bf16[1152,256]{1,0:T(8,128)(2,1)}, u32[]{:S(2)}, u32[]{:S(2)}) %collective-permute-start) | collective-permute-done | bytes 589856 | tf_op jit(solution)/shard_map/ppermute | solution.py:365
  28.6 13.3 %collective-permute-done.1 = bf16[1152,256]{1,0:T(8,128)(2,1)} collective-permute-done((bf16[1152,256]{1,0:T(8,128)(2,1)}, bf16[1152,256]{1,0:T(8,128)(2,1)}, u32[]{:S(2)}, u32[]{:S(2)}) %collective-permute-start.1) | collective-permute-done | bytes 589856 | tf_op jit(solution)/shard_map/ppermute | solution.py:365
  41.9 1.7 pad_maximum_fusion
  44.8 1.3 collective-permute-start.4
  46.1 4.6 %collective-permute-start.3 = (bf16[1152,256]{1,0:T(8,128)(2,1)S(1)}, bf16[1152,256]{1,0:T(8,128)(2,1)S(1)}, u32[]{:S(2)}, u32[]{:S(2)}) collective-permute-start(bf16[1152,256]{1,0:T(8,128)(2,1)S(1)} %bitcast.117), channel_id=1, source_target_pairs={{0,2},{1,3},{2,4},{3,5},{4,6},{5,7},{8,10},{9,11},{10,12},{11,13},... | collective-permute-start | bytes 1769480 | tf_op jit(solution)/shard_map/ppermute | solution.py:407
  50.6 24.4 %collective-permute-done.4 = bf16[1152,256]{1,0:T(8,128)(2,1)S(1)} collective-permute-done((bf16[1152,256]{1,0:T(8,128)(2,1)S(1)}, bf16[1152,256]{1,0:T(8,128)(2,1)S(1)}, u32[]{:S(2)}, u32[]{:S(2)}) %collective-permute-start.4) | collective-permute-done | bytes 589856 | tf_op jit(solution)/shard_map/ppermute | solution.py:408
  75.1 1.3 collective-permute-start.10
  77.1 22.1 %collective-permute-done.10 = bf16[1152,256]{1,0:T(8,128)(2,1)S(1)} collective-permute-done((bf16[1152,256]{1,0:T(8,128)(2,1)S(1)}, bf16[1152,256]{1,0:T(8,128)(2,1)S(1)}, u32[]{:S(2)}, u32[]{:S(2)}) %collective-permute-start.10) | collective-permute-done | bytes 589856 | tf_op jit(solution)/shard_map/ppermute | solution.py:408
  99.2 1.3 collective-permute-start.11
  100.5 1.5 collective-permute-start.9
  102.0 41.9 %collective-permute-done.11 = bf16[1152,256]{1,0:T(8,128)(2,1)S(1)} collective-permute-done((bf16[1152,256]{1,0:T(8,128)(2,1)S(1)}, bf16[1152,256]{1,0:T(8,128)(2,1)S(1)}, u32[]{:S(2)}, u32[]{:S(2)}) %collective-permute-start.11) | collective-permute-done | bytes 589856 | tf_op jit(solution)/shard_map/ppermute | solution.py:408
  146.7 2.3 copy-done
  149.0 2.3 copy-done.8
  153.3 4.0 forward_block.4
  157.3 2.8 collective-permute-start.7
  160.8 6.5 %collective-permute-done.7.refs_3_ = bf16[512,256]{1,0:T(8,128)(2,1)S(1)} collective-permute-done((bf16[512,256]{1,0:T(8,128)(2,1)S(1)}, bf16[512,256]{1,0:T(8,128)(2,1)S(1)}, u32[]{:S(2)}, u32[]{:S(2)}) %collective-permute-start.7) | collective-permute-done | bytes 262176 | tf_op jit(solution)/shard_map/ppermute | solution.py:365
  167.4 5.3 %collective-permute-done.6.refs_2_ = bf16[512,256]{1,0:T(8,128)(2,1)S(1)} collective-permute-done((bf16[512,256]{1,0:T(8,128)(2,1)S(1)}, bf16[512,256]{1,0:T(8,128)(2,1)S(1)}, u32[]{:S(2)}, u32[]{:S(2)}) %collective-permute-start.6) | collective-permute-done | bytes 262176 | tf_op jit(solution)/shard_map/ppermute | solution.py:365
  172.7 4.0 forward_block.5
  177.6 3.4 collective-permute-start.15
  182.8 5.4 %collective-permute-done.15.refs_3_ = bf16[512,256]{1,0:T(8,128)(2,1)S(1)} collective-permute-done((bf16[512,256]{1,0:T(8,128)(2,1)S(1)}, bf16[512,256]{1,0:T(8,128)(2,1)S(1)}, u32[]{:S(2)}, u32[]{:S(2)}) %collective-permute-start.15) | collective-permute-done | bytes 262176 | tf_op jit(solution)/shard_map/ppermute | solution.py:365
  188.9 3.9 collective-permute-done.14.refs_2_
  194.8 3.7 all-gather.10.cloned.1.call-done.refs_7_.refs_5_.refs_8_
  198.5 2.3 copy-done.1
  200.8 2.3 copy-done.4
  206.9 6.3 %forward_block.6 = (bf16[512,256]{1,0:T(8,128)(2,1)}, f32[2,512,128]{2,1,0:T(8,128)S(1)}) custom-call(s32[3]{0:T(128)S(1)} %pad_add_fusion.scal, bf16[512,256]{1,0:T(8,128)(2,1)S(1)} %copy-done.21, bf16[512,256]{1,0:T(8,128)(2,1)S(1)} %copy-done.27, bf16[512,256]{1,0:T(8,128)(2,1)S(1)} %copy-done.25, bf16[512,256]{1,0:T(8,128)(2,1)S(1)} %copy-done.23, ...), custom_call_target="tpu_custom_call" | custom-call | flops 2415919104 | bytes 4718592 | tf_op jit(solution)/shard_map/forward_block/pallas_call | solution.py:256
  214.8 2.1 collective-permute-start.17
  217.5 6.9 %collective-permute-done.18.refs_3_ = bf16[512,256]{1,0:T(8,128)(2,1)} collective-permute-done((bf16[512,256]{1,0:T(8,128)(2,1)}, bf16[512,256]{1,0:T(8,128)(2,1)}, u32[]{:S(2)}, u32[]{:S(2)}) %collective-permute-start.18) | collective-permute-done | bytes 262176 | tf_op jit(solution)/shard_map/ppermute | solution.py:365
  224.4 4.9 %collective-permute-done.17.refs_2_ = bf16[512,256]{1,0:T(8,128)(2,1)} collective-permute-done((bf16[512,256]{1,0:T(8,128)(2,1)}, bf16[512,256]{1,0:T(8,128)(2,1)}, u32[]{:S(2)}, u32[]{:S(2)}) %collective-permute-start.17) | collective-permute-done | bytes 262176 | tf_op jit(solution)/shard_map/ppermute | solution.py:365
  229.3 2.2 maximum_select_fusion
  232.8 2.3 copy-done.2
  235.1 2.4 copy-done.5
  237.6 1.3 copy-done.10
  238.9 6.4 %forward_block.7 = (bf16[512,256]{1,0:T(8,128)(2,1)}, f32[2,512,128]{2,1,0:T(8,128)S(1)}, f32[4,1024]{1,0:T(4,128)S(1)}) custom-call(s32[3]{0:T(128)S(1)} %pad_add_fusion.scal, bf16[512,256]{1,0:T(8,128)(2,1)} %get-tuple-element.36.refs_0_, bf16[512,256]{1,0:T(8,128)(2,1)} %collective-permute-done.16.refs_1_, ...), custom_call_target="tpu_custom_call" | custom-call | flops 2415919104 | bytes 4718592 | tf_op jit(solution)/shard_map/forward_block/pallas_call | solution.py:256
  245.3 1.4 collective-permute-start.21
  247.3 1.6 collective-permute-start.19
  251.0 2.4 copy-done.3
  253.5 2.3 copy-done.6
  257.0 6.6 %backward_block.4 = (bf16[512,256]{1,0:T(8,128)(2,1)S(1)}, f32[512,256]{1,0:T(8,128)S(1)}, bf16[512,256]{1,0:T(8,128)(2,1)S(1)}, bf16[512,256]{1,0:T(8,128)(2,1)S(1)}, bf16[512,256]{1,0:T(8,128)(2,1)S(1)}) custom-call(s32[3]{0:T(128)S(1)} %pad_add_fusion.scal, f32[4,1024]{1,0:T(4,128)S(1)} %get-tuple-element.37.refs_0_, ...), custom_call_target="tpu_custom_call" | custom-call | flops 2429026304 | bytes 5767168 | tf_op jit(solution)/shard_map/backward_block/pallas_call | solution.py:307
  263.6 1.6 collective-permute-start.22
  265.7 1.5 collective-permute-start.24
  267.2 5.8 %collective-permute-done.22.refs_1_ = bf16[512,256]{1,0:T(8,128)(2,1)S(1)} collective-permute-done((bf16[512,256]{1,0:T(8,128)(2,1)S(1)}, bf16[512,256]{1,0:T(8,128)(2,1)S(1)}, u32[]{:S(2)}, u32[]{:S(2)}) %collective-permute-start.22) | collective-permute-done | bytes 262176 | tf_op jit(solution)/shard_map/ppermute | solution.py:365
  272.9 4.5 %collective-permute-done.23.refs_2_ = bf16[512,256]{1,0:T(8,128)(2,1)S(1)} collective-permute-done((bf16[512,256]{1,0:T(8,128)(2,1)S(1)}, bf16[512,256]{1,0:T(8,128)(2,1)S(1)}, u32[]{:S(2)}, u32[]{:S(2)}) %collective-permute-start.23) | collective-permute-done | bytes 262176 | tf_op jit(solution)/shard_map/ppermute | solution.py:365
  277.4 5.4 %backward_block.5 = (bf16[512,256]{1,0:T(8,128)(2,1)S(1)}, f32[512,256]{1,0:T(8,128)S(1)}, bf16[512,256]{1,0:T(8,128)(2,1)S(1)}, bf16[512,256]{1,0:T(8,128)(2,1)S(1)}, bf16[512,256]{1,0:T(8,128)(2,1)S(1)}) custom-call(s32[3]{0:T(128)S(1)} %pad_add_fusion.scal, f32[512,256]{1,0:T(8,128)S(1)} %get-tuple-element.39.refs_0_, ...), custom_call_target="tpu_custom_call" | custom-call | flops 2429026304 | bytes 5767168 | tf_op jit(solution)/shard_map/backward_block/pallas_call | solution.py:307
  283.4 2.9 collective-permute-start.27
  286.4 3.8 collective-permute-done.25.refs_1_
  290.2 4.0 collective-permute-done.26.refs_2_
  294.2 4.4 %backward_block.6 = (bf16[512,256]{1,0:T(8,128)(2,1)S(1)}, f32[512,256]{1,0:T(8,128)S(1)}, bf16[512,256]{1,0:T(8,128)(2,1)S(1)}, bf16[512,256]{1,0:T(8,128)(2,1)S(1)}, bf16[512,256]{1,0:T(8,128)(2,1)S(1)}) custom-call(s32[3]{0:T(128)S(1)} %pad_add_fusion.scal, f32[512,256]{1,0:T(8,128)S(1)} %get-tuple-element.44.refs_0_, ...), custom_call_target="tpu_custom_call" | custom-call | flops 2429026304 | bytes 5767168 | tf_op jit(solution)/shard_map/backward_block/pallas_call | solution.py:307
  298.6 1.4 collective-permute-start.28
  299.9 1.5 collective-permute-start.29
  302.1 3.2 collective-permute-done.28.refs_1_
  305.3 7.3 %collective-permute-done.29.refs_2_ = bf16[512,256]{1,0:T(8,128)(2,1)S(1)} collective-permute-done((bf16[512,256]{1,0:T(8,128)(2,1)S(1)}, bf16[512,256]{1,0:T(8,128)(2,1)S(1)}, u32[]{:S(2)}, u32[]{:S(2)}) %collective-permute-start.29) | collective-permute-done | bytes 262176 | tf_op jit(solution)/shard_map/ppermute | solution.py:365
  313.9 1.8 collective-permute-start.33
  315.7 1.7 collective-permute-start.31
  317.4 3.9 collective-permute-done.33
  321.3 2.7 collective-permute-done.32
  325.5 7.1 %pad_dynamic-slice_fusion = (bf16[8,4,4,32,1024]{4,3,2,1,0:T(8,128)(2,1)S(1)}, bf16[8,4,4,32,1024]{4,3,2,1,0:T(8,128)(2,1)S(1)}) fusion(s32[]{:T(128)S(6)} %select_n.180, s32[]{:T(128)S(6)} %select_n.182, bf16[8,4,4,32,1024]{4,3,2,1,0:T(8,128)(2,1)} %bitcast.114, s32[]{:T(128)S(6)} %select_n.176, s32[]{:T(128)S(6)} %select_n.178), kind=kLoop, calls=%fused_computation | loop fusion | bytes 25165840 | tf_op jit(solution)/shard_map/dynamic_slice | solution.py:463
  332.6 6.9 %fusion = bf16[4096,1152]{1,0:T(8,128)(2,1)} fusion(s32[]{:T(128)S(6)} %select_n.184, bf16[4096,1024]{1,0:T(8,128)(2,1)S(1)} %bitcast.113, bf16[4096,1024]{1,0:T(8,128)(2,1)S(1)} %bitcast.112), kind=kLoop, calls=%fused_computation.4 | loop fusion | flops 18874368 | bytes 26214404 | tf_op jit(solution)/shard_map/concatenate | solution.py:469
  339.5 66.1 %all-gather.12.cloned.1.call-done = bf16[4096,1024]{1,0:T(8,128)(2,1)} async-done(((bf16[512,1024]{1,0:T(8,128)(2,1)}), bf16[4096,1024]{1,0:T(8,128)(2,1)}) %all-gather.12.cloned.1.call-update) | async-done | bytes 8388624 | tf_op jit(solution)/shard_map/all_gather | solution.py:471
  405.7 23.2 %divide_subtract_fusion = (f32[1,1152,1024]{2,1,0:T(8,128)}, f32[1,1152,1024]{2,1,0:T(8,128)}, f32[1,1152,1024]{2,1,0:T(8,128)}) fusion(f32[1,1152,1024]{2,1,0:T(8,128)} %param.9, f32[1,1152,1024]{2,1,0:T(8,128)} %param.10, f32[1,1152,1024]{2,1,0:T(8,128)} %param.11, bf16[4096,1152]{1,0:T(8,128)(2,1)} %fusion, ...), kind=kOutput, calls=%fused_computation.9 | convolution fusion | flops 9676652544 | bytes 46137344 | tf_op jit(solution)/shard_map/dot_general | solution.py:473
  (140 shorter events, 30.6 us)
Async XLA Ops:
  7.2 67.8 %all-gather.14.cloned.1.call-start = ((), (), s32[]{:S(2)}) async-start(), calls=%async_computation.3 | async-start | bytes 5308416 | tf_op jit(solution)/shard_map/all_gather | solution.py:418
  11.1 133.6 %all-gather.8.cloned.1.call-start = ((), (), s32[]{:S(2)}) async-start(), calls=%async_computation | async-start | bytes 5308416 | tf_op jit(solution)/shard_map/all_gather | solution.py:418
  11.1 17.5 %collective-permute-start = (bf16[1152,256]{1,0:T(8,128)(2,1)}, bf16[1152,256]{1,0:T(8,128)(2,1)}, u32[]{:S(2)}, u32[]{:S(2)}) collective-permute-start(bf16[1152,256]{1,0:T(8,128)(2,1)} %get-tuple-element.64), channel_id=1, source_target_pairs={{0,8},{8,0},{16,24},{24,16},{1,9},{9,1},{17,25},{25,17},{2,10},{10... | collective-permute-start | bytes 1769480 | tf_op jit(solution)/shard_map/ppermute | solution.py:365
  14.1 27.7 %collective-permute-start.1 = (bf16[1152,256]{1,0:T(8,128)(2,1)}, bf16[1152,256]{1,0:T(8,128)(2,1)}, u32[]{:S(2)}, u32[]{:S(2)}) collective-permute-start(bf16[1152,256]{1,0:T(8,128)(2,1)} %get-tuple-element.65), channel_id=1, source_target_pairs={{0,16},{8,24},{16,0},{24,8},{1,17},{9,25},{17,1},{25,9},{2,18},{10... | collective-permute-start | bytes 1769480 | tf_op jit(solution)/shard_map/ppermute | solution.py:365
  15.7 26.2 %collective-permute-start.2 = (bf16[1152,256]{1,0:T(8,128)(2,1)}, bf16[1152,256]{1,0:T(8,128)(2,1)}, u32[]{:S(2)}, u32[]{:S(2)}) collective-permute-start(bf16[1152,256]{1,0:T(8,128)(2,1)} %get-tuple-element.67), channel_id=1, source_target_pairs={{0,24},{8,16},{16,8},{24,0},{1,25},{9,17},{17,9},{25,1},{2,26},{10... | collective-permute-start | bytes 1769480 | tf_op jit(solution)/shard_map/ppermute | solution.py:365
  15.7 26.2 %copy-start.34 = (bf16[1,1152,256]{2,1,0:T(8,128)(2,1)S(1)}, bf16[1,1152,256]{2,1,0:T(8,128)(2,1)}, u32[]{:S(2)}) copy-start(bf16[1,1152,256]{2,1,0:T(8,128)(2,1)} %get-tuple-element.66) | copy-start | bytes 1769476
  44.8 30.2 %collective-permute-start.4 = (bf16[1152,256]{1,0:T(8,128)(2,1)S(1)}, bf16[1152,256]{1,0:T(8,128)(2,1)S(1)}, u32[]{:S(2)}, u32[]{:S(2)}) collective-permute-start(bf16[1152,256]{1,0:T(8,128)(2,1)S(1)} %bitcast.116), channel_id=1, source_target_pairs={{2,0},{3,1},{4,2},{5,3},{6,4},{7,5},{10,8},{11,9},{12,10},{13,11},... | collective-permute-start | bytes 1769480 | tf_op jit(solution)/shard_map/ppermute | solution.py:408
  46.1 28.9 %collective-permute-start.3 = (bf16[1152,256]{1,0:T(8,128)(2,1)S(1)}, bf16[1152,256]{1,0:T(8,128)(2,1)S(1)}, u32[]{:S(2)}, u32[]{:S(2)}) collective-permute-start(bf16[1152,256]{1,0:T(8,128)(2,1)S(1)} %bitcast.117), channel_id=1, source_target_pairs={{0,2},{1,3},{2,4},{3,5},{4,6},{5,7},{8,10},{9,11},{10,12},{11,13},... | collective-permute-start | bytes 1769480 | tf_op jit(solution)/shard_map/ppermute | solution.py:407
  75.0 123.4 %all-gather.10.cloned.1.call-start = ((), (), s32[]{:S(2)}) async-start(), calls=%async_computation.1 | async-start | bytes 5308416 | tf_op jit(solution)/shard_map/all_gather | solution.py:418
  75.1 24.1 %collective-permute-start.10 = (bf16[1152,256]{1,0:T(8,128)(2,1)S(1)}, bf16[1152,256]{1,0:T(8,128)(2,1)S(1)}, u32[]{:S(2)}, u32[]{:S(2)}) collective-permute-start(bf16[1152,256]{1,0:T(8,128)(2,1)S(1)} %collective-permute-done.4), channel_id=1, source_target_pairs={{2,0},{3,1},{4,2},{5,3},{10,8},{11,9},{12,10},{13,11},{18,16},{19,... | collective-permute-start | bytes 1769480 | tf_op jit(solution)/shard_map/ppermute | solution.py:408
  76.4 24.1 %collective-permute-start.8 = (bf16[1152,256]{1,0:T(8,128)(2,1)S(1)}, bf16[1152,256]{1,0:T(8,128)(2,1)S(1)}, u32[]{:S(2)}, u32[]{:S(2)}) collective-permute-start(bf16[1152,256]{1,0:T(8,128)(2,1)S(1)} %collective-permute-done.3), channel_id=1, source_target_pairs={{2,4},{3,5},{4,6},{5,7},{10,12},{11,13},{12,14},{13,15},{18,20},{1... | collective-permute-start | bytes 1769480 | tf_op jit(solution)/shard_map/ppermute | solution.py:407
  99.2 44.7 %collective-permute-start.11 = (bf16[1152,256]{1,0:T(8,128)(2,1)S(1)}, bf16[1152,256]{1,0:T(8,128)(2,1)S(1)}, u32[]{:S(2)}, u32[]{:S(2)}) collective-permute-start(bf16[1152,256]{1,0:T(8,128)(2,1)S(1)} %collective-permute-done.10), channel_id=1, source_target_pairs={{2,0},{3,1},{10,8},{11,9},{18,16},{19,17},{26,24},{27,25}} | collective-permute-start | bytes 1769480 | tf_op jit(solution)/shard_map/ppermute | solution.py:408
  100.5 44.2 %collective-permute-start.9 = (bf16[1152,256]{1,0:T(8,128)(2,1)S(1)}, bf16[1152,256]{1,0:T(8,128)(2,1)}, u32[]{:S(2)}, u32[]{:S(2)}) collective-permute-start(bf16[1152,256]{1,0:T(8,128)(2,1)S(1)} %collective-permute-done.8), channel_id=1, source_target_pairs={{4,6},{5,7},{12,14},{13,15},{20,22},{21,23},{28,30},{29,31}} | collective-permute-start | bytes 1769480 | tf_op jit(solution)/shard_map/ppermute | solution.py:407
  144.8 180.8 %all-gather.16.cloned.1.call-start = ((), (), s32[]{:S(2)}) async-start(), calls=%async_computation.4 | async-start | bytes 9437184 | tf_op jit(solution)/shard_map/all_gather | solution.py:438
  146.2 26.5 %slice-start = ((s8[4718592]{0:T(1024)(128)(4,1)}), s8[524288]{0:T(1024)(128)(4,1)S(1)}, s32[]{:S(2)}) async-start(s8[4718592]{0:T(1024)(128)(4,1)} %bitcast.86), calls=%async_computation.5 | async-start | bytes 1048576
  146.5 14.3 %collective-permute-start.12 = (bf16[4,1152,256]{2,1,0:T(8,128)(2,1)S(1)}, bf16[4,1152,256]{2,1,0:T(8,128)(2,1)}, u32[]{:S(2)}, u32[]{:S(2)}) collective-permute-start(bf16[4,1152,256]{2,1,0:T(8,128)(2,1)S(1)} %pad_maximum_fusion.1.refs_6_.refs_5_.refs_7_), channel_id=1, source_target_pairs={{0,1},{1,0},{2,3},{3,2},{4,5},{5,4},{6,7},{7,6},{8,9},{9,8},{10,11... | collective-permute-start | bytes 7077896 | tf_op jit(solution)/shard_map/ppermute | solution.py:337
  146.7 2.3 copy-start
  149.0 2.3 copy-start.8
  153.3 19.4 %slice-start.1 = ((s8[4718592]{0:T(1024)(128)(4,1)}), s8[4194304]{0:T(1024)(128)(4,1)S(1)}, s32[]{:S(2)}) async-start(s8[4718592]{0:T(1024)(128)(4,1)} %bitcast.86), calls=%async_computation.6 | async-start | bytes 8388608
  153.3 19.4 %copy-start.9 = (bf16[9216,256]{1,0:T(8,128)(2,1)S(1)}, bf16[9216,256]{1,0:T(8,128)(2,1)}, u32[]{:S(2)}) copy-start(bf16[9216,256]{1,0:T(8,128)(2,1)} %all-gather.8.cloned.1.call-done.refs_5_.refs_6_) | copy-start | bytes 14155780
  157.3 19.5 %copy-start.14 = (bf16[512,256]{1,0:T(8,128)(2,1)}, bf16[512,256]{1,0:T(8,128)(2,1)S(1)}, u32[]{:S(2)}) copy-start(bf16[512,256]{1,0:T(8,128)(2,1)S(1)} %get-tuple-element.33.refs_0_) | copy-start | bytes 786436
  157.3 19.5 %copy-start.28 = (f32[2,512,128]{2,1,0:T(8,128)}, f32[2,512,128]{2,1,0:T(8,128)S(1)}, u32[]{:S(2)}) copy-start(f32[2,512,128]{2,1,0:T(8,128)S(1)} %get-tuple-element.53.refs_4_) | copy-start | bytes 1572868
  157.3 10.1 %collective-permute-start.7 = (bf16[512,256]{1,0:T(8,128)(2,1)S(1)}, bf16[512,256]{1,0:T(8,128)(2,1)S(1)}, u32[]{:S(2)}, u32[]{:S(2)}) collective-permute-start(bf16[512,256]{1,0:T(8,128)(2,1)S(1)} %get-tuple-element.33.refs_0_), channel_id=1, source_target_pairs={{0,24},{8,16},{16,8},{24,0},{1,25},{9,17},{17,9},{25,1},{2,26},{10... | collective-permute-start | bytes 786440 | tf_op jit(solution)/shard_map/ppermute | solution.py:365
  160.1 12.6 %collective-permute-start.6 = (bf16[512,256]{1,0:T(8,128)(2,1)S(1)}, bf16[512,256]{1,0:T(8,128)(2,1)S(1)}, u32[]{:S(2)}, u32[]{:S(2)}) collective-permute-start(bf16[512,256]{1,0:T(8,128)(2,1)S(1)} %get-tuple-element.33.refs_0_), channel_id=1, source_target_pairs={{0,16},{8,24},{16,0},{24,8},{1,17},{9,25},{17,1},{25,9},{2,18},{10... | collective-permute-start | bytes 786440 | tf_op jit(solution)/shard_map/ppermute | solution.py:365
  160.3 12.4 %collective-permute-start.5 = (bf16[512,256]{1,0:T(8,128)(2,1)S(1)}, bf16[512,256]{1,0:T(8,128)(2,1)S(1)}, u32[]{:S(2)}, u32[]{:S(2)}) collective-permute-start(bf16[512,256]{1,0:T(8,128)(2,1)S(1)} %get-tuple-element.33.refs_0_), channel_id=1, source_target_pairs={{0,8},{8,0},{16,24},{24,16},{1,9},{9,1},{17,25},{25,17},{2,10},{10... | collective-permute-start | bytes 786440 | tf_op jit(solution)/shard_map/ppermute | solution.py:365
  167.4 9.4 %copy-start.16 = (bf16[512,256]{1,0:T(8,128)(2,1)}, bf16[512,256]{1,0:T(8,128)(2,1)S(1)}, u32[]{:S(2)}) copy-start(bf16[512,256]{1,0:T(8,128)(2,1)S(1)} %collective-permute-done.7.refs_3_) | copy-start | bytes 786436
  172.7 4.9 %copy-start.18 = (bf16[512,256]{1,0:T(8,128)(2,1)}, bf16[512,256]{1,0:T(8,128)(2,1)S(1)}, u32[]{:S(2)}) copy-start(bf16[512,256]{1,0:T(8,128)(2,1)S(1)} %collective-permute-done.6.refs_2_) | copy-start | bytes 786436
  172.7 8.3 %copy-start.19 = (bf16[512,256]{1,0:T(8,128)(2,1)}, bf16[512,256]{1,0:T(8,128)(2,1)S(1)}, u32[]{:S(2)}) copy-start(bf16[512,256]{1,0:T(8,128)(2,1)S(1)} %collective-permute-done.5.refs_1_) | copy-start | bytes 786436
  177.6 10.6 %collective-permute-start.15 = (bf16[512,256]{1,0:T(8,128)(2,1)S(1)}, bf16[512,256]{1,0:T(8,128)(2,1)S(1)}, u32[]{:S(2)}, u32[]{:S(2)}) collective-permute-start(bf16[512,256]{1,0:T(8,128)(2,1)S(1)} %get-tuple-element.34.refs_0_), channel_id=1, source_target_pairs={{0,24},{8,16},{16,8},{24,0},{1,25},{9,17},{17,9},{25,1},{2,26},{10... | collective-permute-start | bytes 786440 | tf_op jit(solution)/shard_map/ppermute | solution.py:365
  181.0 11.8 %collective-permute-start.14 = (bf16[512,256]{1,0:T(8,128)(2,1)S(1)}, bf16[512,256]{1,0:T(8,128)(2,1)S(1)}, u32[]{:S(2)}, u32[]{:S(2)}) collective-permute-start(bf16[512,256]{1,0:T(8,128)(2,1)S(1)} %get-tuple-element.34.refs_0_), channel_id=1, source_target_pairs={{0,16},{8,24},{16,0},{24,8},{1,17},{9,25},{17,1},{25,9},{2,18},{10... | collective-permute-start | bytes 786440 | tf_op jit(solution)/shard_map/ppermute | solution.py:365
  181.0 13.0 %collective-permute-start.13 = (bf16[512,256]{1,0:T(8,128)(2,1)S(1)}, bf16[512,256]{1,0:T(8,128)(2,1)S(1)}, u32[]{:S(2)}, u32[]{:S(2)}) collective-permute-start(bf16[512,256]{1,0:T(8,128)(2,1)S(1)} %get-tuple-element.34.refs_0_), channel_id=1, source_target_pairs={{0,8},{8,0},{16,24},{24,16},{1,9},{9,1},{17,25},{25,17},{2,10},{10... | collective-permute-start | bytes 786440 | tf_op jit(solution)/shard_map/ppermute | solution.py:365
  198.5 2.3 copy-start.1
  206.9 22.4 %copy-start.15 = (bf16[512,256]{1,0:T(8,128)(2,1)S(1)}, bf16[512,256]{1,0:T(8,128)(2,1)}, u32[]{:S(2)}) copy-start(bf16[512,256]{1,0:T(8,128)(2,1)} %copy-done.14) | copy-start | bytes 786436
  206.9 22.4 %copy-start.17 = (bf16[512,256]{1,0:T(8,128)(2,1)S(1)}, bf16[512,256]{1,0:T(8,128)(2,1)}, u32[]{:S(2)}) copy-start(bf16[512,256]{1,0:T(8,128)(2,1)} %copy-done.16) | copy-start | bytes 786436
  214.0 10.4 %collective-permute-start.18 = (bf16[512,256]{1,0:T(8,128)(2,1)}, bf16[512,256]{1,0:T(8,128)(2,1)}, u32[]{:S(2)}, u32[]{:S(2)}) collective-permute-start(bf16[512,256]{1,0:T(8,128)(2,1)} %get-tuple-element.36.refs_0_), channel_id=1, source_target_pairs={{0,24},{8,16},{16,8},{24,0},{1,25},{9,17},{17,9},{25,1},{2,26},{10... | collective-permute-start | bytes 786440 | tf_op jit(solution)/shard_map/ppermute | solution.py:365
  214.8 14.4 %collective-permute-start.17 = (bf16[512,256]{1,0:T(8,128)(2,1)}, bf16[512,256]{1,0:T(8,128)(2,1)}, u32[]{:S(2)}, u32[]{:S(2)}) collective-permute-start(bf16[512,256]{1,0:T(8,128)(2,1)} %get-tuple-element.36.refs_0_), channel_id=1, source_target_pairs={{0,16},{8,24},{16,0},{24,8},{1,17},{9,25},{17,1},{25,9},{2,18},{10... | collective-permute-start | bytes 786440 | tf_op jit(solution)/shard_map/ppermute | solution.py:365
  216.9 12.4 %collective-permute-start.16 = (bf16[512,256]{1,0:T(8,128)(2,1)}, bf16[512,256]{1,0:T(8,128)(2,1)}, u32[]{:S(2)}, u32[]{:S(2)}) collective-permute-start(bf16[512,256]{1,0:T(8,128)(2,1)} %get-tuple-element.36.refs_0_), channel_id=1, source_target_pairs={{0,8},{8,0},{16,24},{24,16},{1,9},{9,1},{17,25},{25,17},{2,10},{10... | collective-permute-start | bytes 786440 | tf_op jit(solution)/shard_map/ppermute | solution.py:365
  232.7 172.9 %all-gather.12.cloned.1.call-start = ((), (), s32[]{:S(2)}) async-start(), calls=%async_computation.2 | async-start | bytes 9437184 | tf_op jit(solution)/shard_map/all_gather | solution.py:471
  232.8 2.3 copy-start.2
  235.1 2.4 copy-start.5
  238.9 9.9 %copy-start.38 = (s32[4]{0:T(128)S(1)}, s32[4]{0:T(128)}, u32[]{:S(2)}) copy-start(s32[4]{0:T(128)} %param.7) | copy-start | bytes 52
  245.3 4.7 %collective-permute-start.21 = (f32[4,1024]{1,0:T(4,128)S(1)}, f32[4,1024]{1,0:T(4,128)S(1)}, u32[]{:S(2)}, u32[]{:S(2)}) collective-permute-start(f32[4,1024]{1,0:T(4,128)S(1)} %get-tuple-element.37.refs_0_), channel_id=1, source_target_pairs={{0,24},{8,16},{16,8},{24,0},{1,25},{9,17},{17,9},{25,1},{2,26},{10... | collective-permute-start | bytes 49160 | tf_op jit(solution)/shard_map/ppermute | solution.py:365
  246.7 3.7 collective-permute-start.20
  247.3 3.7 collective-permute-start.19
  251.0 2.4 copy-start.3
  253.4 2.3 copy-start.6
  257.0 20.4 %copy-start.7 = (bf16[9216,256]{1,0:T(8,128)(2,1)S(1)}, bf16[9216,256]{1,0:T(8,128)(2,1)}, u32[]{:S(2)}) copy-start(bf16[9216,256]{1,0:T(8,128)(2,1)} %all-gather.10.cloned.1.call-done.refs_7_.refs_5_.refs_8_) | copy-start | bytes 14155780
  257.0 20.4 %copy-start.33 = (f32[2,512,128]{2,1,0:T(8,128)S(1)}, f32[2,512,128]{2,1,0:T(8,128)}, u32[]{:S(2)}) copy-start(f32[2,512,128]{2,1,0:T(8,128)} %copy-done.32) | copy-start | bytes 1572868
  257.0 37.1 %slice-start.2 = ((s8[4718592]{0:T(1024)(128)(4,1)}), s8[4194304]{0:T(1024)(128)(4,1)S(1)}, s32[]{:S(2)}) async-start(s8[4718592]{0:T(1024)(128)(4,1)} %bitcast.94), calls=%async_computation.7 | async-start | bytes 8388608
  263.6 9.3 %collective-permute-start.22 = (bf16[512,256]{1,0:T(8,128)(2,1)S(1)}, bf16[512,256]{1,0:T(8,128)(2,1)S(1)}, u32[]{:S(2)}, u32[]{:S(2)}) collective-permute-start(bf16[512,256]{1,0:T(8,128)(2,1)S(1)} %get-tuple-element.40), channel_id=1, source_target_pairs={{0,8},{8,0},{16,24},{24,16},{1,9},{9,1},{17,25},{25,17},{2,10},{10... | collective-permute-start | bytes 786440 | tf_op jit(solution)/shard_map/ppermute | solution.py:365
  265.3 12.1 %collective-permute-start.23 = (bf16[512,256]{1,0:T(8,128)(2,1)S(1)}, bf16[512,256]{1,0:T(8,128)(2,1)S(1)}, u32[]{:S(2)}, u32[]{:S(2)}) collective-permute-start(bf16[512,256]{1,0:T(8,128)(2,1)S(1)} %get-tuple-element.41), channel_id=1, source_target_pairs={{0,16},{8,24},{16,0},{24,8},{1,17},{9,25},{17,1},{25,9},{2,18},{10... | collective-permute-start | bytes 786440 | tf_op jit(solution)/shard_map/ppermute | solution.py:365
  265.7 11.7 %collective-permute-start.24 = (bf16[512,256]{1,0:T(8,128)(2,1)S(1)}, bf16[512,256]{1,0:T(8,128)(2,1)S(1)}, u32[]{:S(2)}, u32[]{:S(2)}) collective-permute-start(bf16[512,256]{1,0:T(8,128)(2,1)S(1)} %get-tuple-element.42), channel_id=1, source_target_pairs={{0,24},{8,16},{16,8},{24,0},{1,25},{9,17},{17,9},{25,1},{2,26},{10... | collective-permute-start | bytes 786440 | tf_op jit(solution)/shard_map/ppermute | solution.py:365
  277.4 16.7 %slice-start.3 = ((s8[4718592]{0:T(1024)(128)(4,1)}), s8[524288]{0:T(1024)(128)(4,1)S(1)}, s32[]{:S(2)}) async-start(s8[4718592]{0:T(1024)(128)(4,1)} %bitcast.94), calls=%async_computation.8 | async-start | bytes 1048576
  277.4 16.7 %copy-start.31 = (f32[2,512,128]{2,1,0:T(8,128)S(1)}, f32[2,512,128]{2,1,0:T(8,128)}, u32[]{:S(2)}) copy-start(f32[2,512,128]{2,1,0:T(8,128)} %copy-done.30) | copy-start | bytes 1572868
  282.8 7.3 %collective-permute-start.25 = (bf16[512,256]{1,0:T(8,128)(2,1)S(1)}, bf16[512,256]{1,0:T(8,128)(2,1)S(1)}, u32[]{:S(2)}, u32[]{:S(2)}) collective-permute-start(bf16[512,256]{1,0:T(8,128)(2,1)S(1)} %get-tuple-element.45), channel_id=1, source_target_pairs={{0,8},{8,0},{16,24},{24,16},{1,9},{9,1},{17,25},{25,17},{2,10},{10... | collective-permute-start | bytes 786440 | tf_op jit(solution)/shard_map/ppermute | solution.py:365
  283.2 10.9 %collective-permute-start.26 = (bf16[512,256]{1,0:T(8,128)(2,1)S(1)}, bf16[512,256]{1,0:T(8,128)(2,1)S(1)}, u32[]{:S(2)}, u32[]{:S(2)}) collective-permute-start(bf16[512,256]{1,0:T(8,128)(2,1)S(1)} %get-tuple-element.46), channel_id=1, source_target_pairs={{0,16},{8,24},{16,0},{24,8},{1,17},{9,25},{17,1},{25,9},{2,18},{10... | collective-permute-start | bytes 786440 | tf_op jit(solution)/shard_map/ppermute | solution.py:365
  283.4 10.7 %collective-permute-start.27 = (bf16[512,256]{1,0:T(8,128)(2,1)S(1)}, bf16[512,256]{1,0:T(8,128)(2,1)S(1)}, u32[]{:S(2)}, u32[]{:S(2)}) collective-permute-start(bf16[512,256]{1,0:T(8,128)(2,1)S(1)} %get-tuple-element.47), channel_id=1, source_target_pairs={{0,24},{8,16},{16,8},{24,0},{1,25},{9,17},{17,9},{25,1},{2,26},{10... | collective-permute-start | bytes 786440 | tf_op jit(solution)/shard_map/ppermute | solution.py:365
  294.2 18.4 %copy-start.29 = (f32[2,512,128]{2,1,0:T(8,128)S(1)}, f32[2,512,128]{2,1,0:T(8,128)}, u32[]{:S(2)}) copy-start(f32[2,512,128]{2,1,0:T(8,128)} %copy-done.28) | copy-start | bytes 1572868
  298.6 6.7 %collective-permute-start.28 = (bf16[512,256]{1,0:T(8,128)(2,1)S(1)}, bf16[512,256]{1,0:T(8,128)(2,1)S(1)}, u32[]{:S(2)}, u32[]{:S(2)}) collective-permute-start(bf16[512,256]{1,0:T(8,128)(2,1)S(1)} %get-tuple-element.50), channel_id=1, source_target_pairs={{0,8},{8,0},{16,24},{24,16},{1,9},{9,1},{17,25},{25,17},{2,10},{10... | collective-permute-start | bytes 786440 | tf_op jit(solution)/shard_map/ppermute | solution.py:365
  299.9 12.6 %collective-permute-start.29 = (bf16[512,256]{1,0:T(8,128)(2,1)S(1)}, bf16[512,256]{1,0:T(8,128)(2,1)S(1)}, u32[]{:S(2)}, u32[]{:S(2)}) collective-permute-start(bf16[512,256]{1,0:T(8,128)(2,1)S(1)} %get-tuple-element.51), channel_id=1, source_target_pairs={{0,16},{8,24},{16,0},{24,8},{1,17},{9,25},{17,1},{25,9},{2,18},{10... | collective-permute-start | bytes 786440 | tf_op jit(solution)/shard_map/ppermute | solution.py:365
  301.4 11.1 %collective-permute-start.30 = (bf16[512,256]{1,0:T(8,128)(2,1)S(1)}, bf16[512,256]{1,0:T(8,128)(2,1)S(1)}, u32[]{:S(2)}, u32[]{:S(2)}) collective-permute-start(bf16[512,256]{1,0:T(8,128)(2,1)S(1)} %get-tuple-element.52), channel_id=1, source_target_pairs={{0,24},{8,16},{16,8},{24,0},{1,25},{9,17},{17,9},{25,1},{2,26},{10... | collective-permute-start | bytes 786440 | tf_op jit(solution)/shard_map/ppermute | solution.py:365
  313.9 7.4 %collective-permute-start.33 = (bf16[512,256]{1,0:T(8,128)(2,1)S(1)}, bf16[512,256]{1,0:T(8,128)(2,1)S(1)}, u32[]{:S(2)}, u32[]{:S(2)}) collective-permute-start(bf16[512,256]{1,0:T(8,128)(2,1)S(1)} %get-tuple-element.80), channel_id=1, source_target_pairs={{0,24},{8,16},{16,8},{24,0},{1,25},{9,17},{17,9},{25,1},{2,26},{10... | collective-permute-start | bytes 786440 | tf_op jit(solution)/shard_map/ppermute | solution.py:365
  315.7 8.3 %collective-permute-start.32 = (bf16[512,256]{1,0:T(8,128)(2,1)S(1)}, bf16[512,256]{1,0:T(8,128)(2,1)S(1)}, u32[]{:S(2)}, u32[]{:S(2)}) collective-permute-start(bf16[512,256]{1,0:T(8,128)(2,1)S(1)} %get-tuple-element.81), channel_id=1, source_target_pairs={{0,16},{8,24},{16,0},{24,8},{1,17},{9,25},{17,1},{25,9},{2,18},{10... | collective-permute-start | bytes 786440 | tf_op jit(solution)/shard_map/ppermute | solution.py:365
  315.7 8.3 %collective-permute-start.31 = (bf16[512,256]{1,0:T(8,128)(2,1)S(1)}, bf16[512,256]{1,0:T(8,128)(2,1)S(1)}, u32[]{:S(2)}, u32[]{:S(2)}) collective-permute-start(bf16[512,256]{1,0:T(8,128)(2,1)S(1)} %get-tuple-element.82), channel_id=1, source_target_pairs={{0,8},{8,0},{16,24},{24,16},{1,9},{9,1},{17,25},{25,17},{2,10},{10... | collective-permute-start | bytes 786440 | tf_op jit(solution)/shard_map/ppermute | solution.py:365
  (18 other events, 18.5 us)
Sparse Core Ops, SparseCore 0:
  11.2 60.0 all-gather.13
  75.1 67.3 all-gather.7
  144.9 53.5 all-gather.9
  232.9 79.9 all-gather.15
  325.5 80.1 all-gather.11
where the time goes:
time: 436 us; the launch traced here: 435 us
  waiting for transfers between devices  250 us (57%)
  local copies, waits for them, and re-layouts  50.3 us (12%)
  starting transfers between devices  44.7 us (10%)
  Pallas kernels  38.1 us (9%)
  matrix products  23.2 us (5%)
  other arithmetic  15.1 us (3%)
  between operations  14.4 us (3%)
    ppermute x27, waiting for transfers between devices, exchange(): lax.ppermute(values[k], 'section', [(i, i ^ k + 1) for i in range(section...  91.3 us
    ppermute x3, waiting for transfers between devices, shards(): down = lax.ppermute(down, 'dp', hops(step, -1, ring))  88.4 us
    all_gather x1, waiting for transfers between devices, shards(): raw_all = lax.all_gather(own_raw, 'dp', axis=0, tiled=True)  66.1 us
    ppermute x27, starting transfers between devices, exchange(): lax.ppermute(values[k], 'section', [(i, i ^ k + 1) for i in range(section...  33.8 us
    unnamed x87, local copies, waits for them, and re-layouts  32.8 us
    dot_general x1, matrix products, shards(): lax.dot_general(cols, raw_all, (((0,), (0,)), ((), ())), preferred_elemen...  23.2 us
    pallas_call x4, Pallas kernels, run_forward(): pl.pallas_call(functools.partial(forward_kernel, dims, block), out_shape=...  20.6 us
    pallas_call x4, Pallas kernels, run_backward(): pl.pallas_call(functools.partial(backward_kernel, dims, block, classes),...  17.5 us
  transfers between devices with their start and end apart: 39, of which 25 were waited for; matrix products, arithmetic and copies ran while one was open for 6% of the time, Pallas kernels for 7%

commit v1 on v0

--- a/solution.py
+++ b/solution.py
@@ -33,10 +33,18 @@
     slots = slots_of(block, sections)
     sources = list(sources)
 
-    def copies(arrays):
+    def copies(arrays, only=None):
+        result = []
         if len(arrays) == 1:
-            return [pltpu.make_async_copy(arrays[0], weights, sems.at[0])]
-        result = []
+            rows = weights.shape[0] // 9
+            for offset in range(9) if only is None else [only]:
+                part = pl.ds(offset * rows, rows)
+                result.append(
+                    pltpu.make_async_copy(
+                        arrays[0].at[part, :], weights.at[part, :], sems.at[offset]
+                    )
+                )
+            return result
         for which, source in enumerate(arrays):
             ring, depth = source.shape[:2]
             owner_core = core if which == 0 else 1 - core
@@ -47,7 +55,7 @@
                     pltpu.make_async_copy(
                         source.at[j],
                         weights.at[pl.ds(row, depth), :],
-                        sems.at[1 + which * ring + j],
+                        sems.at[9 + which * ring + j],
                     )
                 )
         return result
@@ -65,13 +73,14 @@
             for copy in copies(arrays):
                 copy.start()
 
-    def wait():
+    def wait(offset):
         for chosen, arrays in choices:
-
-            @pl.when(chosen)
-            def _():
-                for copy in copies(arrays):
-                    copy.wait()
+            if len(arrays) == 1 or offset == 0:
+
+                @pl.when(chosen)
+                def _():
+                    for copy in copies(arrays, offset if len(arrays) == 1 else None):
+                        copy.wait()
 
     return wait
 
@@ -97,10 +106,10 @@
         padded[scal[0] ^ k, 1 : height + 1, 1 : width + 1] = slices[k][...].reshape(
             height, width, group, lanes
         )
-    wait()
     total = jnp.zeros((rows, lanes), jnp.float32)
     for offset in range(9):
         r, c = divmod(offset, 3)
+        wait(offset)
         lhs = jnp.concatenate(
             [
                 padded[j, r : r + height, c : c + width].reshape(rows, lanes)
@@ -215,11 +224,12 @@
     if stage == 2:
         return
     padded[1 : height + 1, 1 : width + 1] = raw.reshape(height, width, group, lanes)
-    wait()
     for k in list(range(1, sections)) + [0]:
         total = jnp.zeros((rows, lanes), jnp.float32)
         for offset in range(9):
             r, c = divmod(offset, 3)
+            if k == 1:
+                wait(offset)
             lhs = padded[2 - r : 2 - r + height, 2 - c : 2 - c + width].reshape(rows, lanes)
             row = pl.multiple_of(offset * channels + (scal[0] ^ k) * lanes, lanes)
             total += lax.dot_general(
@@ -234,6 +244,10 @@
             sends[k - 1][...] = total.astype(jnp.bfloat16)
 
 
+def stay(arrays):
+    return [pltpu.with_memory_space_constraint(array, pltpu.HBM) for array in arrays]
+
+
 def vmem(count):
     return [pl.BlockSpec(memory_space=VMEM)] * count
 
@@ -247,7 +261,7 @@
         jax.ShapeDtypeStruct((rows, lanes), jnp.bfloat16),
         jax.ShapeDtypeStruct((lanes // 128, rows, 128), jnp.float32),
     ]
-    operands = [scal, *slices, *sources]
+    operands = [scal, *slices, *stay(sources)]
     extra = []
     if last:
         shapes.append(jax.ShapeDtypeStruct((images, readout.shape[1]), jnp.float32))
@@ -265,7 +279,7 @@
             VMEM((depth, lanes), jnp.bfloat16),
             VMEM((sections, height + 2, width + 2, images * steps, lanes), jnp.bfloat16),
             VMEM((lanes // 128, rows, 128), jnp.float32),
-            pltpu.SemaphoreType.DMA((1 + devices,)),
+            pltpu.SemaphoreType.DMA((9 + devices,)),
         ],
         compiler_params=pltpu.CompilerParams(vmem_limit_bytes=LIMIT),
         cost_estimate=pl.CostEstimate(
@@ -290,7 +304,7 @@
     cost = 0
     if stage < 2:
         depth = 9 * sections * lanes
-        operands += list(sources)
+        operands += stay(sources)
         specs += [pl.BlockSpec(memory_space=pltpu.HBM)] * len(sources)
         shapes = [half, full] + [half] * (sections - 1)
         work = (
@@ -299,7 +313,7 @@
                 VMEM((height + 2, width + 2, images * steps, lanes), jnp.bfloat16),
             ]
             + work
-            + [pltpu.SemaphoreType.DMA((1 + devices,))]
+            + [pltpu.SemaphoreType.DMA((9 + devices,))]
         )
         cost = depth
     else:
@@ -417,7 +431,7 @@
         piece = after(piece_of(slot), *gates) if gates else piece_of(slot)
         gathered = lax.all_gather(piece, "dp", axis=0, tiled=True)
         slots[slot] = [gathered]
-        gates = [gathered] + done.get((2, 1) if slot == 0 else (slot + 1, ring - 1), [])
+        gates = [gathered] + done.get((2, 1) if slot == 0 else (slot + 1, max(1, ring - 2)), [])
     for b in range(sections):
         forward(b)
     result = results[-1]

time: 436 us -> 458 us (1.050)
  local copies, waits for them, and re-layouts: 50.3 us -> 26.2 us
  waiting for transfers between devices: 250 us -> 274 us
  Pallas kernels: 38.1 us -> 56 us
    all_gather x3, waiting for transfers between devices: 3.7 us -> 32.9 us  [shards(): gathered = lax.all_gather(piece, 'dp', axis=0, tiled=True)]
    unnamed x87 -> x31, local copies, waits for them, and re-layouts: 32.8 us -> 8.48 us
    ppermute x3, waiting for transfers between devices: 88.4 us -> 67 us  [shards(): down = lax.ppermute(down, 'dp', hops(step, -1, ring))]
    pallas_call x4, Pallas kernels: 20.6 us -> 32.6 us  [run_forward(): pl.pallas_call(functools.partial(forward_kernel, dims, block), out_shape=...]
    all_gather x1, waiting for transfers between devices: 66.1 us -> 76.3 us  [shards(): raw_all = lax.all_gather(own_raw, 'dp', axis=0, tiled=True)]
    all_gather x1, waiting for transfers between devices: 0.02 us -> 8.59 us  [shards(): x_all = lax.all_gather(own_x, 'dp')]
    pallas_call x4, Pallas kernels: 17.5 us -> 23.3 us  [run_backward(): pl.pallas_call(functools.partial(backward_kernel, dims, block, classes),...]
  transfers between devices with their start and end apart: 39 -> 39, of which waited for: 25 -> 27; matrix products, arithmetic and copies ran while one was open for 6% -> 6% of each run, Pallas kernels for 7% -> 10%
where the time goes in v1:
time: 458 us; the launch traced here: 457 us
  waiting for transfers between devices  274 us (60%)
  Pallas kernels  56 us (12%)
  starting transfers between devices  46.2 us (10%)
  local copies, waits for them, and re-layouts  26.2 us (6%)
  matrix products  23.2 us (5%)
  other arithmetic  17.1 us (4%)
  between operations  14.2 us (3%)
    ppermute x27, waiting for transfers between devices, exchange(): lax.ppermute(values[k], 'section', [(i, i ^ k + 1) for i in range(section...  89.2 us
    all_gather x1, waiting for transfers between devices, shards(): raw_all = lax.all_gather(own_raw, 'dp', axis=0, tiled=True)  76.3 us
    ppermute x3, waiting for transfers between devices, shards(): down = lax.ppermute(down, 'dp', hops(step, -1, ring))  67 us
    ppermute x27, starting transfers between devices, exchange(): lax.ppermute(values[k], 'section', [(i, i ^ k + 1) for i in range(section...  34.2 us
    all_gather x3, waiting for transfers between devices, shards(): gathered = lax.all_gather(piece, 'dp', axis=0, tiled=True)  32.9 us
    pallas_call x4, Pallas kernels, run_forward(): pl.pallas_call(functools.partial(forward_kernel, dims, block), out_shape=...  32.6 us
    pallas_call x4, Pallas kernels, run_backward(): pl.pallas_call(functools.partial(backward_kernel, dims, block, classes),...  23.3 us
    dot_general x1, matrix products, shards(): lax.dot_general(cols, raw_all, (((0,), (0,)), ((), ())), preferred_elemen...  23.2 us
  transfers between devices with their start and end apart: 39, of which 27 were waited for; matrix products, arithmetic and copies ran while one was open for 6% of the time, Pallas kernels for 10%

profile of v1, /device:TPU:0, one launch (start us, length us, event | category | flops | bytes accessed | tf_op | source)
XLA Modules:
  0.0 456.9 jit_solution(18167628313910734023)
XLA Ops:
  7.2 3.9 fusion.3
  11.2 3.0 collective-permute-start
  14.2 1.5 collective-permute-start.1
  15.7 1.3 constant_dynamic-slice_fusion.1
  17.4 2.8 copy.9
  20.3 1.4 constant_dynamic-slice_fusion.3
  21.6 6.9 %collective-permute-done = bf16[1152,256]{1,0:T(8,128)(2,1)S(1)} collective-permute-done((bf16[1152,256]{1,0:T(8,128)(2,1)}, bf16[1152,256]{1,0:T(8,128)(2,1)S(1)}, u32[]{:S(2)}, u32[]{:S(2)}) %collective-permute-start) | collective-permute-done | bytes 589856 | tf_op jit(solution)/shard_map/ppermute | solution.py:379
  28.5 13.4 %collective-permute-done.1 = bf16[1152,256]{1,0:T(8,128)(2,1)} collective-permute-done((bf16[1152,256]{1,0:T(8,128)(2,1)}, bf16[1152,256]{1,0:T(8,128)(2,1)}, u32[]{:S(2)}, u32[]{:S(2)}) %collective-permute-start.1) | collective-permute-done | bytes 589856 | tf_op jit(solution)/shard_map/ppermute | solution.py:379
  41.9 1.5 pad_maximum_fusion
  43.5 1.1 dynamic-slice_bitcast_fusion
  44.6 1.3 collective-permute-start.4
  45.9 5.4 %collective-permute-start.3 = (bf16[1152,256]{1,0:T(8,128)(2,1)S(1)}, bf16[1152,256]{1,0:T(8,128)(2,1)}, u32[]{:S(2)}, u32[]{:S(2)}) collective-permute-start(bf16[1152,256]{1,0:T(8,128)(2,1)S(1)} %bitcast.113), channel_id=1, source_target_pairs={{0,2},{1,3},{2,4},{3,5},{4,6},{5,7},{8,10},{9,11},{10,12},{11,13},... | collective-permute-start | bytes 1769480 | tf_op jit(solution)/shard_map/ppermute | solution.py:421
  51.3 23.7 %collective-permute-done.4 = bf16[1152,256]{1,0:T(8,128)(2,1)S(1)} collective-permute-done((bf16[1152,256]{1,0:T(8,128)(2,1)S(1)}, bf16[1152,256]{1,0:T(8,128)(2,1)S(1)}, u32[]{:S(2)}, u32[]{:S(2)}) %collective-permute-start.4) | collective-permute-done | bytes 589856 | tf_op jit(solution)/shard_map/ppermute | solution.py:422
  75.1 1.3 collective-permute-start.10
  76.4 1.5 collective-permute-start.8
  77.9 21.4 %collective-permute-done.10 = bf16[1152,256]{1,0:T(8,128)(2,1)S(1)} collective-permute-done((bf16[1152,256]{1,0:T(8,128)(2,1)S(1)}, bf16[1152,256]{1,0:T(8,128)(2,1)S(1)}, u32[]{:S(2)}, u32[]{:S(2)}) %collective-permute-start.10) | collective-permute-done | bytes 589856 | tf_op jit(solution)/shard_map/ppermute | solution.py:422
  100.1 32.9 %all-gather.8.cloned.1.call-done.refs_5_.refs_6_ = bf16[9216,256]{1,0:T(8,128)(2,1)} async-done(((bf16[1152,256]{1,0:T(8,128)(2,1)}), bf16[9216,256]{1,0:T(8,128)(2,1)}) %all-gather.8.cloned.1.call-update) | async-done | bytes 4718608 | tf_op jit(solution)/shard_map/all_gather | solution.py:432
  133.1 1.3 collective-permute-start.11
  135.3 1.1 select_bitcast_fusion.1
  136.4 21.9 %collective-permute-done.11 = bf16[1152,256]{1,0:T(8,128)(2,1)} collective-permute-done((bf16[1152,256]{1,0:T(8,128)(2,1)}, bf16[1152,256]{1,0:T(8,128)(2,1)}, u32[]{:S(2)}, u32[]{:S(2)}) %collective-permute-start.11) | collective-permute-done | bytes 589856 | tf_op jit(solution)/shard_map/ppermute | solution.py:422
  158.3 1.1 select_bitcast_fusion
  159.5 1.7 pad_maximum_fusion.1.refs_6_.refs_5_.refs_7_
  161.3 7.2 %forward_block.4 = (bf16[512,256]{1,0:T(8,128)(2,1)S(1)}, f32[2,512,128]{2,1,0:T(8,128)S(1)}) custom-call(s32[3]{0:T(128)S(1)} %pad_add_fusion.scal, bf16[512,256]{1,0:T(8,128)(2,1)S(1)} %get-tuple-element.86.refs_0_, bf16[512,256]{1,0:T(8,128)(2,1)S(1)} %get-tuple-element.85.refs_1_, bf16[512,256]{1,0:T(8,128)(2,1)S(1)} %get-tuple-element.84.refs_2_, ...), custom_call_target="tpu_custom_call" | custom-call | flops 2415919104 | bytes 4718592 | tf_op jit(solution)/shard_map/forward_block/pallas_call | solution.py:270
  169.3 3.1 collective-permute-start.7
  173.0 6.6 %collective-permute-done.7.refs_3_ = bf16[512,256]{1,0:T(8,128)(2,1)S(1)} collective-permute-done((bf16[512,256]{1,0:T(8,128)(2,1)S(1)}, bf16[512,256]{1,0:T(8,128)(2,1)S(1)}, u32[]{:S(2)}, u32[]{:S(2)}) %collective-permute-start.7) | collective-permute-done | bytes 262176 | tf_op jit(solution)/shard_map/ppermute | solution.py:379
  179.6 5.4 %collective-permute-done.6.refs_2_ = bf16[512,256]{1,0:T(8,128)(2,1)S(1)} collective-permute-done((bf16[512,256]{1,0:T(8,128)(2,1)S(1)}, bf16[512,256]{1,0:T(8,128)(2,1)S(1)}, u32[]{:S(2)}, u32[]{:S(2)}) %collective-permute-start.6) | collective-permute-done | bytes 262176 | tf_op jit(solution)/shard_map/ppermute | solution.py:379
  185.0 7.2 %forward_block.5 = (bf16[512,256]{1,0:T(8,128)(2,1)S(1)}, f32[2,512,128]{2,1,0:T(8,128)S(1)}) custom-call(s32[3]{0:T(128)S(1)} %pad_add_fusion.scal, bf16[512,256]{1,0:T(8,128)(2,1)S(1)} %get-tuple-element.33.refs_0_, bf16[512,256]{1,0:T(8,128)(2,1)S(1)} %collective-permute-done.5.refs_1_, bf16[512,256]{1,0:T(8,128)(2,1)S(1)} %collective-permute-done.6.refs_2_, ...), custom_call_target="tpu_custom_call" | custom-call | flops 2415919104 | bytes 4718592 | tf_op jit(solution)/shard_map/forward_block/pallas_call | solution.py:270
  193.0 3.0 collective-permute-start.15
  197.2 6.1 %collective-permute-done.15.refs_3_ = bf16[512,256]{1,0:T(8,128)(2,1)S(1)} collective-permute-done((bf16[512,256]{1,0:T(8,128)(2,1)S(1)}, bf16[512,256]{1,0:T(8,128)(2,1)S(1)}, u32[]{:S(2)}, u32[]{:S(2)}) %collective-permute-start.15) | collective-permute-done | bytes 262176 | tf_op jit(solution)/shard_map/ppermute | solution.py:379
  204.0 4.0 collective-permute-done.14.refs_2_
  212.8 9.2 %forward_block.6 = (bf16[512,256]{1,0:T(8,128)(2,1)}, f32[2,512,128]{2,1,0:T(8,128)S(1)}) custom-call(s32[3]{0:T(128)S(1)} %pad_add_fusion.scal, bf16[512,256]{1,0:T(8,128)(2,1)S(1)} %get-tuple-element.34.refs_0_, bf16[512,256]{1,0:T(8,128)(2,1)S(1)} %copy-done.5, bf16[512,256]{1,0:T(8,128)(2,1)S(1)} %copy-done.3, bf16[512,256]{1,0:T(8,128)(2,1)S(1)} %copy-done.1, ...), custom_call_target="tpu_custom_call" | custom-call | flops 2415919104 | bytes 4718592 | tf_op jit(solution)/shard_map/forward_block/pallas_call | solution.py:270
  223.7 1.5 collective-permute-start.17
  226.2 7.0 %collective-permute-done.18.refs_3_ = bf16[512,256]{1,0:T(8,128)(2,1)} collective-permute-done((bf16[512,256]{1,0:T(8,128)(2,1)}, bf16[512,256]{1,0:T(8,128)(2,1)}, u32[]{:S(2)}, u32[]{:S(2)}) %collective-permute-start.18) | collective-permute-done | bytes 262176 | tf_op jit(solution)/shard_map/ppermute | solution.py:379
  233.2 4.1 collective-permute-done.17.refs_2_
  237.3 1.9 maximum_select_fusion
  239.2 1.1 pad_maximum_fusion.5
  240.7 9.0 %forward_block.7 = (bf16[512,256]{1,0:T(8,128)(2,1)}, f32[2,512,128]{2,1,0:T(8,128)S(1)}, f32[4,1024]{1,0:T(4,128)S(1)}) custom-call(s32[3]{0:T(128)S(1)} %pad_add_fusion.scal, bf16[512,256]{1,0:T(8,128)(2,1)} %get-tuple-element.36.refs_0_, bf16[512,256]{1,0:T(8,128)(2,1)} %collective-permute-done.16.refs_1_, ...), custom_call_target="tpu_custom_call" | custom-call | flops 2415919104 | bytes 4718592 | tf_op jit(solution)/shard_map/forward_block/pallas_call | solution.py:270
  249.7 1.5 collective-permute-start.21
  251.8 1.4 collective-permute-start.19
  255.6 8.5 %backward_block.4 = (bf16[512,256]{1,0:T(8,128)(2,1)S(1)}, f32[512,256]{1,0:T(8,128)S(1)}, bf16[512,256]{1,0:T(8,128)(2,1)S(1)}, bf16[512,256]{1,0:T(8,128)(2,1)S(1)}, bf16[512,256]{1,0:T(8,128)(2,1)S(1)}) custom-call(s32[3]{0:T(128)S(1)} %pad_add_fusion.scal, f32[4,1024]{1,0:T(4,128)S(1)} %get-tuple-element.37.refs_0_, ...), custom_call_target="tpu_custom_call" | custom-call | flops 2429026304 | bytes 5767168 | tf_op jit(solution)/shard_map/backward_block/pallas_call | solution.py:321
  264.1 1.5 collective-permute-start.22
  266.2 1.5 collective-permute-start.24
  267.6 5.8 %collective-permute-done.22.refs_1_ = bf16[512,256]{1,0:T(8,128)(2,1)S(1)} collective-permute-done((bf16[512,256]{1,0:T(8,128)(2,1)S(1)}, bf16[512,256]{1,0:T(8,128)(2,1)S(1)}, u32[]{:S(2)}, u32[]{:S(2)}) %collective-permute-start.22) | collective-permute-done | bytes 262176 | tf_op jit(solution)/shard_map/ppermute | solution.py:379
  273.4 4.3 collective-permute-done.23.refs_2_
  277.7 7.3 %backward_block.5 = (bf16[512,256]{1,0:T(8,128)(2,1)S(1)}, f32[512,256]{1,0:T(8,128)S(1)}, bf16[512,256]{1,0:T(8,128)(2,1)S(1)}, bf16[512,256]{1,0:T(8,128)(2,1)S(1)}, bf16[512,256]{1,0:T(8,128)(2,1)S(1)}) custom-call(s32[3]{0:T(128)S(1)} %pad_add_fusion.scal, f32[512,256]{1,0:T(8,128)S(1)} %get-tuple-element.39.refs_0_, ...), custom_call_target="tpu_custom_call" | custom-call | flops 2429026304 | bytes 5767168 | tf_op jit(solution)/shard_map/backward_block/pallas_call | solution.py:321
  285.9 2.7 collective-permute-start.27
  288.6 4.9 %collective-permute-done.25.refs_1_ = bf16[512,256]{1,0:T(8,128)(2,1)S(1)} collective-permute-done((bf16[512,256]{1,0:T(8,128)(2,1)S(1)}, bf16[512,256]{1,0:T(8,128)(2,1)S(1)}, u32[]{:S(2)}, u32[]{:S(2)}) %collective-permute-start.25) | collective-permute-done | bytes 262176 | tf_op jit(solution)/shard_map/ppermute | solution.py:379
  293.5 2.9 collective-permute-done.26.refs_2_
  296.4 6.4 %backward_block.6 = (bf16[512,256]{1,0:T(8,128)(2,1)S(1)}, f32[512,256]{1,0:T(8,128)S(1)}, bf16[512,256]{1,0:T(8,128)(2,1)S(1)}, bf16[512,256]{1,0:T(8,128)(2,1)S(1)}, bf16[512,256]{1,0:T(8,128)(2,1)S(1)}) custom-call(s32[3]{0:T(128)S(1)} %pad_add_fusion.scal, f32[512,256]{1,0:T(8,128)S(1)} %get-tuple-element.44.refs_0_, ...), custom_call_target="tpu_custom_call" | custom-call | flops 2429026304 | bytes 5767168 | tf_op jit(solution)/shard_map/backward_block/pallas_call | solution.py:321
  302.8 1.7 collective-permute-start.28
  304.5 1.5 collective-permute-start.29
  306.9 3.0 collective-permute-done.28.refs_1_
  309.9 3.4 collective-permute-done.29.refs_2_
  313.3 1.8 collective-permute-done.30.refs_3_
  316.5 1.8 collective-permute-start.33
  318.6 1.5 collective-permute-start.31
  320.1 4.2 collective-permute-done.33
  324.3 2.7 collective-permute-done.32
  327.2 1.1 pad_maximum_fusion.4
  328.4 8.6 %all-gather.16.cloned.1.call-done = bf16[4096,1024]{1,0:T(8,128)(2,1)} async-done(((bf16[512,1024]{1,0:T(8,128)(2,1)}), bf16[4096,1024]{1,0:T(8,128)(2,1)}) %all-gather.16.cloned.1.call-update) | async-done | bytes 8388624 | tf_op jit(solution)/shard_map/all_gather | solution.py:452
  337.0 6.8 %pad_dynamic-slice_fusion = (bf16[8,4,4,32,1024]{4,3,2,1,0:T(8,128)(2,1)S(1)}, bf16[8,4,4,32,1024]{4,3,2,1,0:T(8,128)(2,1)S(1)}) fusion(s32[]{:T(128)S(6)} %select_n.180, s32[]{:T(128)S(6)} %select_n.182, bf16[8,4,4,32,1024]{4,3,2,1,0:T(8,128)(2,1)} %bitcast.110, s32[]{:T(128)S(6)} %select_n.176, s32[]{:T(128)S(6)} %select_n.178), kind=kLoop, calls=%fused_computation | loop fusion | bytes 25165840 | tf_op jit(solution)/shard_map/dynamic_slice | solution.py:477
  343.8 7.1 %fusion = bf16[4096,1152]{1,0:T(8,128)(2,1)} fusion(s32[]{:T(128)S(6)} %select_n.184, bf16[4096,1024]{1,0:T(8,128)(2,1)S(1)} %bitcast.109, bf16[4096,1024]{1,0:T(8,128)(2,1)S(1)} %bitcast.108), kind=kLoop, calls=%fused_computation.4 | loop fusion | flops 18874368 | bytes 26214404 | tf_op jit(solution)/shard_map/concatenate | solution.py:483
  350.9 76.3 %all-gather.12.cloned.1.call-done = bf16[4096,1024]{1,0:T(8,128)(2,1)} async-done(((bf16[512,1024]{1,0:T(8,128)(2,1)}), bf16[4096,1024]{1,0:T(8,128)(2,1)}) %all-gather.12.cloned.1.call-update) | async-done | bytes 8388624 | tf_op jit(solution)/shard_map/all_gather | solution.py:485
  427.2 23.2 %divide_subtract_fusion = (f32[1,1152,1024]{2,1,0:T(8,128)}, f32[1,1152,1024]{2,1,0:T(8,128)}, f32[1,1152,1024]{2,1,0:T(8,128)}) fusion(f32[1,1152,1024]{2,1,0:T(8,128)} %param.9, f32[1,1152,1024]{2,1,0:T(8,128)} %param.10, f32[1,1152,1024]{2,1,0:T(8,128)} %param.11, bf16[4096,1152]{1,0:T(8,128)(2,1)} %fusion, ...), kind=kOutput, calls=%fused_computation.9 | convolution fusion | flops 9676652544 | bytes 46137344 | tf_op jit(solution)/shard_map/dot_general | solution.py:487
  (82 shorter events, 21.5 us)
Async XLA Ops:
  7.2 67.9 %all-gather.14.cloned.1.call-start = ((), (), s32[]{:S(2)}) async-start(), calls=%async_computation.3 | async-start | bytes 5308416 | tf_op jit(solution)/shard_map/all_gather | solution.py:432
  11.1 121.9 %all-gather.8.cloned.1.call-start = ((), (), s32[]{:S(2)}) async-start(), calls=%async_computation | async-start | bytes 5308416 | tf_op jit(solution)/shard_map/all_gather | solution.py:432
  11.2 17.4 %collective-permute-start = (bf16[1152,256]{1,0:T(8,128)(2,1)}, bf16[1152,256]{1,0:T(8,128)(2,1)S(1)}, u32[]{:S(2)}, u32[]{:S(2)}) collective-permute-start(bf16[1152,256]{1,0:T(8,128)(2,1)} %get-tuple-element.64), channel_id=1, source_target_pairs={{0,8},{8,0},{16,24},{24,16},{1,9},{9,1},{17,25},{25,17},{2,10},{10... | collective-permute-start | bytes 1769480 | tf_op jit(solution)/shard_map/ppermute | solution.py:379
  14.2 27.7 %collective-permute-start.1 = (bf16[1152,256]{1,0:T(8,128)(2,1)}, bf16[1152,256]{1,0:T(8,128)(2,1)}, u32[]{:S(2)}, u32[]{:S(2)}) collective-permute-start(bf16[1152,256]{1,0:T(8,128)(2,1)} %get-tuple-element.65), channel_id=1, source_target_pairs={{0,16},{8,24},{16,0},{24,8},{1,17},{9,25},{17,1},{25,9},{2,18},{10... | collective-permute-start | bytes 1769480 | tf_op jit(solution)/shard_map/ppermute | solution.py:379
  15.7 26.2 %collective-permute-start.2 = (bf16[1152,256]{1,0:T(8,128)(2,1)}, bf16[1152,256]{1,0:T(8,128)(2,1)}, u32[]{:S(2)}, u32[]{:S(2)}) collective-permute-start(bf16[1152,256]{1,0:T(8,128)(2,1)} %get-tuple-element.67), channel_id=1, source_target_pairs={{0,24},{8,16},{16,8},{24,0},{1,25},{9,17},{17,9},{25,1},{2,26},{10... | collective-permute-start | bytes 1769480 | tf_op jit(solution)/shard_map/ppermute | solution.py:379
  15.7 26.2 %copy-start.12 = (bf16[1,1152,256]{2,1,0:T(8,128)(2,1)S(1)}, bf16[1,1152,256]{2,1,0:T(8,128)(2,1)}, u32[]{:S(2)}) copy-start(bf16[1,1152,256]{2,1,0:T(8,128)(2,1)} %get-tuple-element.66) | copy-start | bytes 1769476
  44.6 30.4 %collective-permute-start.4 = (bf16[1152,256]{1,0:T(8,128)(2,1)S(1)}, bf16[1152,256]{1,0:T(8,128)(2,1)S(1)}, u32[]{:S(2)}, u32[]{:S(2)}) collective-permute-start(bf16[1152,256]{1,0:T(8,128)(2,1)S(1)} %bitcast.112), channel_id=1, source_target_pairs={{2,0},{3,1},{4,2},{5,3},{6,4},{7,5},{10,8},{11,9},{12,10},{13,11},... | collective-permute-start | bytes 1769480 | tf_op jit(solution)/shard_map/ppermute | solution.py:422
  45.9 29.1 %collective-permute-start.3 = (bf16[1152,256]{1,0:T(8,128)(2,1)S(1)}, bf16[1152,256]{1,0:T(8,128)(2,1)}, u32[]{:S(2)}, u32[]{:S(2)}) collective-permute-start(bf16[1152,256]{1,0:T(8,128)(2,1)S(1)} %bitcast.113), channel_id=1, source_target_pairs={{0,2},{1,3},{2,4},{3,5},{4,6},{5,7},{8,10},{9,11},{10,12},{11,13},... | collective-permute-start | bytes 1769480 | tf_op jit(solution)/shard_map/ppermute | solution.py:421
  75.0 134.9 %all-gather.10.cloned.1.call-start = ((), (), s32[]{:S(2)}) async-start(), calls=%async_computation.1 | async-start | bytes 5308416 | tf_op jit(solution)/shard_map/all_gather | solution.py:432
  75.1 24.2 %collective-permute-start.10 = (bf16[1152,256]{1,0:T(8,128)(2,1)S(1)}, bf16[1152,256]{1,0:T(8,128)(2,1)S(1)}, u32[]{:S(2)}, u32[]{:S(2)}) collective-permute-start(bf16[1152,256]{1,0:T(8,128)(2,1)S(1)} %collective-permute-done.4), channel_id=1, source_target_pairs={{2,0},{3,1},{4,2},{5,3},{10,8},{11,9},{12,10},{13,11},{18,16},{19,... | collective-permute-start | bytes 1769480 | tf_op jit(solution)/shard_map/ppermute | solution.py:422
  76.4 23.7 %collective-permute-start.8 = (bf16[1152,256]{1,0:T(8,128)(2,1)}, bf16[1152,256]{1,0:T(8,128)(2,1)}, u32[]{:S(2)}, u32[]{:S(2)}) collective-permute-start(bf16[1152,256]{1,0:T(8,128)(2,1)} %collective-permute-done.3), channel_id=1, source_target_pairs={{2,4},{3,5},{4,6},{5,7},{10,12},{11,13},{12,14},{13,15},{18,20},{1... | collective-permute-start | bytes 1769480 | tf_op jit(solution)/shard_map/ppermute | solution.py:421
  99.3 0.8 copy-start.13
  133.0 204.0 %all-gather.16.cloned.1.call-start = ((), (), s32[]{:S(2)}) async-start(), calls=%async_computation.4 | async-start | bytes 9437184 | tf_op jit(solution)/shard_map/all_gather | solution.py:452
  133.1 25.2 %collective-permute-start.11 = (bf16[1152,256]{1,0:T(8,128)(2,1)}, bf16[1152,256]{1,0:T(8,128)(2,1)}, u32[]{:S(2)}, u32[]{:S(2)}) collective-permute-start(bf16[1152,256]{1,0:T(8,128)(2,1)} %copy-done.13), channel_id=1, source_target_pairs={{2,0},{3,1},{10,8},{11,9},{18,16},{19,17},{26,24},{27,25}} | collective-permute-start | bytes 1769480 | tf_op jit(solution)/shard_map/ppermute | solution.py:422
  134.4 25.0 %collective-permute-start.9 = (bf16[1152,256]{1,0:T(8,128)(2,1)}, bf16[1152,256]{1,0:T(8,128)(2,1)S(1)}, u32[]{:S(2)}, u32[]{:S(2)}) collective-permute-start(bf16[1152,256]{1,0:T(8,128)(2,1)} %collective-permute-done.8), channel_id=1, source_target_pairs={{4,6},{5,7},{12,14},{13,15},{20,22},{21,23},{28,30},{29,31}} | collective-permute-start | bytes 1769480 | tf_op jit(solution)/shard_map/ppermute | solution.py:421
  161.2 11.8 %collective-permute-start.12 = (bf16[4,1152,256]{2,1,0:T(8,128)(2,1)}, bf16[4,1152,256]{2,1,0:T(8,128)(2,1)}, u32[]{:S(2)}, u32[]{:S(2)}) collective-permute-start(bf16[4,1152,256]{2,1,0:T(8,128)(2,1)} %pad_maximum_fusion.1.refs_6_.refs_5_.refs_7_), channel_id=1, source_target_pairs={{0,1},{1,0},{2,3},{3,2},{4,5},{5,4},{6,7},{7,6},{8,9},{9,8},{10,11... | collective-permute-start | bytes 7077896 | tf_op jit(solution)/shard_map/ppermute | solution.py:351
  168.5 0.8 copy-start.6
  169.3 10.3 %collective-permute-start.7 = (bf16[512,256]{1,0:T(8,128)(2,1)S(1)}, bf16[512,256]{1,0:T(8,128)(2,1)S(1)}, u32[]{:S(2)}, u32[]{:S(2)}) collective-permute-start(bf16[512,256]{1,0:T(8,128)(2,1)S(1)} %get-tuple-element.33.refs_0_), channel_id=1, source_target_pairs={{0,24},{8,16},{16,8},{24,0},{1,25},{9,17},{17,9},{25,1},{2,26},{10... | collective-permute-start | bytes 786440 | tf_op jit(solution)/shard_map/ppermute | solution.py:379
  172.4 12.6 %collective-permute-start.6 = (bf16[512,256]{1,0:T(8,128)(2,1)S(1)}, bf16[512,256]{1,0:T(8,128)(2,1)S(1)}, u32[]{:S(2)}, u32[]{:S(2)}) collective-permute-start(bf16[512,256]{1,0:T(8,128)(2,1)S(1)} %get-tuple-element.33.refs_0_), channel_id=1, source_target_pairs={{0,16},{8,24},{16,0},{24,8},{1,17},{9,25},{17,1},{25,9},{2,18},{10... | collective-permute-start | bytes 786440 | tf_op jit(solution)/shard_map/ppermute | solution.py:379
  172.4 12.6 %collective-permute-start.5 = (bf16[512,256]{1,0:T(8,128)(2,1)S(1)}, bf16[512,256]{1,0:T(8,128)(2,1)S(1)}, u32[]{:S(2)}, u32[]{:S(2)}) collective-permute-start(bf16[512,256]{1,0:T(8,128)(2,1)S(1)} %get-tuple-element.33.refs_0_), channel_id=1, source_target_pairs={{0,8},{8,0},{16,24},{24,16},{1,9},{9,1},{17,25},{25,17},{2,10},{10... | collective-permute-start | bytes 786440 | tf_op jit(solution)/shard_map/ppermute | solution.py:379
  192.2 0.8 copy-start.8
  193.0 10.2 %collective-permute-start.15 = (bf16[512,256]{1,0:T(8,128)(2,1)S(1)}, bf16[512,256]{1,0:T(8,128)(2,1)S(1)}, u32[]{:S(2)}, u32[]{:S(2)}) collective-permute-start(bf16[512,256]{1,0:T(8,128)(2,1)S(1)} %get-tuple-element.34.refs_0_), channel_id=1, source_target_pairs={{0,24},{8,16},{16,8},{24,0},{1,25},{9,17},{17,9},{25,1},{2,26},{10... | collective-permute-start | bytes 786440 | tf_op jit(solution)/shard_map/ppermute | solution.py:379
  196.1 11.9 %collective-permute-start.14 = (bf16[512,256]{1,0:T(8,128)(2,1)S(1)}, bf16[512,256]{1,0:T(8,128)(2,1)S(1)}, u32[]{:S(2)}, u32[]{:S(2)}) collective-permute-start(bf16[512,256]{1,0:T(8,128)(2,1)S(1)} %get-tuple-element.34.refs_0_), channel_id=1, source_target_pairs={{0,16},{8,24},{16,0},{24,8},{1,17},{9,25},{17,1},{25,9},{2,18},{10... | collective-permute-start | bytes 786440 | tf_op jit(solution)/shard_map/ppermute | solution.py:379
  196.3 12.9 %collective-permute-start.13 = (bf16[512,256]{1,0:T(8,128)(2,1)S(1)}, bf16[512,256]{1,0:T(8,128)(2,1)S(1)}, u32[]{:S(2)}, u32[]{:S(2)}) collective-permute-start(bf16[512,256]{1,0:T(8,128)(2,1)S(1)} %get-tuple-element.34.refs_0_), channel_id=1, source_target_pairs={{0,8},{8,0},{16,24},{24,16},{1,9},{9,1},{17,25},{25,17},{2,10},{10... | collective-permute-start | bytes 786440 | tf_op jit(solution)/shard_map/ppermute | solution.py:379
  203.3 0.7 copy-start
  208.0 0.7 copy-start.2
  209.2 0.7 copy-start.4
  209.9 1.0 copy-start.1
  210.8 0.9 copy-start.3
  211.8 0.9 copy-start.5
  221.9 0.8 copy-start.10
  222.7 10.5 %collective-permute-start.18 = (bf16[512,256]{1,0:T(8,128)(2,1)}, bf16[512,256]{1,0:T(8,128)(2,1)}, u32[]{:S(2)}, u32[]{:S(2)}) collective-permute-start(bf16[512,256]{1,0:T(8,128)(2,1)} %get-tuple-element.36.refs_0_), channel_id=1, source_target_pairs={{0,24},{8,16},{16,8},{24,0},{1,25},{9,17},{17,9},{25,1},{2,26},{10... | collective-permute-start | bytes 786440 | tf_op jit(solution)/shard_map/ppermute | solution.py:379
  223.7 13.6 %collective-permute-start.17 = (bf16[512,256]{1,0:T(8,128)(2,1)}, bf16[512,256]{1,0:T(8,128)(2,1)}, u32[]{:S(2)}, u32[]{:S(2)}) collective-permute-start(bf16[512,256]{1,0:T(8,128)(2,1)} %get-tuple-element.36.refs_0_), channel_id=1, source_target_pairs={{0,16},{8,24},{16,0},{24,8},{1,17},{9,25},{17,1},{25,9},{2,18},{10... | collective-permute-start | bytes 786440 | tf_op jit(solution)/shard_map/ppermute | solution.py:379
  225.1 12.2 %collective-permute-start.16 = (bf16[512,256]{1,0:T(8,128)(2,1)}, bf16[512,256]{1,0:T(8,128)(2,1)}, u32[]{:S(2)}, u32[]{:S(2)}) collective-permute-start(bf16[512,256]{1,0:T(8,128)(2,1)} %get-tuple-element.36.refs_0_), channel_id=1, source_target_pairs={{0,8},{8,0},{16,24},{24,16},{1,9},{9,1},{17,25},{25,17},{2,10},{10... | collective-permute-start | bytes 786440 | tf_op jit(solution)/shard_map/ppermute | solution.py:379
  240.4 12.9 %copy-start.14 = (s32[4]{0:T(128)S(1)}, s32[4]{0:T(128)}, u32[]{:S(2)}) copy-start(s32[4]{0:T(128)} %param.7) | copy-start | bytes 52
  240.4 186.8 %all-gather.12.cloned.1.call-start = ((), (), s32[]{:S(2)}) async-start(), calls=%async_computation.2 | async-start | bytes 9437184 | tf_op jit(solution)/shard_map/all_gather | solution.py:485
  249.7 4.7 %collective-permute-start.21 = (f32[4,1024]{1,0:T(4,128)S(1)}, f32[4,1024]{1,0:T(4,128)S(1)}, u32[]{:S(2)}, u32[]{:S(2)}) collective-permute-start(f32[4,1024]{1,0:T(4,128)S(1)} %get-tuple-element.37.refs_0_), channel_id=1, source_target_pairs={{0,24},{8,16},{16,8},{24,0},{1,25},{9,17},{17,9},{25,1},{2,26},{10... | collective-permute-start | bytes 49160 | tf_op jit(solution)/shard_map/ppermute | solution.py:379
  251.2 3.7 collective-permute-start.20
  251.8 3.7 collective-permute-start.19
  255.6 22.2 %copy-start.11 = (f32[2,512,128]{2,1,0:T(8,128)S(1)}, f32[2,512,128]{2,1,0:T(8,128)}, u32[]{:S(2)}) copy-start(f32[2,512,128]{2,1,0:T(8,128)} %copy-done.10) | copy-start | bytes 1572868
  264.1 9.3 %collective-permute-start.22 = (bf16[512,256]{1,0:T(8,128)(2,1)S(1)}, bf16[512,256]{1,0:T(8,128)(2,1)S(1)}, u32[]{:S(2)}, u32[]{:S(2)}) collective-permute-start(bf16[512,256]{1,0:T(8,128)(2,1)S(1)} %get-tuple-element.40), channel_id=1, source_target_pairs={{0,8},{8,0},{16,24},{24,16},{1,9},{9,1},{17,25},{25,17},{2,10},{10... | collective-permute-start | bytes 786440 | tf_op jit(solution)/shard_map/ppermute | solution.py:379
  265.6 12.2 %collective-permute-start.23 = (bf16[512,256]{1,0:T(8,128)(2,1)S(1)}, bf16[512,256]{1,0:T(8,128)(2,1)S(1)}, u32[]{:S(2)}, u32[]{:S(2)}) collective-permute-start(bf16[512,256]{1,0:T(8,128)(2,1)S(1)} %get-tuple-element.41), channel_id=1, source_target_pairs={{0,16},{8,24},{16,0},{24,8},{1,17},{9,25},{17,1},{25,9},{2,18},{10... | collective-permute-start | bytes 786440 | tf_op jit(solution)/shard_map/ppermute | solution.py:379
  266.2 11.6 %collective-permute-start.24 = (bf16[512,256]{1,0:T(8,128)(2,1)S(1)}, bf16[512,256]{1,0:T(8,128)(2,1)S(1)}, u32[]{:S(2)}, u32[]{:S(2)}) collective-permute-start(bf16[512,256]{1,0:T(8,128)(2,1)S(1)} %get-tuple-element.42), channel_id=1, source_target_pairs={{0,24},{8,16},{16,8},{24,0},{1,25},{9,17},{17,9},{25,1},{2,26},{10... | collective-permute-start | bytes 786440 | tf_op jit(solution)/shard_map/ppermute | solution.py:379
  277.7 18.7 %copy-start.9 = (f32[2,512,128]{2,1,0:T(8,128)S(1)}, f32[2,512,128]{2,1,0:T(8,128)}, u32[]{:S(2)}) copy-start(f32[2,512,128]{2,1,0:T(8,128)} %copy-done.8) | copy-start | bytes 1572868
  285.0 8.4 %collective-permute-start.25 = (bf16[512,256]{1,0:T(8,128)(2,1)S(1)}, bf16[512,256]{1,0:T(8,128)(2,1)S(1)}, u32[]{:S(2)}, u32[]{:S(2)}) collective-permute-start(bf16[512,256]{1,0:T(8,128)(2,1)S(1)} %get-tuple-element.45), channel_id=1, source_target_pairs={{0,8},{8,0},{16,24},{24,16},{1,9},{9,1},{17,25},{25,17},{2,10},{10... | collective-permute-start | bytes 786440 | tf_op jit(solution)/shard_map/ppermute | solution.py:379
  285.4 10.9 %collective-permute-start.26 = (bf16[512,256]{1,0:T(8,128)(2,1)S(1)}, bf16[512,256]{1,0:T(8,128)(2,1)S(1)}, u32[]{:S(2)}, u32[]{:S(2)}) collective-permute-start(bf16[512,256]{1,0:T(8,128)(2,1)S(1)} %get-tuple-element.46), channel_id=1, source_target_pairs={{0,16},{8,24},{16,0},{24,8},{1,17},{9,25},{17,1},{25,9},{2,18},{10... | collective-permute-start | bytes 786440 | tf_op jit(solution)/shard_map/ppermute | solution.py:379
  285.9 10.4 %collective-permute-start.27 = (bf16[512,256]{1,0:T(8,128)(2,1)S(1)}, bf16[512,256]{1,0:T(8,128)(2,1)S(1)}, u32[]{:S(2)}, u32[]{:S(2)}) collective-permute-start(bf16[512,256]{1,0:T(8,128)(2,1)S(1)} %get-tuple-element.47), channel_id=1, source_target_pairs={{0,24},{8,16},{16,8},{24,0},{1,25},{9,17},{17,9},{25,1},{2,26},{10... | collective-permute-start | bytes 786440 | tf_op jit(solution)/shard_map/ppermute | solution.py:379
  296.4 18.8 %copy-start.7 = (f32[2,512,128]{2,1,0:T(8,128)S(1)}, f32[2,512,128]{2,1,0:T(8,128)}, u32[]{:S(2)}) copy-start(f32[2,512,128]{2,1,0:T(8,128)} %copy-done.6) | copy-start | bytes 1572868
  302.8 7.1 %collective-permute-start.28 = (bf16[512,256]{1,0:T(8,128)(2,1)S(1)}, bf16[512,256]{1,0:T(8,128)(2,1)S(1)}, u32[]{:S(2)}, u32[]{:S(2)}) collective-permute-start(bf16[512,256]{1,0:T(8,128)(2,1)S(1)} %get-tuple-element.50), channel_id=1, source_target_pairs={{0,8},{8,0},{16,24},{24,16},{1,9},{9,1},{17,25},{25,17},{2,10},{10... | collective-permute-start | bytes 786440 | tf_op jit(solution)/shard_map/ppermute | solution.py:379
  304.5 8.8 %collective-permute-start.29 = (bf16[512,256]{1,0:T(8,128)(2,1)S(1)}, bf16[512,256]{1,0:T(8,128)(2,1)S(1)}, u32[]{:S(2)}, u32[]{:S(2)}) collective-permute-start(bf16[512,256]{1,0:T(8,128)(2,1)S(1)} %get-tuple-element.51), channel_id=1, source_target_pairs={{0,16},{8,24},{16,0},{24,8},{1,17},{9,25},{17,1},{25,9},{2,18},{10... | collective-permute-start | bytes 786440 | tf_op jit(solution)/shard_map/ppermute | solution.py:379
  306.0 9.1 %collective-permute-start.30 = (bf16[512,256]{1,0:T(8,128)(2,1)S(1)}, bf16[512,256]{1,0:T(8,128)(2,1)S(1)}, u32[]{:S(2)}, u32[]{:S(2)}) collective-permute-start(bf16[512,256]{1,0:T(8,128)(2,1)S(1)} %get-tuple-element.52), channel_id=1, source_target_pairs={{0,24},{8,16},{16,8},{24,0},{1,25},{9,17},{17,9},{25,1},{2,26},{10... | collective-permute-start | bytes 786440 | tf_op jit(solution)/shard_map/ppermute | solution.py:379
  316.5 7.8 %collective-permute-start.33 = (bf16[512,256]{1,0:T(8,128)(2,1)S(1)}, bf16[512,256]{1,0:T(8,128)(2,1)S(1)}, u32[]{:S(2)}, u32[]{:S(2)}) collective-permute-start(bf16[512,256]{1,0:T(8,128)(2,1)S(1)} %get-tuple-element.80), channel_id=1, source_target_pairs={{0,24},{8,16},{16,8},{24,0},{1,25},{9,17},{17,9},{25,1},{2,26},{10... | collective-permute-start | bytes 786440 | tf_op jit(solution)/shard_map/ppermute | solution.py:379
  318.3 8.6 %collective-permute-start.32 = (bf16[512,256]{1,0:T(8,128)(2,1)S(1)}, bf16[512,256]{1,0:T(8,128)(2,1)S(1)}, u32[]{:S(2)}, u32[]{:S(2)}) collective-permute-start(bf16[512,256]{1,0:T(8,128)(2,1)S(1)} %get-tuple-element.81), channel_id=1, source_target_pairs={{0,16},{8,24},{16,0},{24,8},{1,17},{9,25},{17,1},{25,9},{2,18},{10... | collective-permute-start | bytes 786440 | tf_op jit(solution)/shard_map/ppermute | solution.py:379
  318.6 8.4 %collective-permute-start.31 = (bf16[512,256]{1,0:T(8,128)(2,1)S(1)}, bf16[512,256]{1,0:T(8,128)(2,1)S(1)}, u32[]{:S(2)}, u32[]{:S(2)}) collective-permute-start(bf16[512,256]{1,0:T(8,128)(2,1)S(1)} %get-tuple-element.82), channel_id=1, source_target_pairs={{0,8},{8,0},{16,24},{24,16},{1,9},{9,1},{17,25},{25,17},{2,10},{10... | collective-permute-start | bytes 786440 | tf_op jit(solution)/shard_map/ppermute | solution.py:379
Sparse Core Ops, SparseCore 0:
  11.2 60.1 all-gather.13
  75.2 57.8 all-gather.7
  135.2 56.1 all-gather.9
  240.5 96.4 all-gather.15
  339.0 88.0 all-gather.11

commit v2 on v0

--- a/solution.py
+++ b/solution.py
@@ -27,53 +27,35 @@
     return slot > 0 and slot % 2 == 0
 
 
-def fetch_weights(block, sections, scal, sources, weights, sems):
+def fetch_weights(block, sections, scal, sources, weights, sem):
     s, z, core = scal[0], scal[1], scal[2]
     slot = jnp.where(block == s, 0, jnp.where(block < s, block + 1, block))
     slots = slots_of(block, sections)
     sources = list(sources)
 
-    def copies(arrays):
+    def start(arrays):
         if len(arrays) == 1:
-            return [pltpu.make_async_copy(arrays[0], weights, sems.at[0])]
-        result = []
+            pltpu.make_async_copy(arrays[0], weights, sem).start()
+            return
         for which, source in enumerate(arrays):
             ring, depth = source.shape[:2]
             owner_core = core if which == 0 else 1 - core
             for j in range(ring):
                 place = lax.rem(z + j, ring)
                 row = pl.multiple_of((place * 2 + owner_core) * depth, depth)
-                result.append(
-                    pltpu.make_async_copy(
-                        source.at[j],
-                        weights.at[pl.ds(row, depth), :],
-                        sems.at[1 + which * ring + j],
-                    )
-                )
-        return result
-
-    choices = []
+                pltpu.make_async_copy(
+                    source.at[j], weights.at[pl.ds(row, depth), :], sem
+                ).start()
+
     for candidate in slots:
         count = 2 if by_ring(candidate) else 1
-        choices.append((slot == candidate, sources[:count]))
-        sources = sources[count:]
-
-    for chosen, arrays in choices:
-
-        @pl.when(chosen)
+        arrays, sources = sources[:count], sources[count:]
+
+        @pl.when(slot == candidate)
         def _():
-            for copy in copies(arrays):
-                copy.start()
-
-    def wait():
-        for chosen, arrays in choices:
-
-            @pl.when(chosen)
-            def _():
-                for copy in copies(arrays):
-                    copy.wait()
-
-    return wait
+            start(arrays)
+
+    return lambda: pltpu.make_async_copy(weights, weights, sem).wait()
 
 
 def forward_kernel(dims, block, scal, *refs):
@@ -85,10 +67,10 @@
     sources = refs[:count]
     refs = refs[count:]
     if last:
-        readout, out, fired_out, logits_out, weights, padded, work, sems = refs
-    else:
-        out, fired_out, weights, padded, work, sems = refs
-    wait = fetch_weights(block, sections, scal, sources, weights, sems)
+        readout, out, fired_out, logits_out, weights, padded, work, sem = refs
+    else:
+        out, fired_out, weights, padded, work, sem = refs
+    wait = fetch_weights(block, sections, scal, sources, weights, sem)
     rows, lanes = slices[0].shape
     group = images * steps
     channels = sections * lanes
@@ -161,8 +143,8 @@
         refs = refs[count:]
         raw_out, own_out = refs[:2]
         sends = refs[2 : 1 + sections]
-        weights, padded, upstream, work, sems = refs[1 + sections :]
-        wait = fetch_weights(block, sections, scal, sources, weights, sems)
+        weights, padded, upstream, work, sem = refs[1 + sections :]
+        wait = fetch_weights(block, sections, scal, sources, weights, sem)
         padded[...] = jnp.zeros_like(padded)
     else:
         raw_out, upstream, work = refs
@@ -234,11 +216,15 @@
             sends[k - 1][...] = total.astype(jnp.bfloat16)
 
 
+def stay(arrays):
+    return [pltpu.with_memory_space_constraint(array, pltpu.HBM) for array in arrays]
+
+
 def vmem(count):
     return [pl.BlockSpec(memory_space=VMEM)] * count
 
 
-def run_forward(dims, block, devices, scal, slices, sources, readout):
+def run_forward(dims, block, scal, slices, sources, readout):
     sections, height, width, images, steps = dims
     rows, lanes = slices[0].shape
     depth = 9 * sections * lanes
@@ -247,7 +233,7 @@
         jax.ShapeDtypeStruct((rows, lanes), jnp.bfloat16),
         jax.ShapeDtypeStruct((lanes // 128, rows, 128), jnp.float32),
     ]
-    operands = [scal, *slices, *sources]
+    operands = [scal, *(slices if last else stay(slices)), *stay(sources)]
     extra = []
     if last:
         shapes.append(jax.ShapeDtypeStruct((images, readout.shape[1]), jnp.float32))
@@ -265,7 +251,7 @@
             VMEM((depth, lanes), jnp.bfloat16),
             VMEM((sections, height + 2, width + 2, images * steps, lanes), jnp.bfloat16),
             VMEM((lanes // 128, rows, 128), jnp.float32),
-            pltpu.SemaphoreType.DMA((1 + devices,)),
+            pltpu.SemaphoreType.DMA,
         ],
         compiler_params=pltpu.CompilerParams(vmem_limit_bytes=LIMIT),
         cost_estimate=pl.CostEstimate(
@@ -277,20 +263,20 @@
     )(*operands)
 
 
-def run_backward(dims, block, devices, classes, scal, heads, fired, sources):
+def run_backward(dims, block, classes, scal, heads, fired, sources):
     sections, height, width, images, steps = dims
     stage = 0 if block == sections - 1 else (2 if block == 0 else 1)
     tiles, rows = fired.shape[:2]
     lanes = tiles * 128
     half = jax.ShapeDtypeStruct((rows, lanes), jnp.bfloat16)
     full = jax.ShapeDtypeStruct((rows, lanes), jnp.float32)
-    operands = [scal, *heads, fired]
+    operands = [scal, *heads, *stay([fired])]
     specs = [pl.BlockSpec(memory_space=pltpu.SMEM)] + vmem(len(heads) + 1)
     work = [VMEM(fired.shape, jnp.float32), VMEM(fired.shape, jnp.float32)]
     cost = 0
     if stage < 2:
         depth = 9 * sections * lanes
-        operands += list(sources)
+        operands += stay(sources)
         specs += [pl.BlockSpec(memory_space=pltpu.HBM)] * len(sources)
         shapes = [half, full] + [half] * (sections - 1)
         work = (
@@ -299,7 +285,7 @@
                 VMEM((height + 2, width + 2, images * steps, lanes), jnp.bfloat16),
             ]
             + work
-            + [pltpu.SemaphoreType.DMA((1 + devices,))]
+            + [pltpu.SemaphoreType.DMA]
         )
         cost = depth
     else:
@@ -388,7 +374,7 @@
 
     def forward(b):
         nonlocal own_inputs
-        results.append(run_forward(dims, b, devices, scal, inputs[b], holding(b), readout_own))
+        results.append(run_forward(dims, b, scal, inputs[b], holding(b), readout_own))
         if b < sections - 1:
             out = results[b][0]
             inputs.append([out] + exchange([out] * (sections - 1)))
@@ -440,7 +426,7 @@
     raws = [None] * sections
     for b in reversed(range(sections)):
         held = holding(b) if b > 0 else None
-        result = run_backward(dims, b, devices, classes, scal, heads, results[b][1], held)
+        result = run_backward(dims, b, classes, scal, heads, results[b][1], held)
         raws[b] = result[0]
         if b > 0:
             heads = [result[1]] + exchange(result[2:])

time: 436 us -> 420 us (0.963)
  local copies, waits for them, and re-layouts: 50.3 us -> 26.2 us
  Pallas kernels: 38.1 us -> 48.2 us
    unnamed x87 -> x43, local copies, waits for them, and re-layouts: 32.8 us -> 7.95 us
    pallas_call x4, Pallas kernels: 20.6 us -> 26.3 us  [run_forward(): pl.pallas_call(functools.partial(forward_kernel, dims, block), out_shape=...]
    pallas_call x4, Pallas kernels: 17.5 us -> 21.9 us  [run_backward(): pl.pallas_call(functools.partial(backward_kernel, dims, block, classes),...]
  transfers between devices with their start and end apart: 39 -> 39, of which waited for: 25 -> 27; matrix products, arithmetic and copies ran while one was open for 6% -> 7% of each run, Pallas kernels for 7% -> 10%
where the time goes in v2:
time: 420 us; the launch traced here: 419 us
  waiting for transfers between devices  247 us (59%)
  Pallas kernels  48.2 us (11%)
  starting transfers between devices  43.8 us (10%)
  local copies, waits for them, and re-layouts  26.2 us (6%)
  matrix products  23.2 us (6%)
  other arithmetic  16 us (4%)
  between operations  14.3 us (3%)
    ppermute x27, waiting for transfers between devices, exchange(): lax.ppermute(values[k], 'section', [(i, i ^ k + 1) for i in range(section...  89.6 us
    ppermute x3, waiting for transfers between devices, shards(): down = lax.ppermute(down, 'dp', hops(step, -1, ring))  88.6 us
    all_gather x1, waiting for transfers between devices, shards(): raw_all = lax.all_gather(own_raw, 'dp', axis=0, tiled=True)  66.1 us
    ppermute x27, starting transfers between devices, exchange(): lax.ppermute(values[k], 'section', [(i, i ^ k + 1) for i in range(section...  32.8 us
    pallas_call x4, Pallas kernels, run_forward(): pl.pallas_call(functools.partial(forward_kernel, dims, block), out_shape=...  26.3 us
    dot_general x1, matrix products, shards(): lax.dot_general(cols, raw_all, (((0,), (0,)), ((), ())), preferred_elemen...  23.2 us
    pallas_call x4, Pallas kernels, run_backward(): pl.pallas_call(functools.partial(backward_kernel, dims, block, classes),...  21.9 us
  transfers between devices with their start and end apart: 39, of which 27 were waited for; matrix products, arithmetic and copies ran while one was open for 7% of the time, Pallas kernels for 10%

profile of v2, /device:TPU:0, one launch (start us, length us, event | category | flops | bytes accessed | tf_op | source)
XLA Modules:
  0.0 419.1 jit_solution(3395380684025791692)
XLA Ops:
  7.2 3.8 fusion.3
  11.1 3.0 collective-permute-start
  14.1 1.5 collective-permute-start.1
  15.7 1.3 constant_dynamic-slice_fusion.1
  17.0 1.3 copy.12
  18.3 1.8 copy.9
  20.2 1.4 pad.8.refs_6_.refs_5_
  22.6 5.9 %collective-permute-done = bf16[1152,256]{1,0:T(8,128)(2,1)S(1)} collective-permute-done((bf16[1152,256]{1,0:T(8,128)(2,1)}, bf16[1152,256]{1,0:T(8,128)(2,1)S(1)}, u32[]{:S(2)}, u32[]{:S(2)}) %collective-permute-start) | collective-permute-done | bytes 589856 | tf_op jit(solution)/shard_map/ppermute | solution.py:351
  28.5 13.4 %collective-permute-done.1 = bf16[1152,256]{1,0:T(8,128)(2,1)} collective-permute-done((bf16[1152,256]{1,0:T(8,128)(2,1)}, bf16[1152,256]{1,0:T(8,128)(2,1)}, u32[]{:S(2)}, u32[]{:S(2)}) %collective-permute-start.1) | collective-permute-done | bytes 589856 | tf_op jit(solution)/shard_map/ppermute | solution.py:351
  41.9 1.5 pad_maximum_fusion
  43.4 1.1 dynamic-slice_bitcast_fusion
  44.6 1.3 collective-permute-start.4
  45.9 4.6 %collective-permute-start.3 = (bf16[1152,256]{1,0:T(8,128)(2,1)S(1)}, bf16[1152,256]{1,0:T(8,128)(2,1)S(1)}, u32[]{:S(2)}, u32[]{:S(2)}) collective-permute-start(bf16[1152,256]{1,0:T(8,128)(2,1)S(1)} %bitcast.107), channel_id=1, source_target_pairs={{0,2},{1,3},{2,4},{3,5},{4,6},{5,7},{8,10},{9,11},{10,12},{11,13},... | collective-permute-start | bytes 1769480 | tf_op jit(solution)/shard_map/ppermute | solution.py:393
  50.4 24.5 %collective-permute-done.4 = bf16[1152,256]{1,0:T(8,128)(2,1)S(1)} collective-permute-done((bf16[1152,256]{1,0:T(8,128)(2,1)S(1)}, bf16[1152,256]{1,0:T(8,128)(2,1)S(1)}, u32[]{:S(2)}, u32[]{:S(2)}) %collective-permute-start.4) | collective-permute-done | bytes 589856 | tf_op jit(solution)/shard_map/ppermute | solution.py:394
  75.1 1.3 collective-permute-start.10
  77.1 22.2 %collective-permute-done.10 = bf16[1152,256]{1,0:T(8,128)(2,1)S(1)} collective-permute-done((bf16[1152,256]{1,0:T(8,128)(2,1)S(1)}, bf16[1152,256]{1,0:T(8,128)(2,1)S(1)}, u32[]{:S(2)}, u32[]{:S(2)}) %collective-permute-start.10) | collective-permute-done | bytes 589856 | tf_op jit(solution)/shard_map/ppermute | solution.py:394
  99.3 1.3 collective-permute-start.11
  100.6 1.5 collective-permute-start.9
  102.1 41.9 %collective-permute-done.11 = bf16[1152,256]{1,0:T(8,128)(2,1)S(1)} collective-permute-done((bf16[1152,256]{1,0:T(8,128)(2,1)S(1)}, bf16[1152,256]{1,0:T(8,128)(2,1)S(1)}, u32[]{:S(2)}, u32[]{:S(2)}) %collective-permute-start.11) | collective-permute-done | bytes 589856 | tf_op jit(solution)/shard_map/ppermute | solution.py:394
  144.9 1.1 select_bitcast_fusion
  146.2 1.7 pad_maximum_fusion.1.refs_6_.refs_5_.refs_7_
  147.9 6.4 %forward_block.4 = (bf16[512,256]{1,0:T(8,128)(2,1)S(1)}, f32[2,512,128]{2,1,0:T(8,128)S(1)}) custom-call(s32[3]{0:T(128)S(1)} %pad_add_fusion.scal, bf16[512,256]{1,0:T(8,128)(2,1)} %get-tuple-element.86.refs_0_, bf16[512,256]{1,0:T(8,128)(2,1)} %get-tuple-element.85.refs_1_, bf16[512,256]{1,0:T(8,128)(2,1)} %get-tuple-element.84.refs_2_, ...), custom_call_target="tpu_custom_call" | custom-call | flops 2415919104 | bytes 4718592 | tf_op jit(solution)/shard_map/forward_block/pallas_call | solution.py:242
  155.1 2.8 collective-permute-start.7
  158.6 6.5 %collective-permute-done.7.refs_3_ = bf16[512,256]{1,0:T(8,128)(2,1)S(1)} collective-permute-done((bf16[512,256]{1,0:T(8,128)(2,1)S(1)}, bf16[512,256]{1,0:T(8,128)(2,1)S(1)}, u32[]{:S(2)}, u32[]{:S(2)}) %collective-permute-start.7) | collective-permute-done | bytes 262176 | tf_op jit(solution)/shard_map/ppermute | solution.py:351
  165.1 5.3 %collective-permute-done.6.refs_2_ = bf16[512,256]{1,0:T(8,128)(2,1)S(1)} collective-permute-done((bf16[512,256]{1,0:T(8,128)(2,1)S(1)}, bf16[512,256]{1,0:T(8,128)(2,1)S(1)}, u32[]{:S(2)}, u32[]{:S(2)}) %collective-permute-start.6) | collective-permute-done | bytes 262176 | tf_op jit(solution)/shard_map/ppermute | solution.py:351
  171.9 6.4 %forward_block.5 = (bf16[512,256]{1,0:T(8,128)(2,1)S(1)}, f32[2,512,128]{2,1,0:T(8,128)S(1)}) custom-call(s32[3]{0:T(128)S(1)} %pad_add_fusion.scal, bf16[512,256]{1,0:T(8,128)(2,1)} %copy-done, bf16[512,256]{1,0:T(8,128)(2,1)} %copy-done.14, bf16[512,256]{1,0:T(8,128)(2,1)} %copy-done.13, bf16[512,256]{1,0:T(8,128)(2,1)} %copy-done.12, ...), custom_call_target="tpu_custom_call" | custom-call | flops 2415919104 | bytes 4718592 | tf_op jit(solution)/shard_map/forward_block/pallas_call | solution.py:242
  179.1 1.8 collective-permute-start.15
  182.7 6.6 %collective-permute-done.15.refs_3_ = bf16[512,256]{1,0:T(8,128)(2,1)S(1)} collective-permute-done((bf16[512,256]{1,0:T(8,128)(2,1)S(1)}, bf16[512,256]{1,0:T(8,128)(2,1)S(1)}, u32[]{:S(2)}, u32[]{:S(2)}) %collective-permute-start.15) | collective-permute-done | bytes 262176 | tf_op jit(solution)/shard_map/ppermute | solution.py:351
  189.3 4.7 %collective-permute-done.14.refs_2_ = bf16[512,256]{1,0:T(8,128)(2,1)S(1)} collective-permute-done((bf16[512,256]{1,0:T(8,128)(2,1)S(1)}, bf16[512,256]{1,0:T(8,128)(2,1)S(1)}, u32[]{:S(2)}, u32[]{:S(2)}) %collective-permute-start.14) | collective-permute-done | bytes 262176 | tf_op jit(solution)/shard_map/ppermute | solution.py:351
  195.4 3.1 all-gather.10.cloned.1.call-done.refs_7_.refs_5_.refs_8_
  198.5 6.4 %forward_block.6 = (bf16[512,256]{1,0:T(8,128)(2,1)S(1)}, f32[2,512,128]{2,1,0:T(8,128)S(1)}) custom-call(s32[3]{0:T(128)S(1)} %pad_add_fusion.scal, bf16[512,256]{1,0:T(8,128)(2,1)} %copy-done.2, bf16[512,256]{1,0:T(8,128)(2,1)} %copy-done.17, bf16[512,256]{1,0:T(8,128)(2,1)} %copy-done.16, bf16[512,256]{1,0:T(8,128)(2,1)} %copy-done.15, ...), custom_call_target="tpu_custom_call" | custom-call | flops 2415919104 | bytes 4718592 | tf_op jit(solution)/shard_map/forward_block/pallas_call | solution.py:242
  205.7 2.5 collective-permute-start.18
  209.2 6.6 %collective-permute-done.18.refs_3_ = bf16[512,256]{1,0:T(8,128)(2,1)S(1)} collective-permute-done((bf16[512,256]{1,0:T(8,128)(2,1)S(1)}, bf16[512,256]{1,0:T(8,128)(2,1)S(1)}, u32[]{:S(2)}, u32[]{:S(2)}) %collective-permute-start.18) | collective-permute-done | bytes 262176 | tf_op jit(solution)/shard_map/ppermute | solution.py:351
  215.8 4.9 %collective-permute-done.17.refs_2_ = bf16[512,256]{1,0:T(8,128)(2,1)S(1)} collective-permute-done((bf16[512,256]{1,0:T(8,128)(2,1)S(1)}, bf16[512,256]{1,0:T(8,128)(2,1)S(1)}, u32[]{:S(2)}, u32[]{:S(2)}) %collective-permute-start.17) | collective-permute-done | bytes 262176 | tf_op jit(solution)/shard_map/ppermute | solution.py:351
  220.7 1.9 maximum_select_fusion
  224.1 7.1 %forward_block.7 = (bf16[512,256]{1,0:T(8,128)(2,1)}, f32[2,512,128]{2,1,0:T(8,128)S(1)}, f32[4,1024]{1,0:T(4,128)S(1)}) custom-call(s32[3]{0:T(128)S(1)} %pad_add_fusion.scal, bf16[512,256]{1,0:T(8,128)(2,1)S(1)} %get-tuple-element.36.refs_0_, bf16[512,256]{1,0:T(8,128)(2,1)S(1)} %collective-permute-done.16.refs_1_, ...), custom_call_target="tpu_custom_call" | custom-call | flops 2415919104 | bytes 4718592 | tf_op jit(solution)/shard_map/forward_block/pallas_call | solution.py:242
  232.0 1.7 collective-permute-start.21
  233.7 1.4 collective-permute-start.20
  237.5 1.4 collective-permute-done.19.refs_1_
  238.8 8.2 %backward_block.4 = (bf16[512,256]{1,0:T(8,128)(2,1)S(1)}, f32[512,256]{1,0:T(8,128)S(1)}, bf16[512,256]{1,0:T(8,128)(2,1)S(1)}, bf16[512,256]{1,0:T(8,128)(2,1)S(1)}, bf16[512,256]{1,0:T(8,128)(2,1)S(1)}) custom-call(s32[3]{0:T(128)S(1)} %pad_add_fusion.scal, f32[4,1024]{1,0:T(4,128)S(1)} %get-tuple-element.37.refs_0_, ...), custom_call_target="tpu_custom_call" | custom-call | flops 2429026304 | bytes 5767168 | tf_op jit(solution)/shard_map/backward_block/pallas_call | solution.py:293
  247.5 1.4 collective-permute-start.23
  248.9 1.7 collective-permute-start.24
  250.7 5.8 %collective-permute-done.22.refs_1_ = bf16[512,256]{1,0:T(8,128)(2,1)S(1)} collective-permute-done((bf16[512,256]{1,0:T(8,128)(2,1)S(1)}, bf16[512,256]{1,0:T(8,128)(2,1)S(1)}, u32[]{:S(2)}, u32[]{:S(2)}) %collective-permute-start.22) | collective-permute-done | bytes 262176 | tf_op jit(solution)/shard_map/ppermute | solution.py:351
  256.4 3.3 collective-permute-done.23.refs_2_
  259.7 6.0 %backward_block.5 = (bf16[512,256]{1,0:T(8,128)(2,1)S(1)}, f32[512,256]{1,0:T(8,128)S(1)}, bf16[512,256]{1,0:T(8,128)(2,1)S(1)}, bf16[512,256]{1,0:T(8,128)(2,1)S(1)}, bf16[512,256]{1,0:T(8,128)(2,1)S(1)}) custom-call(s32[3]{0:T(128)S(1)} %pad_add_fusion.scal, f32[512,256]{1,0:T(8,128)S(1)} %get-tuple-element.39.refs_0_, ...), custom_call_target="tpu_custom_call" | custom-call | flops 2429026304 | bytes 5767168 | tf_op jit(solution)/shard_map/backward_block/pallas_call | solution.py:293
  265.8 1.6 collective-permute-start.25
  268.0 1.3 collective-permute-start.27
  269.3 4.9 %collective-permute-done.25.refs_1_ = bf16[512,256]{1,0:T(8,128)(2,1)S(1)} collective-permute-done((bf16[512,256]{1,0:T(8,128)(2,1)S(1)}, bf16[512,256]{1,0:T(8,128)(2,1)S(1)}, u32[]{:S(2)}, u32[]{:S(2)}) %collective-permute-start.25) | collective-permute-done | bytes 262176 | tf_op jit(solution)/shard_map/ppermute | solution.py:351
  274.2 4.3 %collective-permute-done.26.refs_2_ = bf16[512,256]{1,0:T(8,128)(2,1)S(1)} collective-permute-done((bf16[512,256]{1,0:T(8,128)(2,1)S(1)}, bf16[512,256]{1,0:T(8,128)(2,1)S(1)}, u32[]{:S(2)}, u32[]{:S(2)}) %collective-permute-start.26) | collective-permute-done | bytes 262176 | tf_op jit(solution)/shard_map/ppermute | solution.py:351
  278.5 6.0 %backward_block.6 = (bf16[512,256]{1,0:T(8,128)(2,1)S(1)}, f32[512,256]{1,0:T(8,128)S(1)}, bf16[512,256]{1,0:T(8,128)(2,1)S(1)}, bf16[512,256]{1,0:T(8,128)(2,1)S(1)}, bf16[512,256]{1,0:T(8,128)(2,1)S(1)}) custom-call(s32[3]{0:T(128)S(1)} %pad_add_fusion.scal, f32[512,256]{1,0:T(8,128)S(1)} %get-tuple-element.44.refs_0_, ...), custom_call_target="tpu_custom_call" | custom-call | flops 2429026304 | bytes 5767168 | tf_op jit(solution)/shard_map/backward_block/pallas_call | solution.py:293
  285.0 1.5 collective-permute-start.29
  286.6 1.5 collective-permute-start.30
  288.1 3.8 collective-permute-done.28.refs_1_
  291.9 3.3 collective-permute-done.29.refs_2_
  295.2 1.6 backward_block.7
  297.2 1.6 collective-permute-start.33
  298.8 1.5 collective-permute-start.32
  300.8 3.9 collective-permute-done.33
  304.7 2.7 collective-permute-done.32
  307.8 1.1 pad_maximum_fusion.4
  309.1 7.2 %pad_dynamic-slice_fusion = (bf16[8,4,4,32,1024]{4,3,2,1,0:T(8,128)(2,1)S(1)}, bf16[8,4,4,32,1024]{4,3,2,1,0:T(8,128)(2,1)S(1)}) fusion(s32[]{:T(128)S(6)} %select_n.180, s32[]{:T(128)S(6)} %select_n.182, bf16[8,4,4,32,1024]{4,3,2,1,0:T(8,128)(2,1)} %bitcast.104, s32[]{:T(128)S(6)} %select_n.176, s32[]{:T(128)S(6)} %select_n.178), kind=kLoop, calls=%fused_computation | loop fusion | bytes 25165840 | tf_op jit(solution)/shard_map/dynamic_slice | solution.py:449
  316.2 7.0 %fusion = bf16[4096,1152]{1,0:T(8,128)(2,1)} fusion(s32[]{:T(128)S(6)} %select_n.184, bf16[4096,1024]{1,0:T(8,128)(2,1)S(1)} %bitcast.103, bf16[4096,1024]{1,0:T(8,128)(2,1)S(1)} %bitcast.102), kind=kLoop, calls=%fused_computation.4 | loop fusion | flops 18874368 | bytes 26214404 | tf_op jit(solution)/shard_map/concatenate | solution.py:455
  323.3 66.1 %all-gather.12.cloned.1.call-done = bf16[4096,1024]{1,0:T(8,128)(2,1)} async-done(((bf16[512,1024]{1,0:T(8,128)(2,1)}), bf16[4096,1024]{1,0:T(8,128)(2,1)}) %all-gather.12.cloned.1.call-update) | async-done | bytes 8388624 | tf_op jit(solution)/shard_map/all_gather | solution.py:457
  389.3 23.2 %divide_subtract_fusion = (f32[1,1152,1024]{2,1,0:T(8,128)}, f32[1,1152,1024]{2,1,0:T(8,128)}, f32[1,1152,1024]{2,1,0:T(8,128)}) fusion(f32[1,1152,1024]{2,1,0:T(8,128)} %param.9, f32[1,1152,1024]{2,1,0:T(8,128)} %param.10, f32[1,1152,1024]{2,1,0:T(8,128)} %param.11, bf16[4096,1152]{1,0:T(8,128)(2,1)} %fusion, ...), kind=kOutput, calls=%fused_computation.9 | convolution fusion | flops 9676652544 | bytes 46137344 | tf_op jit(solution)/shard_map/dot_general | solution.py:459
  (94 shorter events, 19.2 us)
Async XLA Ops:
  7.2 67.8 %all-gather.14.cloned.1.call-start = ((), (), s32[]{:S(2)}) async-start(), calls=%async_computation.3 | async-start | bytes 5308416 | tf_op jit(solution)/shard_map/all_gather | solution.py:404
  11.1 133.7 %all-gather.8.cloned.1.call-start = ((), (), s32[]{:S(2)}) async-start(), calls=%async_computation | async-start | bytes 5308416 | tf_op jit(solution)/shard_map/all_gather | solution.py:404
  11.1 17.4 %collective-permute-start = (bf16[1152,256]{1,0:T(8,128)(2,1)}, bf16[1152,256]{1,0:T(8,128)(2,1)S(1)}, u32[]{:S(2)}, u32[]{:S(2)}) collective-permute-start(bf16[1152,256]{1,0:T(8,128)(2,1)} %get-tuple-element.64), channel_id=1, source_target_pairs={{0,8},{8,0},{16,24},{24,16},{1,9},{9,1},{17,25},{25,17},{2,10},{10... | collective-permute-start | bytes 1769480 | tf_op jit(solution)/shard_map/ppermute | solution.py:351
  14.1 27.7 %collective-permute-start.1 = (bf16[1152,256]{1,0:T(8,128)(2,1)}, bf16[1152,256]{1,0:T(8,128)(2,1)}, u32[]{:S(2)}, u32[]{:S(2)}) collective-permute-start(bf16[1152,256]{1,0:T(8,128)(2,1)} %get-tuple-element.65), channel_id=1, source_target_pairs={{0,16},{8,24},{16,0},{24,8},{1,17},{9,25},{17,1},{25,9},{2,18},{10... | collective-permute-start | bytes 1769480 | tf_op jit(solution)/shard_map/ppermute | solution.py:351
  15.7 26.2 %collective-permute-start.2 = (bf16[1152,256]{1,0:T(8,128)(2,1)}, bf16[1152,256]{1,0:T(8,128)(2,1)}, u32[]{:S(2)}, u32[]{:S(2)}) collective-permute-start(bf16[1152,256]{1,0:T(8,128)(2,1)} %get-tuple-element.67), channel_id=1, source_target_pairs={{0,24},{8,16},{16,8},{24,0},{1,25},{9,17},{17,9},{25,1},{2,26},{10... | collective-permute-start | bytes 1769480 | tf_op jit(solution)/shard_map/ppermute | solution.py:351
  15.7 26.2 %copy-start.7 = (bf16[1,1152,256]{2,1,0:T(8,128)(2,1)S(1)}, bf16[1,1152,256]{2,1,0:T(8,128)(2,1)}, u32[]{:S(2)}) copy-start(bf16[1,1152,256]{2,1,0:T(8,128)(2,1)} %get-tuple-element.66) | copy-start | bytes 1769476
  44.6 30.4 %collective-permute-start.4 = (bf16[1152,256]{1,0:T(8,128)(2,1)S(1)}, bf16[1152,256]{1,0:T(8,128)(2,1)S(1)}, u32[]{:S(2)}, u32[]{:S(2)}) collective-permute-start(bf16[1152,256]{1,0:T(8,128)(2,1)S(1)} %bitcast.106), channel_id=1, source_target_pairs={{2,0},{3,1},{4,2},{5,3},{6,4},{7,5},{10,8},{11,9},{12,10},{13,11},... | collective-permute-start | bytes 1769480 | tf_op jit(solution)/shard_map/ppermute | solution.py:394
  45.9 29.1 %collective-permute-start.3 = (bf16[1152,256]{1,0:T(8,128)(2,1)S(1)}, bf16[1152,256]{1,0:T(8,128)(2,1)S(1)}, u32[]{:S(2)}, u32[]{:S(2)}) collective-permute-start(bf16[1152,256]{1,0:T(8,128)(2,1)S(1)} %bitcast.107), channel_id=1, source_target_pairs={{0,2},{1,3},{2,4},{3,5},{4,6},{5,7},{8,10},{9,11},{10,12},{11,13},... | collective-permute-start | bytes 1769480 | tf_op jit(solution)/shard_map/ppermute | solution.py:393
  75.0 123.5 %all-gather.10.cloned.1.call-start = ((), (), s32[]{:S(2)}) async-start(), calls=%async_computation.1 | async-start | bytes 5308416 | tf_op jit(solution)/shard_map/all_gather | solution.py:404
  75.1 24.2 %collective-permute-start.10 = (bf16[1152,256]{1,0:T(8,128)(2,1)S(1)}, bf16[1152,256]{1,0:T(8,128)(2,1)S(1)}, u32[]{:S(2)}, u32[]{:S(2)}) collective-permute-start(bf16[1152,256]{1,0:T(8,128)(2,1)S(1)} %collective-permute-done.4), channel_id=1, source_target_pairs={{2,0},{3,1},{4,2},{5,3},{10,8},{11,9},{12,10},{13,11},{18,16},{19,... | collective-permute-start | bytes 1769480 | tf_op jit(solution)/shard_map/ppermute | solution.py:394
  76.4 24.2 %collective-permute-start.8 = (bf16[1152,256]{1,0:T(8,128)(2,1)S(1)}, bf16[1152,256]{1,0:T(8,128)(2,1)S(1)}, u32[]{:S(2)}, u32[]{:S(2)}) collective-permute-start(bf16[1152,256]{1,0:T(8,128)(2,1)S(1)} %collective-permute-done.3), channel_id=1, source_target_pairs={{2,4},{3,5},{4,6},{5,7},{10,12},{11,13},{12,14},{13,15},{18,20},{1... | collective-permute-start | bytes 1769480 | tf_op jit(solution)/shard_map/ppermute | solution.py:393
  99.3 44.7 %collective-permute-start.11 = (bf16[1152,256]{1,0:T(8,128)(2,1)S(1)}, bf16[1152,256]{1,0:T(8,128)(2,1)S(1)}, u32[]{:S(2)}, u32[]{:S(2)}) collective-permute-start(bf16[1152,256]{1,0:T(8,128)(2,1)S(1)} %collective-permute-done.10), channel_id=1, source_target_pairs={{2,0},{3,1},{10,8},{11,9},{18,16},{19,17},{26,24},{27,25}} | collective-permute-start | bytes 1769480 | tf_op jit(solution)/shard_map/ppermute | solution.py:394
  100.6 43.4 %copy-start.18 = (bf16[1152,256]{1,0:T(8,128)(2,1)}, bf16[1152,256]{1,0:T(8,128)(2,1)S(1)}, u32[]{:S(2)}) copy-start(bf16[1152,256]{1,0:T(8,128)(2,1)S(1)} %collective-permute-done.8) | copy-start | bytes 1769476
  100.6 44.2 %collective-permute-start.9 = (bf16[1152,256]{1,0:T(8,128)(2,1)S(1)}, bf16[1152,256]{1,0:T(8,128)(2,1)}, u32[]{:S(2)}, u32[]{:S(2)}) collective-permute-start(bf16[1152,256]{1,0:T(8,128)(2,1)S(1)} %collective-permute-done.8), channel_id=1, source_target_pairs={{4,6},{5,7},{12,14},{13,15},{20,22},{21,23},{28,30},{29,31}} | collective-permute-start | bytes 1769480 | tf_op jit(solution)/shard_map/ppermute | solution.py:393
  143.9 0.8 copy-start.19
  144.8 164.3 %all-gather.16.cloned.1.call-start = ((), (), s32[]{:S(2)}) async-start(), calls=%async_computation.4 | async-start | bytes 9437184 | tf_op jit(solution)/shard_map/all_gather | solution.py:424
  147.9 10.7 %collective-permute-start.12 = (bf16[4,1152,256]{2,1,0:T(8,128)(2,1)}, bf16[4,1152,256]{2,1,0:T(8,128)(2,1)}, u32[]{:S(2)}, u32[]{:S(2)}) collective-permute-start(bf16[4,1152,256]{2,1,0:T(8,128)(2,1)} %pad_maximum_fusion.1.refs_6_.refs_5_.refs_7_), channel_id=1, source_target_pairs={{0,1},{1,0},{2,3},{3,2},{4,5},{5,4},{6,7},{7,6},{8,9},{9,8},{10,11... | collective-permute-start | bytes 7077896 | tf_op jit(solution)/shard_map/ppermute | solution.py:323
  154.3 0.8 copy-start.3
  155.1 15.4 %copy-start = (bf16[512,256]{1,0:T(8,128)(2,1)}, bf16[512,256]{1,0:T(8,128)(2,1)S(1)}, u32[]{:S(2)}) copy-start(bf16[512,256]{1,0:T(8,128)(2,1)S(1)} %get-tuple-element.33.refs_0_) | copy-start | bytes 786436
  155.1 10.0 %collective-permute-start.7 = (bf16[512,256]{1,0:T(8,128)(2,1)S(1)}, bf16[512,256]{1,0:T(8,128)(2,1)S(1)}, u32[]{:S(2)}, u32[]{:S(2)}) collective-permute-start(bf16[512,256]{1,0:T(8,128)(2,1)S(1)} %get-tuple-element.33.refs_0_), channel_id=1, source_target_pairs={{0,24},{8,16},{16,8},{24,0},{1,25},{9,17},{17,9},{25,1},{2,26},{10... | collective-permute-start | bytes 786440 | tf_op jit(solution)/shard_map/ppermute | solution.py:351
  157.9 12.6 %collective-permute-start.6 = (bf16[512,256]{1,0:T(8,128)(2,1)S(1)}, bf16[512,256]{1,0:T(8,128)(2,1)S(1)}, u32[]{:S(2)}, u32[]{:S(2)}) collective-permute-start(bf16[512,256]{1,0:T(8,128)(2,1)S(1)} %get-tuple-element.33.refs_0_), channel_id=1, source_target_pairs={{0,16},{8,24},{16,0},{24,8},{1,17},{9,25},{17,1},{25,9},{2,18},{10... | collective-permute-start | bytes 786440 | tf_op jit(solution)/shard_map/ppermute | solution.py:351
  158.1 12.4 %collective-permute-start.5 = (bf16[512,256]{1,0:T(8,128)(2,1)S(1)}, bf16[512,256]{1,0:T(8,128)(2,1)S(1)}, u32[]{:S(2)}, u32[]{:S(2)}) collective-permute-start(bf16[512,256]{1,0:T(8,128)(2,1)S(1)} %get-tuple-element.33.refs_0_), channel_id=1, source_target_pairs={{0,8},{8,0},{16,24},{24,16},{1,9},{9,1},{17,25},{25,17},{2,10},{10... | collective-permute-start | bytes 786440 | tf_op jit(solution)/shard_map/ppermute | solution.py:351
  165.1 5.4 %copy-start.12 = (bf16[512,256]{1,0:T(8,128)(2,1)}, bf16[512,256]{1,0:T(8,128)(2,1)S(1)}, u32[]{:S(2)}) copy-start(bf16[512,256]{1,0:T(8,128)(2,1)S(1)} %collective-permute-done.7.refs_3_) | copy-start | bytes 786436
  170.5 0.7 copy-start.13
  171.2 0.7 copy-start.14
  178.3 0.8 copy-start.4
  179.1 19.4 %copy-start.2 = (bf16[512,256]{1,0:T(8,128)(2,1)}, bf16[512,256]{1,0:T(8,128)(2,1)S(1)}, u32[]{:S(2)}) copy-start(bf16[512,256]{1,0:T(8,128)(2,1)S(1)} %get-tuple-element.34.refs_0_) | copy-start | bytes 786436
  179.1 41.6 %copy-start.1 = (bf16[512,256]{1,0:T(8,128)(2,1)S(1)}, bf16[512,256]{1,0:T(8,128)(2,1)}, u32[]{:S(2)}) copy-start(bf16[512,256]{1,0:T(8,128)(2,1)} %copy-done) | copy-start | bytes 786436
  179.1 41.6 %copy-start.8 = (bf16[512,256]{1,0:T(8,128)(2,1)S(1)}, bf16[512,256]{1,0:T(8,128)(2,1)}, u32[]{:S(2)}) copy-start(bf16[512,256]{1,0:T(8,128)(2,1)} %get-tuple-element.83.refs_3_) | copy-start | bytes 786436
  179.1 41.6 %copy-start.9 = (bf16[512,256]{1,0:T(8,128)(2,1)S(1)}, bf16[512,256]{1,0:T(8,128)(2,1)}, u32[]{:S(2)}) copy-start(bf16[512,256]{1,0:T(8,128)(2,1)} %get-tuple-element.84.refs_2_) | copy-start | bytes 786436
  179.1 41.6 %copy-start.10 = (bf16[512,256]{1,0:T(8,128)(2,1)S(1)}, bf16[512,256]{1,0:T(8,128)(2,1)}, u32[]{:S(2)}) copy-start(bf16[512,256]{1,0:T(8,128)(2,1)} %get-tuple-element.85.refs_1_) | copy-start | bytes 786436
  179.1 41.6 %copy-start.11 = (bf16[512,256]{1,0:T(8,128)(2,1)S(1)}, bf16[512,256]{1,0:T(8,128)(2,1)}, u32[]{:S(2)}) copy-start(bf16[512,256]{1,0:T(8,128)(2,1)} %get-tuple-element.86.refs_0_) | copy-start | bytes 786436
  179.1 10.2 %collective-permute-start.15 = (bf16[512,256]{1,0:T(8,128)(2,1)S(1)}, bf16[512,256]{1,0:T(8,128)(2,1)S(1)}, u32[]{:S(2)}, u32[]{:S(2)}) collective-permute-start(bf16[512,256]{1,0:T(8,128)(2,1)S(1)} %get-tuple-element.34.refs_0_), channel_id=1, source_target_pairs={{0,24},{8,16},{16,8},{24,0},{1,25},{9,17},{17,9},{25,1},{2,26},{10... | collective-permute-start | bytes 786440 | tf_op jit(solution)/shard_map/ppermute | solution.py:351
  181.0 13.1 %collective-permute-start.14 = (bf16[512,256]{1,0:T(8,128)(2,1)S(1)}, bf16[512,256]{1,0:T(8,128)(2,1)S(1)}, u32[]{:S(2)}, u32[]{:S(2)}) collective-permute-start(bf16[512,256]{1,0:T(8,128)(2,1)S(1)} %get-tuple-element.34.refs_0_), channel_id=1, source_target_pairs={{0,16},{8,24},{16,0},{24,8},{1,17},{9,25},{17,1},{25,9},{2,18},{10... | collective-permute-start | bytes 786440 | tf_op jit(solution)/shard_map/ppermute | solution.py:351
  182.1 12.1 %collective-permute-start.13 = (bf16[512,256]{1,0:T(8,128)(2,1)S(1)}, bf16[512,256]{1,0:T(8,128)(2,1)S(1)}, u32[]{:S(2)}, u32[]{:S(2)}) collective-permute-start(bf16[512,256]{1,0:T(8,128)(2,1)S(1)} %get-tuple-element.34.refs_0_), channel_id=1, source_target_pairs={{0,8},{8,0},{16,24},{24,16},{1,9},{9,1},{17,25},{25,17},{2,10},{10... | collective-permute-start | bytes 786440 | tf_op jit(solution)/shard_map/ppermute | solution.py:351
  189.3 4.9 %copy-start.15 = (bf16[512,256]{1,0:T(8,128)(2,1)}, bf16[512,256]{1,0:T(8,128)(2,1)S(1)}, u32[]{:S(2)}) copy-start(bf16[512,256]{1,0:T(8,128)(2,1)S(1)} %collective-permute-done.15.refs_3_) | copy-start | bytes 786436
  194.0 0.7 copy-start.16
  194.7 0.7 copy-start.17
  204.9 0.8 copy-start.5
  205.7 10.1 %collective-permute-start.18 = (bf16[512,256]{1,0:T(8,128)(2,1)S(1)}, bf16[512,256]{1,0:T(8,128)(2,1)S(1)}, u32[]{:S(2)}, u32[]{:S(2)}) collective-permute-start(bf16[512,256]{1,0:T(8,128)(2,1)S(1)} %get-tuple-element.36.refs_0_), channel_id=1, source_target_pairs={{0,24},{8,16},{16,8},{24,0},{1,25},{9,17},{17,9},{25,1},{2,26},{10... | collective-permute-start | bytes 786440 | tf_op jit(solution)/shard_map/ppermute | solution.py:351
  208.2 12.4 %collective-permute-start.17 = (bf16[512,256]{1,0:T(8,128)(2,1)S(1)}, bf16[512,256]{1,0:T(8,128)(2,1)S(1)}, u32[]{:S(2)}, u32[]{:S(2)}) collective-permute-start(bf16[512,256]{1,0:T(8,128)(2,1)S(1)} %get-tuple-element.36.refs_0_), channel_id=1, source_target_pairs={{0,16},{8,24},{16,0},{24,8},{1,17},{9,25},{17,1},{25,9},{2,18},{10... | collective-permute-start | bytes 786440 | tf_op jit(solution)/shard_map/ppermute | solution.py:351
  208.6 12.1 %collective-permute-start.16 = (bf16[512,256]{1,0:T(8,128)(2,1)S(1)}, bf16[512,256]{1,0:T(8,128)(2,1)S(1)}, u32[]{:S(2)}, u32[]{:S(2)}) collective-permute-start(bf16[512,256]{1,0:T(8,128)(2,1)S(1)} %get-tuple-element.36.refs_0_), channel_id=1, source_target_pairs={{0,8},{8,0},{16,24},{24,16},{1,9},{9,1},{17,25},{25,17},{2,10},{10... | collective-permute-start | bytes 786440 | tf_op jit(solution)/shard_map/ppermute | solution.py:351
  223.8 11.7 %copy-start.20 = (s32[4]{0:T(128)S(1)}, s32[4]{0:T(128)}, u32[]{:S(2)}) copy-start(s32[4]{0:T(128)} %param.7) | copy-start | bytes 52
  223.9 165.5 %all-gather.12.cloned.1.call-start = ((), (), s32[]{:S(2)}) async-start(), calls=%async_computation.2 | async-start | bytes 9437184 | tf_op jit(solution)/shard_map/all_gather | solution.py:457
  231.2 0.8 copy-start.6
  232.0 4.6 %collective-permute-start.21 = (f32[4,1024]{1,0:T(4,128)S(1)}, f32[4,1024]{1,0:T(4,128)S(1)}, u32[]{:S(2)}, u32[]{:S(2)}) collective-permute-start(f32[4,1024]{1,0:T(4,128)S(1)} %get-tuple-element.37.refs_0_), channel_id=1, source_target_pairs={{0,24},{8,16},{16,8},{24,0},{1,25},{9,17},{17,9},{25,1},{2,26},{10... | collective-permute-start | bytes 49160 | tf_op jit(solution)/shard_map/ppermute | solution.py:351
  233.7 3.7 collective-permute-start.20
  235.1 3.7 collective-permute-start.19
  247.1 9.3 %collective-permute-start.22 = (bf16[512,256]{1,0:T(8,128)(2,1)S(1)}, bf16[512,256]{1,0:T(8,128)(2,1)S(1)}, u32[]{:S(2)}, u32[]{:S(2)}) collective-permute-start(bf16[512,256]{1,0:T(8,128)(2,1)S(1)} %get-tuple-element.40), channel_id=1, source_target_pairs={{0,8},{8,0},{16,24},{24,16},{1,9},{9,1},{17,25},{25,17},{2,10},{10... | collective-permute-start | bytes 786440 | tf_op jit(solution)/shard_map/ppermute | solution.py:351
  247.5 12.2 %collective-permute-start.23 = (bf16[512,256]{1,0:T(8,128)(2,1)S(1)}, bf16[512,256]{1,0:T(8,128)(2,1)S(1)}, u32[]{:S(2)}, u32[]{:S(2)}) collective-permute-start(bf16[512,256]{1,0:T(8,128)(2,1)S(1)} %get-tuple-element.41), channel_id=1, source_target_pairs={{0,16},{8,24},{16,0},{24,8},{1,17},{9,25},{17,1},{25,9},{2,18},{10... | collective-permute-start | bytes 786440 | tf_op jit(solution)/shard_map/ppermute | solution.py:351
  248.9 10.8 %collective-permute-start.24 = (bf16[512,256]{1,0:T(8,128)(2,1)S(1)}, bf16[512,256]{1,0:T(8,128)(2,1)S(1)}, u32[]{:S(2)}, u32[]{:S(2)}) collective-permute-start(bf16[512,256]{1,0:T(8,128)(2,1)S(1)} %get-tuple-element.42), channel_id=1, source_target_pairs={{0,24},{8,16},{16,8},{24,0},{1,25},{9,17},{17,9},{25,1},{2,26},{10... | collective-permute-start | bytes 786440 | tf_op jit(solution)/shard_map/ppermute | solution.py:351
  265.8 8.5 %collective-permute-start.25 = (bf16[512,256]{1,0:T(8,128)(2,1)S(1)}, bf16[512,256]{1,0:T(8,128)(2,1)S(1)}, u32[]{:S(2)}, u32[]{:S(2)}) collective-permute-start(bf16[512,256]{1,0:T(8,128)(2,1)S(1)} %get-tuple-element.45), channel_id=1, source_target_pairs={{0,8},{8,0},{16,24},{24,16},{1,9},{9,1},{17,25},{25,17},{2,10},{10... | collective-permute-start | bytes 786440 | tf_op jit(solution)/shard_map/ppermute | solution.py:351
  267.3 11.2 %collective-permute-start.26 = (bf16[512,256]{1,0:T(8,128)(2,1)S(1)}, bf16[512,256]{1,0:T(8,128)(2,1)S(1)}, u32[]{:S(2)}, u32[]{:S(2)}) collective-permute-start(bf16[512,256]{1,0:T(8,128)(2,1)S(1)} %get-tuple-element.46), channel_id=1, source_target_pairs={{0,16},{8,24},{16,0},{24,8},{1,17},{9,25},{17,1},{25,9},{2,18},{10... | collective-permute-start | bytes 786440 | tf_op jit(solution)/shard_map/ppermute | solution.py:351
  268.0 10.5 %collective-permute-start.27 = (bf16[512,256]{1,0:T(8,128)(2,1)S(1)}, bf16[512,256]{1,0:T(8,128)(2,1)S(1)}, u32[]{:S(2)}, u32[]{:S(2)}) collective-permute-start(bf16[512,256]{1,0:T(8,128)(2,1)S(1)} %get-tuple-element.47), channel_id=1, source_target_pairs={{0,24},{8,16},{16,8},{24,0},{1,25},{9,17},{17,9},{25,1},{2,26},{10... | collective-permute-start | bytes 786440 | tf_op jit(solution)/shard_map/ppermute | solution.py:351
  284.5 7.4 %collective-permute-start.28 = (bf16[512,256]{1,0:T(8,128)(2,1)S(1)}, bf16[512,256]{1,0:T(8,128)(2,1)S(1)}, u32[]{:S(2)}, u32[]{:S(2)}) collective-permute-start(bf16[512,256]{1,0:T(8,128)(2,1)S(1)} %get-tuple-element.50), channel_id=1, source_target_pairs={{0,8},{8,0},{16,24},{24,16},{1,9},{9,1},{17,25},{25,17},{2,10},{10... | collective-permute-start | bytes 786440 | tf_op jit(solution)/shard_map/ppermute | solution.py:351
  285.0 10.2 %collective-permute-start.29 = (bf16[512,256]{1,0:T(8,128)(2,1)S(1)}, bf16[512,256]{1,0:T(8,128)(2,1)S(1)}, u32[]{:S(2)}, u32[]{:S(2)}) collective-permute-start(bf16[512,256]{1,0:T(8,128)(2,1)S(1)} %get-tuple-element.51), channel_id=1, source_target_pairs={{0,16},{8,24},{16,0},{24,8},{1,17},{9,25},{17,1},{25,9},{2,18},{10... | collective-permute-start | bytes 786440 | tf_op jit(solution)/shard_map/ppermute | solution.py:351
  286.6 8.6 %collective-permute-start.30 = (bf16[512,256]{1,0:T(8,128)(2,1)S(1)}, bf16[512,256]{1,0:T(8,128)(2,1)S(1)}, u32[]{:S(2)}, u32[]{:S(2)}) collective-permute-start(bf16[512,256]{1,0:T(8,128)(2,1)S(1)} %get-tuple-element.52), channel_id=1, source_target_pairs={{0,24},{8,16},{16,8},{24,0},{1,25},{9,17},{17,9},{25,1},{2,26},{10... | collective-permute-start | bytes 786440 | tf_op jit(solution)/shard_map/ppermute | solution.py:351
  297.2 7.4 %collective-permute-start.33 = (bf16[512,256]{1,0:T(8,128)(2,1)S(1)}, bf16[512,256]{1,0:T(8,128)(2,1)S(1)}, u32[]{:S(2)}, u32[]{:S(2)}) collective-permute-start(bf16[512,256]{1,0:T(8,128)(2,1)S(1)} %get-tuple-element.80), channel_id=1, source_target_pairs={{0,24},{8,16},{16,8},{24,0},{1,25},{9,17},{17,9},{25,1},{2,26},{10... | collective-permute-start | bytes 786440 | tf_op jit(solution)/shard_map/ppermute | solution.py:351
  298.8 8.5 %collective-permute-start.32 = (bf16[512,256]{1,0:T(8,128)(2,1)S(1)}, bf16[512,256]{1,0:T(8,128)(2,1)S(1)}, u32[]{:S(2)}, u32[]{:S(2)}) collective-permute-start(bf16[512,256]{1,0:T(8,128)(2,1)S(1)} %get-tuple-element.81), channel_id=1, source_target_pairs={{0,16},{8,24},{16,0},{24,8},{1,17},{9,25},{17,1},{25,9},{2,18},{10... | collective-permute-start | bytes 786440 | tf_op jit(solution)/shard_map/ppermute | solution.py:351
  300.4 7.2 %collective-permute-start.31 = (bf16[512,256]{1,0:T(8,128)(2,1)S(1)}, bf16[512,256]{1,0:T(8,128)(2,1)S(1)}, u32[]{:S(2)}, u32[]{:S(2)}) collective-permute-start(bf16[512,256]{1,0:T(8,128)(2,1)S(1)} %get-tuple-element.82), channel_id=1, source_target_pairs={{0,8},{8,0},{16,24},{24,16},{1,9},{9,1},{17,25},{25,17},{2,10},{10... | collective-permute-start | bytes 786440 | tf_op jit(solution)/shard_map/ppermute | solution.py:351
Sparse Core Ops, SparseCore 0:
  11.2 60.1 all-gather.13
  75.1 67.3 all-gather.7
  144.9 53.5 all-gather.9
  224.0 80.7 all-gather.15
  309.1 80.2 all-gather.11

commit v3 on v2

--- a/solution.py
+++ b/solution.py
@@ -23,39 +23,37 @@
     return sorted({0, block, min(block + 1, sections - 1)})
 
 
-def by_ring(slot):
-    return slot > 0 and slot % 2 == 0
-
-
-def fetch_weights(block, sections, scal, sources, weights, sem):
-    s, z, core = scal[0], scal[1], scal[2]
+offsets = (4, 0, 1, 2, 3, 5, 6, 7, 8)
+
+
+def overlap(offset, height, width):
+    r, c = divmod(offset, 3)
+    cells = slice(max(0, 1 - r), min(height, height + 1 - r)), slice(
+        max(0, 1 - c), min(width, width + 1 - c)
+    )
+    neighbours = slice(max(0, r - 1), min(height, height + r - 1)), slice(
+        max(0, c - 1), min(width, width + c - 1)
+    )
+    return cells, neighbours
+
+
+def fetch_weights(block, sections, scal, sources, weights, sems):
+    s = scal[0]
     slot = jnp.where(block == s, 0, jnp.where(block < s, block + 1, block))
-    slots = slots_of(block, sections)
-    sources = list(sources)
-
-    def start(arrays):
-        if len(arrays) == 1:
-            pltpu.make_async_copy(arrays[0], weights, sem).start()
-            return
-        for which, source in enumerate(arrays):
-            ring, depth = source.shape[:2]
-            owner_core = core if which == 0 else 1 - core
-            for j in range(ring):
-                place = lax.rem(z + j, ring)
-                row = pl.multiple_of((place * 2 + owner_core) * depth, depth)
-                pltpu.make_async_copy(
-                    source.at[j], weights.at[pl.ds(row, depth), :], sem
-                ).start()
-
-    for candidate in slots:
-        count = 2 if by_ring(candidate) else 1
-        arrays, sources = sources[:count], sources[count:]
+    rows = weights.shape[0] // 9
+
+    def copy(source, offset):
+        part = pl.ds(offset * rows, rows)
+        return pltpu.make_async_copy(source.at[part, :], weights.at[part, :], sems.at[offset])
+
+    for candidate, source in zip(slots_of(block, sections), sources):
 
         @pl.when(slot == candidate)
         def _():
-            start(arrays)
-
-    return lambda: pltpu.make_async_copy(weights, weights, sem).wait()
+            for offset in offsets:
+                copy(source, offset).start()
+
+    return lambda offset: copy(weights, offset).wait()
 
 
 def forward_kernel(dims, block, scal, *refs):
@@ -63,40 +61,33 @@
     sections, height, width, images, steps = dims
     slices = refs[:sections]
     refs = refs[sections:]
-    count = sum(2 if by_ring(slot) else 1 for slot in slots_of(block, sections))
+    count = len(slots_of(block, sections))
     sources = refs[:count]
     refs = refs[count:]
     if last:
-        readout, out, fired_out, logits_out, weights, padded, work, sem = refs
+        readout, out, fired_out, logits_out, weights, held, work, total, sems = refs
     else:
-        out, fired_out, weights, padded, work, sem = refs
-    wait = fetch_weights(block, sections, scal, sources, weights, sem)
+        out, fired_out, weights, held, work, total, sems = refs
+    wait = fetch_weights(block, sections, scal, sources, weights, sems)
     rows, lanes = slices[0].shape
     group = images * steps
     channels = sections * lanes
-    padded[...] = jnp.zeros_like(padded)
     for k in range(sections):
-        padded[scal[0] ^ k, 1 : height + 1, 1 : width + 1] = slices[k][...].reshape(
-            height, width, group, lanes
-        )
-    wait()
-    total = jnp.zeros((rows, lanes), jnp.float32)
-    for offset in range(9):
-        r, c = divmod(offset, 3)
+        held[scal[0] ^ k] = slices[k][...].reshape(height, width, group, lanes)
+    for offset in offsets:
+        cells, neighbours = overlap(offset, height, width)
+        wait(offset)
         lhs = jnp.concatenate(
-            [
-                padded[j, r : r + height, c : c + width].reshape(rows, lanes)
-                for j in range(sections)
-            ],
-            axis=1,
-        )
-        total += jnp.dot(
+            [held[(j, *neighbours)].reshape(-1, lanes) for j in range(sections)], axis=1
+        )
+        part = jnp.dot(
             lhs,
             weights[offset * channels : (offset + 1) * channels, :],
             preferred_element_type=jnp.float32,
-        )
+        ).reshape(*total[cells].shape)
+        total[cells] = part if offset == offsets[0] else total[cells] + part
     scale = float(9 * channels) ** (-0.5)
-    current = total * scale
+    current = total[...].reshape(rows, lanes) * scale
     count = rows // steps
     tiles = lanes // 128
     for tile in range(tiles):
@@ -138,14 +129,13 @@
     fired = refs[0]
     refs = refs[1:]
     if stage < 2:
-        count = sum(2 if by_ring(slot) else 1 for slot in slots_of(block, sections))
+        count = len(slots_of(block, sections))
         sources = refs[:count]
         refs = refs[count:]
         raw_out, own_out = refs[:2]
         sends = refs[2 : 1 + sections]
-        weights, padded, upstream, work, sem = refs[1 + sections :]
-        wait = fetch_weights(block, sections, scal, sources, weights, sem)
-        padded[...] = jnp.zeros_like(padded)
+        weights, held, upstream, work, total, sems = refs[1 + sections :]
+        wait = fetch_weights(block, sections, scal, sources, weights, sems)
     else:
         raw_out, upstream, work = refs
     tiles, rows = fired.shape[:2]
@@ -196,24 +186,25 @@
     raw_out[...] = raw
     if stage == 2:
         return
-    padded[1 : height + 1, 1 : width + 1] = raw.reshape(height, width, group, lanes)
-    wait()
+    held[...] = raw.reshape(height, width, group, lanes)
     for k in list(range(1, sections)) + [0]:
-        total = jnp.zeros((rows, lanes), jnp.float32)
-        for offset in range(9):
-            r, c = divmod(offset, 3)
-            lhs = padded[2 - r : 2 - r + height, 2 - c : 2 - c + width].reshape(rows, lanes)
+        for offset in offsets:
+            cells, neighbours = overlap(offset, height, width)
+            if k == 1 or sections == 1:
+                wait(offset)
             row = pl.multiple_of(offset * channels + (scal[0] ^ k) * lanes, lanes)
-            total += lax.dot_general(
-                lhs,
+            part = lax.dot_general(
+                held[cells].reshape(-1, lanes),
                 weights[pl.ds(row, lanes), :],
                 (((1,), (1,)), ((), ())),
                 preferred_element_type=jnp.float32,
-            )
+            ).reshape(*total[neighbours].shape)
+            total[neighbours] = part if offset == offsets[0] else total[neighbours] + part
+        whole = total[...].reshape(rows, lanes)
         if k == 0:
-            own_out[...] = total + jnp.concatenate([upstream[tile] for tile in range(tiles)], axis=1)
+            own_out[...] = whole + jnp.concatenate([upstream[tile] for tile in range(tiles)], axis=1)
         else:
-            sends[k - 1][...] = total.astype(jnp.bfloat16)
+            sends[k - 1][...] = whole.astype(jnp.bfloat16)
 
 
 def stay(arrays):
@@ -249,9 +240,10 @@
         out_specs=vmem(len(shapes)),
         scratch_shapes=[
             VMEM((depth, lanes), jnp.bfloat16),
-            VMEM((sections, height + 2, width + 2, images * steps, lanes), jnp.bfloat16),
+            VMEM((sections, height, width, images * steps, lanes), jnp.bfloat16),
             VMEM((lanes // 128, rows, 128), jnp.float32),
-            pltpu.SemaphoreType.DMA,
+            VMEM((height, width, images * steps, lanes), jnp.float32),
+            pltpu.SemaphoreType.DMA((9,)),
         ],
         compiler_params=pltpu.CompilerParams(vmem_limit_bytes=LIMIT),
         cost_estimate=pl.CostEstimate(
@@ -282,10 +274,13 @@
         work = (
             [
                 VMEM((depth, lanes), jnp.bfloat16),
-                VMEM((height + 2, width + 2, images * steps, lanes), jnp.bfloat16),
+                VMEM((height, width, images * steps, lanes), jnp.bfloat16),
             ]
             + work
-            + [pltpu.SemaphoreType.DMA]
+            + [
+                VMEM((height, width, images * steps, lanes), jnp.float32),
+                pltpu.SemaphoreType.DMA((9,)),
+            ]
         )
         cost = depth
     else:
@@ -323,11 +318,46 @@
     return lax.ppermute(value, "dp", [(i, i ^ 1) for i in range(count)])
 
 
-def adam_update(weights, first_moment, second_moment, grad_total):
-    new_first = beta_first * first_moment + (1.0 - beta_first) * grad_total
-    new_second = beta_second * second_moment + (1.0 - beta_second) * grad_total * grad_total
-    new_weights = weights - learn_rate * new_first / (jnp.sqrt(new_second) + adam_eps)
-    return (new_weights, new_first, new_second)
+def update_kernel(cols, raw, weights, first_moment, second_moment, *outs):
+    grad = jnp.dot(cols[...], raw[...], preferred_element_type=jnp.float32)
+    new_first = beta_first * first_moment[...] + (1.0 - beta_first) * grad
+    new_second = beta_second * second_moment[...] + (1.0 - beta_second) * grad * grad
+    outs[0][...] = weights[...] - learn_rate * new_first / (jnp.sqrt(new_second) + adam_eps)
+    outs[1][...] = new_first
+    outs[2][...] = new_second
+
+
+def run_update(cols, raw, weights, first_moment, second_moment):
+    depth, channels = weights.shape
+    rows = raw.shape[0]
+    tile = min(256, channels)
+    state = pl.BlockSpec((depth, tile), lambda i: (0, i))
+    return pl.pallas_call(
+        update_kernel,
+        grid=(channels // tile,),
+        out_shape=[jax.ShapeDtypeStruct(weights.shape, jnp.float32)] * 3,
+        in_specs=[
+            pl.BlockSpec(memory_space=VMEM),
+            pl.BlockSpec((rows, tile), lambda i: (0, i)),
+            state,
+            state,
+            state,
+        ],
+        out_specs=[state] * 3,
+        compiler_params=pltpu.CompilerParams(vmem_limit_bytes=40 * 2**20),
+        cost_estimate=pl.CostEstimate(
+            flops=2 * rows * depth * channels,
+            bytes_accessed=24 * depth * channels + 2 * rows * channels,
+            transcendentals=0,
+        ),
+        name="update",
+    )(
+        pltpu.with_memory_space_constraint(cols, VMEM),
+        raw,
+        weights,
+        first_moment,
+        second_moment,
+    )
 
 
 def shards(spikes, labels, readout, weights, first_moment, second_moment):
@@ -366,14 +396,25 @@
     readout_own = lax.dynamic_slice_in_dim(readout, s * lanes, lanes, 0)
     readout_own = jnp.pad(readout_own, ((0, 0), (0, padded_classes - classes)))
 
-    inputs, results, slots, done = [slices], [], {}, {}
+    inputs, results, slots, rings, done = [slices], [], {}, {}, {}
     own_inputs = jnp.stack(slices)
 
     def holding(b):
-        return [array for slot in slots_of(b, sections) for array in slots[slot]]
+        return [slots[slot] for slot in slots_of(b, sections)]
+
+    def lay_out(slot, earlier):
+        whole = jnp.zeros((devices, depth, lanes), jnp.bfloat16)
+        for place, pieces_held in zip((core, 1 - core), rings[slot]):
+            pieces_held = after(pieces_held, earlier)
+            for j in range(ring):
+                spot = lax.rem(z + j, ring) * 2 + place
+                whole = lax.dynamic_update_index_in_dim(whole, pieces_held[j], spot, 0)
+        return whole.reshape(devices * depth, lanes)
 
     def forward(b):
         nonlocal own_inputs
+        if b + 1 in rings:
+            slots[b + 1] = lay_out(b + 1, results[b - 1][0])
         results.append(run_forward(dims, b, scal, inputs[b], holding(b), readout_own))
         if b < sections - 1:
             out = results[b][0]
@@ -397,12 +438,12 @@
         for j in range(1, ring):
             held.append(jnp.where(z + j < ring, done[slot, j][1], done[slot, ring - j][0]))
         held = jnp.stack(held)
-        slots[slot] = [held, swap_core(held)]
+        rings[slot] = (held, swap_core(held))
     gates = []
     for slot in [0] + list(range(1, sections, 2)):
         piece = after(piece_of(slot), *gates) if gates else piece_of(slot)
         gathered = lax.all_gather(piece, "dp", axis=0, tiled=True)
-        slots[slot] = [gathered]
+        slots[slot] = gathered
         gates = [gathered] + done.get((2, 1) if slot == 0 else (slot + 1, ring - 1), [])
     for b in range(sections):
         forward(b)
@@ -455,11 +496,8 @@
     cols = lax.dynamic_slice_in_dim(jnp.concatenate(shifted, axis=1), channel, depth, 1)
 
     raw_all = lax.all_gather(own_raw, "dp", axis=0, tiled=True)
-    raw_all, cols = lax.optimization_barrier((raw_all, cols))
-    grad = lax.dot_general(
-        cols, raw_all, (((0,), (0,)), ((), ())), preferred_element_type=jnp.float32
-    )
-    return adam_update(weights, first_moment, second_moment, grad[None])
+    outs = run_update(cols.T, raw_all, weights[0], first_moment[0], second_moment[0])
+    return tuple(out[None] for out in outs)
 
 
 def solution(mesh):

time: 420 us -> 420 us (level)
  local copies, waits for them, and re-layouts: 26.2 us -> 63.6 us
  waiting for transfers between devices: 247 us -> 210 us
  matrix products: 23.2 us -> 0 us
  Pallas kernels: 48.2 us -> 65.4 us
  other arithmetic: 16 us -> 21.1 us
    all_gather x1, waiting for transfers between devices: 66.1 us -> 33.2 us  [shards(): raw_all = lax.all_gather(own_raw, 'dp', axis=0, tiled=True)]
    dot_general x1 -> x0, matrix products: 23.2 us -> none  [shards(): lax.dot_general(cols, raw_all, (((0,), (0,)), ((), ())), preferred_elemen...]
    reshape x0 -> x2, local copies, waits for them, and re-layouts: none -> 22.7 us  [shards(): shifted.append(lax.dynamic_slice(fields, (0, offset // 3, offset % 3, 0,...]
    pallas_call x0 -> x1, Pallas kernels: none -> 17.4 us  [run_update(): pl.pallas_call(update_kernel, grid=(channels // tile,), out_shape=[jax.Sh...]
    transpose x0 -> x1, other arithmetic: none -> 11.5 us  [shards(): outs = run_update(cols.T, raw_all, weights[0], first_moment[0], second_mo...]
    concatenate x1 -> x0, other arithmetic: 7.02 us -> none  [shards(): jnp.concatenate(shifted, axis=1)]
    dynamic_slice x1, local copies, waits for them, and re-layouts: 7.16 us -> 12.3 us  [shards(): lax.dynamic_slice(fields, (0, offset // 3, offset % 3, 0, 0), (devices, h...]
    ppermute x27, waiting for transfers between devices: 89.6 us -> 84.7 us  [exchange(): lax.ppermute(values[k], 'section', [(i, i ^ k + 1) for i in range(section...]
  transfers between devices with their start and end apart: 39 -> 39, of which waited for: 27 -> 27; matrix products, arithmetic and copies ran while one was open for 7% -> 16% of each run, Pallas kernels for 10% -> 10%
where the time goes in v3:
time: 420 us; the launch traced here: 418 us
  waiting for transfers between devices  210 us (50%)
  Pallas kernels  65.4 us (16%)
  local copies, waits for them, and re-layouts  63.6 us (15%)
  starting transfers between devices  44.1 us (10%)
  other arithmetic  21.1 us (5%)
  between operations  14.5 us (3%)
    ppermute x3, waiting for transfers between devices, shards(): down = lax.ppermute(down, 'dp', hops(step, -1, ring))  86.6 us
    ppermute x27, waiting for transfers between devices, exchange(): lax.ppermute(values[k], 'section', [(i, i ^ k + 1) for i in range(section...  84.7 us
    all_gather x1, waiting for transfers between devices, shards(): raw_all = lax.all_gather(own_raw, 'dp', axis=0, tiled=True)  33.2 us
    ppermute x27, starting transfers between devices, exchange(): lax.ppermute(values[k], 'section', [(i, i ^ k + 1) for i in range(section...  32.8 us
    pallas_call x4, Pallas kernels, run_forward(): pl.pallas_call(functools.partial(forward_kernel, dims, block), out_shape=...  28.4 us
    reshape x2, local copies, waits for them, and re-layouts, shards(): shifted.append(lax.dynamic_slice(fields, (0, offset // 3, offset % 3, 0,...  22.7 us
    pallas_call x4, Pallas kernels, run_backward(): pl.pallas_call(functools.partial(backward_kernel, dims, block, classes),...  19.6 us
    pallas_call x1, Pallas kernels, run_update(): pl.pallas_call(update_kernel, grid=(channels // tile,), out_shape=[jax.Sh...  17.4 us
  transfers between devices with their start and end apart: 39, of which 27 were waited for; matrix products, arithmetic and copies ran while one was open for 16% of the time, Pallas kernels for 10%

profile of v3, /device:TPU:0, one launch (start us, length us, event | category | flops | bytes accessed | tf_op | source)
XLA Modules:
  0.0 418.4 jit_solution(961951091433145972)
XLA Ops:
  7.2 3.8 fusion.2
  11.1 3.0 collective-permute-start
  14.1 1.5 collective-permute-start.1
  15.7 1.3 constant_dynamic-slice_fusion.1
  17.0 1.3 copy.17
  18.3 1.8 copy.12
  20.2 1.4 pad.8.refs_6_.refs_5_
  22.6 5.9 %collective-permute-done = bf16[1152,256]{1,0:T(8,128)(2,1)S(1)} collective-permute-done((bf16[1152,256]{1,0:T(8,128)(2,1)}, bf16[1152,256]{1,0:T(8,128)(2,1)S(1)}, u32[]{:S(2)}, u32[]{:S(2)}) %collective-permute-start) | collective-permute-done | bytes 589856 | tf_op jit(solution)/shard_map/ppermute | solution.py:381
  28.5 13.4 %collective-permute-done.1 = bf16[1152,256]{1,0:T(8,128)(2,1)} collective-permute-done((bf16[1152,256]{1,0:T(8,128)(2,1)}, bf16[1152,256]{1,0:T(8,128)(2,1)}, u32[]{:S(2)}, u32[]{:S(2)}) %collective-permute-start.1) | collective-permute-done | bytes 589856 | tf_op jit(solution)/shard_map/ppermute | solution.py:381
  41.9 1.5 pad_maximum_fusion
  45.9 4.6 %collective-permute-start.3 = (bf16[1152,256]{1,0:T(8,128)(2,1)S(1)}, bf16[1152,256]{1,0:T(8,128)(2,1)S(1)}, u32[]{:S(2)}, u32[]{:S(2)}) collective-permute-start(bf16[1152,256]{1,0:T(8,128)(2,1)S(1)} %bitcast.111), channel_id=1, source_target_pairs={{0,2},{1,3},{2,4},{3,5},{4,6},{5,7},{8,10},{9,11},{10,12},{11,13},... | collective-permute-start | bytes 1769480 | tf_op jit(solution)/shard_map/ppermute | solution.py:434
  50.5 24.5 %collective-permute-done.4 = bf16[1152,256]{1,0:T(8,128)(2,1)S(1)} collective-permute-done((bf16[1152,256]{1,0:T(8,128)(2,1)S(1)}, bf16[1152,256]{1,0:T(8,128)(2,1)S(1)}, u32[]{:S(2)}, u32[]{:S(2)}) %collective-permute-start.4) | collective-permute-done | bytes 589856 | tf_op jit(solution)/shard_map/ppermute | solution.py:435
  75.1 1.3 collective-permute-start.10
  76.4 1.5 collective-permute-start.8
  77.9 21.5 %collective-permute-done.10 = bf16[1152,256]{1,0:T(8,128)(2,1)} collective-permute-done((bf16[1152,256]{1,0:T(8,128)(2,1)S(1)}, bf16[1152,256]{1,0:T(8,128)(2,1)}, u32[]{:S(2)}, u32[]{:S(2)}) %collective-permute-start.10) | collective-permute-done | bytes 589856 | tf_op jit(solution)/shard_map/ppermute | solution.py:435
  99.4 1.3 collective-permute-start.11
  101.4 2.0 select_bitcast_fusion.1
  103.3 40.6 %collective-permute-done.11 = bf16[1152,256]{1,0:T(8,128)(2,1)S(1)} collective-permute-done((bf16[1152,256]{1,0:T(8,128)(2,1)}, bf16[1152,256]{1,0:T(8,128)(2,1)S(1)}, u32[]{:S(2)}, u32[]{:S(2)}) %collective-permute-start.11) | collective-permute-done | bytes 589856 | tf_op jit(solution)/shard_map/ppermute | solution.py:435
  144.3 1.5 pad_maximum_fusion.1
  146.1 7.0 %forward_block.4 = (bf16[512,256]{1,0:T(8,128)(2,1)S(1)}, f32[2,512,128]{2,1,0:T(8,128)S(1)}) custom-call(s32[3]{0:T(128)S(1)} %pad_add_fusion.scal, bf16[512,256]{1,0:T(8,128)(2,1)} %get-tuple-element.89.refs_0_, bf16[512,256]{1,0:T(8,128)(2,1)} %get-tuple-element.88.refs_1_, bf16[512,256]{1,0:T(8,128)(2,1)} %get-tuple-element.87.refs_2_, ...), custom_call_target="tpu_custom_call" | custom-call | flops 2415919104 | bytes 4718592 | tf_op jit(solution)/shard_map/forward_block/pallas_call | solution.py:233
  153.9 2.8 collective-permute-start.7
  162.5 1.5 collective-permute-done.7.refs_3_
  164.0 5.2 %collective-permute-done.6.refs_2_ = bf16[512,256]{1,0:T(8,128)(2,1)S(1)} collective-permute-done((bf16[512,256]{1,0:T(8,128)(2,1)S(1)}, bf16[512,256]{1,0:T(8,128)(2,1)S(1)}, u32[]{:S(2)}, u32[]{:S(2)}) %collective-permute-start.6) | collective-permute-done | bytes 262176 | tf_op jit(solution)/shard_map/ppermute | solution.py:381
  170.0 7.0 %forward_block.5 = (bf16[512,256]{1,0:T(8,128)(2,1)S(1)}, f32[2,512,128]{2,1,0:T(8,128)S(1)}) custom-call(s32[3]{0:T(128)S(1)} %pad_add_fusion.scal, bf16[512,256]{1,0:T(8,128)(2,1)} %copy-done.2, bf16[512,256]{1,0:T(8,128)(2,1)} %copy-done.18, bf16[512,256]{1,0:T(8,128)(2,1)} %copy-done.17, bf16[512,256]{1,0:T(8,128)(2,1)} %copy-done.16, ...), custom_call_target="tpu_custom_call" | custom-call | flops 2415919104 | bytes 4718592 | tf_op jit(solution)/shard_map/forward_block/pallas_call | solution.py:233
  177.8 1.9 collective-permute-start.15
  179.6 1.4 collective-permute-start.14
  181.4 6.6 %collective-permute-done.15.refs_3_ = bf16[512,256]{1,0:T(8,128)(2,1)S(1)} collective-permute-done((bf16[512,256]{1,0:T(8,128)(2,1)S(1)}, bf16[512,256]{1,0:T(8,128)(2,1)S(1)}, u32[]{:S(2)}, u32[]{:S(2)}) %collective-permute-start.15) | collective-permute-done | bytes 262176 | tf_op jit(solution)/shard_map/ppermute | solution.py:381
  188.0 4.8 %collective-permute-done.14.refs_2_ = bf16[512,256]{1,0:T(8,128)(2,1)S(1)} collective-permute-done((bf16[512,256]{1,0:T(8,128)(2,1)S(1)}, bf16[512,256]{1,0:T(8,128)(2,1)S(1)}, u32[]{:S(2)}, u32[]{:S(2)}) %collective-permute-start.14) | collective-permute-done | bytes 262176 | tf_op jit(solution)/shard_map/ppermute | solution.py:381
  194.1 5.0 %all-gather.10.cloned.1.call-done.refs_6_.refs_5_.refs_8_.refs_7_ = bf16[9216,256]{1,0:T(8,128)(2,1)} async-done(((bf16[1152,256]{1,0:T(8,128)(2,1)}), bf16[9216,256]{1,0:T(8,128)(2,1)}) %all-gather.10.cloned.1.call-update) | async-done | bytes 4718608 | tf_op jit(solution)/shard_map/all_gather | solution.py:445
  199.2 7.0 %forward_block.6 = (bf16[512,256]{1,0:T(8,128)(2,1)S(1)}, f32[2,512,128]{2,1,0:T(8,128)S(1)}) custom-call(s32[3]{0:T(128)S(1)} %pad_add_fusion.scal, bf16[512,256]{1,0:T(8,128)(2,1)} %copy-done.4, bf16[512,256]{1,0:T(8,128)(2,1)} %copy-done.21, bf16[512,256]{1,0:T(8,128)(2,1)} %copy-done.20, bf16[512,256]{1,0:T(8,128)(2,1)} %copy-done.19, ...), custom_call_target="tpu_custom_call" | custom-call | flops 2415919104 | bytes 4718592 | tf_op jit(solution)/shard_map/forward_block/pallas_call | solution.py:233
  207.0 2.4 collective-permute-start.18
  210.5 6.6 %collective-permute-done.18.refs_3_ = bf16[512,256]{1,0:T(8,128)(2,1)S(1)} collective-permute-done((bf16[512,256]{1,0:T(8,128)(2,1)S(1)}, bf16[512,256]{1,0:T(8,128)(2,1)S(1)}, u32[]{:S(2)}, u32[]{:S(2)}) %collective-permute-start.18) | collective-permute-done | bytes 262176 | tf_op jit(solution)/shard_map/ppermute | solution.py:381
  217.1 4.9 %collective-permute-done.17.refs_2_ = bf16[512,256]{1,0:T(8,128)(2,1)S(1)} collective-permute-done((bf16[512,256]{1,0:T(8,128)(2,1)S(1)}, bf16[512,256]{1,0:T(8,128)(2,1)S(1)}, u32[]{:S(2)}, u32[]{:S(2)}) %collective-permute-start.17) | collective-permute-done | bytes 262176 | tf_op jit(solution)/shard_map/ppermute | solution.py:381
  222.1 1.9 maximum_select_fusion
  225.5 7.5 %forward_block.7 = (bf16[512,256]{1,0:T(8,128)(2,1)}, f32[2,512,128]{2,1,0:T(8,128)S(1)}, f32[4,1024]{1,0:T(4,128)S(1)}) custom-call(s32[3]{0:T(128)S(1)} %pad_add_fusion.scal, bf16[512,256]{1,0:T(8,128)(2,1)S(1)} %get-tuple-element.41.refs_0_, bf16[512,256]{1,0:T(8,128)(2,1)S(1)} %collective-permute-done.16.refs_1_, ...), custom_call_target="tpu_custom_call" | custom-call | flops 2415919104 | bytes 4718592 | tf_op jit(solution)/shard_map/forward_block/pallas_call | solution.py:233
  233.7 1.7 collective-permute-start.21
  240.4 6.9 %backward_block.4 = (bf16[512,256]{1,0:T(8,128)(2,1)S(1)}, f32[512,256]{1,0:T(8,128)S(1)}, bf16[512,256]{1,0:T(8,128)(2,1)S(1)}, bf16[512,256]{1,0:T(8,128)(2,1)S(1)}, bf16[512,256]{1,0:T(8,128)(2,1)S(1)}) custom-call(s32[3]{0:T(128)S(1)} %pad_add_fusion.scal, f32[4,1024]{1,0:T(4,128)S(1)} %get-tuple-element.42.refs_0_, ...), custom_call_target="tpu_custom_call" | custom-call | flops 2429026304 | bytes 5767168 | tf_op jit(solution)/shard_map/backward_block/pallas_call | solution.py:288
  248.0 1.4 collective-permute-start.23
  249.4 1.5 collective-permute-start.24
  250.9 5.8 %collective-permute-done.22.refs_1_ = bf16[512,256]{1,0:T(8,128)(2,1)S(1)} collective-permute-done((bf16[512,256]{1,0:T(8,128)(2,1)S(1)}, bf16[512,256]{1,0:T(8,128)(2,1)S(1)}, u32[]{:S(2)}, u32[]{:S(2)}) %collective-permute-start.22) | collective-permute-done | bytes 262176 | tf_op jit(solution)/shard_map/ppermute | solution.py:381
  256.7 3.5 collective-permute-done.23.refs_2_
  260.2 5.6 %backward_block.5 = (bf16[512,256]{1,0:T(8,128)(2,1)S(1)}, f32[512,256]{1,0:T(8,128)S(1)}, bf16[512,256]{1,0:T(8,128)(2,1)S(1)}, bf16[512,256]{1,0:T(8,128)(2,1)S(1)}, bf16[512,256]{1,0:T(8,128)(2,1)S(1)}) custom-call(s32[3]{0:T(128)S(1)} %pad_add_fusion.scal, f32[512,256]{1,0:T(8,128)S(1)} %get-tuple-element.44.refs_0_, ...), custom_call_target="tpu_custom_call" | custom-call | flops 2429026304 | bytes 5767168 | tf_op jit(solution)/shard_map/backward_block/pallas_call | solution.py:288
  265.8 1.6 collective-permute-start.25
  267.9 1.4 collective-permute-start.27
  269.3 4.8 %collective-permute-done.25.refs_1_ = bf16[512,256]{1,0:T(8,128)(2,1)S(1)} collective-permute-done((bf16[512,256]{1,0:T(8,128)(2,1)S(1)}, bf16[512,256]{1,0:T(8,128)(2,1)S(1)}, u32[]{:S(2)}, u32[]{:S(2)}) %collective-permute-start.25) | collective-permute-done | bytes 262176 | tf_op jit(solution)/shard_map/ppermute | solution.py:381
  274.2 4.4 %collective-permute-done.26.refs_2_ = bf16[512,256]{1,0:T(8,128)(2,1)S(1)} collective-permute-done((bf16[512,256]{1,0:T(8,128)(2,1)S(1)}, bf16[512,256]{1,0:T(8,128)(2,1)S(1)}, u32[]{:S(2)}, u32[]{:S(2)}) %collective-permute-start.26) | collective-permute-done | bytes 262176 | tf_op jit(solution)/shard_map/ppermute | solution.py:381
  278.5 5.6 %backward_block.6 = (bf16[512,256]{1,0:T(8,128)(2,1)S(1)}, f32[512,256]{1,0:T(8,128)S(1)}, bf16[512,256]{1,0:T(8,128)(2,1)S(1)}, bf16[512,256]{1,0:T(8,128)(2,1)S(1)}, bf16[512,256]{1,0:T(8,128)(2,1)S(1)}) custom-call(s32[3]{0:T(128)S(1)} %pad_add_fusion.scal, f32[512,256]{1,0:T(8,128)S(1)} %get-tuple-element.49.refs_0_, ...), custom_call_target="tpu_custom_call" | custom-call | flops 2429026304 | bytes 5767168 | tf_op jit(solution)/shard_map/backward_block/pallas_call | solution.py:288
  284.5 1.8 collective-permute-start.29
  286.2 1.4 collective-permute-start.30
  287.6 4.1 collective-permute-done.28.refs_1_
  291.8 2.9 collective-permute-done.29.refs_2_
  294.6 1.6 backward_block.7
  296.7 1.5 collective-permute-start.33
  298.2 1.7 collective-permute-start.32
  300.3 3.9 collective-permute-done.33
  304.2 2.7 collective-permute-done.32
  308.8 12.3 %pad_dynamic-slice_fusion = (bf16[8,4,4,32,1024]{4,3,2,1,0:T(8,128)(2,1)}, bf16[8,4,4,32,1024]{4,3,2,1,0:T(8,128)(2,1)}) fusion(s32[]{:T(128)S(6)} %select_n.213, s32[]{:T(128)S(6)} %select_n.215, bf16[8,4,4,32,1024]{4,3,2,1,0:T(8,128)(2,1)} %bitcast.108, s32[]{:T(128)S(6)} %select_n.209, s32[]{:T(128)S(6)} %select_n.211), kind=kLoop, calls=%fused_computation | loop fusion | bytes 25165840 | tf_op jit(solution)/shard_map/dynamic_slice | solution.py:490
  321.1 11.3 %copy.15 = bf16[4096,1024]{0,1:T(8,128)(2,1)} copy(bf16[4096,1024]{1,0:T(8,128)(2,1)} %bitcast.107) | data formatting | bytes 16777216 | tf_op jit(solution)/shard_map/reshape | solution.py:494
  332.3 11.4 %copy.14 = bf16[4096,1024]{0,1:T(8,128)(2,1)} copy(bf16[4096,1024]{1,0:T(8,128)(2,1)} %bitcast.106) | data formatting | bytes 16777216 | tf_op jit(solution)/shard_map/reshape | solution.py:494
  343.8 11.5 %fusion.1.cols = bf16[1152,4096]{1,0:T(8,128)(2,1)} fusion(s32[]{:T(128)S(6)} %select_n.217, bf16[4096,1024]{0,1:T(8,128)(2,1)} %copy.14, bf16[4096,1024]{0,1:T(8,128)(2,1)} %copy.15), kind=kLoop, calls=%fused_computation.5 | loop fusion | flops 18874368 | bytes 26214404 | tf_op jit(solution)/shard_map/transpose | solution.py:499
  355.3 33.2 %all-gather.12.cloned.1.call-done.raw = bf16[4096,1024]{1,0:T(8,128)(2,1)} async-done(((bf16[512,1024]{1,0:T(8,128)(2,1)}), bf16[4096,1024]{1,0:T(8,128)(2,1)}) %all-gather.12.cloned.1.call-update) | async-done | bytes 8388624 | tf_op jit(solution)/shard_map/all_gather | solution.py:498
  388.5 3.7 copy-done
  392.2 2.3 copy-done.1
  394.5 17.4 %update.1 = (f32[1152,1024]{1,0:T(8,128)}, f32[1152,1024]{1,0:T(8,128)}, f32[1152,1024]{1,0:T(8,128)}) custom-call(bf16[1152,4096]{1,0:T(8,128)(2,1)S(1)} %copy-done, bf16[4096,1024]{1,0:T(8,128)(2,1)} %all-gather.12.cloned.1.call-done.raw, f32[1152,1024]{1,0:T(8,128)S(1)} %bitcast.84, f32[1152,1024]{1,0:T(8,128)} %bitcast.128, f32[1152,1024]{1,0:T(8,128)} %bitcast.129), custom_call_target="tpu_custom_call" | custom-call | flops 9663676416 | bytes 36700160 | tf_op jit(solution)/shard_map/update/pallas_call | solution.py:335
  (109 shorter events, 28.2 us)
Async XLA Ops:
  7.2 67.8 %all-gather.14.cloned.1.call-start = ((), (), s32[]{:S(2)}) async-start(), calls=%async_computation.3 | async-start | bytes 5308416 | tf_op jit(solution)/shard_map/all_gather | solution.py:445
  11.1 132.8 %all-gather.8.cloned.1.call-start = ((), (), s32[]{:S(2)}) async-start(), calls=%async_computation | async-start | bytes 5308416 | tf_op jit(solution)/shard_map/all_gather | solution.py:445
  11.1 17.4 %collective-permute-start = (bf16[1152,256]{1,0:T(8,128)(2,1)}, bf16[1152,256]{1,0:T(8,128)(2,1)S(1)}, u32[]{:S(2)}, u32[]{:S(2)}) collective-permute-start(bf16[1152,256]{1,0:T(8,128)(2,1)} %get-tuple-element.67), channel_id=1, source_target_pairs={{0,8},{8,0},{16,24},{24,16},{1,9},{9,1},{17,25},{25,17},{2,10},{10... | collective-permute-start | bytes 1769480 | tf_op jit(solution)/shard_map/ppermute | solution.py:381
  14.1 27.7 %collective-permute-start.1 = (bf16[1152,256]{1,0:T(8,128)(2,1)}, bf16[1152,256]{1,0:T(8,128)(2,1)}, u32[]{:S(2)}, u32[]{:S(2)}) collective-permute-start(bf16[1152,256]{1,0:T(8,128)(2,1)} %get-tuple-element.68), channel_id=1, source_target_pairs={{0,16},{8,24},{16,0},{24,8},{1,17},{9,25},{17,1},{25,9},{2,18},{10... | collective-permute-start | bytes 1769480 | tf_op jit(solution)/shard_map/ppermute | solution.py:381
  15.7 26.2 %collective-permute-start.2 = (bf16[1152,256]{1,0:T(8,128)(2,1)}, bf16[1152,256]{1,0:T(8,128)(2,1)}, u32[]{:S(2)}, u32[]{:S(2)}) collective-permute-start(bf16[1152,256]{1,0:T(8,128)(2,1)} %get-tuple-element.70), channel_id=1, source_target_pairs={{0,24},{8,16},{16,8},{24,0},{1,25},{9,17},{17,9},{25,1},{2,26},{10... | collective-permute-start | bytes 1769480 | tf_op jit(solution)/shard_map/ppermute | solution.py:381
  15.7 26.2 %copy-start.10 = (bf16[1,1152,256]{2,1,0:T(8,128)(2,1)S(1)}, bf16[1,1152,256]{2,1,0:T(8,128)(2,1)}, u32[]{:S(2)}) copy-start(bf16[1,1152,256]{2,1,0:T(8,128)(2,1)} %get-tuple-element.69) | copy-start | bytes 1769476
  44.6 1.3 copy-start.11
  44.6 30.4 %collective-permute-start.4 = (bf16[1152,256]{1,0:T(8,128)(2,1)S(1)}, bf16[1152,256]{1,0:T(8,128)(2,1)S(1)}, u32[]{:S(2)}, u32[]{:S(2)}) collective-permute-start(bf16[1152,256]{1,0:T(8,128)(2,1)S(1)} %bitcast.110), channel_id=1, source_target_pairs={{2,0},{3,1},{4,2},{5,3},{6,4},{7,5},{10,8},{11,9},{12,10},{13,11},... | collective-permute-start | bytes 1769480 | tf_op jit(solution)/shard_map/ppermute | solution.py:435
  45.9 29.1 %collective-permute-start.3 = (bf16[1152,256]{1,0:T(8,128)(2,1)S(1)}, bf16[1152,256]{1,0:T(8,128)(2,1)S(1)}, u32[]{:S(2)}, u32[]{:S(2)}) collective-permute-start(bf16[1152,256]{1,0:T(8,128)(2,1)S(1)} %bitcast.111), channel_id=1, source_target_pairs={{0,2},{1,3},{2,4},{3,5},{4,6},{5,7},{8,10},{9,11},{10,12},{11,13},... | collective-permute-start | bytes 1769480 | tf_op jit(solution)/shard_map/ppermute | solution.py:434
  75.0 124.2 %all-gather.10.cloned.1.call-start = ((), (), s32[]{:S(2)}) async-start(), calls=%async_computation.1 | async-start | bytes 5308416 | tf_op jit(solution)/shard_map/all_gather | solution.py:445
  75.1 24.3 %collective-permute-start.10 = (bf16[1152,256]{1,0:T(8,128)(2,1)S(1)}, bf16[1152,256]{1,0:T(8,128)(2,1)}, u32[]{:S(2)}, u32[]{:S(2)}) collective-permute-start(bf16[1152,256]{1,0:T(8,128)(2,1)S(1)} %collective-permute-done.4), channel_id=1, source_target_pairs={{2,0},{3,1},{4,2},{5,3},{10,8},{11,9},{12,10},{13,11},{18,16},{19,... | collective-permute-start | bytes 1769480 | tf_op jit(solution)/shard_map/ppermute | solution.py:435
  76.4 24.3 %collective-permute-start.8 = (bf16[1152,256]{1,0:T(8,128)(2,1)S(1)}, bf16[1152,256]{1,0:T(8,128)(2,1)}, u32[]{:S(2)}, u32[]{:S(2)}) collective-permute-start(bf16[1152,256]{1,0:T(8,128)(2,1)S(1)} %collective-permute-done.3), channel_id=1, source_target_pairs={{2,4},{3,5},{4,6},{5,7},{10,12},{11,13},{12,14},{13,15},{18,20},{1... | collective-permute-start | bytes 1769480 | tf_op jit(solution)/shard_map/ppermute | solution.py:434
  99.4 44.6 %collective-permute-start.11 = (bf16[1152,256]{1,0:T(8,128)(2,1)}, bf16[1152,256]{1,0:T(8,128)(2,1)S(1)}, u32[]{:S(2)}, u32[]{:S(2)}) collective-permute-start(bf16[1152,256]{1,0:T(8,128)(2,1)} %collective-permute-done.10), channel_id=1, source_target_pairs={{2,0},{3,1},{10,8},{11,9},{18,16},{19,17},{26,24},{27,25}} | collective-permute-start | bytes 1769480 | tf_op jit(solution)/shard_map/ppermute | solution.py:435
  100.7 43.3 %collective-permute-start.9 = (bf16[1152,256]{1,0:T(8,128)(2,1)}, bf16[1152,256]{1,0:T(8,128)(2,1)S(1)}, u32[]{:S(2)}, u32[]{:S(2)}) collective-permute-start(bf16[1152,256]{1,0:T(8,128)(2,1)} %collective-permute-done.8), channel_id=1, source_target_pairs={{4,6},{5,7},{12,14},{13,15},{20,22},{21,23},{28,30},{29,31}} | collective-permute-start | bytes 1769480 | tf_op jit(solution)/shard_map/ppermute | solution.py:434
  144.0 164.8 %all-gather.16.cloned.1.call-start = ((), (), s32[]{:S(2)}) async-start(), calls=%async_computation.4 | async-start | bytes 9437184 | tf_op jit(solution)/shard_map/all_gather | solution.py:465
  145.9 11.6 %collective-permute-start.12 = (bf16[4,1152,256]{2,1,0:T(8,128)(2,1)S(1)}, bf16[4,1152,256]{2,1,0:T(8,128)(2,1)}, u32[]{:S(2)}, u32[]{:S(2)}) collective-permute-start(bf16[4,1152,256]{2,1,0:T(8,128)(2,1)S(1)} %pad_maximum_fusion.1), channel_id=1, source_target_pairs={{0,1},{1,0},{2,3},{3,2},{4,5},{5,4},{6,7},{7,6},{8,9},{9,8},{10,11... | collective-permute-start | bytes 7077896 | tf_op jit(solution)/shard_map/ppermute | solution.py:318
  153.1 0.8 copy-start.5
  153.9 4.1 copy-start.2
  153.9 10.1 %collective-permute-start.7 = (bf16[512,256]{1,0:T(8,128)(2,1)S(1)}, bf16[512,256]{1,0:T(8,128)(2,1)S(1)}, u32[]{:S(2)}, u32[]{:S(2)}) collective-permute-start(bf16[512,256]{1,0:T(8,128)(2,1)S(1)} %get-tuple-element.36.refs_0_), channel_id=1, source_target_pairs={{0,24},{8,16},{16,8},{24,0},{1,25},{9,17},{17,9},{25,1},{2,26},{10... | collective-permute-start | bytes 786440 | tf_op jit(solution)/shard_map/ppermute | solution.py:381
  156.7 12.5 %collective-permute-start.6 = (bf16[512,256]{1,0:T(8,128)(2,1)S(1)}, bf16[512,256]{1,0:T(8,128)(2,1)S(1)}, u32[]{:S(2)}, u32[]{:S(2)}) collective-permute-start(bf16[512,256]{1,0:T(8,128)(2,1)S(1)} %get-tuple-element.36.refs_0_), channel_id=1, source_target_pairs={{0,16},{8,24},{16,0},{24,8},{1,17},{9,25},{17,1},{25,9},{2,18},{10... | collective-permute-start | bytes 786440 | tf_op jit(solution)/shard_map/ppermute | solution.py:381
  157.0 12.3 %collective-permute-start.5 = (bf16[512,256]{1,0:T(8,128)(2,1)S(1)}, bf16[512,256]{1,0:T(8,128)(2,1)S(1)}, u32[]{:S(2)}, u32[]{:S(2)}) collective-permute-start(bf16[512,256]{1,0:T(8,128)(2,1)S(1)} %get-tuple-element.36.refs_0_), channel_id=1, source_target_pairs={{0,8},{8,0},{16,24},{24,16},{1,9},{9,1},{17,25},{25,17},{2,10},{10... | collective-permute-start | bytes 786440 | tf_op jit(solution)/shard_map/ppermute | solution.py:381
  162.4 6.8 %copy-start.9 = (bf16[8,1152,256]{2,1,0:T(8,128)(2,1)}, bf16[8,1152,256]{2,1,0:T(8,128)(2,1)S(1)}, u32[]{:S(2)}) copy-start(bf16[8,1152,256]{2,1,0:T(8,128)(2,1)S(1)} %slice_dynamic-update-slice_fusion) | copy-start | bytes 14155780
  164.0 5.3 %copy-start.16 = (bf16[512,256]{1,0:T(8,128)(2,1)}, bf16[512,256]{1,0:T(8,128)(2,1)S(1)}, u32[]{:S(2)}) copy-start(bf16[512,256]{1,0:T(8,128)(2,1)S(1)} %collective-permute-done.7.refs_3_) | copy-start | bytes 786436
  169.2 0.7 copy-start.17
  169.3 0.7 copy-start.18
  177.0 0.8 copy-start.6
  177.8 21.4 %copy-start.4 = (bf16[512,256]{1,0:T(8,128)(2,1)}, bf16[512,256]{1,0:T(8,128)(2,1)S(1)}, u32[]{:S(2)}) copy-start(bf16[512,256]{1,0:T(8,128)(2,1)S(1)} %get-tuple-element.39.refs_0_) | copy-start | bytes 786436
  177.8 44.3 %copy-start.3 = (bf16[512,256]{1,0:T(8,128)(2,1)S(1)}, bf16[512,256]{1,0:T(8,128)(2,1)}, u32[]{:S(2)}) copy-start(bf16[512,256]{1,0:T(8,128)(2,1)} %copy-done.2) | copy-start | bytes 786436
  177.8 44.3 %copy-start.12 = (bf16[512,256]{1,0:T(8,128)(2,1)S(1)}, bf16[512,256]{1,0:T(8,128)(2,1)}, u32[]{:S(2)}) copy-start(bf16[512,256]{1,0:T(8,128)(2,1)} %get-tuple-element.86.refs_3_) | copy-start | bytes 786436
  177.8 44.3 %copy-start.13 = (bf16[512,256]{1,0:T(8,128)(2,1)S(1)}, bf16[512,256]{1,0:T(8,128)(2,1)}, u32[]{:S(2)}) copy-start(bf16[512,256]{1,0:T(8,128)(2,1)} %get-tuple-element.87.refs_2_) | copy-start | bytes 786436
  177.8 44.3 %copy-start.14 = (bf16[512,256]{1,0:T(8,128)(2,1)S(1)}, bf16[512,256]{1,0:T(8,128)(2,1)}, u32[]{:S(2)}) copy-start(bf16[512,256]{1,0:T(8,128)(2,1)} %get-tuple-element.88.refs_1_) | copy-start | bytes 786436
  177.8 44.3 %copy-start.15 = (bf16[512,256]{1,0:T(8,128)(2,1)S(1)}, bf16[512,256]{1,0:T(8,128)(2,1)}, u32[]{:S(2)}) copy-start(bf16[512,256]{1,0:T(8,128)(2,1)} %get-tuple-element.89.refs_0_) | copy-start | bytes 786436
  177.8 10.2 %collective-permute-start.15 = (bf16[512,256]{1,0:T(8,128)(2,1)S(1)}, bf16[512,256]{1,0:T(8,128)(2,1)S(1)}, u32[]{:S(2)}, u32[]{:S(2)}) collective-permute-start(bf16[512,256]{1,0:T(8,128)(2,1)S(1)} %get-tuple-element.39.refs_0_), channel_id=1, source_target_pairs={{0,24},{8,16},{16,8},{24,0},{1,25},{9,17},{17,9},{25,1},{2,26},{10... | collective-permute-start | bytes 786440 | tf_op jit(solution)/shard_map/ppermute | solution.py:381
  179.6 13.1 %collective-permute-start.14 = (bf16[512,256]{1,0:T(8,128)(2,1)S(1)}, bf16[512,256]{1,0:T(8,128)(2,1)S(1)}, u32[]{:S(2)}, u32[]{:S(2)}) collective-permute-start(bf16[512,256]{1,0:T(8,128)(2,1)S(1)} %get-tuple-element.39.refs_0_), channel_id=1, source_target_pairs={{0,16},{8,24},{16,0},{24,8},{1,17},{9,25},{17,1},{25,9},{2,18},{10... | collective-permute-start | bytes 786440 | tf_op jit(solution)/shard_map/ppermute | solution.py:381
  181.1 11.8 %collective-permute-start.13 = (bf16[512,256]{1,0:T(8,128)(2,1)S(1)}, bf16[512,256]{1,0:T(8,128)(2,1)S(1)}, u32[]{:S(2)}, u32[]{:S(2)}) collective-permute-start(bf16[512,256]{1,0:T(8,128)(2,1)S(1)} %get-tuple-element.39.refs_0_), channel_id=1, source_target_pairs={{0,8},{8,0},{16,24},{24,16},{1,9},{9,1},{17,25},{25,17},{2,10},{10... | collective-permute-start | bytes 786440 | tf_op jit(solution)/shard_map/ppermute | solution.py:381
  188.0 4.9 %copy-start.19 = (bf16[512,256]{1,0:T(8,128)(2,1)}, bf16[512,256]{1,0:T(8,128)(2,1)S(1)}, u32[]{:S(2)}) copy-start(bf16[512,256]{1,0:T(8,128)(2,1)S(1)} %collective-permute-done.15.refs_3_) | copy-start | bytes 786436
  192.7 0.7 copy-start.20
  193.4 0.7 copy-start.21
  206.2 0.8 copy-start.7
  207.0 10.1 %collective-permute-start.18 = (bf16[512,256]{1,0:T(8,128)(2,1)S(1)}, bf16[512,256]{1,0:T(8,128)(2,1)S(1)}, u32[]{:S(2)}, u32[]{:S(2)}) collective-permute-start(bf16[512,256]{1,0:T(8,128)(2,1)S(1)} %get-tuple-element.41.refs_0_), channel_id=1, source_target_pairs={{0,24},{8,16},{16,8},{24,0},{1,25},{9,17},{17,9},{25,1},{2,26},{10... | collective-permute-start | bytes 786440 | tf_op jit(solution)/shard_map/ppermute | solution.py:381
  209.4 12.6 %collective-permute-start.17 = (bf16[512,256]{1,0:T(8,128)(2,1)S(1)}, bf16[512,256]{1,0:T(8,128)(2,1)S(1)}, u32[]{:S(2)}, u32[]{:S(2)}) collective-permute-start(bf16[512,256]{1,0:T(8,128)(2,1)S(1)} %get-tuple-element.41.refs_0_), channel_id=1, source_target_pairs={{0,16},{8,24},{16,0},{24,8},{1,17},{9,25},{17,1},{25,9},{2,18},{10... | collective-permute-start | bytes 786440 | tf_op jit(solution)/shard_map/ppermute | solution.py:381
  210.0 12.1 %collective-permute-start.16 = (bf16[512,256]{1,0:T(8,128)(2,1)S(1)}, bf16[512,256]{1,0:T(8,128)(2,1)S(1)}, u32[]{:S(2)}, u32[]{:S(2)}) collective-permute-start(bf16[512,256]{1,0:T(8,128)(2,1)S(1)} %get-tuple-element.41.refs_0_), channel_id=1, source_target_pairs={{0,8},{8,0},{16,24},{24,16},{1,9},{9,1},{17,25},{25,17},{2,10},{10... | collective-permute-start | bytes 786440 | tf_op jit(solution)/shard_map/ppermute | solution.py:381
  225.2 12.1 %copy-start.22 = (s32[4]{0:T(128)S(1)}, s32[4]{0:T(128)}, u32[]{:S(2)}) copy-start(s32[4]{0:T(128)} %param.7) | copy-start | bytes 52
  225.2 163.3 %all-gather.12.cloned.1.call-start = ((), (), s32[]{:S(2)}) async-start(), calls=%async_computation.2 | async-start | bytes 9437184 | tf_op jit(solution)/shard_map/all_gather | solution.py:498
  232.9 0.8 copy-start.8
  233.7 4.6 %collective-permute-start.21 = (f32[4,1024]{1,0:T(4,128)S(1)}, f32[4,1024]{1,0:T(4,128)S(1)}, u32[]{:S(2)}, u32[]{:S(2)}) collective-permute-start(f32[4,1024]{1,0:T(4,128)S(1)} %get-tuple-element.42.refs_0_), channel_id=1, source_target_pairs={{0,24},{8,16},{16,8},{24,0},{1,25},{9,17},{17,9},{25,1},{2,26},{10... | collective-permute-start | bytes 49160 | tf_op jit(solution)/shard_map/ppermute | solution.py:381
  235.4 3.7 collective-permute-start.20
  236.7 3.7 collective-permute-start.19
  247.4 9.3 %collective-permute-start.22 = (bf16[512,256]{1,0:T(8,128)(2,1)S(1)}, bf16[512,256]{1,0:T(8,128)(2,1)S(1)}, u32[]{:S(2)}, u32[]{:S(2)}) collective-permute-start(bf16[512,256]{1,0:T(8,128)(2,1)S(1)} %get-tuple-element.45), channel_id=1, source_target_pairs={{0,8},{8,0},{16,24},{24,16},{1,9},{9,1},{17,25},{25,17},{2,10},{10... | collective-permute-start | bytes 786440 | tf_op jit(solution)/shard_map/ppermute | solution.py:381
  248.0 12.2 %collective-permute-start.23 = (bf16[512,256]{1,0:T(8,128)(2,1)S(1)}, bf16[512,256]{1,0:T(8,128)(2,1)S(1)}, u32[]{:S(2)}, u32[]{:S(2)}) collective-permute-start(bf16[512,256]{1,0:T(8,128)(2,1)S(1)} %get-tuple-element.46), channel_id=1, source_target_pairs={{0,16},{8,24},{16,0},{24,8},{1,17},{9,25},{17,1},{25,9},{2,18},{10... | collective-permute-start | bytes 786440 | tf_op jit(solution)/shard_map/ppermute | solution.py:381
  249.4 10.8 %collective-permute-start.24 = (bf16[512,256]{1,0:T(8,128)(2,1)S(1)}, bf16[512,256]{1,0:T(8,128)(2,1)S(1)}, u32[]{:S(2)}, u32[]{:S(2)}) collective-permute-start(bf16[512,256]{1,0:T(8,128)(2,1)S(1)} %get-tuple-element.47), channel_id=1, source_target_pairs={{0,24},{8,16},{16,8},{24,0},{1,25},{9,17},{17,9},{25,1},{2,26},{10... | collective-permute-start | bytes 786440 | tf_op jit(solution)/shard_map/ppermute | solution.py:381
  265.8 8.4 %collective-permute-start.25 = (bf16[512,256]{1,0:T(8,128)(2,1)S(1)}, bf16[512,256]{1,0:T(8,128)(2,1)S(1)}, u32[]{:S(2)}, u32[]{:S(2)}) collective-permute-start(bf16[512,256]{1,0:T(8,128)(2,1)S(1)} %get-tuple-element.50), channel_id=1, source_target_pairs={{0,8},{8,0},{16,24},{24,16},{1,9},{9,1},{17,25},{25,17},{2,10},{10... | collective-permute-start | bytes 786440 | tf_op jit(solution)/shard_map/ppermute | solution.py:381
  267.3 11.2 %collective-permute-start.26 = (bf16[512,256]{1,0:T(8,128)(2,1)S(1)}, bf16[512,256]{1,0:T(8,128)(2,1)S(1)}, u32[]{:S(2)}, u32[]{:S(2)}) collective-permute-start(bf16[512,256]{1,0:T(8,128)(2,1)S(1)} %get-tuple-element.51), channel_id=1, source_target_pairs={{0,16},{8,24},{16,0},{24,8},{1,17},{9,25},{17,1},{25,9},{2,18},{10... | collective-permute-start | bytes 786440 | tf_op jit(solution)/shard_map/ppermute | solution.py:381
  267.9 10.6 %collective-permute-start.27 = (bf16[512,256]{1,0:T(8,128)(2,1)S(1)}, bf16[512,256]{1,0:T(8,128)(2,1)S(1)}, u32[]{:S(2)}, u32[]{:S(2)}) collective-permute-start(bf16[512,256]{1,0:T(8,128)(2,1)S(1)} %get-tuple-element.52), channel_id=1, source_target_pairs={{0,24},{8,16},{16,8},{24,0},{1,25},{9,17},{17,9},{25,1},{2,26},{10... | collective-permute-start | bytes 786440 | tf_op jit(solution)/shard_map/ppermute | solution.py:381
  284.1 7.7 %collective-permute-start.28 = (bf16[512,256]{1,0:T(8,128)(2,1)S(1)}, bf16[512,256]{1,0:T(8,128)(2,1)S(1)}, u32[]{:S(2)}, u32[]{:S(2)}) collective-permute-start(bf16[512,256]{1,0:T(8,128)(2,1)S(1)} %get-tuple-element.55), channel_id=1, source_target_pairs={{0,8},{8,0},{16,24},{24,16},{1,9},{9,1},{17,25},{25,17},{2,10},{10... | collective-permute-start | bytes 786440 | tf_op jit(solution)/shard_map/ppermute | solution.py:381
  284.5 10.2 %collective-permute-start.29 = (bf16[512,256]{1,0:T(8,128)(2,1)S(1)}, bf16[512,256]{1,0:T(8,128)(2,1)S(1)}, u32[]{:S(2)}, u32[]{:S(2)}) collective-permute-start(bf16[512,256]{1,0:T(8,128)(2,1)S(1)} %get-tuple-element.56), channel_id=1, source_target_pairs={{0,16},{8,24},{16,0},{24,8},{1,17},{9,25},{17,1},{25,9},{2,18},{10... | collective-permute-start | bytes 786440 | tf_op jit(solution)/shard_map/ppermute | solution.py:381
  286.2 8.4 %collective-permute-start.30 = (bf16[512,256]{1,0:T(8,128)(2,1)S(1)}, bf16[512,256]{1,0:T(8,128)(2,1)S(1)}, u32[]{:S(2)}, u32[]{:S(2)}) collective-permute-start(bf16[512,256]{1,0:T(8,128)(2,1)S(1)} %get-tuple-element.57), channel_id=1, source_target_pairs={{0,24},{8,16},{16,8},{24,0},{1,25},{9,17},{17,9},{25,1},{2,26},{10... | collective-permute-start | bytes 786440 | tf_op jit(solution)/shard_map/ppermute | solution.py:381
  296.7 7.4 %collective-permute-start.33 = (bf16[512,256]{1,0:T(8,128)(2,1)S(1)}, bf16[512,256]{1,0:T(8,128)(2,1)S(1)}, u32[]{:S(2)}, u32[]{:S(2)}) collective-permute-start(bf16[512,256]{1,0:T(8,128)(2,1)S(1)} %get-tuple-element.79), channel_id=1, source_target_pairs={{0,24},{8,16},{16,8},{24,0},{1,25},{9,17},{17,9},{25,1},{2,26},{10... | collective-permute-start | bytes 786440 | tf_op jit(solution)/shard_map/ppermute | solution.py:381
  298.2 8.6 %collective-permute-start.32 = (bf16[512,256]{1,0:T(8,128)(2,1)S(1)}, bf16[512,256]{1,0:T(8,128)(2,1)S(1)}, u32[]{:S(2)}, u32[]{:S(2)}) collective-permute-start(bf16[512,256]{1,0:T(8,128)(2,1)S(1)} %get-tuple-element.80), channel_id=1, source_target_pairs={{0,16},{8,24},{16,0},{24,8},{1,17},{9,25},{17,1},{25,9},{2,18},{10... | collective-permute-start | bytes 786440 | tf_op jit(solution)/shard_map/ppermute | solution.py:381
  299.9 7.4 %collective-permute-start.31 = (bf16[512,256]{1,0:T(8,128)(2,1)S(1)}, bf16[512,256]{1,0:T(8,128)(2,1)S(1)}, u32[]{:S(2)}, u32[]{:S(2)}) collective-permute-start(bf16[512,256]{1,0:T(8,128)(2,1)S(1)} %get-tuple-element.81), channel_id=1, source_target_pairs={{0,8},{8,0},{16,24},{24,16},{1,9},{9,1},{17,25},{25,17},{2,10},{10... | collective-permute-start | bytes 786440 | tf_op jit(solution)/shard_map/ppermute | solution.py:381
  388.5 3.7 copy-start
  392.2 2.3 copy-start.1
Sparse Core Ops, SparseCore 0:
  11.2 60.1 all-gather.13
  75.1 67.2 all-gather.7
  144.7 54.4 all-gather.9
  225.3 80.1 all-gather.15
  308.8 79.6 all-gather.11

commit v4 on v3

--- a/solution.py
+++ b/solution.py
@@ -65,29 +65,37 @@
     sources = refs[:count]
     refs = refs[count:]
     if last:
-        readout, out, fired_out, logits_out, weights, held, work, total, sems = refs
+        readout, out, fired_out, logits_out, weights, held, work, sems = refs
     else:
-        out, fired_out, weights, held, work, total, sems = refs
+        out, fired_out, weights, held, work, sems = refs
     wait = fetch_weights(block, sections, scal, sources, weights, sems)
     rows, lanes = slices[0].shape
     group = images * steps
     channels = sections * lanes
+    held[...] = jnp.zeros_like(held)
     for k in range(sections):
-        held[scal[0] ^ k] = slices[k][...].reshape(height, width, group, lanes)
+        held[scal[0] ^ k, 1 : height + 1, 1 : width + 1] = slices[k][...].reshape(
+            height, width, group, lanes
+        )
     for offset in offsets:
-        cells, neighbours = overlap(offset, height, width)
         wait(offset)
+    total = jnp.zeros((rows, lanes), jnp.float32)
+    for offset in range(9):
+        r, c = divmod(offset, 3)
         lhs = jnp.concatenate(
-            [held[(j, *neighbours)].reshape(-1, lanes) for j in range(sections)], axis=1
-        )
-        part = jnp.dot(
+            [
+                held[j, r : r + height, c : c + width].reshape(rows, lanes)
+                for j in range(sections)
+            ],
+            axis=1,
+        )
+        total += jnp.dot(
             lhs,
             weights[offset * channels : (offset + 1) * channels, :],
             preferred_element_type=jnp.float32,
-        ).reshape(*total[cells].shape)
-        total[cells] = part if offset == offsets[0] else total[cells] + part
+        )
     scale = float(9 * channels) ** (-0.5)
-    current = total[...].reshape(rows, lanes) * scale
+    current = total * scale
     count = rows // steps
     tiles = lanes // 128
     for tile in range(tiles):
@@ -222,7 +230,7 @@
     last = block == sections - 1
     shapes = [
         jax.ShapeDtypeStruct((rows, lanes), jnp.bfloat16),
-        jax.ShapeDtypeStruct((lanes // 128, rows, 128), jnp.float32),
+        pltpu.HBM((lanes // 128, rows, 128), jnp.float32),
     ]
     operands = [scal, *(slices if last else stay(slices)), *stay(sources)]
     extra = []
@@ -240,9 +248,8 @@
         out_specs=vmem(len(shapes)),
         scratch_shapes=[
             VMEM((depth, lanes), jnp.bfloat16),
-            VMEM((sections, height, width, images * steps, lanes), jnp.bfloat16),
+            VMEM((sections, height + 2, width + 2, images * steps, lanes), jnp.bfloat16),
             VMEM((lanes // 128, rows, 128), jnp.float32),
-            VMEM((height, width, images * steps, lanes), jnp.float32),
             pltpu.SemaphoreType.DMA((9,)),
         ],
         compiler_params=pltpu.CompilerParams(vmem_limit_bytes=LIMIT),
@@ -318,10 +325,33 @@
     return lax.ppermute(value, "dp", [(i, i ^ 1) for i in range(count)])
 
 
-def update_kernel(cols, raw, weights, first_moment, second_moment, *outs):
-    grad = jnp.dot(cols[...], raw[...], preferred_element_type=jnp.float32)
-    new_first = beta_first * first_moment[...] + (1.0 - beta_first) * grad
-    new_second = beta_second * second_moment[...] + (1.0 - beta_second) * grad * grad
+def update_kernel(cols, raw, weights, first_moment, second_moment, *refs):
+    outs, (held, grad, sems) = refs[:3], refs[3:]
+    chunks = sems.shape[0]
+    size = held.shape[1] // chunks
+    first = pl.program_id(0) == 0
+
+    def copy(i):
+        part = pl.ds(i * size, size)
+        return pltpu.make_async_copy(cols.at[:, part], held.at[:, part], sems.at[i])
+
+    @pl.when(first)
+    def _():
+        for i in range(chunks):
+            copy(i).start()
+
+    for i in range(chunks):
+
+        @pl.when(first)
+        def _():
+            copy(i).wait()
+
+        part = slice(i * size, (i + 1) * size)
+        term = jnp.dot(held[:, part], raw[part, :], preferred_element_type=jnp.float32)
+        grad[...] = term if i == 0 else grad[...] + term
+    total = grad[...]
+    new_first = beta_first * first_moment[...] + (1.0 - beta_first) * total
+    new_second = beta_second * second_moment[...] + (1.0 - beta_second) * total * total
     outs[0][...] = weights[...] - learn_rate * new_first / (jnp.sqrt(new_second) + adam_eps)
     outs[1][...] = new_first
     outs[2][...] = new_second
@@ -337,27 +367,26 @@
         grid=(channels // tile,),
         out_shape=[jax.ShapeDtypeStruct(weights.shape, jnp.float32)] * 3,
         in_specs=[
-            pl.BlockSpec(memory_space=VMEM),
+            pl.BlockSpec(memory_space=pl.ANY),
             pl.BlockSpec((rows, tile), lambda i: (0, i)),
             state,
             state,
             state,
         ],
         out_specs=[state] * 3,
-        compiler_params=pltpu.CompilerParams(vmem_limit_bytes=40 * 2**20),
+        scratch_shapes=[
+            VMEM((depth, rows), jnp.bfloat16),
+            VMEM((depth, tile), jnp.float32),
+            pltpu.SemaphoreType.DMA((4,)),
+        ],
+        compiler_params=pltpu.CompilerParams(vmem_limit_bytes=48 * 2**20),
         cost_estimate=pl.CostEstimate(
             flops=2 * rows * depth * channels,
             bytes_accessed=24 * depth * channels + 2 * rows * channels,
             transcendentals=0,
         ),
         name="update",
-    )(
-        pltpu.with_memory_space_constraint(cols, VMEM),
-        raw,
-        weights,
-        first_moment,
-        second_moment,
-    )
+    )(*stay([cols, raw, weights, first_moment, second_moment]))
 
 
 def shards(spikes, labels, readout, weights, first_moment, second_moment):
@@ -403,18 +432,24 @@
         return [slots[slot] for slot in slots_of(b, sections)]
 
     def lay_out(slot, earlier):
+        held = [rings[slot]]
+        for j in range(1, ring):
+            near, far = done[slot, j][1], done[slot, ring - j][0]
+            held.append(
+                jnp.where(z + j < ring, after(near, *earlier), after(far, *earlier))
+            )
+        held = jnp.stack(held)
         whole = jnp.zeros((devices, depth, lanes), jnp.bfloat16)
-        for place, pieces_held in zip((core, 1 - core), rings[slot]):
-            pieces_held = after(pieces_held, earlier)
+        for place, part in ((core, held), (1 - core, swap_core(held))):
             for j in range(ring):
                 spot = lax.rem(z + j, ring) * 2 + place
-                whole = lax.dynamic_update_index_in_dim(whole, pieces_held[j], spot, 0)
+                whole = lax.dynamic_update_index_in_dim(whole, part[j], spot, 0)
         return whole.reshape(devices * depth, lanes)
 
     def forward(b):
         nonlocal own_inputs
         if b + 1 in rings:
-            slots[b + 1] = lay_out(b + 1, results[b - 1][0])
+            slots[b + 1] = lay_out(b + 1, inputs[b][1:])
         results.append(run_forward(dims, b, scal, inputs[b], holding(b), readout_own))
         if b < sections - 1:
             out = results[b][0]
@@ -434,17 +469,13 @@
             up = lax.ppermute(up, "dp", hops(step, 1, ring))
             down = lax.ppermute(down, "dp", hops(step, -1, ring))
             done[slot, step] = [up, down]
-        held = [piece]
-        for j in range(1, ring):
-            held.append(jnp.where(z + j < ring, done[slot, j][1], done[slot, ring - j][0]))
-        held = jnp.stack(held)
-        rings[slot] = (held, swap_core(held))
+        rings[slot] = piece
     gates = []
     for slot in [0] + list(range(1, sections, 2)):
         piece = after(piece_of(slot), *gates) if gates else piece_of(slot)
         gathered = lax.all_gather(piece, "dp", axis=0, tiled=True)
         slots[slot] = gathered
-        gates = [gathered] + done.get((2, 1) if slot == 0 else (slot + 1, ring - 1), [])
+        gates = [gathered] + done.get((2, 1) if slot == 0 else (slot + 1, max(1, ring - 2)), [])
     for b in range(sections):
         forward(b)
     result = results[-1]

time: 420 us -> 445 us (1.060)
  Pallas kernels: 65.4 us -> 78.8 us
  waiting for transfers between devices: 210 us -> 220 us
  local copies, waits for them, and re-layouts: 63.6 us -> 59.1 us
    ppermute x3, waiting for transfers between devices: 86.6 us -> 42.3 us  [shards(): down = lax.ppermute(down, 'dp', hops(step, -1, ring))]
    all_gather x3, waiting for transfers between devices: 5.05 us -> 34.3 us  [shards(): gathered = lax.all_gather(piece, 'dp', axis=0, tiled=True)]
    all_gather x1, waiting for transfers between devices: 0.02 us -> 13.8 us  [shards(): x_all = lax.all_gather(own_x, 'dp')]
    pallas_call x1, Pallas kernels: 17.4 us -> 30.4 us  [run_update(): pl.pallas_call(update_kernel, grid=(channels // tile,), out_shape=[jax.Sh...]
    unnamed x47 -> x35, local copies, waits for them, and re-layouts: 12.5 us -> 2.9 us
    dynamic_update_slice x0 -> x3, other arithmetic: none -> 6.21 us  [lay_out(): whole = lax.dynamic_update_index_in_dim(whole, part[j], spot, 0)]
    ppermute x1, waiting for transfers between devices: 0.01 us -> 4.77 us  [swap_core(): return lax.ppermute(value, 'dp', [(i, i ^ 1) for i in range(count)])]
    dynamic_update_slice x8 -> x5, local copies, waits for them, and re-layouts: 4.63 us -> 8.93 us  [lay_out(): whole = lax.dynamic_update_index_in_dim(whole, part[j], spot, 0)]
  transfers between devices with their start and end apart: 39 -> 39, of which waited for: 27 -> 29; matrix products, arithmetic and copies ran while one was open for 16% -> 17% of each run, Pallas kernels for 10% -> 9%
where the time goes in v4:
time: 445 us; the launch traced here: 443 us
  waiting for transfers between devices  220 us (49%)
  Pallas kernels  78.8 us (18%)
  local copies, waits for them, and re-layouts  59.1 us (13%)
  starting transfers between devices  45.3 us (10%)
  other arithmetic  25.4 us (6%)
  between operations  14.3 us (3%)
    ppermute x27, waiting for transfers between devices, exchange(): lax.ppermute(values[k], 'section', [(i, i ^ k + 1) for i in range(section...  88.7 us
    ppermute x3, waiting for transfers between devices, shards(): down = lax.ppermute(down, 'dp', hops(step, -1, ring))  42.3 us
    all_gather x1, waiting for transfers between devices, shards(): raw_all = lax.all_gather(own_raw, 'dp', axis=0, tiled=True)  36.2 us
    all_gather x3, waiting for transfers between devices, shards(): gathered = lax.all_gather(piece, 'dp', axis=0, tiled=True)  34.3 us
    ppermute x27, starting transfers between devices, exchange(): lax.ppermute(values[k], 'section', [(i, i ^ k + 1) for i in range(section...  33.2 us
    pallas_call x1, Pallas kernels, run_update(): pl.pallas_call(update_kernel, grid=(channels // tile,), out_shape=[jax.Sh...  30.4 us
    pallas_call x4, Pallas kernels, run_forward(): pl.pallas_call(functools.partial(forward_kernel, dims, block), out_shape=...  28.8 us
    reshape x2, local copies, waits for them, and re-layouts, shards(): shifted.append(lax.dynamic_slice(fields, (0, offset // 3, offset % 3, 0,...  23 us
  transfers between devices with their start and end apart: 39, of which 29 were waited for; matrix products, arithmetic and copies ran while one was open for 17% of the time, Pallas kernels for 9%

profile of v4, /device:TPU:0, one launch (start us, length us, event | category | flops | bytes accessed | tf_op | source)
XLA Modules:
  0.0 442.9 jit_solution(8114841700917874490)
XLA Ops:
  7.2 3.8 fusion.2
  11.2 3.0 collective-permute-start
  14.2 1.5 collective-permute-start.1
  18.4 1.8 copy.12
  22.6 5.9 %collective-permute-done = bf16[1152,256]{1,0:T(8,128)(2,1)S(1)} collective-permute-done((bf16[1152,256]{1,0:T(8,128)(2,1)}, bf16[1152,256]{1,0:T(8,128)(2,1)S(1)}, u32[]{:S(2)}, u32[]{:S(2)}) %collective-permute-start) | collective-permute-done | bytes 589856 | tf_op jit(solution)/shard_map/ppermute | solution.py:410
  28.5 13.4 %collective-permute-done.1 = bf16[1152,256]{1,0:T(8,128)(2,1)} collective-permute-done((bf16[1152,256]{1,0:T(8,128)(2,1)}, bf16[1152,256]{1,0:T(8,128)(2,1)}, u32[]{:S(2)}, u32[]{:S(2)}) %collective-permute-start.1) | collective-permute-done | bytes 589856 | tf_op jit(solution)/shard_map/ppermute | solution.py:410
  41.9 1.5 pad_maximum_fusion
  43.5 2.5 broadcast_in_dim.30
  48.5 4.6 %collective-permute-start.3 = (bf16[1152,256]{1,0:T(8,128)(2,1)S(1)}, bf16[1152,256]{1,0:T(8,128)(2,1)S(1)}, u32[]{:S(2)}, u32[]{:S(2)}) collective-permute-start(bf16[1152,256]{1,0:T(8,128)(2,1)S(1)} %bitcast.109), channel_id=1, source_target_pairs={{0,2},{1,3},{2,4},{3,5},{4,6},{5,7},{8,10},{9,11},{10,12},{11,13},... | collective-permute-start | bytes 1769480 | tf_op jit(solution)/shard_map/ppermute | solution.py:469
  53.1 21.9 %collective-permute-done.4 = bf16[1152,256]{1,0:T(8,128)(2,1)S(1)} collective-permute-done((bf16[1152,256]{1,0:T(8,128)(2,1)S(1)}, bf16[1152,256]{1,0:T(8,128)(2,1)S(1)}, u32[]{:S(2)}, u32[]{:S(2)}) %collective-permute-start.4) | collective-permute-done | bytes 589856 | tf_op jit(solution)/shard_map/ppermute | solution.py:470
  76.4 1.5 collective-permute-start.8
  77.9 20.4 %collective-permute-done.10 = bf16[1152,256]{1,0:T(8,128)(2,1)S(1)} collective-permute-done((bf16[1152,256]{1,0:T(8,128)(2,1)S(1)}, bf16[1152,256]{1,0:T(8,128)(2,1)S(1)}, u32[]{:S(2)}, u32[]{:S(2)}) %collective-permute-start.10) | collective-permute-done | bytes 589856 | tf_op jit(solution)/shard_map/ppermute | solution.py:470
  99.1 34.3 %all-gather.8.cloned.1.call-done.refs_5_.refs_6_ = bf16[9216,256]{1,0:T(8,128)(2,1)} async-done(((bf16[1152,256]{1,0:T(8,128)(2,1)}), bf16[9216,256]{1,0:T(8,128)(2,1)}) %all-gather.8.cloned.1.call-update) | async-done | bytes 4718608 | tf_op jit(solution)/shard_map/all_gather | solution.py:476
  134.8 1.5 collective-permute-start.9
  136.4 7.2 %forward_block.4 = (bf16[512,256]{1,0:T(8,128)(2,1)S(1)}, f32[2,512,128]{2,1,0:T(8,128)}) custom-call(s32[3]{0:T(128)S(1)} %pad_add_fusion.scal, bf16[512,256]{1,0:T(8,128)(2,1)} %get-tuple-element.104.refs_0_, bf16[512,256]{1,0:T(8,128)(2,1)} %get-tuple-element.103.refs_1_, bf16[512,256]{1,0:T(8,128)(2,1)} %get-tuple-element.102.refs_2_, ...), custom_call_target="tpu_custom_call" | custom-call | flops 2415919104 | bytes 4718592 | tf_op jit(solution)/shard_map/forward_block/pallas_call | solution.py:241
  144.8 1.8 collective-permute-start.6
  147.1 6.6 %collective-permute-done.7.refs_3_ = bf16[512,256]{1,0:T(8,128)(2,1)S(1)} collective-permute-done((bf16[512,256]{1,0:T(8,128)(2,1)S(1)}, bf16[512,256]{1,0:T(8,128)(2,1)S(1)}, u32[]{:S(2)}, u32[]{:S(2)}) %collective-permute-start.7) | collective-permute-done | bytes 262176 | tf_op jit(solution)/shard_map/ppermute | solution.py:410
  153.7 4.9 %collective-permute-done.6.refs_2_ = bf16[512,256]{1,0:T(8,128)(2,1)S(1)} collective-permute-done((bf16[512,256]{1,0:T(8,128)(2,1)S(1)}, bf16[512,256]{1,0:T(8,128)(2,1)S(1)}, u32[]{:S(2)}, u32[]{:S(2)}) %collective-permute-start.6) | collective-permute-done | bytes 262176 | tf_op jit(solution)/shard_map/ppermute | solution.py:410
  158.7 2.1 constant_dynamic-update-slice_fusion.2
  160.9 2.0 constant_dynamic-update-slice_fusion.1
  162.9 2.1 constant_dynamic-update-slice_fusion
  164.9 1.7 pad_maximum_fusion.1
  166.8 4.8 %collective-permute-done.12 = bf16[4,1152,256]{2,1,0:T(8,128)(2,1)} collective-permute-done((bf16[4,1152,256]{2,1,0:T(8,128)(2,1)}, bf16[4,1152,256]{2,1,0:T(8,128)(2,1)}, u32[]{:S(2)}, u32[]{:S(2)}) %collective-permute-start.12) | collective-permute-done | bytes 2359328 | tf_op jit(solution)/shard_map/ppermute | solution.py:325
  171.6 1.9 slice_dynamic-update-slice_fusion.3
  173.5 1.9 slice_dynamic-update-slice_fusion.2
  175.4 1.9 slice_dynamic-update-slice_fusion.1
  177.4 1.9 slice_dynamic-update-slice_fusion
  179.3 7.2 %forward_block.5 = (bf16[512,256]{1,0:T(8,128)(2,1)S(1)}, f32[2,512,128]{2,1,0:T(8,128)}) custom-call(s32[3]{0:T(128)S(1)} %pad_add_fusion.scal, bf16[512,256]{1,0:T(8,128)(2,1)} %copy-done, bf16[512,256]{1,0:T(8,128)(2,1)} %copy-done.10, bf16[512,256]{1,0:T(8,128)(2,1)} %copy-done.9, bf16[512,256]{1,0:T(8,128)(2,1)} %copy-done.8, ...), custom_call_target="tpu_custom_call" | custom-call | flops 2415919104 | bytes 4718592 | tf_op jit(solution)/shard_map/forward_block/pallas_call | solution.py:241
  186.6 1.5 collective-permute-start.15
  188.1 1.5 collective-permute-start.14
  190.1 6.6 %collective-permute-done.15.refs_3_ = bf16[512,256]{1,0:T(8,128)(2,1)S(1)} collective-permute-done((bf16[512,256]{1,0:T(8,128)(2,1)S(1)}, bf16[512,256]{1,0:T(8,128)(2,1)S(1)}, u32[]{:S(2)}, u32[]{:S(2)}) %collective-permute-start.15) | collective-permute-done | bytes 262176 | tf_op jit(solution)/shard_map/ppermute | solution.py:410
  196.7 4.7 %collective-permute-done.14.refs_2_ = bf16[512,256]{1,0:T(8,128)(2,1)S(1)} collective-permute-done((bf16[512,256]{1,0:T(8,128)(2,1)S(1)}, bf16[512,256]{1,0:T(8,128)(2,1)S(1)}, u32[]{:S(2)}, u32[]{:S(2)}) %collective-permute-start.14) | collective-permute-done | bytes 262176 | tf_op jit(solution)/shard_map/ppermute | solution.py:410
  202.3 7.2 %forward_block.6 = (bf16[512,256]{1,0:T(8,128)(2,1)S(1)}, f32[2,512,128]{2,1,0:T(8,128)}) custom-call(s32[3]{0:T(128)S(1)} %pad_add_fusion.scal, bf16[512,256]{1,0:T(8,128)(2,1)} %copy-done.2, bf16[512,256]{1,0:T(8,128)(2,1)} %copy-done.13, bf16[512,256]{1,0:T(8,128)(2,1)} %copy-done.12, bf16[512,256]{1,0:T(8,128)(2,1)} %copy-done.11, ...), custom_call_target="tpu_custom_call" | custom-call | flops 2415919104 | bytes 4718592 | tf_op jit(solution)/shard_map/forward_block/pallas_call | solution.py:241
  209.5 1.5 collective-permute-start.18
  213.1 6.6 %collective-permute-done.18.refs_3_ = bf16[512,256]{1,0:T(8,128)(2,1)S(1)} collective-permute-done((bf16[512,256]{1,0:T(8,128)(2,1)S(1)}, bf16[512,256]{1,0:T(8,128)(2,1)S(1)}, u32[]{:S(2)}, u32[]{:S(2)}) %collective-permute-start.18) | collective-permute-done | bytes 262176 | tf_op jit(solution)/shard_map/ppermute | solution.py:410
  219.7 4.6 %collective-permute-done.17.refs_2_ = bf16[512,256]{1,0:T(8,128)(2,1)S(1)} collective-permute-done((bf16[512,256]{1,0:T(8,128)(2,1)S(1)}, bf16[512,256]{1,0:T(8,128)(2,1)S(1)}, u32[]{:S(2)}, u32[]{:S(2)}) %collective-permute-start.17) | collective-permute-done | bytes 262176 | tf_op jit(solution)/shard_map/ppermute | solution.py:410
  224.4 1.9 maximum_select_fusion
  227.8 7.2 %forward_block.7 = (bf16[512,256]{1,0:T(8,128)(2,1)}, f32[2,512,128]{2,1,0:T(8,128)}, f32[4,1024]{1,0:T(4,128)S(1)}) custom-call(s32[3]{0:T(128)S(1)} %pad_add_fusion.scal, bf16[512,256]{1,0:T(8,128)(2,1)S(1)} %get-tuple-element.49.refs_0_, bf16[512,256]{1,0:T(8,128)(2,1)S(1)} %collective-permute-done.16.refs_1_, ...), custom_call_target="tpu_custom_call" | custom-call | flops 2415919104 | bytes 4718592 | tf_op jit(solution)/shard_map/forward_block/pallas_call | solution.py:241
  235.0 1.5 collective-permute-start.21
  236.5 1.4 collective-permute-start.20
  241.6 6.9 %backward_block.4 = (bf16[512,256]{1,0:T(8,128)(2,1)S(1)}, f32[512,256]{1,0:T(8,128)S(1)}, bf16[512,256]{1,0:T(8,128)(2,1)S(1)}, bf16[512,256]{1,0:T(8,128)(2,1)S(1)}, bf16[512,256]{1,0:T(8,128)(2,1)S(1)}) custom-call(s32[3]{0:T(128)S(1)} %pad_add_fusion.scal, f32[4,1024]{1,0:T(4,128)S(1)} %get-tuple-element.50.refs_0_, ...), custom_call_target="tpu_custom_call" | custom-call | flops 2429026304 | bytes 5767168 | tf_op jit(solution)/shard_map/backward_block/pallas_call | solution.py:295
  252.1 5.8 %collective-permute-done.22.refs_1_ = bf16[512,256]{1,0:T(8,128)(2,1)S(1)} collective-permute-done((bf16[512,256]{1,0:T(8,128)(2,1)S(1)}, bf16[512,256]{1,0:T(8,128)(2,1)S(1)}, u32[]{:S(2)}, u32[]{:S(2)}) %collective-permute-start.22) | collective-permute-done | bytes 262176 | tf_op jit(solution)/shard_map/ppermute | solution.py:410
  257.9 3.5 collective-permute-done.23.refs_2_
  261.3 5.6 %backward_block.5 = (bf16[512,256]{1,0:T(8,128)(2,1)S(1)}, f32[512,256]{1,0:T(8,128)S(1)}, bf16[512,256]{1,0:T(8,128)(2,1)S(1)}, bf16[512,256]{1,0:T(8,128)(2,1)S(1)}, bf16[512,256]{1,0:T(8,128)(2,1)S(1)}) custom-call(s32[3]{0:T(128)S(1)} %pad_add_fusion.scal, f32[512,256]{1,0:T(8,128)S(1)} %get-tuple-element.52.refs_0_, ...), custom_call_target="tpu_custom_call" | custom-call | flops 2429026304 | bytes 5767168 | tf_op jit(solution)/shard_map/backward_block/pallas_call | solution.py:295
  266.9 1.5 collective-permute-start.25
  270.4 5.0 %collective-permute-done.25.refs_1_ = bf16[512,256]{1,0:T(8,128)(2,1)S(1)} collective-permute-done((bf16[512,256]{1,0:T(8,128)(2,1)S(1)}, bf16[512,256]{1,0:T(8,128)(2,1)S(1)}, u32[]{:S(2)}, u32[]{:S(2)}) %collective-permute-start.25) | collective-permute-done | bytes 262176 | tf_op jit(solution)/shard_map/ppermute | solution.py:410
  275.5 4.0 collective-permute-done.26.refs_2_
  279.5 5.6 %backward_block.6 = (bf16[512,256]{1,0:T(8,128)(2,1)S(1)}, f32[512,256]{1,0:T(8,128)S(1)}, bf16[512,256]{1,0:T(8,128)(2,1)S(1)}, bf16[512,256]{1,0:T(8,128)(2,1)S(1)}, bf16[512,256]{1,0:T(8,128)(2,1)S(1)}) custom-call(s32[3]{0:T(128)S(1)} %pad_add_fusion.scal, f32[512,256]{1,0:T(8,128)S(1)} %get-tuple-element.57.refs_0_, ...), custom_call_target="tpu_custom_call" | custom-call | flops 2429026304 | bytes 5767168 | tf_op jit(solution)/shard_map/backward_block/pallas_call | solution.py:295
  285.7 1.5 collective-permute-start.29
  287.2 1.4 collective-permute-start.30
  288.6 3.9 collective-permute-done.28.refs_1_
  292.5 3.1 collective-permute-done.29.refs_2_
  295.6 1.6 backward_block.7
  297.4 1.8 collective-permute-start.33
  299.3 1.5 collective-permute-start.32
  301.3 3.9 collective-permute-done.33
  305.2 2.7 collective-permute-done.32
  309.5 13.8 %all-gather.16.cloned.1.call-done = bf16[4096,1024]{1,0:T(8,128)(2,1)} async-done(((bf16[512,1024]{1,0:T(8,128)(2,1)}), bf16[4096,1024]{1,0:T(8,128)(2,1)}) %all-gather.16.cloned.1.call-update) | async-done | bytes 8388624 | tf_op jit(solution)/shard_map/all_gather | solution.py:496
  323.3 12.1 %pad_dynamic-slice_fusion = (bf16[8,4,4,32,1024]{4,3,2,1,0:T(8,128)(2,1)}, bf16[8,4,4,32,1024]{4,3,2,1,0:T(8,128)(2,1)}) fusion(s32[]{:T(128)S(6)} %select_n.213, s32[]{:T(128)S(6)} %select_n.215, bf16[8,4,4,32,1024]{4,3,2,1,0:T(8,128)(2,1)} %bitcast.106, s32[]{:T(128)S(6)} %select_n.209, s32[]{:T(128)S(6)} %select_n.211), kind=kLoop, calls=%fused_computation | loop fusion | bytes 25165840 | tf_op jit(solution)/shard_map/dynamic_slice | solution.py:521
  335.3 11.8 %copy.15 = bf16[4096,1024]{0,1:T(8,128)(2,1)} copy(bf16[4096,1024]{1,0:T(8,128)(2,1)} %bitcast.105) | data formatting | bytes 16777216 | tf_op jit(solution)/shard_map/reshape | solution.py:525
  347.1 11.2 %copy.14 = bf16[4096,1024]{0,1:T(8,128)(2,1)} copy(bf16[4096,1024]{1,0:T(8,128)(2,1)} %bitcast.104) | data formatting | bytes 16777216 | tf_op jit(solution)/shard_map/reshape | solution.py:525
  358.3 11.5 %fusion.1.cols = bf16[1152,4096]{1,0:T(8,128)(2,1)} fusion(s32[]{:T(128)S(6)} %select_n.217, bf16[4096,1024]{0,1:T(8,128)(2,1)} %copy.14, bf16[4096,1024]{0,1:T(8,128)(2,1)} %copy.15), kind=kLoop, calls=%fused_computation.5 | loop fusion | flops 18874368 | bytes 26214404 | tf_op jit(solution)/shard_map/transpose | solution.py:530
  369.8 36.2 %all-gather.12.cloned.1.call-done.raw = bf16[4096,1024]{1,0:T(8,128)(2,1)} async-done(((bf16[512,1024]{1,0:T(8,128)(2,1)}), bf16[4096,1024]{1,0:T(8,128)(2,1)}) %all-gather.12.cloned.1.call-update) | async-done | bytes 8388624 | tf_op jit(solution)/shard_map/all_gather | solution.py:529
  405.9 30.4 %update.1 = (f32[1152,1024]{1,0:T(8,128)}, f32[1152,1024]{1,0:T(8,128)}, f32[1152,1024]{1,0:T(8,128)}) custom-call(bf16[1152,4096]{1,0:T(8,128)(2,1)} %fusion.1.cols, bf16[4096,1024]{1,0:T(8,128)(2,1)} %all-gather.12.cloned.1.call-done.raw, f32[1152,1024]{1,0:T(8,128)} %bitcast.114, f32[1152,1024]{1,0:T(8,128)} %bitcast.127, f32[1152,1024]{1,0:T(8,128)} %bitcast.128), custom_call_target="tpu_custom_call" | custom-call | flops 9663676416 | bytes 36700160 | tf_op jit(solution)/shard_map/update/pallas_call | solution.py:365
  (93 shorter events, 30.4 us)
Async XLA Ops:
  7.2 67.8 %all-gather.14.cloned.1.call-start = ((), (), s32[]{:S(2)}) async-start(), calls=%async_computation.3 | async-start | bytes 5308416 | tf_op jit(solution)/shard_map/all_gather | solution.py:476
  11.1 122.3 %all-gather.8.cloned.1.call-start = ((), (), s32[]{:S(2)}) async-start(), calls=%async_computation | async-start | bytes 5308416 | tf_op jit(solution)/shard_map/all_gather | solution.py:476
  11.2 17.4 %collective-permute-start = (bf16[1152,256]{1,0:T(8,128)(2,1)}, bf16[1152,256]{1,0:T(8,128)(2,1)S(1)}, u32[]{:S(2)}, u32[]{:S(2)}) collective-permute-start(bf16[1152,256]{1,0:T(8,128)(2,1)} %get-tuple-element.83), channel_id=1, source_target_pairs={{0,8},{8,0},{16,24},{24,16},{1,9},{9,1},{17,25},{25,17},{2,10},{10... | collective-permute-start | bytes 1769480 | tf_op jit(solution)/shard_map/ppermute | solution.py:410
  14.2 27.7 %collective-permute-start.1 = (bf16[1152,256]{1,0:T(8,128)(2,1)}, bf16[1152,256]{1,0:T(8,128)(2,1)}, u32[]{:S(2)}, u32[]{:S(2)}) collective-permute-start(bf16[1152,256]{1,0:T(8,128)(2,1)} %get-tuple-element.84), channel_id=1, source_target_pairs={{0,16},{8,24},{16,0},{24,8},{1,17},{9,25},{17,1},{25,9},{2,18},{10... | collective-permute-start | bytes 1769480 | tf_op jit(solution)/shard_map/ppermute | solution.py:410
  15.7 26.2 %collective-permute-start.2 = (bf16[1152,256]{1,0:T(8,128)(2,1)}, bf16[1152,256]{1,0:T(8,128)(2,1)}, u32[]{:S(2)}, u32[]{:S(2)}) collective-permute-start(bf16[1152,256]{1,0:T(8,128)(2,1)} %get-tuple-element.86), channel_id=1, source_target_pairs={{0,24},{8,16},{16,8},{24,0},{1,25},{9,17},{17,9},{25,1},{2,26},{10... | collective-permute-start | bytes 1769480 | tf_op jit(solution)/shard_map/ppermute | solution.py:410
  15.7 26.2 %copy-start.3 = (bf16[1,1152,256]{2,1,0:T(8,128)(2,1)S(1)}, bf16[1,1152,256]{2,1,0:T(8,128)(2,1)}, u32[]{:S(2)}) copy-start(bf16[1,1152,256]{2,1,0:T(8,128)(2,1)} %get-tuple-element.85) | copy-start | bytes 1769476
  47.2 27.8 %collective-permute-start.4 = (bf16[1152,256]{1,0:T(8,128)(2,1)S(1)}, bf16[1152,256]{1,0:T(8,128)(2,1)S(1)}, u32[]{:S(2)}, u32[]{:S(2)}) collective-permute-start(bf16[1152,256]{1,0:T(8,128)(2,1)S(1)} %bitcast.108), channel_id=1, source_target_pairs={{2,0},{3,1},{4,2},{5,3},{6,4},{7,5},{10,8},{11,9},{12,10},{13,11},... | collective-permute-start | bytes 1769480 | tf_op jit(solution)/shard_map/ppermute | solution.py:470
  48.5 26.5 %collective-permute-start.3 = (bf16[1152,256]{1,0:T(8,128)(2,1)S(1)}, bf16[1152,256]{1,0:T(8,128)(2,1)S(1)}, u32[]{:S(2)}, u32[]{:S(2)}) collective-permute-start(bf16[1152,256]{1,0:T(8,128)(2,1)S(1)} %bitcast.109), channel_id=1, source_target_pairs={{0,2},{1,3},{2,4},{3,5},{4,6},{5,7},{8,10},{9,11},{10,12},{11,13},... | collective-permute-start | bytes 1769480 | tf_op jit(solution)/shard_map/ppermute | solution.py:469
  75.0 68.5 %copy-start.14 = (bf16[1152,256]{1,0:T(8,128)(2,1)}, bf16[1152,256]{1,0:T(8,128)(2,1)S(1)}, u32[]{:S(2)}) copy-start(bf16[1152,256]{1,0:T(8,128)(2,1)S(1)} %collective-permute-done.4) | copy-start | bytes 1769476
  75.0 127.3 %all-gather.10.cloned.1.call-start = ((), (), s32[]{:S(2)}) async-start(), calls=%async_computation.1 | async-start | bytes 5308416 | tf_op jit(solution)/shard_map/all_gather | solution.py:476
  75.1 23.2 %collective-permute-start.10 = (bf16[1152,256]{1,0:T(8,128)(2,1)S(1)}, bf16[1152,256]{1,0:T(8,128)(2,1)S(1)}, u32[]{:S(2)}, u32[]{:S(2)}) collective-permute-start(bf16[1152,256]{1,0:T(8,128)(2,1)S(1)} %collective-permute-done.4), channel_id=1, source_target_pairs={{2,0},{3,1},{4,2},{5,3},{10,8},{11,9},{12,10},{13,11},{18,16},{19,... | collective-permute-start | bytes 1769480 | tf_op jit(solution)/shard_map/ppermute | solution.py:470
  76.4 22.7 %collective-permute-start.8 = (bf16[1152,256]{1,0:T(8,128)(2,1)S(1)}, bf16[1152,256]{1,0:T(8,128)(2,1)}, u32[]{:S(2)}, u32[]{:S(2)}) collective-permute-start(bf16[1152,256]{1,0:T(8,128)(2,1)S(1)} %collective-permute-done.3), channel_id=1, source_target_pairs={{2,4},{3,5},{4,6},{5,7},{10,12},{11,13},{12,14},{13,15},{18,20},{1... | collective-permute-start | bytes 1769480 | tf_op jit(solution)/shard_map/ppermute | solution.py:469
  98.3 0.8 copy-start.15
  133.4 189.9 %all-gather.16.cloned.1.call-start = ((), (), s32[]{:S(2)}) async-start(), calls=%async_computation.4 | async-start | bytes 9437184 | tf_op jit(solution)/shard_map/all_gather | solution.py:496
  133.5 25.3 %collective-permute-start.11 = (bf16[1152,256]{1,0:T(8,128)(2,1)}, bf16[1152,256]{1,0:T(8,128)(2,1)}, u32[]{:S(2)}, u32[]{:S(2)}) collective-permute-start(bf16[1152,256]{1,0:T(8,128)(2,1)} %copy-done.15), channel_id=1, source_target_pairs={{2,0},{3,1},{10,8},{11,9},{18,16},{19,17},{26,24},{27,25}} | collective-permute-start | bytes 1769480 | tf_op jit(solution)/shard_map/ppermute | solution.py:470
  134.8 24.0 %collective-permute-start.9 = (bf16[1152,256]{1,0:T(8,128)(2,1)}, bf16[1152,256]{1,0:T(8,128)(2,1)}, u32[]{:S(2)}, u32[]{:S(2)}) collective-permute-start(bf16[1152,256]{1,0:T(8,128)(2,1)} %collective-permute-done.8), channel_id=1, source_target_pairs={{4,6},{5,7},{12,14},{13,15},{20,22},{21,23},{28,30},{29,31}} | collective-permute-start | bytes 1769480 | tf_op jit(solution)/shard_map/ppermute | solution.py:469
  143.6 23.1 %copy-start = (bf16[512,256]{1,0:T(8,128)(2,1)}, bf16[512,256]{1,0:T(8,128)(2,1)S(1)}, u32[]{:S(2)}) copy-start(bf16[512,256]{1,0:T(8,128)(2,1)S(1)} %get-tuple-element.40.refs_0_) | copy-start | bytes 786436
  143.6 10.2 %collective-permute-start.7 = (bf16[512,256]{1,0:T(8,128)(2,1)S(1)}, bf16[512,256]{1,0:T(8,128)(2,1)S(1)}, u32[]{:S(2)}, u32[]{:S(2)}) collective-permute-start(bf16[512,256]{1,0:T(8,128)(2,1)S(1)} %get-tuple-element.40.refs_0_), channel_id=1, source_target_pairs={{0,24},{8,16},{16,8},{24,0},{1,25},{9,17},{17,9},{25,1},{2,26},{10... | collective-permute-start | bytes 786440 | tf_op jit(solution)/shard_map/ppermute | solution.py:410
  144.8 13.8 %collective-permute-start.6 = (bf16[512,256]{1,0:T(8,128)(2,1)S(1)}, bf16[512,256]{1,0:T(8,128)(2,1)S(1)}, u32[]{:S(2)}, u32[]{:S(2)}) collective-permute-start(bf16[512,256]{1,0:T(8,128)(2,1)S(1)} %get-tuple-element.40.refs_0_), channel_id=1, source_target_pairs={{0,16},{8,24},{16,0},{24,8},{1,17},{9,25},{17,1},{25,9},{2,18},{10... | collective-permute-start | bytes 786440 | tf_op jit(solution)/shard_map/ppermute | solution.py:410
  146.6 12.1 %collective-permute-start.5 = (bf16[512,256]{1,0:T(8,128)(2,1)S(1)}, bf16[512,256]{1,0:T(8,128)(2,1)S(1)}, u32[]{:S(2)}, u32[]{:S(2)}) collective-permute-start(bf16[512,256]{1,0:T(8,128)(2,1)S(1)} %get-tuple-element.40.refs_0_), channel_id=1, source_target_pairs={{0,8},{8,0},{16,24},{24,16},{1,9},{9,1},{17,25},{25,17},{2,10},{10... | collective-permute-start | bytes 786440 | tf_op jit(solution)/shard_map/ppermute | solution.py:410
  153.7 12.9 %copy-start.8 = (bf16[512,256]{1,0:T(8,128)(2,1)}, bf16[512,256]{1,0:T(8,128)(2,1)S(1)}, u32[]{:S(2)}) copy-start(bf16[512,256]{1,0:T(8,128)(2,1)S(1)} %collective-permute-done.7.refs_3_) | copy-start | bytes 786436
  158.6 8.0 %copy-start.9 = (bf16[512,256]{1,0:T(8,128)(2,1)}, bf16[512,256]{1,0:T(8,128)(2,1)S(1)}, u32[]{:S(2)}) copy-start(bf16[512,256]{1,0:T(8,128)(2,1)S(1)} %collective-permute-done.6.refs_2_) | copy-start | bytes 786436
  158.7 7.9 %copy-start.10 = (bf16[512,256]{1,0:T(8,128)(2,1)}, bf16[512,256]{1,0:T(8,128)(2,1)S(1)}, u32[]{:S(2)}) copy-start(bf16[512,256]{1,0:T(8,128)(2,1)S(1)} %collective-permute-done.5.refs_1_) | copy-start | bytes 786436
  166.7 4.9 %collective-permute-start.12 = (bf16[4,1152,256]{2,1,0:T(8,128)(2,1)}, bf16[4,1152,256]{2,1,0:T(8,128)(2,1)}, u32[]{:S(2)}, u32[]{:S(2)}) collective-permute-start(bf16[4,1152,256]{2,1,0:T(8,128)(2,1)} %pad_maximum_fusion.1), channel_id=1, source_target_pairs={{0,1},{1,0},{2,3},{3,2},{4,5},{5,4},{6,7},{7,6},{8,9},{9,8},{10,11... | collective-permute-start | bytes 7077896 | tf_op jit(solution)/shard_map/ppermute | solution.py:325
  186.5 15.8 %copy-start.2 = (bf16[512,256]{1,0:T(8,128)(2,1)}, bf16[512,256]{1,0:T(8,128)(2,1)S(1)}, u32[]{:S(2)}) copy-start(bf16[512,256]{1,0:T(8,128)(2,1)S(1)} %get-tuple-element.47.refs_0_) | copy-start | bytes 786436
  186.5 37.9 %copy-start.1 = (bf16[512,256]{1,0:T(8,128)(2,1)S(1)}, bf16[512,256]{1,0:T(8,128)(2,1)}, u32[]{:S(2)}) copy-start(bf16[512,256]{1,0:T(8,128)(2,1)} %copy-done) | copy-start | bytes 786436
  186.5 37.9 %copy-start.4 = (bf16[512,256]{1,0:T(8,128)(2,1)S(1)}, bf16[512,256]{1,0:T(8,128)(2,1)}, u32[]{:S(2)}) copy-start(bf16[512,256]{1,0:T(8,128)(2,1)} %get-tuple-element.101.refs_3_) | copy-start | bytes 786436
  186.5 37.9 %copy-start.5 = (bf16[512,256]{1,0:T(8,128)(2,1)S(1)}, bf16[512,256]{1,0:T(8,128)(2,1)}, u32[]{:S(2)}) copy-start(bf16[512,256]{1,0:T(8,128)(2,1)} %get-tuple-element.102.refs_2_) | copy-start | bytes 786436
  186.6 37.9 %copy-start.6 = (bf16[512,256]{1,0:T(8,128)(2,1)S(1)}, bf16[512,256]{1,0:T(8,128)(2,1)}, u32[]{:S(2)}) copy-start(bf16[512,256]{1,0:T(8,128)(2,1)} %get-tuple-element.103.refs_1_) | copy-start | bytes 786436
  186.6 37.9 %copy-start.7 = (bf16[512,256]{1,0:T(8,128)(2,1)S(1)}, bf16[512,256]{1,0:T(8,128)(2,1)}, u32[]{:S(2)}) copy-start(bf16[512,256]{1,0:T(8,128)(2,1)} %get-tuple-element.104.refs_0_) | copy-start | bytes 786436
  186.6 10.2 %collective-permute-start.15 = (bf16[512,256]{1,0:T(8,128)(2,1)S(1)}, bf16[512,256]{1,0:T(8,128)(2,1)S(1)}, u32[]{:S(2)}, u32[]{:S(2)}) collective-permute-start(bf16[512,256]{1,0:T(8,128)(2,1)S(1)} %get-tuple-element.47.refs_0_), channel_id=1, source_target_pairs={{0,24},{8,16},{16,8},{24,0},{1,25},{9,17},{17,9},{25,1},{2,26},{10... | collective-permute-start | bytes 786440 | tf_op jit(solution)/shard_map/ppermute | solution.py:410
  188.1 13.4 %collective-permute-start.14 = (bf16[512,256]{1,0:T(8,128)(2,1)S(1)}, bf16[512,256]{1,0:T(8,128)(2,1)S(1)}, u32[]{:S(2)}, u32[]{:S(2)}) collective-permute-start(bf16[512,256]{1,0:T(8,128)(2,1)S(1)} %get-tuple-element.47.refs_0_), channel_id=1, source_target_pairs={{0,16},{8,24},{16,0},{24,8},{1,17},{9,25},{17,1},{25,9},{2,18},{10... | collective-permute-start | bytes 786440 | tf_op jit(solution)/shard_map/ppermute | solution.py:410
  189.6 12.0 %collective-permute-start.13 = (bf16[512,256]{1,0:T(8,128)(2,1)S(1)}, bf16[512,256]{1,0:T(8,128)(2,1)S(1)}, u32[]{:S(2)}, u32[]{:S(2)}) collective-permute-start(bf16[512,256]{1,0:T(8,128)(2,1)S(1)} %get-tuple-element.47.refs_0_), channel_id=1, source_target_pairs={{0,8},{8,0},{16,24},{24,16},{1,9},{9,1},{17,25},{25,17},{2,10},{10... | collective-permute-start | bytes 786440 | tf_op jit(solution)/shard_map/ppermute | solution.py:410
  196.7 5.6 %copy-start.11 = (bf16[512,256]{1,0:T(8,128)(2,1)}, bf16[512,256]{1,0:T(8,128)(2,1)S(1)}, u32[]{:S(2)}) copy-start(bf16[512,256]{1,0:T(8,128)(2,1)S(1)} %collective-permute-done.15.refs_3_) | copy-start | bytes 786436
  201.5 0.8 copy-start.12
  201.6 0.7 copy-start.13
  209.5 10.2 %collective-permute-start.18 = (bf16[512,256]{1,0:T(8,128)(2,1)S(1)}, bf16[512,256]{1,0:T(8,128)(2,1)S(1)}, u32[]{:S(2)}, u32[]{:S(2)}) collective-permute-start(bf16[512,256]{1,0:T(8,128)(2,1)S(1)} %get-tuple-element.49.refs_0_), channel_id=1, source_target_pairs={{0,24},{8,16},{16,8},{24,0},{1,25},{9,17},{17,9},{25,1},{2,26},{10... | collective-permute-start | bytes 786440 | tf_op jit(solution)/shard_map/ppermute | solution.py:410
  211.1 13.2 %collective-permute-start.17 = (bf16[512,256]{1,0:T(8,128)(2,1)S(1)}, bf16[512,256]{1,0:T(8,128)(2,1)S(1)}, u32[]{:S(2)}, u32[]{:S(2)}) collective-permute-start(bf16[512,256]{1,0:T(8,128)(2,1)S(1)} %get-tuple-element.49.refs_0_), channel_id=1, source_target_pairs={{0,16},{8,24},{16,0},{24,8},{1,17},{9,25},{17,1},{25,9},{2,18},{10... | collective-permute-start | bytes 786440 | tf_op jit(solution)/shard_map/ppermute | solution.py:410
  212.5 11.9 %collective-permute-start.16 = (bf16[512,256]{1,0:T(8,128)(2,1)S(1)}, bf16[512,256]{1,0:T(8,128)(2,1)S(1)}, u32[]{:S(2)}, u32[]{:S(2)}) collective-permute-start(bf16[512,256]{1,0:T(8,128)(2,1)S(1)} %get-tuple-element.49.refs_0_), channel_id=1, source_target_pairs={{0,8},{8,0},{16,24},{24,16},{1,9},{9,1},{17,25},{25,17},{2,10},{10... | collective-permute-start | bytes 786440 | tf_op jit(solution)/shard_map/ppermute | solution.py:410
  227.5 11.0 %copy-start.16 = (s32[4]{0:T(128)S(1)}, s32[4]{0:T(128)}, u32[]{:S(2)}) copy-start(s32[4]{0:T(128)} %param.7) | copy-start | bytes 52
  227.6 178.4 %all-gather.12.cloned.1.call-start = ((), (), s32[]{:S(2)}) async-start(), calls=%async_computation.2 | async-start | bytes 9437184 | tf_op jit(solution)/shard_map/all_gather | solution.py:529
  235.0 4.7 %collective-permute-start.21 = (f32[4,1024]{1,0:T(4,128)S(1)}, f32[4,1024]{1,0:T(4,128)S(1)}, u32[]{:S(2)}, u32[]{:S(2)}) collective-permute-start(f32[4,1024]{1,0:T(4,128)S(1)} %get-tuple-element.50.refs_0_), channel_id=1, source_target_pairs={{0,24},{8,16},{16,8},{24,0},{1,25},{9,17},{17,9},{25,1},{2,26},{10... | collective-permute-start | bytes 49160 | tf_op jit(solution)/shard_map/ppermute | solution.py:410
  236.5 3.7 collective-permute-start.20
  237.9 3.7 collective-permute-start.19
  248.6 9.3 %collective-permute-start.22 = (bf16[512,256]{1,0:T(8,128)(2,1)S(1)}, bf16[512,256]{1,0:T(8,128)(2,1)S(1)}, u32[]{:S(2)}, u32[]{:S(2)}) collective-permute-start(bf16[512,256]{1,0:T(8,128)(2,1)S(1)} %get-tuple-element.53), channel_id=1, source_target_pairs={{0,8},{8,0},{16,24},{24,16},{1,9},{9,1},{17,25},{25,17},{2,10},{10... | collective-permute-start | bytes 786440 | tf_op jit(solution)/shard_map/ppermute | solution.py:410
  249.3 12.0 %collective-permute-start.23 = (bf16[512,256]{1,0:T(8,128)(2,1)S(1)}, bf16[512,256]{1,0:T(8,128)(2,1)S(1)}, u32[]{:S(2)}, u32[]{:S(2)}) collective-permute-start(bf16[512,256]{1,0:T(8,128)(2,1)S(1)} %get-tuple-element.54), channel_id=1, source_target_pairs={{0,16},{8,24},{16,0},{24,8},{1,17},{9,25},{17,1},{25,9},{2,18},{10... | collective-permute-start | bytes 786440 | tf_op jit(solution)/shard_map/ppermute | solution.py:410
  250.7 10.6 %collective-permute-start.24 = (bf16[512,256]{1,0:T(8,128)(2,1)S(1)}, bf16[512,256]{1,0:T(8,128)(2,1)S(1)}, u32[]{:S(2)}, u32[]{:S(2)}) collective-permute-start(bf16[512,256]{1,0:T(8,128)(2,1)S(1)} %get-tuple-element.55), channel_id=1, source_target_pairs={{0,24},{8,16},{16,8},{24,0},{1,25},{9,17},{17,9},{25,1},{2,26},{10... | collective-permute-start | bytes 786440 | tf_op jit(solution)/shard_map/ppermute | solution.py:410
  266.9 8.6 %collective-permute-start.25 = (bf16[512,256]{1,0:T(8,128)(2,1)S(1)}, bf16[512,256]{1,0:T(8,128)(2,1)S(1)}, u32[]{:S(2)}, u32[]{:S(2)}) collective-permute-start(bf16[512,256]{1,0:T(8,128)(2,1)S(1)} %get-tuple-element.58), channel_id=1, source_target_pairs={{0,8},{8,0},{16,24},{24,16},{1,9},{9,1},{17,25},{25,17},{2,10},{10... | collective-permute-start | bytes 786440 | tf_op jit(solution)/shard_map/ppermute | solution.py:410
  268.4 11.1 %collective-permute-start.26 = (bf16[512,256]{1,0:T(8,128)(2,1)S(1)}, bf16[512,256]{1,0:T(8,128)(2,1)S(1)}, u32[]{:S(2)}, u32[]{:S(2)}) collective-permute-start(bf16[512,256]{1,0:T(8,128)(2,1)S(1)} %get-tuple-element.59), channel_id=1, source_target_pairs={{0,16},{8,24},{16,0},{24,8},{1,17},{9,25},{17,1},{25,9},{2,18},{10... | collective-permute-start | bytes 786440 | tf_op jit(solution)/shard_map/ppermute | solution.py:410
  269.1 10.5 %collective-permute-start.27 = (bf16[512,256]{1,0:T(8,128)(2,1)S(1)}, bf16[512,256]{1,0:T(8,128)(2,1)S(1)}, u32[]{:S(2)}, u32[]{:S(2)}) collective-permute-start(bf16[512,256]{1,0:T(8,128)(2,1)S(1)} %get-tuple-element.60), channel_id=1, source_target_pairs={{0,24},{8,16},{16,8},{24,0},{1,25},{9,17},{17,9},{25,1},{2,26},{10... | collective-permute-start | bytes 786440 | tf_op jit(solution)/shard_map/ppermute | solution.py:410
  285.1 7.4 %collective-permute-start.28 = (bf16[512,256]{1,0:T(8,128)(2,1)S(1)}, bf16[512,256]{1,0:T(8,128)(2,1)S(1)}, u32[]{:S(2)}, u32[]{:S(2)}) collective-permute-start(bf16[512,256]{1,0:T(8,128)(2,1)S(1)} %get-tuple-element.63), channel_id=1, source_target_pairs={{0,8},{8,0},{16,24},{24,16},{1,9},{9,1},{17,25},{25,17},{2,10},{10... | collective-permute-start | bytes 786440 | tf_op jit(solution)/shard_map/ppermute | solution.py:410
  285.7 9.9 %collective-permute-start.29 = (bf16[512,256]{1,0:T(8,128)(2,1)S(1)}, bf16[512,256]{1,0:T(8,128)(2,1)S(1)}, u32[]{:S(2)}, u32[]{:S(2)}) collective-permute-start(bf16[512,256]{1,0:T(8,128)(2,1)S(1)} %get-tuple-element.64), channel_id=1, source_target_pairs={{0,16},{8,24},{16,0},{24,8},{1,17},{9,25},{17,1},{25,9},{2,18},{10... | collective-permute-start | bytes 786440 | tf_op jit(solution)/shard_map/ppermute | solution.py:410
  287.2 8.4 %collective-permute-start.30 = (bf16[512,256]{1,0:T(8,128)(2,1)S(1)}, bf16[512,256]{1,0:T(8,128)(2,1)S(1)}, u32[]{:S(2)}, u32[]{:S(2)}) collective-permute-start(bf16[512,256]{1,0:T(8,128)(2,1)S(1)} %get-tuple-element.65), channel_id=1, source_target_pairs={{0,24},{8,16},{16,8},{24,0},{1,25},{9,17},{17,9},{25,1},{2,26},{10... | collective-permute-start | bytes 786440 | tf_op jit(solution)/shard_map/ppermute | solution.py:410
  297.4 7.7 %collective-permute-start.33 = (bf16[512,256]{1,0:T(8,128)(2,1)S(1)}, bf16[512,256]{1,0:T(8,128)(2,1)S(1)}, u32[]{:S(2)}, u32[]{:S(2)}) collective-permute-start(bf16[512,256]{1,0:T(8,128)(2,1)S(1)} %get-tuple-element.94), channel_id=1, source_target_pairs={{0,24},{8,16},{16,8},{24,0},{1,25},{9,17},{17,9},{25,1},{2,26},{10... | collective-permute-start | bytes 786440 | tf_op jit(solution)/shard_map/ppermute | solution.py:410
  299.3 8.6 %collective-permute-start.32 = (bf16[512,256]{1,0:T(8,128)(2,1)S(1)}, bf16[512,256]{1,0:T(8,128)(2,1)S(1)}, u32[]{:S(2)}, u32[]{:S(2)}) collective-permute-start(bf16[512,256]{1,0:T(8,128)(2,1)S(1)} %get-tuple-element.95), channel_id=1, source_target_pairs={{0,16},{8,24},{16,0},{24,8},{1,17},{9,25},{17,1},{25,9},{2,18},{10... | collective-permute-start | bytes 786440 | tf_op jit(solution)/shard_map/ppermute | solution.py:410
  300.8 7.2 %collective-permute-start.31 = (bf16[512,256]{1,0:T(8,128)(2,1)S(1)}, bf16[512,256]{1,0:T(8,128)(2,1)S(1)}, u32[]{:S(2)}, u32[]{:S(2)}) collective-permute-start(bf16[512,256]{1,0:T(8,128)(2,1)S(1)} %get-tuple-element.96), channel_id=1, source_target_pairs={{0,8},{8,0},{16,24},{24,16},{1,9},{9,1},{17,25},{25,17},{2,10},{10... | collective-permute-start | bytes 786440 | tf_op jit(solution)/shard_map/ppermute | solution.py:410
Sparse Core Ops, SparseCore 0:
  11.2 58.8 all-gather.13
  75.2 58.1 all-gather.7
  135.6 54.9 all-gather.9
  227.7 95.5 all-gather.15
  325.3 80.5 all-gather.11

commit v5 on v3

--- a/solution.py
+++ b/solution.py
@@ -65,29 +65,37 @@
     sources = refs[:count]
     refs = refs[count:]
     if last:
-        readout, out, fired_out, logits_out, weights, held, work, total, sems = refs
+        readout, out, fired_out, logits_out, weights, held, work, sems = refs
     else:
-        out, fired_out, weights, held, work, total, sems = refs
+        out, fired_out, weights, held, work, sems = refs
     wait = fetch_weights(block, sections, scal, sources, weights, sems)
     rows, lanes = slices[0].shape
     group = images * steps
     channels = sections * lanes
+    held[...] = jnp.zeros_like(held)
     for k in range(sections):
-        held[scal[0] ^ k] = slices[k][...].reshape(height, width, group, lanes)
+        held[scal[0] ^ k, 1 : height + 1, 1 : width + 1] = slices[k][...].reshape(
+            height, width, group, lanes
+        )
     for offset in offsets:
-        cells, neighbours = overlap(offset, height, width)
         wait(offset)
+    total = jnp.zeros((rows, lanes), jnp.float32)
+    for offset in range(9):
+        r, c = divmod(offset, 3)
         lhs = jnp.concatenate(
-            [held[(j, *neighbours)].reshape(-1, lanes) for j in range(sections)], axis=1
-        )
-        part = jnp.dot(
+            [
+                held[j, r : r + height, c : c + width].reshape(rows, lanes)
+                for j in range(sections)
+            ],
+            axis=1,
+        )
+        total += jnp.dot(
             lhs,
             weights[offset * channels : (offset + 1) * channels, :],
             preferred_element_type=jnp.float32,
-        ).reshape(*total[cells].shape)
-        total[cells] = part if offset == offsets[0] else total[cells] + part
+        )
     scale = float(9 * channels) ** (-0.5)
-    current = total[...].reshape(rows, lanes) * scale
+    current = total * scale
     count = rows // steps
     tiles = lanes // 128
     for tile in range(tiles):
@@ -222,7 +230,7 @@
     last = block == sections - 1
     shapes = [
         jax.ShapeDtypeStruct((rows, lanes), jnp.bfloat16),
-        jax.ShapeDtypeStruct((lanes // 128, rows, 128), jnp.float32),
+        pltpu.HBM((lanes // 128, rows, 128), jnp.float32),
     ]
     operands = [scal, *(slices if last else stay(slices)), *stay(sources)]
     extra = []
@@ -240,9 +248,8 @@
         out_specs=vmem(len(shapes)),
         scratch_shapes=[
             VMEM((depth, lanes), jnp.bfloat16),
-            VMEM((sections, height, width, images * steps, lanes), jnp.bfloat16),
+            VMEM((sections, height + 2, width + 2, images * steps, lanes), jnp.bfloat16),
             VMEM((lanes // 128, rows, 128), jnp.float32),
-            VMEM((height, width, images * steps, lanes), jnp.float32),
             pltpu.SemaphoreType.DMA((9,)),
         ],
         compiler_params=pltpu.CompilerParams(vmem_limit_bytes=LIMIT),
@@ -344,7 +351,7 @@
             state,
         ],
         out_specs=[state] * 3,
-        compiler_params=pltpu.CompilerParams(vmem_limit_bytes=40 * 2**20),
+        compiler_params=pltpu.CompilerParams(vmem_limit_bytes=48 * 2**20),
         cost_estimate=pl.CostEstimate(
             flops=2 * rows * depth * channels,
             bytes_accessed=24 * depth * channels + 2 * rows * channels,
@@ -352,11 +359,7 @@
         ),
         name="update",
     )(
-        pltpu.with_memory_space_constraint(cols, VMEM),
-        raw,
-        weights,
-        first_moment,
-        second_moment,
+        *stay([cols, raw, weights, first_moment, second_moment])
     )
 
 
@@ -455,14 +458,7 @@
     def ordered(parts):
         return jnp.concatenate([pick(parts, s ^ j) for j in range(sections)], axis=1)
 
-    own_x = jnp.concatenate(
-        [
-            lax.dynamic_index_in_dim(own_inputs, s ^ j, 0, keepdims=False)
-            for j in range(sections)
-        ],
-        axis=1,
-    )
-    x_all = lax.all_gather(own_x, "dp")
+    x_all = lax.all_gather(own_inputs.reshape(sections * rows, lanes), "dp")
 
     raws = [None] * sections
     for b in reversed(range(sections)):
@@ -481,7 +477,14 @@
         step *= 2
     spans = -(-(channels - step + depth) // channels)
 
-    fields = x_all.reshape(devices, height, width, group, channels)
+    x_all = x_all.reshape(devices, sections, height, width, group, lanes)
+    fields = jnp.concatenate(
+        [
+            lax.dynamic_index_in_dim(x_all, s ^ j, 1, keepdims=False)
+            for j in range(sections)
+        ],
+        axis=-1,
+    )
     fields = jnp.pad(fields, ((0, 0), (1, 1), (1, 1), (0, 0), (0, 0)))
     shifted = []
     for i in range(spans):

time: 420 us -> 417 us (level)
  waiting for transfers between devices: 210 us -> 186 us
  other arithmetic: 21.1 us -> 38.5 us
  Pallas kernels: 65.4 us -> 70.5 us
    all_gather x1, waiting for transfers between devices: 33.2 us -> 8.4 us  [shards(): raw_all = lax.all_gather(own_raw, 'dp', axis=0, tiled=True)]
    concatenate x1, other arithmetic: 1.11 us -> 17.8 us  [shards(): jnp.concatenate([lax.dynamic_index_in_dim(x_all, s ^ j, 1, keepdims=False...]
    unnamed x47 -> x35, local copies, waits for them, and re-layouts: 12.5 us -> 2.81 us
    squeeze x1, local copies, waits for them, and re-layouts: 0.08 us -> 6.87 us  [shards(): lax.dynamic_index_in_dim(x_all, s ^ j, 1, keepdims=False)]
    pallas_call x1, Pallas kernels: 17.4 us -> 22 us  [run_update(): pl.pallas_call(update_kernel, grid=(channels // tile,), out_shape=[jax.Sh...]
  transfers between devices with their start and end apart: 39 -> 39, of which waited for: 27 -> 27; matrix products, arithmetic and copies ran while one was open for 16% -> 22% of each run, Pallas kernels for 10% -> 10%
where the time goes in v5:
time: 417 us; the launch traced here: 415 us
  waiting for transfers between devices  186 us (45%)
  Pallas kernels  70.5 us (17%)
  local copies, waits for them, and re-layouts  61.3 us (15%)
  starting transfers between devices  44.1 us (11%)
  other arithmetic  38.5 us (9%)
  between operations  14.4 us (3%)
    ppermute x3, waiting for transfers between devices, shards(): down = lax.ppermute(down, 'dp', hops(step, -1, ring))  86.6 us
    ppermute x27, waiting for transfers between devices, exchange(): lax.ppermute(values[k], 'section', [(i, i ^ k + 1) for i in range(section...  84.4 us
    ppermute x27, starting transfers between devices, exchange(): lax.ppermute(values[k], 'section', [(i, i ^ k + 1) for i in range(section...  33 us
    pallas_call x4, Pallas kernels, run_forward(): pl.pallas_call(functools.partial(forward_kernel, dims, block), out_shape=...  28.8 us
    reshape x2, local copies, waits for them, and re-layouts, shards(): shifted.append(lax.dynamic_slice(fields, (0, offset // 3, offset % 3, 0,...  23.2 us
    pallas_call x1, Pallas kernels, run_update(): pl.pallas_call(update_kernel, grid=(channels // tile,), out_shape=[jax.Sh...  22 us
    pallas_call x4, Pallas kernels, run_backward(): pl.pallas_call(functools.partial(backward_kernel, dims, block, classes),...  19.7 us
    concatenate x1, other arithmetic, shards(): jnp.concatenate([lax.dynamic_index_in_dim(x_all, s ^ j, 1, keepdims=False...  17.8 us
  transfers between devices with their start and end apart: 39, of which 27 were waited for; matrix products, arithmetic and copies ran while one was open for 22% of the time, Pallas kernels for 10%

profile of v5, /device:TPU:0, one launch (start us, length us, event | category | flops | bytes accessed | tf_op | source)
XLA Modules:
  0.0 415.1 jit_solution(1559060582305401800)
XLA Ops:
  7.2 3.8 fusion.8
  11.2 3.0 collective-permute-start
  14.2 1.5 collective-permute-start.1
  15.7 1.3 constant_dynamic-slice_fusion.3
  17.0 1.3 copy.34
  18.4 1.8 copy.25
  20.2 1.4 pad.8.refs_6_.refs_5_
  22.6 5.9 %collective-permute-done = bf16[1152,256]{1,0:T(8,128)(2,1)S(1)} collective-permute-done((bf16[1152,256]{1,0:T(8,128)(2,1)}, bf16[1152,256]{1,0:T(8,128)(2,1)S(1)}, u32[]{:S(2)}, u32[]{:S(2)}) %collective-permute-start) | collective-permute-done | bytes 589856 | tf_op jit(solution)/shard_map/ppermute | solution.py:384
  28.5 13.4 %collective-permute-done.1 = bf16[1152,256]{1,0:T(8,128)(2,1)} collective-permute-done((bf16[1152,256]{1,0:T(8,128)(2,1)}, bf16[1152,256]{1,0:T(8,128)(2,1)}, u32[]{:S(2)}, u32[]{:S(2)}) %collective-permute-start.1) | collective-permute-done | bytes 589856 | tf_op jit(solution)/shard_map/ppermute | solution.py:384
  41.9 1.5 pad_maximum_fusion
  45.9 4.6 %collective-permute-start.3 = (bf16[1152,256]{1,0:T(8,128)(2,1)S(1)}, bf16[1152,256]{1,0:T(8,128)(2,1)S(1)}, u32[]{:S(2)}, u32[]{:S(2)}) collective-permute-start(bf16[1152,256]{1,0:T(8,128)(2,1)S(1)} %bitcast.120), channel_id=1, source_target_pairs={{0,2},{1,3},{2,4},{3,5},{4,6},{5,7},{8,10},{9,11},{10,12},{11,13},... | collective-permute-start | bytes 1769480 | tf_op jit(solution)/shard_map/ppermute | solution.py:437
  50.5 24.5 %collective-permute-done.4 = bf16[1152,256]{1,0:T(8,128)(2,1)S(1)} collective-permute-done((bf16[1152,256]{1,0:T(8,128)(2,1)S(1)}, bf16[1152,256]{1,0:T(8,128)(2,1)S(1)}, u32[]{:S(2)}, u32[]{:S(2)}) %collective-permute-start.4) | collective-permute-done | bytes 589856 | tf_op jit(solution)/shard_map/ppermute | solution.py:438
  75.1 1.3 collective-permute-start.10
  76.4 1.5 collective-permute-start.8
  77.9 21.5 %collective-permute-done.10 = bf16[1152,256]{1,0:T(8,128)(2,1)} collective-permute-done((bf16[1152,256]{1,0:T(8,128)(2,1)S(1)}, bf16[1152,256]{1,0:T(8,128)(2,1)}, u32[]{:S(2)}, u32[]{:S(2)}) %collective-permute-start.10) | collective-permute-done | bytes 589856 | tf_op jit(solution)/shard_map/ppermute | solution.py:438
  99.4 1.3 collective-permute-start.11
  101.4 2.0 select_bitcast_fusion.1
  103.3 40.6 %collective-permute-done.11 = bf16[1152,256]{1,0:T(8,128)(2,1)S(1)} collective-permute-done((bf16[1152,256]{1,0:T(8,128)(2,1)}, bf16[1152,256]{1,0:T(8,128)(2,1)S(1)}, u32[]{:S(2)}, u32[]{:S(2)}) %collective-permute-start.11) | collective-permute-done | bytes 589856 | tf_op jit(solution)/shard_map/ppermute | solution.py:438
  144.2 1.5 pad_maximum_fusion.1
  146.0 7.2 %forward_block.4 = (bf16[512,256]{1,0:T(8,128)(2,1)S(1)}, f32[2,512,128]{2,1,0:T(8,128)}) custom-call(s32[3]{0:T(128)S(1)} %pad_add_fusion.scal, bf16[512,256]{1,0:T(8,128)(2,1)} %get-tuple-element.89.refs_0_, bf16[512,256]{1,0:T(8,128)(2,1)} %get-tuple-element.88.refs_1_, bf16[512,256]{1,0:T(8,128)(2,1)} %get-tuple-element.87.refs_2_, ...), custom_call_target="tpu_custom_call" | custom-call | flops 2415919104 | bytes 4718592 | tf_op jit(solution)/shard_map/forward_block/pallas_call | solution.py:241
  153.2 2.8 collective-permute-start.7
  161.7 1.5 collective-permute-done.7.refs_3_
  163.3 5.2 %collective-permute-done.6.refs_2_ = bf16[512,256]{1,0:T(8,128)(2,1)S(1)} collective-permute-done((bf16[512,256]{1,0:T(8,128)(2,1)S(1)}, bf16[512,256]{1,0:T(8,128)(2,1)S(1)}, u32[]{:S(2)}, u32[]{:S(2)}) %collective-permute-start.6) | collective-permute-done | bytes 262176 | tf_op jit(solution)/shard_map/ppermute | solution.py:384
  169.3 7.2 %forward_block.5 = (bf16[512,256]{1,0:T(8,128)(2,1)S(1)}, f32[2,512,128]{2,1,0:T(8,128)}) custom-call(s32[3]{0:T(128)S(1)} %pad_add_fusion.scal, bf16[512,256]{1,0:T(8,128)(2,1)} %copy-done, bf16[512,256]{1,0:T(8,128)(2,1)} %copy-done.12, bf16[512,256]{1,0:T(8,128)(2,1)} %copy-done.11, bf16[512,256]{1,0:T(8,128)(2,1)} %copy-done.10, ...), custom_call_target="tpu_custom_call" | custom-call | flops 2415919104 | bytes 4718592 | tf_op jit(solution)/shard_map/forward_block/pallas_call | solution.py:241
  176.6 1.9 collective-permute-start.15
  178.5 1.3 collective-permute-start.14
  180.2 6.6 %collective-permute-done.15.refs_3_ = bf16[512,256]{1,0:T(8,128)(2,1)S(1)} collective-permute-done((bf16[512,256]{1,0:T(8,128)(2,1)S(1)}, bf16[512,256]{1,0:T(8,128)(2,1)S(1)}, u32[]{:S(2)}, u32[]{:S(2)}) %collective-permute-start.15) | collective-permute-done | bytes 262176 | tf_op jit(solution)/shard_map/ppermute | solution.py:384
  186.8 4.7 %collective-permute-done.14.refs_2_ = bf16[512,256]{1,0:T(8,128)(2,1)S(1)} collective-permute-done((bf16[512,256]{1,0:T(8,128)(2,1)S(1)}, bf16[512,256]{1,0:T(8,128)(2,1)S(1)}, u32[]{:S(2)}, u32[]{:S(2)}) %collective-permute-start.14) | collective-permute-done | bytes 262176 | tf_op jit(solution)/shard_map/ppermute | solution.py:384
  192.4 6.8 %all-gather.9.cloned.1.call-done.refs_6_.refs_5_.refs_8_.refs_7_ = bf16[9216,256]{1,0:T(8,128)(2,1)} async-done(((bf16[1152,256]{1,0:T(8,128)(2,1)}), bf16[9216,256]{1,0:T(8,128)(2,1)}) %all-gather.9.cloned.1.call-update) | async-done | bytes 4718608 | tf_op jit(solution)/shard_map/all_gather | solution.py:448
  199.2 7.2 %forward_block.6 = (bf16[512,256]{1,0:T(8,128)(2,1)S(1)}, f32[2,512,128]{2,1,0:T(8,128)}) custom-call(s32[3]{0:T(128)S(1)} %pad_add_fusion.scal, bf16[512,256]{1,0:T(8,128)(2,1)} %copy-done.2, bf16[512,256]{1,0:T(8,128)(2,1)} %copy-done.15, bf16[512,256]{1,0:T(8,128)(2,1)} %copy-done.14, bf16[512,256]{1,0:T(8,128)(2,1)} %copy-done.13, ...), custom_call_target="tpu_custom_call" | custom-call | flops 2415919104 | bytes 4718592 | tf_op jit(solution)/shard_map/forward_block/pallas_call | solution.py:241
  206.4 2.5 collective-permute-start.18
  210.0 6.6 %collective-permute-done.18.refs_3_ = bf16[512,256]{1,0:T(8,128)(2,1)S(1)} collective-permute-done((bf16[512,256]{1,0:T(8,128)(2,1)S(1)}, bf16[512,256]{1,0:T(8,128)(2,1)S(1)}, u32[]{:S(2)}, u32[]{:S(2)}) %collective-permute-start.18) | collective-permute-done | bytes 262176 | tf_op jit(solution)/shard_map/ppermute | solution.py:384
  216.6 4.9 %collective-permute-done.17.refs_2_ = bf16[512,256]{1,0:T(8,128)(2,1)S(1)} collective-permute-done((bf16[512,256]{1,0:T(8,128)(2,1)S(1)}, bf16[512,256]{1,0:T(8,128)(2,1)S(1)}, u32[]{:S(2)}, u32[]{:S(2)}) %collective-permute-start.17) | collective-permute-done | bytes 262176 | tf_op jit(solution)/shard_map/ppermute | solution.py:384
  221.5 2.7 maximum_select_fusion
  224.4 7.2 %forward_block.7 = (bf16[512,256]{1,0:T(8,128)(2,1)}, f32[2,512,128]{2,1,0:T(8,128)}, f32[4,1024]{1,0:T(4,128)S(1)}) custom-call(s32[3]{0:T(128)S(1)} %pad_add_fusion.scal, bf16[512,256]{1,0:T(8,128)(2,1)S(1)} %get-tuple-element.41.refs_0_, bf16[512,256]{1,0:T(8,128)(2,1)S(1)} %collective-permute-done.16.refs_1_, ...), custom_call_target="tpu_custom_call" | custom-call | flops 2415919104 | bytes 4718592 | tf_op jit(solution)/shard_map/forward_block/pallas_call | solution.py:241
  231.6 1.8 collective-permute-start.21
  238.3 6.9 %backward_block.4 = (bf16[512,256]{1,0:T(8,128)(2,1)S(1)}, f32[512,256]{1,0:T(8,128)S(1)}, bf16[512,256]{1,0:T(8,128)(2,1)S(1)}, bf16[512,256]{1,0:T(8,128)(2,1)S(1)}, bf16[512,256]{1,0:T(8,128)(2,1)S(1)}) custom-call(s32[3]{0:T(128)S(1)} %pad_add_fusion.scal, f32[4,1024]{1,0:T(4,128)S(1)} %get-tuple-element.42.refs_0_, ...), custom_call_target="tpu_custom_call" | custom-call | flops 2429026304 | bytes 5767168 | tf_op jit(solution)/shard_map/backward_block/pallas_call | solution.py:295
  245.9 1.4 collective-permute-start.23
  247.3 1.5 collective-permute-start.24
  248.8 5.8 %collective-permute-done.22.refs_1_ = bf16[512,256]{1,0:T(8,128)(2,1)S(1)} collective-permute-done((bf16[512,256]{1,0:T(8,128)(2,1)S(1)}, bf16[512,256]{1,0:T(8,128)(2,1)S(1)}, u32[]{:S(2)}, u32[]{:S(2)}) %collective-permute-start.22) | collective-permute-done | bytes 262176 | tf_op jit(solution)/shard_map/ppermute | solution.py:384
  254.6 3.5 collective-permute-done.23.refs_2_
  258.1 5.6 %backward_block.5 = (bf16[512,256]{1,0:T(8,128)(2,1)S(1)}, f32[512,256]{1,0:T(8,128)S(1)}, bf16[512,256]{1,0:T(8,128)(2,1)S(1)}, bf16[512,256]{1,0:T(8,128)(2,1)S(1)}, bf16[512,256]{1,0:T(8,128)(2,1)S(1)}) custom-call(s32[3]{0:T(128)S(1)} %pad_add_fusion.scal, f32[512,256]{1,0:T(8,128)S(1)} %get-tuple-element.44.refs_0_, ...), custom_call_target="tpu_custom_call" | custom-call | flops 2429026304 | bytes 5767168 | tf_op jit(solution)/shard_map/backward_block/pallas_call | solution.py:295
  263.7 1.6 collective-permute-start.25
  265.8 1.4 collective-permute-start.27
  267.2 4.8 %collective-permute-done.25.refs_1_ = bf16[512,256]{1,0:T(8,128)(2,1)S(1)} collective-permute-done((bf16[512,256]{1,0:T(8,128)(2,1)S(1)}, bf16[512,256]{1,0:T(8,128)(2,1)S(1)}, u32[]{:S(2)}, u32[]{:S(2)}) %collective-permute-start.25) | collective-permute-done | bytes 262176 | tf_op jit(solution)/shard_map/ppermute | solution.py:384
  272.1 4.3 %collective-permute-done.26.refs_2_ = bf16[512,256]{1,0:T(8,128)(2,1)S(1)} collective-permute-done((bf16[512,256]{1,0:T(8,128)(2,1)S(1)}, bf16[512,256]{1,0:T(8,128)(2,1)S(1)}, u32[]{:S(2)}, u32[]{:S(2)}) %collective-permute-start.26) | collective-permute-done | bytes 262176 | tf_op jit(solution)/shard_map/ppermute | solution.py:384
  276.3 5.6 %backward_block.6 = (bf16[512,256]{1,0:T(8,128)(2,1)S(1)}, f32[512,256]{1,0:T(8,128)S(1)}, bf16[512,256]{1,0:T(8,128)(2,1)S(1)}, bf16[512,256]{1,0:T(8,128)(2,1)S(1)}, bf16[512,256]{1,0:T(8,128)(2,1)S(1)}) custom-call(s32[3]{0:T(128)S(1)} %pad_add_fusion.scal, f32[512,256]{1,0:T(8,128)S(1)} %get-tuple-element.49.refs_0_, ...), custom_call_target="tpu_custom_call" | custom-call | flops 2429026304 | bytes 5767168 | tf_op jit(solution)/shard_map/backward_block/pallas_call | solution.py:295
  282.5 1.6 collective-permute-start.29
  284.1 1.4 collective-permute-start.30
  285.4 4.0 collective-permute-done.28.refs_1_
  289.5 2.9 collective-permute-done.29.refs_2_
  292.4 1.6 backward_block.7
  294.5 1.5 collective-permute-start.33
  296.0 1.6 collective-permute-start.32
  298.0 3.9 collective-permute-done.33
  301.9 2.7 collective-permute-done.32
  306.4 6.9 %dynamic-slice_bitcast_fusion.3 = (bf16[8,4,4,32,256]{4,3,2,1,0:T(8,128)(2,1)S(1)}, bf16[8,4,4,32,256]{4,3,2,1,0:T(8,128)(2,1)}, bf16[8,4,4,32,256]{4,3,2,1,0:T(8,128)(2,1)}, bf16[8,4,4,32,256]{4,3,2,1,0:T(8,128)(2,1)}) fusion(bf16[8,4,4,4,32,256]{5,4,3,2,1,0:T(8,128)(2,1)} %bitcast.116, s32[]{:T(128)S(6)} %select_n.231, s32[]{:T(128)S(6)} %select_n.233, ...), kind=kLoop, calls=%fused_computation.22 | loop fusion | bytes 16777232 | tf_op jit(solution)/shard_map/jit(dynamic_index_in_dim)/squeeze | solution.py:483
  313.3 17.8 %select_maximum_fusion = bf16[8,6,6,32,1024]{4,3,2,1,0:T(8,128)(2,1)} fusion(bf16[8,4,4,32,256]{4,3,2,1,0:T(8,128)(2,1)} %get-tuple-element.70, bf16[8,4,4,32,256]{4,3,2,1,0:T(8,128)(2,1)} %get-tuple-element.68, bf16[8,4,4,32,256]{4,3,2,1,0:T(8,128)(2,1)} %get-tuple-element.69, bf16[8,4,4,32,256]{4,3,2,1,0:T(8,128)(2,1)S(1)} %get-tuple-element.67), kind=kLoop, calls=%fused_computation.7 | loop fusion | flops 217055232 | bytes 27262976 | tf_op jit(solution)/shard_map/concatenate | solution.py:481
  331.0 12.5 %constant_dynamic-slice_fusion.1 = (bf16[8,4,4,32,1024]{4,3,2,1,0:T(8,128)(2,1)}, bf16[8,4,4,32,1024]{4,3,2,1,0:T(8,128)(2,1)}) fusion(bf16[8,6,6,32,1024]{4,3,2,1,0:T(8,128)(2,1)} %select_maximum_fusion, s32[]{:T(128)S(6)} %select_n.241, s32[]{:T(128)S(6)} %select_n.243, s32[]{:T(128)S(6)} %select_n.237, s32[]{:T(128)S(6)} %select_n.239), kind=kLoop, calls=%fused_computation.57 | loop fusion | bytes 33554448 | tf_op jit(solution)/shard_map/dynamic_slice | solution.py:493
  343.5 11.4 %copy.32 = bf16[4096,1024]{0,1:T(8,128)(2,1)} copy(bf16[4096,1024]{1,0:T(8,128)(2,1)} %bitcast.115) | data formatting | bytes 16777216 | tf_op jit(solution)/shard_map/reshape | solution.py:497
  354.9 11.9 %copy.31 = bf16[4096,1024]{0,1:T(8,128)(2,1)} copy(bf16[4096,1024]{1,0:T(8,128)(2,1)} %bitcast.114) | data formatting | bytes 16777216 | tf_op jit(solution)/shard_map/reshape | solution.py:497
  366.7 11.5 %fusion.7.cols = bf16[1152,4096]{1,0:T(8,128)(2,1)} fusion(s32[]{:T(128)S(6)} %select_n.245, bf16[4096,1024]{0,1:T(8,128)(2,1)} %copy.31, bf16[4096,1024]{0,1:T(8,128)(2,1)} %copy.32), kind=kLoop, calls=%fused_computation.16 | loop fusion | flops 18874368 | bytes 26214404 | tf_op jit(solution)/shard_map/transpose | solution.py:502
  378.2 8.4 %all-gather.13.cloned.1.call-done.raw = bf16[4096,1024]{1,0:T(8,128)(2,1)} async-done(((bf16[512,1024]{1,0:T(8,128)(2,1)}), bf16[4096,1024]{1,0:T(8,128)(2,1)}) %all-gather.13.cloned.1.call-update) | async-done | bytes 8388624 | tf_op jit(solution)/shard_map/all_gather | solution.py:501
  386.6 22.0 %update.1 = (f32[1152,1024]{1,0:T(8,128)}, f32[1152,1024]{1,0:T(8,128)}, f32[1152,1024]{1,0:T(8,128)}) custom-call(bf16[1152,4096]{1,0:T(8,128)(2,1)} %fusion.7.cols, bf16[4096,1024]{1,0:T(8,128)(2,1)} %all-gather.13.cloned.1.call-done.raw, f32[1152,1024]{1,0:T(8,128)} %bitcast.125, f32[1152,1024]{1,0:T(8,128)} %bitcast.138, f32[1152,1024]{1,0:T(8,128)} %bitcast.139), custom_call_target="tpu_custom_call" | custom-call | flops 9663676416 | bytes 36700160 | tf_op jit(solution)/shard_map/update/pallas_call | solution.py:342
  (97 shorter events, 23.0 us)
Async XLA Ops:
  7.2 67.8 %all-gather.15.cloned.1.call-start = ((), (), s32[]{:S(2)}) async-start(), calls=%async_computation.4 | async-start | bytes 5308416 | tf_op jit(solution)/shard_map/all_gather | solution.py:448
  11.1 132.8 %all-gather.7.cloned.1.call-start = ((), (), s32[]{:S(2)}) async-start(), calls=%async_computation | async-start | bytes 5308416 | tf_op jit(solution)/shard_map/all_gather | solution.py:448
  11.2 17.4 %collective-permute-start = (bf16[1152,256]{1,0:T(8,128)(2,1)}, bf16[1152,256]{1,0:T(8,128)(2,1)S(1)}, u32[]{:S(2)}, u32[]{:S(2)}) collective-permute-start(bf16[1152,256]{1,0:T(8,128)(2,1)} %get-tuple-element.71), channel_id=1, source_target_pairs={{0,8},{8,0},{16,24},{24,16},{1,9},{9,1},{17,25},{25,17},{2,10},{10... | collective-permute-start | bytes 1769480 | tf_op jit(solution)/shard_map/ppermute | solution.py:384
  14.2 27.7 %collective-permute-start.1 = (bf16[1152,256]{1,0:T(8,128)(2,1)}, bf16[1152,256]{1,0:T(8,128)(2,1)}, u32[]{:S(2)}, u32[]{:S(2)}) collective-permute-start(bf16[1152,256]{1,0:T(8,128)(2,1)} %get-tuple-element.72), channel_id=1, source_target_pairs={{0,16},{8,24},{16,0},{24,8},{1,17},{9,25},{17,1},{25,9},{2,18},{10... | collective-permute-start | bytes 1769480 | tf_op jit(solution)/shard_map/ppermute | solution.py:384
  15.7 26.2 %collective-permute-start.2 = (bf16[1152,256]{1,0:T(8,128)(2,1)}, bf16[1152,256]{1,0:T(8,128)(2,1)}, u32[]{:S(2)}, u32[]{:S(2)}) collective-permute-start(bf16[1152,256]{1,0:T(8,128)(2,1)} %get-tuple-element.74), channel_id=1, source_target_pairs={{0,24},{8,16},{16,8},{24,0},{1,25},{9,17},{17,9},{25,1},{2,26},{10... | collective-permute-start | bytes 1769480 | tf_op jit(solution)/shard_map/ppermute | solution.py:384
  15.7 26.2 %copy-start.4 = (bf16[1,1152,256]{2,1,0:T(8,128)(2,1)S(1)}, bf16[1,1152,256]{2,1,0:T(8,128)(2,1)}, u32[]{:S(2)}) copy-start(bf16[1,1152,256]{2,1,0:T(8,128)(2,1)} %get-tuple-element.73) | copy-start | bytes 1769476
  44.6 1.3 copy-start.5
  44.6 30.4 %collective-permute-start.4 = (bf16[1152,256]{1,0:T(8,128)(2,1)S(1)}, bf16[1152,256]{1,0:T(8,128)(2,1)S(1)}, u32[]{:S(2)}, u32[]{:S(2)}) collective-permute-start(bf16[1152,256]{1,0:T(8,128)(2,1)S(1)} %bitcast.119), channel_id=1, source_target_pairs={{2,0},{3,1},{4,2},{5,3},{6,4},{7,5},{10,8},{11,9},{12,10},{13,11},... | collective-permute-start | bytes 1769480 | tf_op jit(solution)/shard_map/ppermute | solution.py:438
  45.9 29.1 %collective-permute-start.3 = (bf16[1152,256]{1,0:T(8,128)(2,1)S(1)}, bf16[1152,256]{1,0:T(8,128)(2,1)S(1)}, u32[]{:S(2)}, u32[]{:S(2)}) collective-permute-start(bf16[1152,256]{1,0:T(8,128)(2,1)S(1)} %bitcast.120), channel_id=1, source_target_pairs={{0,2},{1,3},{2,4},{3,5},{4,6},{5,7},{8,10},{9,11},{10,12},{11,13},... | collective-permute-start | bytes 1769480 | tf_op jit(solution)/shard_map/ppermute | solution.py:437
  75.0 124.2 %all-gather.9.cloned.1.call-start = ((), (), s32[]{:S(2)}) async-start(), calls=%async_computation.1 | async-start | bytes 5308416 | tf_op jit(solution)/shard_map/all_gather | solution.py:448
  75.1 24.3 %collective-permute-start.10 = (bf16[1152,256]{1,0:T(8,128)(2,1)S(1)}, bf16[1152,256]{1,0:T(8,128)(2,1)}, u32[]{:S(2)}, u32[]{:S(2)}) collective-permute-start(bf16[1152,256]{1,0:T(8,128)(2,1)S(1)} %collective-permute-done.4), channel_id=1, source_target_pairs={{2,0},{3,1},{4,2},{5,3},{10,8},{11,9},{12,10},{13,11},{18,16},{19,... | collective-permute-start | bytes 1769480 | tf_op jit(solution)/shard_map/ppermute | solution.py:438
  76.4 24.3 %collective-permute-start.8 = (bf16[1152,256]{1,0:T(8,128)(2,1)S(1)}, bf16[1152,256]{1,0:T(8,128)(2,1)}, u32[]{:S(2)}, u32[]{:S(2)}) collective-permute-start(bf16[1152,256]{1,0:T(8,128)(2,1)S(1)} %collective-permute-done.3), channel_id=1, source_target_pairs={{2,4},{3,5},{4,6},{5,7},{10,12},{11,13},{12,14},{13,15},{18,20},{1... | collective-permute-start | bytes 1769480 | tf_op jit(solution)/shard_map/ppermute | solution.py:437
  99.4 44.6 %collective-permute-start.11 = (bf16[1152,256]{1,0:T(8,128)(2,1)}, bf16[1152,256]{1,0:T(8,128)(2,1)S(1)}, u32[]{:S(2)}, u32[]{:S(2)}) collective-permute-start(bf16[1152,256]{1,0:T(8,128)(2,1)} %collective-permute-done.10), channel_id=1, source_target_pairs={{2,0},{3,1},{10,8},{11,9},{18,16},{19,17},{26,24},{27,25}} | collective-permute-start | bytes 1769480 | tf_op jit(solution)/shard_map/ppermute | solution.py:438
  100.7 43.3 %collective-permute-start.9 = (bf16[1152,256]{1,0:T(8,128)(2,1)}, bf16[1152,256]{1,0:T(8,128)(2,1)S(1)}, u32[]{:S(2)}, u32[]{:S(2)}) collective-permute-start(bf16[1152,256]{1,0:T(8,128)(2,1)} %collective-permute-done.8), channel_id=1, source_target_pairs={{4,6},{5,7},{12,14},{13,15},{20,22},{21,23},{28,30},{29,31}} | collective-permute-start | bytes 1769480 | tf_op jit(solution)/shard_map/ppermute | solution.py:437
  144.0 162.4 %all-gather.11.cloned.1.call-start = ((), (), s32[]{:S(2)}) async-start(), calls=%async_computation.2 | async-start | bytes 9437184 | tf_op jit(solution)/shard_map/all_gather | solution.py:461
  145.7 11.0 %collective-permute-start.12 = (bf16[4,1152,256]{2,1,0:T(8,128)(2,1)S(1)}, bf16[4,1152,256]{2,1,0:T(8,128)(2,1)}, u32[]{:S(2)}, u32[]{:S(2)}) collective-permute-start(bf16[4,1152,256]{2,1,0:T(8,128)(2,1)S(1)} %pad_maximum_fusion.1), channel_id=1, source_target_pairs={{0,1},{1,0},{2,3},{3,2},{4,5},{5,4},{6,7},{7,6},{8,9},{9,8},{10,11... | collective-permute-start | bytes 7077896 | tf_op jit(solution)/shard_map/ppermute | solution.py:325
  153.2 4.1 copy-start
  153.2 10.1 %collective-permute-start.7 = (bf16[512,256]{1,0:T(8,128)(2,1)S(1)}, bf16[512,256]{1,0:T(8,128)(2,1)S(1)}, u32[]{:S(2)}, u32[]{:S(2)}) collective-permute-start(bf16[512,256]{1,0:T(8,128)(2,1)S(1)} %get-tuple-element.36.refs_0_), channel_id=1, source_target_pairs={{0,24},{8,16},{16,8},{24,0},{1,25},{9,17},{17,9},{25,1},{2,26},{10... | collective-permute-start | bytes 786440 | tf_op jit(solution)/shard_map/ppermute | solution.py:384
  156.0 12.5 %collective-permute-start.6 = (bf16[512,256]{1,0:T(8,128)(2,1)S(1)}, bf16[512,256]{1,0:T(8,128)(2,1)S(1)}, u32[]{:S(2)}, u32[]{:S(2)}) collective-permute-start(bf16[512,256]{1,0:T(8,128)(2,1)S(1)} %get-tuple-element.36.refs_0_), channel_id=1, source_target_pairs={{0,16},{8,24},{16,0},{24,8},{1,17},{9,25},{17,1},{25,9},{2,18},{10... | collective-permute-start | bytes 786440 | tf_op jit(solution)/shard_map/ppermute | solution.py:384
  156.2 12.4 %collective-permute-start.5 = (bf16[512,256]{1,0:T(8,128)(2,1)S(1)}, bf16[512,256]{1,0:T(8,128)(2,1)S(1)}, u32[]{:S(2)}, u32[]{:S(2)}) collective-permute-start(bf16[512,256]{1,0:T(8,128)(2,1)S(1)} %get-tuple-element.36.refs_0_), channel_id=1, source_target_pairs={{0,8},{8,0},{16,24},{24,16},{1,9},{9,1},{17,25},{25,17},{2,10},{10... | collective-permute-start | bytes 786440 | tf_op jit(solution)/shard_map/ppermute | solution.py:384
  161.7 6.9 %copy-start.3 = (bf16[8,1152,256]{2,1,0:T(8,128)(2,1)}, bf16[8,1152,256]{2,1,0:T(8,128)(2,1)S(1)}, u32[]{:S(2)}) copy-start(bf16[8,1152,256]{2,1,0:T(8,128)(2,1)S(1)} %slice_dynamic-update-slice_fusion) | copy-start | bytes 14155780
  163.3 5.3 %copy-start.10 = (bf16[512,256]{1,0:T(8,128)(2,1)}, bf16[512,256]{1,0:T(8,128)(2,1)S(1)}, u32[]{:S(2)}) copy-start(bf16[512,256]{1,0:T(8,128)(2,1)S(1)} %collective-permute-done.7.refs_3_) | copy-start | bytes 786436
  168.5 0.7 copy-start.11
  168.6 0.7 copy-start.12
  176.6 22.6 %copy-start.2 = (bf16[512,256]{1,0:T(8,128)(2,1)}, bf16[512,256]{1,0:T(8,128)(2,1)S(1)}, u32[]{:S(2)}) copy-start(bf16[512,256]{1,0:T(8,128)(2,1)S(1)} %get-tuple-element.39.refs_0_) | copy-start | bytes 786436
  176.6 44.9 %copy-start.1 = (bf16[512,256]{1,0:T(8,128)(2,1)S(1)}, bf16[512,256]{1,0:T(8,128)(2,1)}, u32[]{:S(2)}) copy-start(bf16[512,256]{1,0:T(8,128)(2,1)} %copy-done) | copy-start | bytes 786436
  176.6 44.9 %copy-start.6 = (bf16[512,256]{1,0:T(8,128)(2,1)S(1)}, bf16[512,256]{1,0:T(8,128)(2,1)}, u32[]{:S(2)}) copy-start(bf16[512,256]{1,0:T(8,128)(2,1)} %get-tuple-element.86.refs_3_) | copy-start | bytes 786436
  176.6 44.9 %copy-start.7 = (bf16[512,256]{1,0:T(8,128)(2,1)S(1)}, bf16[512,256]{1,0:T(8,128)(2,1)}, u32[]{:S(2)}) copy-start(bf16[512,256]{1,0:T(8,128)(2,1)} %get-tuple-element.87.refs_2_) | copy-start | bytes 786436
  176.6 44.9 %copy-start.8 = (bf16[512,256]{1,0:T(8,128)(2,1)S(1)}, bf16[512,256]{1,0:T(8,128)(2,1)}, u32[]{:S(2)}) copy-start(bf16[512,256]{1,0:T(8,128)(2,1)} %get-tuple-element.88.refs_1_) | copy-start | bytes 786436
  176.6 44.9 %copy-start.9 = (bf16[512,256]{1,0:T(8,128)(2,1)S(1)}, bf16[512,256]{1,0:T(8,128)(2,1)}, u32[]{:S(2)}) copy-start(bf16[512,256]{1,0:T(8,128)(2,1)} %get-tuple-element.89.refs_0_) | copy-start | bytes 786436
  176.6 10.2 %collective-permute-start.15 = (bf16[512,256]{1,0:T(8,128)(2,1)S(1)}, bf16[512,256]{1,0:T(8,128)(2,1)S(1)}, u32[]{:S(2)}, u32[]{:S(2)}) collective-permute-start(bf16[512,256]{1,0:T(8,128)(2,1)S(1)} %get-tuple-element.39.refs_0_), channel_id=1, source_target_pairs={{0,24},{8,16},{16,8},{24,0},{1,25},{9,17},{17,9},{25,1},{2,26},{10... | collective-permute-start | bytes 786440 | tf_op jit(solution)/shard_map/ppermute | solution.py:384
  178.5 13.0 %collective-permute-start.14 = (bf16[512,256]{1,0:T(8,128)(2,1)S(1)}, bf16[512,256]{1,0:T(8,128)(2,1)S(1)}, u32[]{:S(2)}, u32[]{:S(2)}) collective-permute-start(bf16[512,256]{1,0:T(8,128)(2,1)S(1)} %get-tuple-element.39.refs_0_), channel_id=1, source_target_pairs={{0,16},{8,24},{16,0},{24,8},{1,17},{9,25},{17,1},{25,9},{2,18},{10... | collective-permute-start | bytes 786440 | tf_op jit(solution)/shard_map/ppermute | solution.py:384
  179.9 11.8 %collective-permute-start.13 = (bf16[512,256]{1,0:T(8,128)(2,1)S(1)}, bf16[512,256]{1,0:T(8,128)(2,1)S(1)}, u32[]{:S(2)}, u32[]{:S(2)}) collective-permute-start(bf16[512,256]{1,0:T(8,128)(2,1)S(1)} %get-tuple-element.39.refs_0_), channel_id=1, source_target_pairs={{0,8},{8,0},{16,24},{24,16},{1,9},{9,1},{17,25},{25,17},{2,10},{10... | collective-permute-start | bytes 786440 | tf_op jit(solution)/shard_map/ppermute | solution.py:384
  186.8 12.4 %copy-start.13 = (bf16[512,256]{1,0:T(8,128)(2,1)}, bf16[512,256]{1,0:T(8,128)(2,1)S(1)}, u32[]{:S(2)}) copy-start(bf16[512,256]{1,0:T(8,128)(2,1)S(1)} %collective-permute-done.15.refs_3_) | copy-start | bytes 786436
  191.5 7.7 %copy-start.14 = (bf16[512,256]{1,0:T(8,128)(2,1)}, bf16[512,256]{1,0:T(8,128)(2,1)S(1)}, u32[]{:S(2)}) copy-start(bf16[512,256]{1,0:T(8,128)(2,1)S(1)} %collective-permute-done.14.refs_2_) | copy-start | bytes 786436
  191.7 0.7 copy-start.15
  206.4 10.1 %collective-permute-start.18 = (bf16[512,256]{1,0:T(8,128)(2,1)S(1)}, bf16[512,256]{1,0:T(8,128)(2,1)S(1)}, u32[]{:S(2)}, u32[]{:S(2)}) collective-permute-start(bf16[512,256]{1,0:T(8,128)(2,1)S(1)} %get-tuple-element.41.refs_0_), channel_id=1, source_target_pairs={{0,24},{8,16},{16,8},{24,0},{1,25},{9,17},{17,9},{25,1},{2,26},{10... | collective-permute-start | bytes 786440 | tf_op jit(solution)/shard_map/ppermute | solution.py:384
  208.9 12.6 %collective-permute-start.17 = (bf16[512,256]{1,0:T(8,128)(2,1)S(1)}, bf16[512,256]{1,0:T(8,128)(2,1)S(1)}, u32[]{:S(2)}, u32[]{:S(2)}) collective-permute-start(bf16[512,256]{1,0:T(8,128)(2,1)S(1)} %get-tuple-element.41.refs_0_), channel_id=1, source_target_pairs={{0,16},{8,24},{16,0},{24,8},{1,17},{9,25},{17,1},{25,9},{2,18},{10... | collective-permute-start | bytes 786440 | tf_op jit(solution)/shard_map/ppermute | solution.py:384
  209.4 12.1 %collective-permute-start.16 = (bf16[512,256]{1,0:T(8,128)(2,1)S(1)}, bf16[512,256]{1,0:T(8,128)(2,1)S(1)}, u32[]{:S(2)}, u32[]{:S(2)}) collective-permute-start(bf16[512,256]{1,0:T(8,128)(2,1)S(1)} %get-tuple-element.41.refs_0_), channel_id=1, source_target_pairs={{0,8},{8,0},{16,24},{24,16},{1,9},{9,1},{17,25},{25,17},{2,10},{10... | collective-permute-start | bytes 786440 | tf_op jit(solution)/shard_map/ppermute | solution.py:384
  224.2 11.0 %copy-start.16 = (s32[4]{0:T(128)S(1)}, s32[4]{0:T(128)}, u32[]{:S(2)}) copy-start(s32[4]{0:T(128)} %param.7) | copy-start | bytes 52
  224.2 162.4 %all-gather.13.cloned.1.call-start = ((), (), s32[]{:S(2)}) async-start(), calls=%async_computation.3 | async-start | bytes 9437184 | tf_op jit(solution)/shard_map/all_gather | solution.py:501
  231.6 4.7 %collective-permute-start.21 = (f32[4,1024]{1,0:T(4,128)S(1)}, f32[4,1024]{1,0:T(4,128)S(1)}, u32[]{:S(2)}, u32[]{:S(2)}) collective-permute-start(f32[4,1024]{1,0:T(4,128)S(1)} %get-tuple-element.42.refs_0_), channel_id=1, source_target_pairs={{0,24},{8,16},{16,8},{24,0},{1,25},{9,17},{17,9},{25,1},{2,26},{10... | collective-permute-start | bytes 49160 | tf_op jit(solution)/shard_map/ppermute | solution.py:384
  233.4 3.7 collective-permute-start.20
  234.6 3.7 collective-permute-start.19
  245.3 9.3 %collective-permute-start.22 = (bf16[512,256]{1,0:T(8,128)(2,1)S(1)}, bf16[512,256]{1,0:T(8,128)(2,1)S(1)}, u32[]{:S(2)}, u32[]{:S(2)}) collective-permute-start(bf16[512,256]{1,0:T(8,128)(2,1)S(1)} %get-tuple-element.45), channel_id=1, source_target_pairs={{0,8},{8,0},{16,24},{24,16},{1,9},{9,1},{17,25},{25,17},{2,10},{10... | collective-permute-start | bytes 786440 | tf_op jit(solution)/shard_map/ppermute | solution.py:384
  245.9 12.2 %collective-permute-start.23 = (bf16[512,256]{1,0:T(8,128)(2,1)S(1)}, bf16[512,256]{1,0:T(8,128)(2,1)S(1)}, u32[]{:S(2)}, u32[]{:S(2)}) collective-permute-start(bf16[512,256]{1,0:T(8,128)(2,1)S(1)} %get-tuple-element.46), channel_id=1, source_target_pairs={{0,16},{8,24},{16,0},{24,8},{1,17},{9,25},{17,1},{25,9},{2,18},{10... | collective-permute-start | bytes 786440 | tf_op jit(solution)/shard_map/ppermute | solution.py:384
  247.3 10.8 %collective-permute-start.24 = (bf16[512,256]{1,0:T(8,128)(2,1)S(1)}, bf16[512,256]{1,0:T(8,128)(2,1)S(1)}, u32[]{:S(2)}, u32[]{:S(2)}) collective-permute-start(bf16[512,256]{1,0:T(8,128)(2,1)S(1)} %get-tuple-element.47), channel_id=1, source_target_pairs={{0,24},{8,16},{16,8},{24,0},{1,25},{9,17},{17,9},{25,1},{2,26},{10... | collective-permute-start | bytes 786440 | tf_op jit(solution)/shard_map/ppermute | solution.py:384
  263.7 8.4 %collective-permute-start.25 = (bf16[512,256]{1,0:T(8,128)(2,1)S(1)}, bf16[512,256]{1,0:T(8,128)(2,1)S(1)}, u32[]{:S(2)}, u32[]{:S(2)}) collective-permute-start(bf16[512,256]{1,0:T(8,128)(2,1)S(1)} %get-tuple-element.50), channel_id=1, source_target_pairs={{0,8},{8,0},{16,24},{24,16},{1,9},{9,1},{17,25},{25,17},{2,10},{10... | collective-permute-start | bytes 786440 | tf_op jit(solution)/shard_map/ppermute | solution.py:384
  265.3 11.1 %collective-permute-start.26 = (bf16[512,256]{1,0:T(8,128)(2,1)S(1)}, bf16[512,256]{1,0:T(8,128)(2,1)S(1)}, u32[]{:S(2)}, u32[]{:S(2)}) collective-permute-start(bf16[512,256]{1,0:T(8,128)(2,1)S(1)} %get-tuple-element.51), channel_id=1, source_target_pairs={{0,16},{8,24},{16,0},{24,8},{1,17},{9,25},{17,1},{25,9},{2,18},{10... | collective-permute-start | bytes 786440 | tf_op jit(solution)/shard_map/ppermute | solution.py:384
  265.8 10.5 %collective-permute-start.27 = (bf16[512,256]{1,0:T(8,128)(2,1)S(1)}, bf16[512,256]{1,0:T(8,128)(2,1)S(1)}, u32[]{:S(2)}, u32[]{:S(2)}) collective-permute-start(bf16[512,256]{1,0:T(8,128)(2,1)S(1)} %get-tuple-element.52), channel_id=1, source_target_pairs={{0,24},{8,16},{16,8},{24,0},{1,25},{9,17},{17,9},{25,1},{2,26},{10... | collective-permute-start | bytes 786440 | tf_op jit(solution)/shard_map/ppermute | solution.py:384
  281.9 7.6 %collective-permute-start.28 = (bf16[512,256]{1,0:T(8,128)(2,1)S(1)}, bf16[512,256]{1,0:T(8,128)(2,1)S(1)}, u32[]{:S(2)}, u32[]{:S(2)}) collective-permute-start(bf16[512,256]{1,0:T(8,128)(2,1)S(1)} %get-tuple-element.55), channel_id=1, source_target_pairs={{0,8},{8,0},{16,24},{24,16},{1,9},{9,1},{17,25},{25,17},{2,10},{10... | collective-permute-start | bytes 786440 | tf_op jit(solution)/shard_map/ppermute | solution.py:384
  282.5 9.9 %collective-permute-start.29 = (bf16[512,256]{1,0:T(8,128)(2,1)S(1)}, bf16[512,256]{1,0:T(8,128)(2,1)S(1)}, u32[]{:S(2)}, u32[]{:S(2)}) collective-permute-start(bf16[512,256]{1,0:T(8,128)(2,1)S(1)} %get-tuple-element.56), channel_id=1, source_target_pairs={{0,16},{8,24},{16,0},{24,8},{1,17},{9,25},{17,1},{25,9},{2,18},{10... | collective-permute-start | bytes 786440 | tf_op jit(solution)/shard_map/ppermute | solution.py:384
  284.1 8.3 %collective-permute-start.30 = (bf16[512,256]{1,0:T(8,128)(2,1)S(1)}, bf16[512,256]{1,0:T(8,128)(2,1)S(1)}, u32[]{:S(2)}, u32[]{:S(2)}) collective-permute-start(bf16[512,256]{1,0:T(8,128)(2,1)S(1)} %get-tuple-element.57), channel_id=1, source_target_pairs={{0,24},{8,16},{16,8},{24,0},{1,25},{9,17},{17,9},{25,1},{2,26},{10... | collective-permute-start | bytes 786440 | tf_op jit(solution)/shard_map/ppermute | solution.py:384
  294.5 7.4 %collective-permute-start.33 = (bf16[512,256]{1,0:T(8,128)(2,1)S(1)}, bf16[512,256]{1,0:T(8,128)(2,1)S(1)}, u32[]{:S(2)}, u32[]{:S(2)}) collective-permute-start(bf16[512,256]{1,0:T(8,128)(2,1)S(1)} %get-tuple-element.83), channel_id=1, source_target_pairs={{0,24},{8,16},{16,8},{24,0},{1,25},{9,17},{17,9},{25,1},{2,26},{10... | collective-permute-start | bytes 786440 | tf_op jit(solution)/shard_map/ppermute | solution.py:384
  296.0 8.6 %collective-permute-start.32 = (bf16[512,256]{1,0:T(8,128)(2,1)S(1)}, bf16[512,256]{1,0:T(8,128)(2,1)S(1)}, u32[]{:S(2)}, u32[]{:S(2)}) collective-permute-start(bf16[512,256]{1,0:T(8,128)(2,1)S(1)} %get-tuple-element.84), channel_id=1, source_target_pairs={{0,16},{8,24},{16,0},{24,8},{1,17},{9,25},{17,1},{25,9},{2,18},{10... | collective-permute-start | bytes 786440 | tf_op jit(solution)/shard_map/ppermute | solution.py:384
  297.6 7.3 %collective-permute-start.31 = (bf16[512,256]{1,0:T(8,128)(2,1)S(1)}, bf16[512,256]{1,0:T(8,128)(2,1)S(1)}, u32[]{:S(2)}, u32[]{:S(2)}) collective-permute-start(bf16[512,256]{1,0:T(8,128)(2,1)S(1)} %get-tuple-element.85), channel_id=1, source_target_pairs={{0,8},{8,0},{16,24},{24,16},{1,9},{9,1},{17,25},{25,17},{2,10},{10... | collective-permute-start | bytes 786440 | tf_op jit(solution)/shard_map/ppermute | solution.py:384
Sparse Core Ops, SparseCore 0:
  11.2 60.1 all-gather.14
  75.1 67.2 all-gather.6
  144.7 54.4 all-gather.8
  224.3 80.1 all-gather.10
  306.4 80.1 all-gather.12

commit v6 on v3

--- a/solution.py
+++ b/solution.py
@@ -37,10 +37,10 @@
     return cells, neighbours
 
 
-def fetch_weights(block, sections, scal, sources, weights, sems):
+def fetch_weights(block, sections, scal, sources, weights, sems, order=offsets):
     s = scal[0]
     slot = jnp.where(block == s, 0, jnp.where(block < s, block + 1, block))
-    rows = weights.shape[0] // 9
+    rows = weights.shape[0] // len(order)
 
     def copy(source, offset):
         part = pl.ds(offset * rows, rows)
@@ -50,7 +50,7 @@
 
         @pl.when(slot == candidate)
         def _():
-            for offset in offsets:
+            for offset in order:
                 copy(source, offset).start()
 
     return lambda offset: copy(weights, offset).wait()
@@ -68,15 +68,15 @@
         readout, out, fired_out, logits_out, weights, held, work, total, sems = refs
     else:
         out, fired_out, weights, held, work, total, sems = refs
-    wait = fetch_weights(block, sections, scal, sources, weights, sems)
+    wait = fetch_weights(block, sections, scal, sources, weights, sems, (0,))
     rows, lanes = slices[0].shape
     group = images * steps
     channels = sections * lanes
     for k in range(sections):
         held[scal[0] ^ k] = slices[k][...].reshape(height, width, group, lanes)
+    wait(0)
     for offset in offsets:
         cells, neighbours = overlap(offset, height, width)
-        wait(offset)
         lhs = jnp.concatenate(
             [held[(j, *neighbours)].reshape(-1, lanes) for j in range(sections)], axis=1
         )
@@ -222,7 +222,7 @@
     last = block == sections - 1
     shapes = [
         jax.ShapeDtypeStruct((rows, lanes), jnp.bfloat16),
-        jax.ShapeDtypeStruct((lanes // 128, rows, 128), jnp.float32),
+        pltpu.HBM((lanes // 128, rows, 128), jnp.float32),
     ]
     operands = [scal, *(slices if last else stay(slices)), *stay(sources)]
     extra = []
@@ -243,7 +243,7 @@
             VMEM((sections, height, width, images * steps, lanes), jnp.bfloat16),
             VMEM((lanes // 128, rows, 128), jnp.float32),
             VMEM((height, width, images * steps, lanes), jnp.float32),
-            pltpu.SemaphoreType.DMA((9,)),
+            pltpu.SemaphoreType.DMA((1,)),
         ],
         compiler_params=pltpu.CompilerParams(vmem_limit_bytes=LIMIT),
         cost_estimate=pl.CostEstimate(
@@ -344,7 +344,7 @@
             state,
         ],
         out_specs=[state] * 3,
-        compiler_params=pltpu.CompilerParams(vmem_limit_bytes=40 * 2**20),
+        compiler_params=pltpu.CompilerParams(vmem_limit_bytes=48 * 2**20),
         cost_estimate=pl.CostEstimate(
             flops=2 * rows * depth * channels,
             bytes_accessed=24 * depth * channels + 2 * rows * channels,
@@ -352,11 +352,7 @@
         ),
         name="update",
     )(
-        pltpu.with_memory_space_constraint(cols, VMEM),
-        raw,
-        weights,
-        first_moment,
-        second_moment,
+        *stay([cols, raw, weights, first_moment, second_moment])
     )
 
 
@@ -455,14 +451,7 @@
     def ordered(parts):
         return jnp.concatenate([pick(parts, s ^ j) for j in range(sections)], axis=1)
 
-    own_x = jnp.concatenate(
-        [
-            lax.dynamic_index_in_dim(own_inputs, s ^ j, 0, keepdims=False)
-            for j in range(sections)
-        ],
-        axis=1,
-    )
-    x_all = lax.all_gather(own_x, "dp")
+    x_all = lax.all_gather(own_inputs.reshape(sections * rows, lanes), "dp")
 
     raws = [None] * sections
     for b in reversed(range(sections)):
@@ -481,7 +470,14 @@
         step *= 2
     spans = -(-(channels - step + depth) // channels)
 
-    fields = x_all.reshape(devices, height, width, group, channels)
+    x_all = x_all.reshape(devices, sections, height, width, group, lanes)
+    fields = jnp.concatenate(
+        [
+            lax.dynamic_index_in_dim(x_all, s ^ j, 1, keepdims=False)
+            for j in range(sections)
+        ],
+        axis=-1,
+    )
     fields = jnp.pad(fields, ((0, 0), (1, 1), (1, 1), (0, 0), (0, 0)))
     shifted = []
     for i in range(spans):

time: 420 us -> 416 us (level)
  waiting for transfers between devices: 210 us -> 189 us
  other arithmetic: 21.1 us -> 38.4 us
    all_gather x1, waiting for transfers between devices: 33.2 us -> 9.23 us  [shards(): raw_all = lax.all_gather(own_raw, 'dp', axis=0, tiled=True)]
    concatenate x1, other arithmetic: 1.11 us -> 17.7 us  [shards(): jnp.concatenate([lax.dynamic_index_in_dim(x_all, s ^ j, 1, keepdims=False...]
    unnamed x47 -> x35, local copies, waits for them, and re-layouts: 12.5 us -> 2.81 us
    squeeze x1, local copies, waits for them, and re-layouts: 0.08 us -> 6.87 us  [shards(): lax.dynamic_index_in_dim(x_all, s ^ j, 1, keepdims=False)]
    pallas_call x1, Pallas kernels: 17.4 us -> 22 us  [run_update(): pl.pallas_call(update_kernel, grid=(channels // tile,), out_shape=[jax.Sh...]
  transfers between devices with their start and end apart: 39 -> 39, of which waited for: 27 -> 28; matrix products, arithmetic and copies ran while one was open for 16% -> 22% of each run, Pallas kernels for 10% -> 9%
where the time goes in v6:
time: 416 us; the launch traced here: 414 us
  waiting for transfers between devices  189 us (45%)
  Pallas kernels  67.5 us (16%)
  local copies, waits for them, and re-layouts  61.6 us (15%)
  starting transfers between devices  44.1 us (11%)
  other arithmetic  38.4 us (9%)
  between operations  14.4 us (3%)
    ppermute x3, waiting for transfers between devices, shards(): down = lax.ppermute(down, 'dp', hops(step, -1, ring))  86.6 us
    ppermute x27, waiting for transfers between devices, exchange(): lax.ppermute(values[k], 'section', [(i, i ^ k + 1) for i in range(section...  84.2 us
    ppermute x27, starting transfers between devices, exchange(): lax.ppermute(values[k], 'section', [(i, i ^ k + 1) for i in range(section...  33 us
    pallas_call x4, Pallas kernels, run_forward(): pl.pallas_call(functools.partial(forward_kernel, dims, block), out_shape=...  25.7 us
    reshape x2, local copies, waits for them, and re-layouts, shards(): shifted.append(lax.dynamic_slice(fields, (0, offset // 3, offset % 3, 0,...  23.4 us
    pallas_call x1, Pallas kernels, run_update(): pl.pallas_call(update_kernel, grid=(channels // tile,), out_shape=[jax.Sh...  22 us
    pallas_call x4, Pallas kernels, run_backward(): pl.pallas_call(functools.partial(backward_kernel, dims, block, classes),...  19.7 us
    concatenate x1, other arithmetic, shards(): jnp.concatenate([lax.dynamic_index_in_dim(x_all, s ^ j, 1, keepdims=False...  17.7 us
  transfers between devices with their start and end apart: 39, of which 28 were waited for; matrix products, arithmetic and copies ran while one was open for 22% of the time, Pallas kernels for 9%

profile of v6, /device:TPU:0, one launch (start us, length us, event | category | flops | bytes accessed | tf_op | source)
XLA Modules:
  0.0 414.4 jit_solution(2412951578163600025)
XLA Ops:
  7.2 3.8 fusion.8
  11.2 3.0 collective-permute-start
  14.2 1.5 collective-permute-start.1
  15.7 1.3 constant_dynamic-slice_fusion.3
  17.0 1.3 copy.34
  18.4 1.8 copy.25
  20.2 1.4 pad.8.refs_6_.refs_5_
  22.6 5.9 %collective-permute-done = bf16[1152,256]{1,0:T(8,128)(2,1)S(1)} collective-permute-done((bf16[1152,256]{1,0:T(8,128)(2,1)}, bf16[1152,256]{1,0:T(8,128)(2,1)S(1)}, u32[]{:S(2)}, u32[]{:S(2)}) %collective-permute-start) | collective-permute-done | bytes 589856 | tf_op jit(solution)/shard_map/ppermute | solution.py:377
  28.5 13.4 %collective-permute-done.1 = bf16[1152,256]{1,0:T(8,128)(2,1)} collective-permute-done((bf16[1152,256]{1,0:T(8,128)(2,1)}, bf16[1152,256]{1,0:T(8,128)(2,1)}, u32[]{:S(2)}, u32[]{:S(2)}) %collective-permute-start.1) | collective-permute-done | bytes 589856 | tf_op jit(solution)/shard_map/ppermute | solution.py:377
  41.9 1.5 pad_maximum_fusion
  45.9 4.6 %collective-permute-start.3 = (bf16[1152,256]{1,0:T(8,128)(2,1)S(1)}, bf16[1152,256]{1,0:T(8,128)(2,1)S(1)}, u32[]{:S(2)}, u32[]{:S(2)}) collective-permute-start(bf16[1152,256]{1,0:T(8,128)(2,1)S(1)} %bitcast.120), channel_id=1, source_target_pairs={{0,2},{1,3},{2,4},{3,5},{4,6},{5,7},{8,10},{9,11},{10,12},{11,13},... | collective-permute-start | bytes 1769480 | tf_op jit(solution)/shard_map/ppermute | solution.py:430
  50.5 24.5 %collective-permute-done.4 = bf16[1152,256]{1,0:T(8,128)(2,1)S(1)} collective-permute-done((bf16[1152,256]{1,0:T(8,128)(2,1)S(1)}, bf16[1152,256]{1,0:T(8,128)(2,1)S(1)}, u32[]{:S(2)}, u32[]{:S(2)}) %collective-permute-start.4) | collective-permute-done | bytes 589856 | tf_op jit(solution)/shard_map/ppermute | solution.py:431
  75.1 1.3 collective-permute-start.10
  76.4 1.5 collective-permute-start.8
  77.9 21.5 %collective-permute-done.10 = bf16[1152,256]{1,0:T(8,128)(2,1)} collective-permute-done((bf16[1152,256]{1,0:T(8,128)(2,1)S(1)}, bf16[1152,256]{1,0:T(8,128)(2,1)}, u32[]{:S(2)}, u32[]{:S(2)}) %collective-permute-start.10) | collective-permute-done | bytes 589856 | tf_op jit(solution)/shard_map/ppermute | solution.py:431
  99.4 1.3 collective-permute-start.11
  101.4 2.0 select_bitcast_fusion.1
  103.3 40.6 %collective-permute-done.11 = bf16[1152,256]{1,0:T(8,128)(2,1)S(1)} collective-permute-done((bf16[1152,256]{1,0:T(8,128)(2,1)}, bf16[1152,256]{1,0:T(8,128)(2,1)S(1)}, u32[]{:S(2)}, u32[]{:S(2)}) %collective-permute-start.11) | collective-permute-done | bytes 589856 | tf_op jit(solution)/shard_map/ppermute | solution.py:431
  144.2 1.5 pad_maximum_fusion.1
  146.0 6.4 %forward_block.4 = (bf16[512,256]{1,0:T(8,128)(2,1)S(1)}, f32[2,512,128]{2,1,0:T(8,128)}) custom-call(s32[3]{0:T(128)S(1)} %pad_add_fusion.scal, bf16[512,256]{1,0:T(8,128)(2,1)} %get-tuple-element.89.refs_0_, bf16[512,256]{1,0:T(8,128)(2,1)} %get-tuple-element.88.refs_1_, bf16[512,256]{1,0:T(8,128)(2,1)} %get-tuple-element.87.refs_2_, ...), custom_call_target="tpu_custom_call" | custom-call | flops 2415919104 | bytes 4718592 | tf_op jit(solution)/shard_map/forward_block/pallas_call | solution.py:233
  152.4 2.8 collective-permute-start.7
  161.0 1.5 collective-permute-done.7.refs_3_
  162.5 5.2 %collective-permute-done.6.refs_2_ = bf16[512,256]{1,0:T(8,128)(2,1)S(1)} collective-permute-done((bf16[512,256]{1,0:T(8,128)(2,1)S(1)}, bf16[512,256]{1,0:T(8,128)(2,1)S(1)}, u32[]{:S(2)}, u32[]{:S(2)}) %collective-permute-start.6) | collective-permute-done | bytes 262176 | tf_op jit(solution)/shard_map/ppermute | solution.py:377
  168.6 6.5 %forward_block.5 = (bf16[512,256]{1,0:T(8,128)(2,1)S(1)}, f32[2,512,128]{2,1,0:T(8,128)}) custom-call(s32[3]{0:T(128)S(1)} %pad_add_fusion.scal, bf16[512,256]{1,0:T(8,128)(2,1)} %copy-done, bf16[512,256]{1,0:T(8,128)(2,1)} %copy-done.12, bf16[512,256]{1,0:T(8,128)(2,1)} %copy-done.11, bf16[512,256]{1,0:T(8,128)(2,1)} %copy-done.10, ...), custom_call_target="tpu_custom_call" | custom-call | flops 2415919104 | bytes 4718592 | tf_op jit(solution)/shard_map/forward_block/pallas_call | solution.py:233
  175.2 1.9 collective-permute-start.15
  177.1 1.3 collective-permute-start.14
  178.7 6.6 %collective-permute-done.15.refs_3_ = bf16[512,256]{1,0:T(8,128)(2,1)S(1)} collective-permute-done((bf16[512,256]{1,0:T(8,128)(2,1)S(1)}, bf16[512,256]{1,0:T(8,128)(2,1)S(1)}, u32[]{:S(2)}, u32[]{:S(2)}) %collective-permute-start.15) | collective-permute-done | bytes 262176 | tf_op jit(solution)/shard_map/ppermute | solution.py:377
  185.3 4.7 %collective-permute-done.14.refs_2_ = bf16[512,256]{1,0:T(8,128)(2,1)S(1)} collective-permute-done((bf16[512,256]{1,0:T(8,128)(2,1)S(1)}, bf16[512,256]{1,0:T(8,128)(2,1)S(1)}, u32[]{:S(2)}, u32[]{:S(2)}) %collective-permute-start.14) | collective-permute-done | bytes 262176 | tf_op jit(solution)/shard_map/ppermute | solution.py:377
  190.9 8.3 %all-gather.9.cloned.1.call-done.refs_6_.refs_5_.refs_8_.refs_7_ = bf16[9216,256]{1,0:T(8,128)(2,1)} async-done(((bf16[1152,256]{1,0:T(8,128)(2,1)}), bf16[9216,256]{1,0:T(8,128)(2,1)}) %all-gather.9.cloned.1.call-update) | async-done | bytes 4718608 | tf_op jit(solution)/shard_map/all_gather | solution.py:441
  199.2 6.5 %forward_block.6 = (bf16[512,256]{1,0:T(8,128)(2,1)S(1)}, f32[2,512,128]{2,1,0:T(8,128)}) custom-call(s32[3]{0:T(128)S(1)} %pad_add_fusion.scal, bf16[512,256]{1,0:T(8,128)(2,1)} %copy-done.2, bf16[512,256]{1,0:T(8,128)(2,1)} %copy-done.15, bf16[512,256]{1,0:T(8,128)(2,1)} %copy-done.14, bf16[512,256]{1,0:T(8,128)(2,1)} %copy-done.13, ...), custom_call_target="tpu_custom_call" | custom-call | flops 2415919104 | bytes 4718592 | tf_op jit(solution)/shard_map/forward_block/pallas_call | solution.py:233
  205.7 2.4 collective-permute-start.18
  209.2 6.6 %collective-permute-done.18.refs_3_ = bf16[512,256]{1,0:T(8,128)(2,1)S(1)} collective-permute-done((bf16[512,256]{1,0:T(8,128)(2,1)S(1)}, bf16[512,256]{1,0:T(8,128)(2,1)S(1)}, u32[]{:S(2)}, u32[]{:S(2)}) %collective-permute-start.18) | collective-permute-done | bytes 262176 | tf_op jit(solution)/shard_map/ppermute | solution.py:377
  215.8 4.9 %collective-permute-done.17.refs_2_ = bf16[512,256]{1,0:T(8,128)(2,1)S(1)} collective-permute-done((bf16[512,256]{1,0:T(8,128)(2,1)S(1)}, bf16[512,256]{1,0:T(8,128)(2,1)S(1)}, u32[]{:S(2)}, u32[]{:S(2)}) %collective-permute-start.17) | collective-permute-done | bytes 262176 | tf_op jit(solution)/shard_map/ppermute | solution.py:377
  220.8 2.7 maximum_select_fusion
  223.7 6.3 %forward_block.7 = (bf16[512,256]{1,0:T(8,128)(2,1)}, f32[2,512,128]{2,1,0:T(8,128)}, f32[4,1024]{1,0:T(4,128)S(1)}) custom-call(s32[3]{0:T(128)S(1)} %pad_add_fusion.scal, bf16[512,256]{1,0:T(8,128)(2,1)S(1)} %get-tuple-element.41.refs_0_, bf16[512,256]{1,0:T(8,128)(2,1)S(1)} %collective-permute-done.16.refs_1_, ...), custom_call_target="tpu_custom_call" | custom-call | flops 2415919104 | bytes 4718592 | tf_op jit(solution)/shard_map/forward_block/pallas_call | solution.py:233
  230.0 1.8 collective-permute-start.21
  236.8 6.9 %backward_block.4 = (bf16[512,256]{1,0:T(8,128)(2,1)S(1)}, f32[512,256]{1,0:T(8,128)S(1)}, bf16[512,256]{1,0:T(8,128)(2,1)S(1)}, bf16[512,256]{1,0:T(8,128)(2,1)S(1)}, bf16[512,256]{1,0:T(8,128)(2,1)S(1)}) custom-call(s32[3]{0:T(128)S(1)} %pad_add_fusion.scal, f32[4,1024]{1,0:T(4,128)S(1)} %get-tuple-element.42.refs_0_, ...), custom_call_target="tpu_custom_call" | custom-call | flops 2429026304 | bytes 5767168 | tf_op jit(solution)/shard_map/backward_block/pallas_call | solution.py:288
  244.3 1.4 collective-permute-start.23
  245.7 1.5 collective-permute-start.24
  247.2 5.8 %collective-permute-done.22.refs_1_ = bf16[512,256]{1,0:T(8,128)(2,1)S(1)} collective-permute-done((bf16[512,256]{1,0:T(8,128)(2,1)S(1)}, bf16[512,256]{1,0:T(8,128)(2,1)S(1)}, u32[]{:S(2)}, u32[]{:S(2)}) %collective-permute-start.22) | collective-permute-done | bytes 262176 | tf_op jit(solution)/shard_map/ppermute | solution.py:377
  253.0 3.5 collective-permute-done.23.refs_2_
  256.5 5.6 %backward_block.5 = (bf16[512,256]{1,0:T(8,128)(2,1)S(1)}, f32[512,256]{1,0:T(8,128)S(1)}, bf16[512,256]{1,0:T(8,128)(2,1)S(1)}, bf16[512,256]{1,0:T(8,128)(2,1)S(1)}, bf16[512,256]{1,0:T(8,128)(2,1)S(1)}) custom-call(s32[3]{0:T(128)S(1)} %pad_add_fusion.scal, f32[512,256]{1,0:T(8,128)S(1)} %get-tuple-element.44.refs_0_, ...), custom_call_target="tpu_custom_call" | custom-call | flops 2429026304 | bytes 5767168 | tf_op jit(solution)/shard_map/backward_block/pallas_call | solution.py:288
  262.1 1.5 collective-permute-start.25
  264.2 1.5 collective-permute-start.27
  265.7 4.8 %collective-permute-done.25.refs_1_ = bf16[512,256]{1,0:T(8,128)(2,1)S(1)} collective-permute-done((bf16[512,256]{1,0:T(8,128)(2,1)S(1)}, bf16[512,256]{1,0:T(8,128)(2,1)S(1)}, u32[]{:S(2)}, u32[]{:S(2)}) %collective-permute-start.25) | collective-permute-done | bytes 262176 | tf_op jit(solution)/shard_map/ppermute | solution.py:377
  270.5 4.3 %collective-permute-done.26.refs_2_ = bf16[512,256]{1,0:T(8,128)(2,1)S(1)} collective-permute-done((bf16[512,256]{1,0:T(8,128)(2,1)S(1)}, bf16[512,256]{1,0:T(8,128)(2,1)S(1)}, u32[]{:S(2)}, u32[]{:S(2)}) %collective-permute-start.26) | collective-permute-done | bytes 262176 | tf_op jit(solution)/shard_map/ppermute | solution.py:377
  274.8 5.6 %backward_block.6 = (bf16[512,256]{1,0:T(8,128)(2,1)S(1)}, f32[512,256]{1,0:T(8,128)S(1)}, bf16[512,256]{1,0:T(8,128)(2,1)S(1)}, bf16[512,256]{1,0:T(8,128)(2,1)S(1)}, bf16[512,256]{1,0:T(8,128)(2,1)S(1)}) custom-call(s32[3]{0:T(128)S(1)} %pad_add_fusion.scal, f32[512,256]{1,0:T(8,128)S(1)} %get-tuple-element.49.refs_0_, ...), custom_call_target="tpu_custom_call" | custom-call | flops 2429026304 | bytes 5767168 | tf_op jit(solution)/shard_map/backward_block/pallas_call | solution.py:288
  280.9 1.5 collective-permute-start.29
  282.4 1.6 collective-permute-start.30
  284.0 3.9 collective-permute-done.28.refs_1_
  287.8 3.1 collective-permute-done.29.refs_2_
  291.0 1.6 backward_block.7
  292.8 1.6 collective-permute-start.33
  294.3 1.5 collective-permute-start.32
  296.3 3.9 collective-permute-done.33
  300.2 2.7 collective-permute-done.32
  304.7 6.9 %dynamic-slice_bitcast_fusion.3 = (bf16[8,4,4,32,256]{4,3,2,1,0:T(8,128)(2,1)S(1)}, bf16[8,4,4,32,256]{4,3,2,1,0:T(8,128)(2,1)}, bf16[8,4,4,32,256]{4,3,2,1,0:T(8,128)(2,1)}, bf16[8,4,4,32,256]{4,3,2,1,0:T(8,128)(2,1)}) fusion(bf16[8,4,4,4,32,256]{5,4,3,2,1,0:T(8,128)(2,1)} %bitcast.116, s32[]{:T(128)S(6)} %select_n.231, s32[]{:T(128)S(6)} %select_n.233, ...), kind=kLoop, calls=%fused_computation.22 | loop fusion | bytes 16777232 | tf_op jit(solution)/shard_map/jit(dynamic_index_in_dim)/squeeze | solution.py:476
  311.6 17.7 %select_maximum_fusion = bf16[8,6,6,32,1024]{4,3,2,1,0:T(8,128)(2,1)} fusion(bf16[8,4,4,32,256]{4,3,2,1,0:T(8,128)(2,1)} %get-tuple-element.70, bf16[8,4,4,32,256]{4,3,2,1,0:T(8,128)(2,1)} %get-tuple-element.68, bf16[8,4,4,32,256]{4,3,2,1,0:T(8,128)(2,1)} %get-tuple-element.69, bf16[8,4,4,32,256]{4,3,2,1,0:T(8,128)(2,1)S(1)} %get-tuple-element.67), kind=kLoop, calls=%fused_computation.7 | loop fusion | flops 217055232 | bytes 27262976 | tf_op jit(solution)/shard_map/concatenate | solution.py:474
  329.2 12.5 %constant_dynamic-slice_fusion.1 = (bf16[8,4,4,32,1024]{4,3,2,1,0:T(8,128)(2,1)}, bf16[8,4,4,32,1024]{4,3,2,1,0:T(8,128)(2,1)}) fusion(bf16[8,6,6,32,1024]{4,3,2,1,0:T(8,128)(2,1)} %select_maximum_fusion, s32[]{:T(128)S(6)} %select_n.241, s32[]{:T(128)S(6)} %select_n.243, s32[]{:T(128)S(6)} %select_n.237, s32[]{:T(128)S(6)} %select_n.239), kind=kLoop, calls=%fused_computation.57 | loop fusion | bytes 33554448 | tf_op jit(solution)/shard_map/dynamic_slice | solution.py:486
  341.7 11.6 %copy.32 = bf16[4096,1024]{0,1:T(8,128)(2,1)} copy(bf16[4096,1024]{1,0:T(8,128)(2,1)} %bitcast.115) | data formatting | bytes 16777216 | tf_op jit(solution)/shard_map/reshape | solution.py:490
  353.3 11.8 %copy.31 = bf16[4096,1024]{0,1:T(8,128)(2,1)} copy(bf16[4096,1024]{1,0:T(8,128)(2,1)} %bitcast.114) | data formatting | bytes 16777216 | tf_op jit(solution)/shard_map/reshape | solution.py:490
  365.2 11.5 %fusion.7.cols = bf16[1152,4096]{1,0:T(8,128)(2,1)} fusion(s32[]{:T(128)S(6)} %select_n.245, bf16[4096,1024]{0,1:T(8,128)(2,1)} %copy.31, bf16[4096,1024]{0,1:T(8,128)(2,1)} %copy.32), kind=kLoop, calls=%fused_computation.16 | loop fusion | flops 18874368 | bytes 26214404 | tf_op jit(solution)/shard_map/transpose | solution.py:495
  376.6 9.2 %all-gather.13.cloned.1.call-done.raw = bf16[4096,1024]{1,0:T(8,128)(2,1)} async-done(((bf16[512,1024]{1,0:T(8,128)(2,1)}), bf16[4096,1024]{1,0:T(8,128)(2,1)}) %all-gather.13.cloned.1.call-update) | async-done | bytes 8388624 | tf_op jit(solution)/shard_map/all_gather | solution.py:494
  385.9 22.0 %update.1 = (f32[1152,1024]{1,0:T(8,128)}, f32[1152,1024]{1,0:T(8,128)}, f32[1152,1024]{1,0:T(8,128)}) custom-call(bf16[1152,4096]{1,0:T(8,128)(2,1)} %fusion.7.cols, bf16[4096,1024]{1,0:T(8,128)(2,1)} %all-gather.13.cloned.1.call-done.raw, f32[1152,1024]{1,0:T(8,128)} %bitcast.125, f32[1152,1024]{1,0:T(8,128)} %bitcast.138, f32[1152,1024]{1,0:T(8,128)} %bitcast.139), custom_call_target="tpu_custom_call" | custom-call | flops 9663676416 | bytes 36700160 | tf_op jit(solution)/shard_map/update/pallas_call | solution.py:335
  (97 shorter events, 22.8 us)
Async XLA Ops:
  7.2 67.8 %all-gather.15.cloned.1.call-start = ((), (), s32[]{:S(2)}) async-start(), calls=%async_computation.4 | async-start | bytes 5308416 | tf_op jit(solution)/shard_map/all_gather | solution.py:441
  11.1 132.8 %all-gather.7.cloned.1.call-start = ((), (), s32[]{:S(2)}) async-start(), calls=%async_computation | async-start | bytes 5308416 | tf_op jit(solution)/shard_map/all_gather | solution.py:441
  11.2 17.4 %collective-permute-start = (bf16[1152,256]{1,0:T(8,128)(2,1)}, bf16[1152,256]{1,0:T(8,128)(2,1)S(1)}, u32[]{:S(2)}, u32[]{:S(2)}) collective-permute-start(bf16[1152,256]{1,0:T(8,128)(2,1)} %get-tuple-element.71), channel_id=1, source_target_pairs={{0,8},{8,0},{16,24},{24,16},{1,9},{9,1},{17,25},{25,17},{2,10},{10... | collective-permute-start | bytes 1769480 | tf_op jit(solution)/shard_map/ppermute | solution.py:377
  14.2 27.7 %collective-permute-start.1 = (bf16[1152,256]{1,0:T(8,128)(2,1)}, bf16[1152,256]{1,0:T(8,128)(2,1)}, u32[]{:S(2)}, u32[]{:S(2)}) collective-permute-start(bf16[1152,256]{1,0:T(8,128)(2,1)} %get-tuple-element.72), channel_id=1, source_target_pairs={{0,16},{8,24},{16,0},{24,8},{1,17},{9,25},{17,1},{25,9},{2,18},{10... | collective-permute-start | bytes 1769480 | tf_op jit(solution)/shard_map/ppermute | solution.py:377
  15.7 26.2 %collective-permute-start.2 = (bf16[1152,256]{1,0:T(8,128)(2,1)}, bf16[1152,256]{1,0:T(8,128)(2,1)}, u32[]{:S(2)}, u32[]{:S(2)}) collective-permute-start(bf16[1152,256]{1,0:T(8,128)(2,1)} %get-tuple-element.74), channel_id=1, source_target_pairs={{0,24},{8,16},{16,8},{24,0},{1,25},{9,17},{17,9},{25,1},{2,26},{10... | collective-permute-start | bytes 1769480 | tf_op jit(solution)/shard_map/ppermute | solution.py:377
  15.7 26.2 %copy-start.4 = (bf16[1,1152,256]{2,1,0:T(8,128)(2,1)S(1)}, bf16[1,1152,256]{2,1,0:T(8,128)(2,1)}, u32[]{:S(2)}) copy-start(bf16[1,1152,256]{2,1,0:T(8,128)(2,1)} %get-tuple-element.73) | copy-start | bytes 1769476
  44.6 1.3 copy-start.5
  44.6 30.4 %collective-permute-start.4 = (bf16[1152,256]{1,0:T(8,128)(2,1)S(1)}, bf16[1152,256]{1,0:T(8,128)(2,1)S(1)}, u32[]{:S(2)}, u32[]{:S(2)}) collective-permute-start(bf16[1152,256]{1,0:T(8,128)(2,1)S(1)} %bitcast.119), channel_id=1, source_target_pairs={{2,0},{3,1},{4,2},{5,3},{6,4},{7,5},{10,8},{11,9},{12,10},{13,11},... | collective-permute-start | bytes 1769480 | tf_op jit(solution)/shard_map/ppermute | solution.py:431
  45.9 29.1 %collective-permute-start.3 = (bf16[1152,256]{1,0:T(8,128)(2,1)S(1)}, bf16[1152,256]{1,0:T(8,128)(2,1)S(1)}, u32[]{:S(2)}, u32[]{:S(2)}) collective-permute-start(bf16[1152,256]{1,0:T(8,128)(2,1)S(1)} %bitcast.120), channel_id=1, source_target_pairs={{0,2},{1,3},{2,4},{3,5},{4,6},{5,7},{8,10},{9,11},{10,12},{11,13},... | collective-permute-start | bytes 1769480 | tf_op jit(solution)/shard_map/ppermute | solution.py:430
  75.0 124.2 %all-gather.9.cloned.1.call-start = ((), (), s32[]{:S(2)}) async-start(), calls=%async_computation.1 | async-start | bytes 5308416 | tf_op jit(solution)/shard_map/all_gather | solution.py:441
  75.1 24.3 %collective-permute-start.10 = (bf16[1152,256]{1,0:T(8,128)(2,1)S(1)}, bf16[1152,256]{1,0:T(8,128)(2,1)}, u32[]{:S(2)}, u32[]{:S(2)}) collective-permute-start(bf16[1152,256]{1,0:T(8,128)(2,1)S(1)} %collective-permute-done.4), channel_id=1, source_target_pairs={{2,0},{3,1},{4,2},{5,3},{10,8},{11,9},{12,10},{13,11},{18,16},{19,... | collective-permute-start | bytes 1769480 | tf_op jit(solution)/shard_map/ppermute | solution.py:431
  76.4 24.3 %collective-permute-start.8 = (bf16[1152,256]{1,0:T(8,128)(2,1)S(1)}, bf16[1152,256]{1,0:T(8,128)(2,1)}, u32[]{:S(2)}, u32[]{:S(2)}) collective-permute-start(bf16[1152,256]{1,0:T(8,128)(2,1)S(1)} %collective-permute-done.3), channel_id=1, source_target_pairs={{2,4},{3,5},{4,6},{5,7},{10,12},{11,13},{12,14},{13,15},{18,20},{1... | collective-permute-start | bytes 1769480 | tf_op jit(solution)/shard_map/ppermute | solution.py:430
  99.4 44.6 %collective-permute-start.11 = (bf16[1152,256]{1,0:T(8,128)(2,1)}, bf16[1152,256]{1,0:T(8,128)(2,1)S(1)}, u32[]{:S(2)}, u32[]{:S(2)}) collective-permute-start(bf16[1152,256]{1,0:T(8,128)(2,1)} %collective-permute-done.10), channel_id=1, source_target_pairs={{2,0},{3,1},{10,8},{11,9},{18,16},{19,17},{26,24},{27,25}} | collective-permute-start | bytes 1769480 | tf_op jit(solution)/shard_map/ppermute | solution.py:431
  100.7 43.3 %collective-permute-start.9 = (bf16[1152,256]{1,0:T(8,128)(2,1)}, bf16[1152,256]{1,0:T(8,128)(2,1)S(1)}, u32[]{:S(2)}, u32[]{:S(2)}) collective-permute-start(bf16[1152,256]{1,0:T(8,128)(2,1)} %collective-permute-done.8), channel_id=1, source_target_pairs={{4,6},{5,7},{12,14},{13,15},{20,22},{21,23},{28,30},{29,31}} | collective-permute-start | bytes 1769480 | tf_op jit(solution)/shard_map/ppermute | solution.py:430
  144.0 160.7 %all-gather.11.cloned.1.call-start = ((), (), s32[]{:S(2)}) async-start(), calls=%async_computation.2 | async-start | bytes 9437184 | tf_op jit(solution)/shard_map/all_gather | solution.py:454
  145.7 10.3 %collective-permute-start.12 = (bf16[4,1152,256]{2,1,0:T(8,128)(2,1)S(1)}, bf16[4,1152,256]{2,1,0:T(8,128)(2,1)}, u32[]{:S(2)}, u32[]{:S(2)}) collective-permute-start(bf16[4,1152,256]{2,1,0:T(8,128)(2,1)S(1)} %pad_maximum_fusion.1), channel_id=1, source_target_pairs={{0,1},{1,0},{2,3},{3,2},{4,5},{5,4},{6,7},{7,6},{8,9},{9,8},{10,11... | collective-permute-start | bytes 7077896 | tf_op jit(solution)/shard_map/ppermute | solution.py:318
  152.4 4.1 copy-start
  152.4 10.1 %collective-permute-start.7 = (bf16[512,256]{1,0:T(8,128)(2,1)S(1)}, bf16[512,256]{1,0:T(8,128)(2,1)S(1)}, u32[]{:S(2)}, u32[]{:S(2)}) collective-permute-start(bf16[512,256]{1,0:T(8,128)(2,1)S(1)} %get-tuple-element.36.refs_0_), channel_id=1, source_target_pairs={{0,24},{8,16},{16,8},{24,0},{1,25},{9,17},{17,9},{25,1},{2,26},{10... | collective-permute-start | bytes 786440 | tf_op jit(solution)/shard_map/ppermute | solution.py:377
  155.3 12.5 %collective-permute-start.6 = (bf16[512,256]{1,0:T(8,128)(2,1)S(1)}, bf16[512,256]{1,0:T(8,128)(2,1)S(1)}, u32[]{:S(2)}, u32[]{:S(2)}) collective-permute-start(bf16[512,256]{1,0:T(8,128)(2,1)S(1)} %get-tuple-element.36.refs_0_), channel_id=1, source_target_pairs={{0,16},{8,24},{16,0},{24,8},{1,17},{9,25},{17,1},{25,9},{2,18},{10... | collective-permute-start | bytes 786440 | tf_op jit(solution)/shard_map/ppermute | solution.py:377
  155.5 12.3 %collective-permute-start.5 = (bf16[512,256]{1,0:T(8,128)(2,1)S(1)}, bf16[512,256]{1,0:T(8,128)(2,1)S(1)}, u32[]{:S(2)}, u32[]{:S(2)}) collective-permute-start(bf16[512,256]{1,0:T(8,128)(2,1)S(1)} %get-tuple-element.36.refs_0_), channel_id=1, source_target_pairs={{0,8},{8,0},{16,24},{24,16},{1,9},{9,1},{17,25},{25,17},{2,10},{10... | collective-permute-start | bytes 786440 | tf_op jit(solution)/shard_map/ppermute | solution.py:377
  161.0 6.9 %copy-start.3 = (bf16[8,1152,256]{2,1,0:T(8,128)(2,1)}, bf16[8,1152,256]{2,1,0:T(8,128)(2,1)S(1)}, u32[]{:S(2)}) copy-start(bf16[8,1152,256]{2,1,0:T(8,128)(2,1)S(1)} %slice_dynamic-update-slice_fusion) | copy-start | bytes 14155780
  162.5 5.3 %copy-start.10 = (bf16[512,256]{1,0:T(8,128)(2,1)}, bf16[512,256]{1,0:T(8,128)(2,1)S(1)}, u32[]{:S(2)}) copy-start(bf16[512,256]{1,0:T(8,128)(2,1)S(1)} %collective-permute-done.7.refs_3_) | copy-start | bytes 786436
  167.7 0.7 copy-start.11
  167.8 0.7 copy-start.12
  175.1 24.1 %copy-start.2 = (bf16[512,256]{1,0:T(8,128)(2,1)}, bf16[512,256]{1,0:T(8,128)(2,1)S(1)}, u32[]{:S(2)}) copy-start(bf16[512,256]{1,0:T(8,128)(2,1)S(1)} %get-tuple-element.39.refs_0_) | copy-start | bytes 786436
  175.1 45.6 %copy-start.1 = (bf16[512,256]{1,0:T(8,128)(2,1)S(1)}, bf16[512,256]{1,0:T(8,128)(2,1)}, u32[]{:S(2)}) copy-start(bf16[512,256]{1,0:T(8,128)(2,1)} %copy-done) | copy-start | bytes 786436
  175.1 45.6 %copy-start.6 = (bf16[512,256]{1,0:T(8,128)(2,1)S(1)}, bf16[512,256]{1,0:T(8,128)(2,1)}, u32[]{:S(2)}) copy-start(bf16[512,256]{1,0:T(8,128)(2,1)} %get-tuple-element.86.refs_3_) | copy-start | bytes 786436
  175.1 45.6 %copy-start.7 = (bf16[512,256]{1,0:T(8,128)(2,1)S(1)}, bf16[512,256]{1,0:T(8,128)(2,1)}, u32[]{:S(2)}) copy-start(bf16[512,256]{1,0:T(8,128)(2,1)} %get-tuple-element.87.refs_2_) | copy-start | bytes 786436
  175.1 45.6 %copy-start.8 = (bf16[512,256]{1,0:T(8,128)(2,1)S(1)}, bf16[512,256]{1,0:T(8,128)(2,1)}, u32[]{:S(2)}) copy-start(bf16[512,256]{1,0:T(8,128)(2,1)} %get-tuple-element.88.refs_1_) | copy-start | bytes 786436
  175.2 45.6 %copy-start.9 = (bf16[512,256]{1,0:T(8,128)(2,1)S(1)}, bf16[512,256]{1,0:T(8,128)(2,1)}, u32[]{:S(2)}) copy-start(bf16[512,256]{1,0:T(8,128)(2,1)} %get-tuple-element.89.refs_0_) | copy-start | bytes 786436
  175.2 10.2 %collective-permute-start.15 = (bf16[512,256]{1,0:T(8,128)(2,1)S(1)}, bf16[512,256]{1,0:T(8,128)(2,1)S(1)}, u32[]{:S(2)}, u32[]{:S(2)}) collective-permute-start(bf16[512,256]{1,0:T(8,128)(2,1)S(1)} %get-tuple-element.39.refs_0_), channel_id=1, source_target_pairs={{0,24},{8,16},{16,8},{24,0},{1,25},{9,17},{17,9},{25,1},{2,26},{10... | collective-permute-start | bytes 786440 | tf_op jit(solution)/shard_map/ppermute | solution.py:377
  177.1 13.0 %collective-permute-start.14 = (bf16[512,256]{1,0:T(8,128)(2,1)S(1)}, bf16[512,256]{1,0:T(8,128)(2,1)S(1)}, u32[]{:S(2)}, u32[]{:S(2)}) collective-permute-start(bf16[512,256]{1,0:T(8,128)(2,1)S(1)} %get-tuple-element.39.refs_0_), channel_id=1, source_target_pairs={{0,16},{8,24},{16,0},{24,8},{1,17},{9,25},{17,1},{25,9},{2,18},{10... | collective-permute-start | bytes 786440 | tf_op jit(solution)/shard_map/ppermute | solution.py:377
  178.4 11.7 %collective-permute-start.13 = (bf16[512,256]{1,0:T(8,128)(2,1)S(1)}, bf16[512,256]{1,0:T(8,128)(2,1)S(1)}, u32[]{:S(2)}, u32[]{:S(2)}) collective-permute-start(bf16[512,256]{1,0:T(8,128)(2,1)S(1)} %get-tuple-element.39.refs_0_), channel_id=1, source_target_pairs={{0,8},{8,0},{16,24},{24,16},{1,9},{9,1},{17,25},{25,17},{2,10},{10... | collective-permute-start | bytes 786440 | tf_op jit(solution)/shard_map/ppermute | solution.py:377
  185.3 13.9 %copy-start.13 = (bf16[512,256]{1,0:T(8,128)(2,1)}, bf16[512,256]{1,0:T(8,128)(2,1)S(1)}, u32[]{:S(2)}) copy-start(bf16[512,256]{1,0:T(8,128)(2,1)S(1)} %collective-permute-done.15.refs_3_) | copy-start | bytes 786436
  190.0 9.2 %copy-start.14 = (bf16[512,256]{1,0:T(8,128)(2,1)}, bf16[512,256]{1,0:T(8,128)(2,1)S(1)}, u32[]{:S(2)}) copy-start(bf16[512,256]{1,0:T(8,128)(2,1)S(1)} %collective-permute-done.14.refs_2_) | copy-start | bytes 786436
  190.1 0.7 copy-start.15
  205.7 10.2 %collective-permute-start.18 = (bf16[512,256]{1,0:T(8,128)(2,1)S(1)}, bf16[512,256]{1,0:T(8,128)(2,1)S(1)}, u32[]{:S(2)}, u32[]{:S(2)}) collective-permute-start(bf16[512,256]{1,0:T(8,128)(2,1)S(1)} %get-tuple-element.41.refs_0_), channel_id=1, source_target_pairs={{0,24},{8,16},{16,8},{24,0},{1,25},{9,17},{17,9},{25,1},{2,26},{10... | collective-permute-start | bytes 786440 | tf_op jit(solution)/shard_map/ppermute | solution.py:377
  208.1 12.6 %collective-permute-start.17 = (bf16[512,256]{1,0:T(8,128)(2,1)S(1)}, bf16[512,256]{1,0:T(8,128)(2,1)S(1)}, u32[]{:S(2)}, u32[]{:S(2)}) collective-permute-start(bf16[512,256]{1,0:T(8,128)(2,1)S(1)} %get-tuple-element.41.refs_0_), channel_id=1, source_target_pairs={{0,16},{8,24},{16,0},{24,8},{1,17},{9,25},{17,1},{25,9},{2,18},{10... | collective-permute-start | bytes 786440 | tf_op jit(solution)/shard_map/ppermute | solution.py:377
  208.7 12.1 %collective-permute-start.16 = (bf16[512,256]{1,0:T(8,128)(2,1)S(1)}, bf16[512,256]{1,0:T(8,128)(2,1)S(1)}, u32[]{:S(2)}, u32[]{:S(2)}) collective-permute-start(bf16[512,256]{1,0:T(8,128)(2,1)S(1)} %get-tuple-element.41.refs_0_), channel_id=1, source_target_pairs={{0,8},{8,0},{16,24},{24,16},{1,9},{9,1},{17,25},{25,17},{2,10},{10... | collective-permute-start | bytes 786440 | tf_op jit(solution)/shard_map/ppermute | solution.py:377
  223.5 10.1 %copy-start.16 = (s32[4]{0:T(128)S(1)}, s32[4]{0:T(128)}, u32[]{:S(2)}) copy-start(s32[4]{0:T(128)} %param.7) | copy-start | bytes 52
  223.5 162.4 %all-gather.13.cloned.1.call-start = ((), (), s32[]{:S(2)}) async-start(), calls=%async_computation.3 | async-start | bytes 9437184 | tf_op jit(solution)/shard_map/all_gather | solution.py:494
  230.0 4.7 %collective-permute-start.21 = (f32[4,1024]{1,0:T(4,128)S(1)}, f32[4,1024]{1,0:T(4,128)S(1)}, u32[]{:S(2)}, u32[]{:S(2)}) collective-permute-start(f32[4,1024]{1,0:T(4,128)S(1)} %get-tuple-element.42.refs_0_), channel_id=1, source_target_pairs={{0,24},{8,16},{16,8},{24,0},{1,25},{9,17},{17,9},{25,1},{2,26},{10... | collective-permute-start | bytes 49160 | tf_op jit(solution)/shard_map/ppermute | solution.py:377
  231.8 3.7 collective-permute-start.20
  233.0 3.7 collective-permute-start.19
  243.7 9.3 %collective-permute-start.22 = (bf16[512,256]{1,0:T(8,128)(2,1)S(1)}, bf16[512,256]{1,0:T(8,128)(2,1)S(1)}, u32[]{:S(2)}, u32[]{:S(2)}) collective-permute-start(bf16[512,256]{1,0:T(8,128)(2,1)S(1)} %get-tuple-element.45), channel_id=1, source_target_pairs={{0,8},{8,0},{16,24},{24,16},{1,9},{9,1},{17,25},{25,17},{2,10},{10... | collective-permute-start | bytes 786440 | tf_op jit(solution)/shard_map/ppermute | solution.py:377
  244.3 12.2 %collective-permute-start.23 = (bf16[512,256]{1,0:T(8,128)(2,1)S(1)}, bf16[512,256]{1,0:T(8,128)(2,1)S(1)}, u32[]{:S(2)}, u32[]{:S(2)}) collective-permute-start(bf16[512,256]{1,0:T(8,128)(2,1)S(1)} %get-tuple-element.46), channel_id=1, source_target_pairs={{0,16},{8,24},{16,0},{24,8},{1,17},{9,25},{17,1},{25,9},{2,18},{10... | collective-permute-start | bytes 786440 | tf_op jit(solution)/shard_map/ppermute | solution.py:377
  245.7 10.8 %collective-permute-start.24 = (bf16[512,256]{1,0:T(8,128)(2,1)S(1)}, bf16[512,256]{1,0:T(8,128)(2,1)S(1)}, u32[]{:S(2)}, u32[]{:S(2)}) collective-permute-start(bf16[512,256]{1,0:T(8,128)(2,1)S(1)} %get-tuple-element.47), channel_id=1, source_target_pairs={{0,24},{8,16},{16,8},{24,0},{1,25},{9,17},{17,9},{25,1},{2,26},{10... | collective-permute-start | bytes 786440 | tf_op jit(solution)/shard_map/ppermute | solution.py:377
  262.1 8.4 %collective-permute-start.25 = (bf16[512,256]{1,0:T(8,128)(2,1)S(1)}, bf16[512,256]{1,0:T(8,128)(2,1)S(1)}, u32[]{:S(2)}, u32[]{:S(2)}) collective-permute-start(bf16[512,256]{1,0:T(8,128)(2,1)S(1)} %get-tuple-element.50), channel_id=1, source_target_pairs={{0,8},{8,0},{16,24},{24,16},{1,9},{9,1},{17,25},{25,17},{2,10},{10... | collective-permute-start | bytes 786440 | tf_op jit(solution)/shard_map/ppermute | solution.py:377
  263.7 11.1 %collective-permute-start.26 = (bf16[512,256]{1,0:T(8,128)(2,1)S(1)}, bf16[512,256]{1,0:T(8,128)(2,1)S(1)}, u32[]{:S(2)}, u32[]{:S(2)}) collective-permute-start(bf16[512,256]{1,0:T(8,128)(2,1)S(1)} %get-tuple-element.51), channel_id=1, source_target_pairs={{0,16},{8,24},{16,0},{24,8},{1,17},{9,25},{17,1},{25,9},{2,18},{10... | collective-permute-start | bytes 786440 | tf_op jit(solution)/shard_map/ppermute | solution.py:377
  264.2 10.6 %collective-permute-start.27 = (bf16[512,256]{1,0:T(8,128)(2,1)S(1)}, bf16[512,256]{1,0:T(8,128)(2,1)S(1)}, u32[]{:S(2)}, u32[]{:S(2)}) collective-permute-start(bf16[512,256]{1,0:T(8,128)(2,1)S(1)} %get-tuple-element.52), channel_id=1, source_target_pairs={{0,24},{8,16},{16,8},{24,0},{1,25},{9,17},{17,9},{25,1},{2,26},{10... | collective-permute-start | bytes 786440 | tf_op jit(solution)/shard_map/ppermute | solution.py:377
  280.4 7.4 %collective-permute-start.28 = (bf16[512,256]{1,0:T(8,128)(2,1)S(1)}, bf16[512,256]{1,0:T(8,128)(2,1)S(1)}, u32[]{:S(2)}, u32[]{:S(2)}) collective-permute-start(bf16[512,256]{1,0:T(8,128)(2,1)S(1)} %get-tuple-element.55), channel_id=1, source_target_pairs={{0,8},{8,0},{16,24},{24,16},{1,9},{9,1},{17,25},{25,17},{2,10},{10... | collective-permute-start | bytes 786440 | tf_op jit(solution)/shard_map/ppermute | solution.py:377
  280.9 10.0 %collective-permute-start.29 = (bf16[512,256]{1,0:T(8,128)(2,1)S(1)}, bf16[512,256]{1,0:T(8,128)(2,1)S(1)}, u32[]{:S(2)}, u32[]{:S(2)}) collective-permute-start(bf16[512,256]{1,0:T(8,128)(2,1)S(1)} %get-tuple-element.56), channel_id=1, source_target_pairs={{0,16},{8,24},{16,0},{24,8},{1,17},{9,25},{17,1},{25,9},{2,18},{10... | collective-permute-start | bytes 786440 | tf_op jit(solution)/shard_map/ppermute | solution.py:377
  282.4 8.6 %collective-permute-start.30 = (bf16[512,256]{1,0:T(8,128)(2,1)S(1)}, bf16[512,256]{1,0:T(8,128)(2,1)S(1)}, u32[]{:S(2)}, u32[]{:S(2)}) collective-permute-start(bf16[512,256]{1,0:T(8,128)(2,1)S(1)} %get-tuple-element.57), channel_id=1, source_target_pairs={{0,24},{8,16},{16,8},{24,0},{1,25},{9,17},{17,9},{25,1},{2,26},{10... | collective-permute-start | bytes 786440 | tf_op jit(solution)/shard_map/ppermute | solution.py:377
  292.8 7.4 %collective-permute-start.33 = (bf16[512,256]{1,0:T(8,128)(2,1)S(1)}, bf16[512,256]{1,0:T(8,128)(2,1)S(1)}, u32[]{:S(2)}, u32[]{:S(2)}) collective-permute-start(bf16[512,256]{1,0:T(8,128)(2,1)S(1)} %get-tuple-element.83), channel_id=1, source_target_pairs={{0,24},{8,16},{16,8},{24,0},{1,25},{9,17},{17,9},{25,1},{2,26},{10... | collective-permute-start | bytes 786440 | tf_op jit(solution)/shard_map/ppermute | solution.py:377
  294.3 8.6 %collective-permute-start.32 = (bf16[512,256]{1,0:T(8,128)(2,1)S(1)}, bf16[512,256]{1,0:T(8,128)(2,1)S(1)}, u32[]{:S(2)}, u32[]{:S(2)}) collective-permute-start(bf16[512,256]{1,0:T(8,128)(2,1)S(1)} %get-tuple-element.84), channel_id=1, source_target_pairs={{0,16},{8,24},{16,0},{24,8},{1,17},{9,25},{17,1},{25,9},{2,18},{10... | collective-permute-start | bytes 786440 | tf_op jit(solution)/shard_map/ppermute | solution.py:377
  295.9 7.1 %collective-permute-start.31 = (bf16[512,256]{1,0:T(8,128)(2,1)S(1)}, bf16[512,256]{1,0:T(8,128)(2,1)S(1)}, u32[]{:S(2)}, u32[]{:S(2)}) collective-permute-start(bf16[512,256]{1,0:T(8,128)(2,1)S(1)} %get-tuple-element.85), channel_id=1, source_target_pairs={{0,8},{8,0},{16,24},{24,16},{1,9},{9,1},{17,25},{25,17},{2,10},{10... | collective-permute-start | bytes 786440 | tf_op jit(solution)/shard_map/ppermute | solution.py:377
Sparse Core Ops, SparseCore 0:
  11.2 60.1 all-gather.14
  75.1 67.2 all-gather.6
  144.7 54.4 all-gather.8
  223.6 80.1 all-gather.10
  305.2 80.5 all-gather.12

commit v7 on v6

--- a/solution.py
+++ b/solution.py
@@ -415,7 +415,9 @@
         if b < sections - 1:
             out = results[b][0]
             inputs.append([out] + exchange([out] * (sections - 1)))
-            own_inputs = jnp.where(s == b + 1, jnp.stack(inputs[b + 1]), own_inputs)
+            for k in [0] + list(range(sections - 1, 0, -1)):
+                value = jnp.where(s == b + 1, inputs[b + 1][k], own_inputs[k])
+                own_inputs = lax.dynamic_update_index_in_dim(own_inputs, value, k, 0)
 
     def piece_of(slot):
         if slot == 0:

time: 416 us -> 418 us (level)
  waiting for transfers between devices: 189 us -> 183 us
  local copies, waits for them, and re-layouts: 61.6 us -> 66.1 us
    dynamic_update_slice x8, local copies, waits for them, and re-layouts: 4.62 us -> 8.93 us  [lay_out(): whole = lax.dynamic_update_index_in_dim(whole, pieces_held[j], spot, 0)]
    ppermute x27, waiting for transfers between devices: 84.2 us -> 80 us  [exchange(): lax.ppermute(values[k], 'section', [(i, i ^ k + 1) for i in range(section...]
  transfers between devices with their start and end apart: 39 -> 39, of which waited for: 28 -> 23; matrix products, arithmetic and copies ran while one was open for 22% -> 24% of each run, Pallas kernels for 9% -> 9%
where the time goes in v7:
time: 418 us; the launch traced here: 415 us
  waiting for transfers between devices  183 us (44%)
  Pallas kernels  67.5 us (16%)
  local copies, waits for them, and re-layouts  66.1 us (16%)
  starting transfers between devices  44.8 us (11%)
  other arithmetic  39.9 us (10%)
  between operations  14.5 us (3%)
    ppermute x3, waiting for transfers between devices, shards(): down = lax.ppermute(down, 'dp', hops(step, -1, ring))  87.3 us
    ppermute x27, waiting for transfers between devices, exchange(): lax.ppermute(values[k], 'section', [(i, i ^ k + 1) for i in range(section...  80 us
    ppermute x27, starting transfers between devices, exchange(): lax.ppermute(values[k], 'section', [(i, i ^ k + 1) for i in range(section...  33.5 us
    pallas_call x4, Pallas kernels, run_forward(): pl.pallas_call(functools.partial(forward_kernel, dims, block), out_shape=...  25.7 us
    reshape x2, local copies, waits for them, and re-layouts, shards(): shifted.append(lax.dynamic_slice(fields, (0, offset // 3, offset % 3, 0,...  23.4 us
    pallas_call x1, Pallas kernels, run_update(): pl.pallas_call(update_kernel, grid=(channels // tile,), out_shape=[jax.Sh...  22 us
    pallas_call x4, Pallas kernels, run_backward(): pl.pallas_call(functools.partial(backward_kernel, dims, block, classes),...  19.7 us
    concatenate x1, other arithmetic, shards(): jnp.concatenate([lax.dynamic_index_in_dim(x_all, s ^ j, 1, keepdims=False...  17.6 us
  transfers between devices with their start and end apart: 39, of which 23 were waited for; matrix products, arithmetic and copies ran while one was open for 24% of the time, Pallas kernels for 9%

profile of v7, /device:TPU:0, one launch (start us, length us, event | category | flops | bytes accessed | tf_op | source)
XLA Modules:
  0.0 415.4 jit_solution(16529788614770501599)
XLA Ops:
  7.2 3.8 fusion.8
  11.2 3.0 collective-permute-start
  14.2 1.5 collective-permute-start.1
  15.7 1.3 constant_dynamic-slice_fusion.3
  17.1 1.3 copy.34
  18.4 1.8 copy.25
  20.2 1.4 pad.8.refs_6_.refs_5_
  22.5 6.1 %collective-permute-done = bf16[1152,256]{1,0:T(8,128)(2,1)} collective-permute-done((bf16[1152,256]{1,0:T(8,128)(2,1)}, bf16[1152,256]{1,0:T(8,128)(2,1)}, u32[]{:S(2)}, u32[]{:S(2)}) %collective-permute-start) | collective-permute-done | bytes 589856 | tf_op jit(solution)/shard_map/ppermute | solution.py:377
  28.6 13.3 %collective-permute-done.1 = bf16[1152,256]{1,0:T(8,128)(2,1)} collective-permute-done((bf16[1152,256]{1,0:T(8,128)(2,1)}, bf16[1152,256]{1,0:T(8,128)(2,1)}, u32[]{:S(2)}, u32[]{:S(2)}) %collective-permute-start.1) | collective-permute-done | bytes 589856 | tf_op jit(solution)/shard_map/ppermute | solution.py:377
  41.9 1.7 pad_maximum_fusion
  44.8 1.3 collective-permute-start.4
  46.1 4.6 %collective-permute-start.3 = (bf16[1152,256]{1,0:T(8,128)(2,1)S(1)}, bf16[1152,256]{1,0:T(8,128)(2,1)S(1)}, u32[]{:S(2)}, u32[]{:S(2)}) collective-permute-start(bf16[1152,256]{1,0:T(8,128)(2,1)S(1)} %bitcast.237), channel_id=1, source_target_pairs={{0,2},{1,3},{2,4},{3,5},{4,6},{5,7},{8,10},{9,11},{10,12},{11,13},... | collective-permute-start | bytes 1769480 | tf_op jit(solution)/shard_map/ppermute | solution.py:432
  50.6 24.4 %collective-permute-done.4 = bf16[1152,256]{1,0:T(8,128)(2,1)S(1)} collective-permute-done((bf16[1152,256]{1,0:T(8,128)(2,1)S(1)}, bf16[1152,256]{1,0:T(8,128)(2,1)S(1)}, u32[]{:S(2)}, u32[]{:S(2)}) %collective-permute-start.4) | collective-permute-done | bytes 589856 | tf_op jit(solution)/shard_map/ppermute | solution.py:433
  75.1 1.3 collective-permute-start.10
  76.4 1.5 collective-permute-start.8
  77.9 21.4 %collective-permute-done.10 = bf16[1152,256]{1,0:T(8,128)(2,1)} collective-permute-done((bf16[1152,256]{1,0:T(8,128)(2,1)S(1)}, bf16[1152,256]{1,0:T(8,128)(2,1)}, u32[]{:S(2)}, u32[]{:S(2)}) %collective-permute-start.10) | collective-permute-done | bytes 589856 | tf_op jit(solution)/shard_map/ppermute | solution.py:433
  99.3 1.3 collective-permute-start.11
  102.5 41.5 %collective-permute-done.11 = bf16[1152,256]{1,0:T(8,128)(2,1)} collective-permute-done((bf16[1152,256]{1,0:T(8,128)(2,1)}, bf16[1152,256]{1,0:T(8,128)(2,1)}, u32[]{:S(2)}, u32[]{:S(2)}) %collective-permute-start.11) | collective-permute-done | bytes 589856 | tf_op jit(solution)/shard_map/ppermute | solution.py:433
  146.3 1.7 pad_maximum_fusion.1
  148.4 1.2 pad_maximum_fusion.2
  149.7 6.5 %forward_block.4 = (bf16[512,256]{1,0:T(8,128)(2,1)S(1)}, f32[2,512,128]{2,1,0:T(8,128)}) custom-call(s32[3]{0:T(128)S(1)} %pad_add_fusion.scal, bf16[512,256]{1,0:T(8,128)(2,1)} %copy-done.5, bf16[512,256]{1,0:T(8,128)(2,1)} %get-tuple-element.89.refs_1_, bf16[512,256]{1,0:T(8,128)(2,1)} %get-tuple-element.88.refs_2_, ...), custom_call_target="tpu_custom_call" | custom-call | flops 2415919104 | bytes 4718592 | tf_op jit(solution)/shard_map/forward_block/pallas_call | solution.py:233
  156.2 1.6 collective-permute-start.7
  157.8 1.8 collective-permute-start.6
  169.1 2.7 collective-permute-done.6.refs_2_
  172.7 6.5 %forward_block.5 = (bf16[512,256]{1,0:T(8,128)(2,1)S(1)}, f32[2,512,128]{2,1,0:T(8,128)}) custom-call(s32[3]{0:T(128)S(1)} %pad_add_fusion.scal, bf16[512,256]{1,0:T(8,128)(2,1)} %copy-done, bf16[512,256]{1,0:T(8,128)(2,1)} %copy-done.7, bf16[512,256]{1,0:T(8,128)(2,1)} %copy-done.8, bf16[512,256]{1,0:T(8,128)(2,1)} %copy-done.9, ...), custom_call_target="tpu_custom_call" | custom-call | flops 2415919104 | bytes 4718592 | tf_op jit(solution)/shard_map/forward_block/pallas_call | solution.py:233
  179.2 1.4 collective-permute-start.15
  181.4 1.4 collective-permute-start.13
  183.3 10.7 %collective-permute-done.13.refs_3_ = bf16[512,256]{1,0:T(8,128)(2,1)S(1)} collective-permute-done((bf16[512,256]{1,0:T(8,128)(2,1)S(1)}, bf16[512,256]{1,0:T(8,128)(2,1)S(1)}, u32[]{:S(2)}, u32[]{:S(2)}) %collective-permute-start.13) | collective-permute-done | bytes 262176 | tf_op jit(solution)/shard_map/ppermute | solution.py:377
  194.2 6.9 %all-gather.9.cloned.1.call-done.refs_6_.refs_5_.refs_8_.refs_7_ = bf16[9216,256]{1,0:T(8,128)(2,1)} async-done(((bf16[1152,256]{1,0:T(8,128)(2,1)}), bf16[9216,256]{1,0:T(8,128)(2,1)}) %all-gather.9.cloned.1.call-update) | async-done | bytes 4718608 | tf_op jit(solution)/shard_map/all_gather | solution.py:443
  201.1 6.4 %forward_block.6 = (bf16[512,256]{1,0:T(8,128)(2,1)S(1)}, f32[2,512,128]{2,1,0:T(8,128)}) custom-call(s32[3]{0:T(128)S(1)} %pad_add_fusion.scal, bf16[512,256]{1,0:T(8,128)(2,1)} %copy-done.1, bf16[512,256]{1,0:T(8,128)(2,1)} %copy-done.10, bf16[512,256]{1,0:T(8,128)(2,1)} %copy-done.11, bf16[512,256]{1,0:T(8,128)(2,1)} %copy-done.12, ...), custom_call_target="tpu_custom_call" | custom-call | flops 2415919104 | bytes 4718592 | tf_op jit(solution)/shard_map/forward_block/pallas_call | solution.py:233
  207.5 2.4 collective-permute-start.16
  211.9 5.8 %collective-permute-done.16.refs_3_ = bf16[512,256]{1,0:T(8,128)(2,1)S(1)} collective-permute-done((bf16[512,256]{1,0:T(8,128)(2,1)S(1)}, bf16[512,256]{1,0:T(8,128)(2,1)S(1)}, u32[]{:S(2)}, u32[]{:S(2)}) %collective-permute-start.16) | collective-permute-done | bytes 262176 | tf_op jit(solution)/shard_map/ppermute | solution.py:377
  217.8 4.8 %collective-permute-done.17.refs_2_ = bf16[512,256]{1,0:T(8,128)(2,1)S(1)} collective-permute-done((bf16[512,256]{1,0:T(8,128)(2,1)S(1)}, bf16[512,256]{1,0:T(8,128)(2,1)S(1)}, u32[]{:S(2)}, u32[]{:S(2)}) %collective-permute-start.17) | collective-permute-done | bytes 262176 | tf_op jit(solution)/shard_map/ppermute | solution.py:377
  224.1 6.3 %forward_block.7 = (bf16[512,256]{1,0:T(8,128)(2,1)}, f32[2,512,128]{2,1,0:T(8,128)}, f32[4,1024]{1,0:T(4,128)S(1)}) custom-call(s32[3]{0:T(128)S(1)} %pad_add_fusion.scal, bf16[512,256]{1,0:T(8,128)(2,1)S(1)} %get-tuple-element.41.refs_0_, bf16[512,256]{1,0:T(8,128)(2,1)S(1)} %collective-permute-done.18.refs_1_, ...), custom_call_target="tpu_custom_call" | custom-call | flops 2415919104 | bytes 4718592 | tf_op jit(solution)/shard_map/forward_block/pallas_call | solution.py:233
  230.4 2.4 collective-permute-start.21
  235.1 1.5 collective-permute-done.20.refs_2_
  237.1 6.9 %backward_block.4 = (bf16[512,256]{1,0:T(8,128)(2,1)S(1)}, f32[512,256]{1,0:T(8,128)S(1)}, bf16[512,256]{1,0:T(8,128)(2,1)S(1)}, bf16[512,256]{1,0:T(8,128)(2,1)S(1)}, bf16[512,256]{1,0:T(8,128)(2,1)S(1)}) custom-call(s32[3]{0:T(128)S(1)} %pad_add_fusion.scal, f32[4,1024]{1,0:T(4,128)S(1)} %get-tuple-element.42.refs_0_, ...), custom_call_target="tpu_custom_call" | custom-call | flops 2429026304 | bytes 5767168 | tf_op jit(solution)/shard_map/backward_block/pallas_call | solution.py:288
  244.7 1.5 collective-permute-start.23
  246.2 1.5 collective-permute-start.24
  247.6 5.8 %collective-permute-done.22.refs_1_ = bf16[512,256]{1,0:T(8,128)(2,1)S(1)} collective-permute-done((bf16[512,256]{1,0:T(8,128)(2,1)S(1)}, bf16[512,256]{1,0:T(8,128)(2,1)S(1)}, u32[]{:S(2)}, u32[]{:S(2)}) %collective-permute-start.22) | collective-permute-done | bytes 262176 | tf_op jit(solution)/shard_map/ppermute | solution.py:377
  253.4 2.6 collective-permute-done.23.refs_2_
  256.0 1.6 collective-permute-done.24.refs_3_
  257.6 5.6 %backward_block.5 = (bf16[512,256]{1,0:T(8,128)(2,1)S(1)}, f32[512,256]{1,0:T(8,128)S(1)}, bf16[512,256]{1,0:T(8,128)(2,1)S(1)}, bf16[512,256]{1,0:T(8,128)(2,1)S(1)}, bf16[512,256]{1,0:T(8,128)(2,1)S(1)}) custom-call(s32[3]{0:T(128)S(1)} %pad_add_fusion.scal, f32[512,256]{1,0:T(8,128)S(1)} %get-tuple-element.44.refs_0_, ...), custom_call_target="tpu_custom_call" | custom-call | flops 2429026304 | bytes 5767168 | tf_op jit(solution)/shard_map/backward_block/pallas_call | solution.py:288
  264.0 1.5 collective-permute-start.26
  266.7 5.4 %collective-permute-done.25.refs_1_ = bf16[512,256]{1,0:T(8,128)(2,1)S(1)} collective-permute-done((bf16[512,256]{1,0:T(8,128)(2,1)S(1)}, bf16[512,256]{1,0:T(8,128)(2,1)S(1)}, u32[]{:S(2)}, u32[]{:S(2)}) %collective-permute-start.25) | collective-permute-done | bytes 262176 | tf_op jit(solution)/shard_map/ppermute | solution.py:377
  272.1 3.1 collective-permute-done.26.refs_2_
  275.3 5.6 %backward_block.6 = (bf16[512,256]{1,0:T(8,128)(2,1)S(1)}, f32[512,256]{1,0:T(8,128)S(1)}, bf16[512,256]{1,0:T(8,128)(2,1)S(1)}, bf16[512,256]{1,0:T(8,128)(2,1)S(1)}, bf16[512,256]{1,0:T(8,128)(2,1)S(1)}) custom-call(s32[3]{0:T(128)S(1)} %pad_add_fusion.scal, f32[512,256]{1,0:T(8,128)S(1)} %get-tuple-element.49.refs_0_, ...), custom_call_target="tpu_custom_call" | custom-call | flops 2429026304 | bytes 5767168 | tf_op jit(solution)/shard_map/backward_block/pallas_call | solution.py:288
  280.9 1.5 collective-permute-start.28
  282.9 1.5 collective-permute-start.30
  284.4 4.0 collective-permute-done.28.refs_1_
  288.4 4.2 %collective-permute-done.29.refs_2_ = bf16[512,256]{1,0:T(8,128)(2,1)S(1)} collective-permute-done((bf16[512,256]{1,0:T(8,128)(2,1)S(1)}, bf16[512,256]{1,0:T(8,128)(2,1)S(1)}, u32[]{:S(2)}, u32[]{:S(2)}) %collective-permute-start.29) | collective-permute-done | bytes 262176 | tf_op jit(solution)/shard_map/ppermute | solution.py:377
  292.5 1.6 backward_block.7
  294.4 1.6 collective-permute-start.33
  296.5 1.5 collective-permute-start.31
  297.9 4.2 collective-permute-done.33
  302.1 2.7 collective-permute-done.32
  306.5 6.9 %dynamic-slice_bitcast_fusion.3 = (bf16[8,4,4,32,256]{4,3,2,1,0:T(8,128)(2,1)S(1)}, bf16[8,4,4,32,256]{4,3,2,1,0:T(8,128)(2,1)}, bf16[8,4,4,32,256]{4,3,2,1,0:T(8,128)(2,1)}, bf16[8,4,4,32,256]{4,3,2,1,0:T(8,128)(2,1)}) fusion(bf16[8,4,4,4,32,256]{5,4,3,2,1,0:T(8,128)(2,1)} %bitcast.233, s32[]{:T(128)S(6)} %select_n.262, s32[]{:T(128)S(6)} %select_n.264, ...), kind=kLoop, calls=%fused_computation.22 | loop fusion | bytes 16777232 | tf_op jit(solution)/shard_map/jit(dynamic_index_in_dim)/squeeze | solution.py:478
  313.4 17.6 %select_maximum_fusion = bf16[8,6,6,32,1024]{4,3,2,1,0:T(8,128)(2,1)} fusion(bf16[8,4,4,32,256]{4,3,2,1,0:T(8,128)(2,1)} %get-tuple-element.70, bf16[8,4,4,32,256]{4,3,2,1,0:T(8,128)(2,1)} %get-tuple-element.68, bf16[8,4,4,32,256]{4,3,2,1,0:T(8,128)(2,1)} %get-tuple-element.69, bf16[8,4,4,32,256]{4,3,2,1,0:T(8,128)(2,1)S(1)} %get-tuple-element.67), kind=kLoop, calls=%fused_computation.7 | loop fusion | flops 217055232 | bytes 27262976 | tf_op jit(solution)/shard_map/concatenate | solution.py:476
  331.1 12.5 %constant_dynamic-slice_fusion.1 = (bf16[8,4,4,32,1024]{4,3,2,1,0:T(8,128)(2,1)}, bf16[8,4,4,32,1024]{4,3,2,1,0:T(8,128)(2,1)}) fusion(bf16[8,6,6,32,1024]{4,3,2,1,0:T(8,128)(2,1)} %select_maximum_fusion, s32[]{:T(128)S(6)} %select_n.272, s32[]{:T(128)S(6)} %select_n.274, s32[]{:T(128)S(6)} %select_n.268, s32[]{:T(128)S(6)} %select_n.270), kind=kLoop, calls=%fused_computation.100 | loop fusion | bytes 33554448 | tf_op jit(solution)/shard_map/dynamic_slice | solution.py:488
  343.6 11.4 %copy.32 = bf16[4096,1024]{0,1:T(8,128)(2,1)} copy(bf16[4096,1024]{1,0:T(8,128)(2,1)} %bitcast.231) | data formatting | bytes 16777216 | tf_op jit(solution)/shard_map/reshape | solution.py:492
  355.0 11.9 %copy.31 = bf16[4096,1024]{0,1:T(8,128)(2,1)} copy(bf16[4096,1024]{1,0:T(8,128)(2,1)} %bitcast.230) | data formatting | bytes 16777216 | tf_op jit(solution)/shard_map/reshape | solution.py:492
  366.9 11.4 %fusion.7.cols = bf16[1152,4096]{1,0:T(8,128)(2,1)} fusion(s32[]{:T(128)S(6)} %select_n.276, bf16[4096,1024]{0,1:T(8,128)(2,1)} %copy.31, bf16[4096,1024]{0,1:T(8,128)(2,1)} %copy.32), kind=kLoop, calls=%fused_computation.16 | loop fusion | flops 18874368 | bytes 26214404 | tf_op jit(solution)/shard_map/transpose | solution.py:497
  378.4 8.5 %all-gather.13.cloned.1.call-done.raw = bf16[4096,1024]{1,0:T(8,128)(2,1)} async-done(((bf16[512,1024]{1,0:T(8,128)(2,1)}), bf16[4096,1024]{1,0:T(8,128)(2,1)}) %all-gather.13.cloned.1.call-update) | async-done | bytes 8388624 | tf_op jit(solution)/shard_map/all_gather | solution.py:496
  386.9 22.0 %update.1 = (f32[1152,1024]{1,0:T(8,128)}, f32[1152,1024]{1,0:T(8,128)}, f32[1152,1024]{1,0:T(8,128)}) custom-call(bf16[1152,4096]{1,0:T(8,128)(2,1)} %fusion.7.cols, bf16[4096,1024]{1,0:T(8,128)(2,1)} %all-gather.13.cloned.1.call-done.raw, f32[1152,1024]{1,0:T(8,128)} %bitcast.241, f32[1152,1024]{1,0:T(8,128)} %bitcast.247, f32[1152,1024]{1,0:T(8,128)} %bitcast.248), custom_call_target="tpu_custom_call" | custom-call | flops 9663676416 | bytes 36700160 | tf_op jit(solution)/shard_map/update/pallas_call | solution.py:335
  (107 shorter events, 30.3 us)
Async XLA Ops:
  7.2 67.9 %all-gather.15.cloned.1.call-start = ((), (), s32[]{:S(2)}) async-start(), calls=%async_computation.4 | async-start | bytes 5308416 | tf_op jit(solution)/shard_map/all_gather | solution.py:443
  11.1 136.9 %all-gather.7.cloned.1.call-start = ((), (), s32[]{:S(2)}) async-start(), calls=%async_computation | async-start | bytes 5308416 | tf_op jit(solution)/shard_map/all_gather | solution.py:443
  11.2 17.5 %collective-permute-start = (bf16[1152,256]{1,0:T(8,128)(2,1)}, bf16[1152,256]{1,0:T(8,128)(2,1)}, u32[]{:S(2)}, u32[]{:S(2)}) collective-permute-start(bf16[1152,256]{1,0:T(8,128)(2,1)} %get-tuple-element.71), channel_id=1, source_target_pairs={{0,8},{8,0},{16,24},{24,16},{1,9},{9,1},{17,25},{25,17},{2,10},{10... | collective-permute-start | bytes 1769480 | tf_op jit(solution)/shard_map/ppermute | solution.py:377
  14.2 27.7 %collective-permute-start.1 = (bf16[1152,256]{1,0:T(8,128)(2,1)}, bf16[1152,256]{1,0:T(8,128)(2,1)}, u32[]{:S(2)}, u32[]{:S(2)}) collective-permute-start(bf16[1152,256]{1,0:T(8,128)(2,1)} %get-tuple-element.72), channel_id=1, source_target_pairs={{0,16},{8,24},{16,0},{24,8},{1,17},{9,25},{17,1},{25,9},{2,18},{10... | collective-permute-start | bytes 1769480 | tf_op jit(solution)/shard_map/ppermute | solution.py:377
  15.7 26.2 %collective-permute-start.2 = (bf16[1152,256]{1,0:T(8,128)(2,1)}, bf16[1152,256]{1,0:T(8,128)(2,1)}, u32[]{:S(2)}, u32[]{:S(2)}) collective-permute-start(bf16[1152,256]{1,0:T(8,128)(2,1)} %get-tuple-element.74), channel_id=1, source_target_pairs={{0,24},{8,16},{16,8},{24,0},{1,25},{9,17},{17,9},{25,1},{2,26},{10... | collective-permute-start | bytes 1769480 | tf_op jit(solution)/shard_map/ppermute | solution.py:377
  15.7 26.2 %copy-start.4 = (bf16[1,1152,256]{2,1,0:T(8,128)(2,1)S(1)}, bf16[1,1152,256]{2,1,0:T(8,128)(2,1)}, u32[]{:S(2)}) copy-start(bf16[1,1152,256]{2,1,0:T(8,128)(2,1)} %get-tuple-element.73) | copy-start | bytes 1769476
  22.5 125.9 %copy-start.5 = (bf16[512,256]{1,0:T(8,128)(2,1)}, bf16[512,256]{1,0:T(8,128)(2,1)S(1)}, u32[]{:S(2)}) copy-start(bf16[512,256]{1,0:T(8,128)(2,1)S(1)} %get-tuple-element.86.refs_0_) | copy-start | bytes 786436
  44.8 30.2 %collective-permute-start.4 = (bf16[1152,256]{1,0:T(8,128)(2,1)S(1)}, bf16[1152,256]{1,0:T(8,128)(2,1)S(1)}, u32[]{:S(2)}, u32[]{:S(2)}) collective-permute-start(bf16[1152,256]{1,0:T(8,128)(2,1)S(1)} %bitcast.236), channel_id=1, source_target_pairs={{2,0},{3,1},{4,2},{5,3},{6,4},{7,5},{10,8},{11,9},{12,10},{13,11},... | collective-permute-start | bytes 1769480 | tf_op jit(solution)/shard_map/ppermute | solution.py:433
  46.1 29.0 %collective-permute-start.3 = (bf16[1152,256]{1,0:T(8,128)(2,1)S(1)}, bf16[1152,256]{1,0:T(8,128)(2,1)S(1)}, u32[]{:S(2)}, u32[]{:S(2)}) collective-permute-start(bf16[1152,256]{1,0:T(8,128)(2,1)S(1)} %bitcast.237), channel_id=1, source_target_pairs={{0,2},{1,3},{2,4},{3,5},{4,6},{5,7},{8,10},{9,11},{10,12},{11,13},... | collective-permute-start | bytes 1769480 | tf_op jit(solution)/shard_map/ppermute | solution.py:432
  75.0 25.6 %copy-start.13 = (bf16[1152,256]{1,0:T(8,128)(2,1)}, bf16[1152,256]{1,0:T(8,128)(2,1)S(1)}, u32[]{:S(2)}) copy-start(bf16[1152,256]{1,0:T(8,128)(2,1)S(1)} %collective-permute-done.4) | copy-start | bytes 1769476
  75.0 27.5 %copy-start.14 = (bf16[1152,256]{1,0:T(8,128)(2,1)}, bf16[1152,256]{1,0:T(8,128)(2,1)S(1)}, u32[]{:S(2)}) copy-start(bf16[1152,256]{1,0:T(8,128)(2,1)S(1)} %collective-permute-done.3) | copy-start | bytes 1769476
  75.1 126.0 %all-gather.9.cloned.1.call-start = ((), (), s32[]{:S(2)}) async-start(), calls=%async_computation.1 | async-start | bytes 5308416 | tf_op jit(solution)/shard_map/all_gather | solution.py:443
  75.1 24.2 %collective-permute-start.10 = (bf16[1152,256]{1,0:T(8,128)(2,1)S(1)}, bf16[1152,256]{1,0:T(8,128)(2,1)}, u32[]{:S(2)}, u32[]{:S(2)}) collective-permute-start(bf16[1152,256]{1,0:T(8,128)(2,1)S(1)} %collective-permute-done.4), channel_id=1, source_target_pairs={{2,0},{3,1},{4,2},{5,3},{10,8},{11,9},{12,10},{13,11},{18,16},{19,... | collective-permute-start | bytes 1769480 | tf_op jit(solution)/shard_map/ppermute | solution.py:433
  76.4 24.2 %collective-permute-start.8 = (bf16[1152,256]{1,0:T(8,128)(2,1)S(1)}, bf16[1152,256]{1,0:T(8,128)(2,1)}, u32[]{:S(2)}, u32[]{:S(2)}) collective-permute-start(bf16[1152,256]{1,0:T(8,128)(2,1)S(1)} %collective-permute-done.3), channel_id=1, source_target_pairs={{2,4},{3,5},{4,6},{5,7},{10,12},{11,13},{12,14},{13,15},{18,20},{1... | collective-permute-start | bytes 1769480 | tf_op jit(solution)/shard_map/ppermute | solution.py:432
  99.3 44.7 %collective-permute-start.11 = (bf16[1152,256]{1,0:T(8,128)(2,1)}, bf16[1152,256]{1,0:T(8,128)(2,1)}, u32[]{:S(2)}, u32[]{:S(2)}) collective-permute-start(bf16[1152,256]{1,0:T(8,128)(2,1)} %collective-permute-done.10), channel_id=1, source_target_pairs={{2,0},{3,1},{10,8},{11,9},{18,16},{19,17},{26,24},{27,25}} | collective-permute-start | bytes 1769480 | tf_op jit(solution)/shard_map/ppermute | solution.py:433
  100.6 44.5 %collective-permute-start.9 = (bf16[1152,256]{1,0:T(8,128)(2,1)}, bf16[1152,256]{1,0:T(8,128)(2,1)S(1)}, u32[]{:S(2)}, u32[]{:S(2)}) collective-permute-start(bf16[1152,256]{1,0:T(8,128)(2,1)} %collective-permute-done.8), channel_id=1, source_target_pairs={{4,6},{5,7},{12,14},{13,15},{20,22},{21,23},{28,30},{29,31}} | collective-permute-start | bytes 1769480 | tf_op jit(solution)/shard_map/ppermute | solution.py:432
  148.0 11.7 %collective-permute-start.12 = (bf16[4,1152,256]{2,1,0:T(8,128)(2,1)}, bf16[4,1152,256]{2,1,0:T(8,128)(2,1)}, u32[]{:S(2)}, u32[]{:S(2)}) collective-permute-start(bf16[4,1152,256]{2,1,0:T(8,128)(2,1)} %pad_maximum_fusion.1), channel_id=1, source_target_pairs={{0,1},{1,0},{2,3},{3,2},{4,5},{5,4},{6,7},{7,6},{8,9},{9,8},{10,11... | collective-permute-start | bytes 7077896 | tf_op jit(solution)/shard_map/ppermute | solution.py:318
  148.0 158.5 %all-gather.11.cloned.1.call-start = ((), (), s32[]{:S(2)}) async-start(), calls=%async_computation.2 | async-start | bytes 9437184 | tf_op jit(solution)/shard_map/all_gather | solution.py:456
  156.2 12.8 %copy-start = (bf16[512,256]{1,0:T(8,128)(2,1)}, bf16[512,256]{1,0:T(8,128)(2,1)S(1)}, u32[]{:S(2)}) copy-start(bf16[512,256]{1,0:T(8,128)(2,1)S(1)} %get-tuple-element.36.refs_0_) | copy-start | bytes 786436
  156.2 12.9 %collective-permute-start.7 = (bf16[512,256]{1,0:T(8,128)(2,1)S(1)}, bf16[512,256]{1,0:T(8,128)(2,1)S(1)}, u32[]{:S(2)}, u32[]{:S(2)}) collective-permute-start(bf16[512,256]{1,0:T(8,128)(2,1)S(1)} %get-tuple-element.36.refs_0_), channel_id=1, source_target_pairs={{0,8},{8,0},{16,24},{24,16},{1,9},{9,1},{17,25},{25,17},{2,10},{10... | collective-permute-start | bytes 786440 | tf_op jit(solution)/shard_map/ppermute | solution.py:377
  157.8 14.1 %collective-permute-start.6 = (bf16[512,256]{1,0:T(8,128)(2,1)S(1)}, bf16[512,256]{1,0:T(8,128)(2,1)S(1)}, u32[]{:S(2)}, u32[]{:S(2)}) collective-permute-start(bf16[512,256]{1,0:T(8,128)(2,1)S(1)} %get-tuple-element.36.refs_0_), channel_id=1, source_target_pairs={{0,16},{8,24},{16,0},{24,8},{1,17},{9,25},{17,1},{25,9},{2,18},{10... | collective-permute-start | bytes 786440 | tf_op jit(solution)/shard_map/ppermute | solution.py:377
  159.6 12.3 %collective-permute-start.5 = (bf16[512,256]{1,0:T(8,128)(2,1)S(1)}, bf16[512,256]{1,0:T(8,128)(2,1)S(1)}, u32[]{:S(2)}, u32[]{:S(2)}) collective-permute-start(bf16[512,256]{1,0:T(8,128)(2,1)S(1)} %get-tuple-element.36.refs_0_), channel_id=1, source_target_pairs={{0,24},{8,16},{16,8},{24,0},{1,25},{9,17},{17,9},{25,1},{2,26},{10... | collective-permute-start | bytes 786440 | tf_op jit(solution)/shard_map/ppermute | solution.py:377
  160.0 9.0 %copy-start.6 = (bf16[512,256]{1,0:T(8,128)(2,1)S(1)}, bf16[512,256]{1,0:T(8,128)(2,1)}, u32[]{:S(2)}) copy-start(bf16[512,256]{1,0:T(8,128)(2,1)} %copy-done.5) | copy-start | bytes 786436
  169.0 2.9 copy-start.2
  169.1 2.8 copy-start.7
  171.9 0.7 copy-start.8
  171.9 0.8 copy-start.9
  179.2 21.9 %copy-start.1 = (bf16[512,256]{1,0:T(8,128)(2,1)}, bf16[512,256]{1,0:T(8,128)(2,1)S(1)}, u32[]{:S(2)}) copy-start(bf16[512,256]{1,0:T(8,128)(2,1)S(1)} %get-tuple-element.39.refs_0_) | copy-start | bytes 786436
  179.2 15.0 %collective-permute-start.15 = (bf16[512,256]{1,0:T(8,128)(2,1)S(1)}, bf16[512,256]{1,0:T(8,128)(2,1)S(1)}, u32[]{:S(2)}, u32[]{:S(2)}) collective-permute-start(bf16[512,256]{1,0:T(8,128)(2,1)S(1)} %get-tuple-element.39.refs_0_), channel_id=1, source_target_pairs={{0,8},{8,0},{16,24},{24,16},{1,9},{9,1},{17,25},{25,17},{2,10},{10... | collective-permute-start | bytes 786440 | tf_op jit(solution)/shard_map/ppermute | solution.py:377
  180.6 13.4 %collective-permute-start.14 = (bf16[512,256]{1,0:T(8,128)(2,1)S(1)}, bf16[512,256]{1,0:T(8,128)(2,1)S(1)}, u32[]{:S(2)}, u32[]{:S(2)}) collective-permute-start(bf16[512,256]{1,0:T(8,128)(2,1)S(1)} %get-tuple-element.39.refs_0_), channel_id=1, source_target_pairs={{0,16},{8,24},{16,0},{24,8},{1,17},{9,25},{17,1},{25,9},{2,18},{10... | collective-permute-start | bytes 786440 | tf_op jit(solution)/shard_map/ppermute | solution.py:377
  181.4 12.5 %collective-permute-start.13 = (bf16[512,256]{1,0:T(8,128)(2,1)S(1)}, bf16[512,256]{1,0:T(8,128)(2,1)S(1)}, u32[]{:S(2)}, u32[]{:S(2)}) collective-permute-start(bf16[512,256]{1,0:T(8,128)(2,1)S(1)} %get-tuple-element.39.refs_0_), channel_id=1, source_target_pairs={{0,24},{8,16},{16,8},{24,0},{1,25},{9,17},{17,9},{25,1},{2,26},{10... | collective-permute-start | bytes 786440 | tf_op jit(solution)/shard_map/ppermute | solution.py:377
  193.9 7.1 %copy-start.12 = (bf16[512,256]{1,0:T(8,128)(2,1)}, bf16[512,256]{1,0:T(8,128)(2,1)S(1)}, u32[]{:S(2)}) copy-start(bf16[512,256]{1,0:T(8,128)(2,1)S(1)} %collective-permute-done.13.refs_3_) | copy-start | bytes 786436
  194.1 7.0 %copy-start.11 = (bf16[512,256]{1,0:T(8,128)(2,1)}, bf16[512,256]{1,0:T(8,128)(2,1)S(1)}, u32[]{:S(2)}) copy-start(bf16[512,256]{1,0:T(8,128)(2,1)S(1)} %collective-permute-done.14.refs_2_) | copy-start | bytes 786436
  194.2 6.9 %copy-start.10 = (bf16[512,256]{1,0:T(8,128)(2,1)}, bf16[512,256]{1,0:T(8,128)(2,1)S(1)}, u32[]{:S(2)}) copy-start(bf16[512,256]{1,0:T(8,128)(2,1)S(1)} %collective-permute-done.15.refs_1_) | copy-start | bytes 786436
  207.5 10.2 %collective-permute-start.16 = (bf16[512,256]{1,0:T(8,128)(2,1)S(1)}, bf16[512,256]{1,0:T(8,128)(2,1)S(1)}, u32[]{:S(2)}, u32[]{:S(2)}) collective-permute-start(bf16[512,256]{1,0:T(8,128)(2,1)S(1)} %get-tuple-element.41.refs_0_), channel_id=1, source_target_pairs={{0,24},{8,16},{16,8},{24,0},{1,25},{9,17},{17,9},{25,1},{2,26},{10... | collective-permute-start | bytes 786440 | tf_op jit(solution)/shard_map/ppermute | solution.py:377
  210.1 12.6 %collective-permute-start.18 = (bf16[512,256]{1,0:T(8,128)(2,1)S(1)}, bf16[512,256]{1,0:T(8,128)(2,1)S(1)}, u32[]{:S(2)}, u32[]{:S(2)}) collective-permute-start(bf16[512,256]{1,0:T(8,128)(2,1)S(1)} %get-tuple-element.41.refs_0_), channel_id=1, source_target_pairs={{0,8},{8,0},{16,24},{24,16},{1,9},{9,1},{17,25},{25,17},{2,10},{10... | collective-permute-start | bytes 786440 | tf_op jit(solution)/shard_map/ppermute | solution.py:377
  210.7 11.8 %collective-permute-start.17 = (bf16[512,256]{1,0:T(8,128)(2,1)S(1)}, bf16[512,256]{1,0:T(8,128)(2,1)S(1)}, u32[]{:S(2)}, u32[]{:S(2)}) collective-permute-start(bf16[512,256]{1,0:T(8,128)(2,1)S(1)} %get-tuple-element.41.refs_0_), channel_id=1, source_target_pairs={{0,16},{8,24},{16,0},{24,8},{1,17},{9,25},{17,1},{25,9},{2,18},{10... | collective-permute-start | bytes 786440 | tf_op jit(solution)/shard_map/ppermute | solution.py:377
  222.8 1.0 copy-start.3
  223.8 10.2 %copy-start.15 = (s32[4]{0:T(128)S(1)}, s32[4]{0:T(128)}, u32[]{:S(2)}) copy-start(s32[4]{0:T(128)} %param.7) | copy-start | bytes 52
  223.8 163.1 %all-gather.13.cloned.1.call-start = ((), (), s32[]{:S(2)}) async-start(), calls=%async_computation.3 | async-start | bytes 9437184 | tf_op jit(solution)/shard_map/all_gather | solution.py:496
  230.4 4.7 %collective-permute-start.21 = (f32[4,1024]{1,0:T(4,128)S(1)}, f32[4,1024]{1,0:T(4,128)S(1)}, u32[]{:S(2)}, u32[]{:S(2)}) collective-permute-start(f32[4,1024]{1,0:T(4,128)S(1)} %get-tuple-element.42.refs_0_), channel_id=1, source_target_pairs={{0,24},{8,16},{16,8},{24,0},{1,25},{9,17},{17,9},{25,1},{2,26},{10... | collective-permute-start | bytes 49160 | tf_op jit(solution)/shard_map/ppermute | solution.py:377
  232.8 3.7 collective-permute-start.20
  233.4 3.7 collective-permute-start.19
  244.1 9.3 %collective-permute-start.22 = (bf16[512,256]{1,0:T(8,128)(2,1)S(1)}, bf16[512,256]{1,0:T(8,128)(2,1)S(1)}, u32[]{:S(2)}, u32[]{:S(2)}) collective-permute-start(bf16[512,256]{1,0:T(8,128)(2,1)S(1)} %get-tuple-element.45), channel_id=1, source_target_pairs={{0,8},{8,0},{16,24},{24,16},{1,9},{9,1},{17,25},{25,17},{2,10},{10... | collective-permute-start | bytes 786440 | tf_op jit(solution)/shard_map/ppermute | solution.py:377
  244.7 11.3 %collective-permute-start.23 = (bf16[512,256]{1,0:T(8,128)(2,1)S(1)}, bf16[512,256]{1,0:T(8,128)(2,1)S(1)}, u32[]{:S(2)}, u32[]{:S(2)}) collective-permute-start(bf16[512,256]{1,0:T(8,128)(2,1)S(1)} %get-tuple-element.46), channel_id=1, source_target_pairs={{0,16},{8,24},{16,0},{24,8},{1,17},{9,25},{17,1},{25,9},{2,18},{10... | collective-permute-start | bytes 786440 | tf_op jit(solution)/shard_map/ppermute | solution.py:377
  246.2 11.4 %collective-permute-start.24 = (bf16[512,256]{1,0:T(8,128)(2,1)S(1)}, bf16[512,256]{1,0:T(8,128)(2,1)S(1)}, u32[]{:S(2)}, u32[]{:S(2)}) collective-permute-start(bf16[512,256]{1,0:T(8,128)(2,1)S(1)} %get-tuple-element.47), channel_id=1, source_target_pairs={{0,24},{8,16},{16,8},{24,0},{1,25},{9,17},{17,9},{25,1},{2,26},{10... | collective-permute-start | bytes 786440 | tf_op jit(solution)/shard_map/ppermute | solution.py:377
  263.2 8.9 %collective-permute-start.25 = (bf16[512,256]{1,0:T(8,128)(2,1)S(1)}, bf16[512,256]{1,0:T(8,128)(2,1)S(1)}, u32[]{:S(2)}, u32[]{:S(2)}) collective-permute-start(bf16[512,256]{1,0:T(8,128)(2,1)S(1)} %get-tuple-element.50), channel_id=1, source_target_pairs={{0,8},{8,0},{16,24},{24,16},{1,9},{9,1},{17,25},{25,17},{2,10},{10... | collective-permute-start | bytes 786440 | tf_op jit(solution)/shard_map/ppermute | solution.py:377
  264.0 11.2 %collective-permute-start.26 = (bf16[512,256]{1,0:T(8,128)(2,1)S(1)}, bf16[512,256]{1,0:T(8,128)(2,1)S(1)}, u32[]{:S(2)}, u32[]{:S(2)}) collective-permute-start(bf16[512,256]{1,0:T(8,128)(2,1)S(1)} %get-tuple-element.51), channel_id=1, source_target_pairs={{0,16},{8,24},{16,0},{24,8},{1,17},{9,25},{17,1},{25,9},{2,18},{10... | collective-permute-start | bytes 786440 | tf_op jit(solution)/shard_map/ppermute | solution.py:377
  265.5 9.7 %collective-permute-start.27 = (bf16[512,256]{1,0:T(8,128)(2,1)S(1)}, bf16[512,256]{1,0:T(8,128)(2,1)S(1)}, u32[]{:S(2)}, u32[]{:S(2)}) collective-permute-start(bf16[512,256]{1,0:T(8,128)(2,1)S(1)} %get-tuple-element.52), channel_id=1, source_target_pairs={{0,24},{8,16},{16,8},{24,0},{1,25},{9,17},{17,9},{25,1},{2,26},{10... | collective-permute-start | bytes 786440 | tf_op jit(solution)/shard_map/ppermute | solution.py:377
  280.9 7.5 %collective-permute-start.28 = (bf16[512,256]{1,0:T(8,128)(2,1)S(1)}, bf16[512,256]{1,0:T(8,128)(2,1)S(1)}, u32[]{:S(2)}, u32[]{:S(2)}) collective-permute-start(bf16[512,256]{1,0:T(8,128)(2,1)S(1)} %get-tuple-element.55), channel_id=1, source_target_pairs={{0,8},{8,0},{16,24},{24,16},{1,9},{9,1},{17,25},{25,17},{2,10},{10... | collective-permute-start | bytes 786440 | tf_op jit(solution)/shard_map/ppermute | solution.py:377
  282.3 10.2 %collective-permute-start.29 = (bf16[512,256]{1,0:T(8,128)(2,1)S(1)}, bf16[512,256]{1,0:T(8,128)(2,1)S(1)}, u32[]{:S(2)}, u32[]{:S(2)}) collective-permute-start(bf16[512,256]{1,0:T(8,128)(2,1)S(1)} %get-tuple-element.56), channel_id=1, source_target_pairs={{0,16},{8,24},{16,0},{24,8},{1,17},{9,25},{17,1},{25,9},{2,18},{10... | collective-permute-start | bytes 786440 | tf_op jit(solution)/shard_map/ppermute | solution.py:377
  282.9 9.6 %collective-permute-start.30 = (bf16[512,256]{1,0:T(8,128)(2,1)S(1)}, bf16[512,256]{1,0:T(8,128)(2,1)S(1)}, u32[]{:S(2)}, u32[]{:S(2)}) collective-permute-start(bf16[512,256]{1,0:T(8,128)(2,1)S(1)} %get-tuple-element.57), channel_id=1, source_target_pairs={{0,24},{8,16},{16,8},{24,0},{1,25},{9,17},{17,9},{25,1},{2,26},{10... | collective-permute-start | bytes 786440 | tf_op jit(solution)/shard_map/ppermute | solution.py:377
  294.4 7.7 %collective-permute-start.33 = (bf16[512,256]{1,0:T(8,128)(2,1)S(1)}, bf16[512,256]{1,0:T(8,128)(2,1)S(1)}, u32[]{:S(2)}, u32[]{:S(2)}) collective-permute-start(bf16[512,256]{1,0:T(8,128)(2,1)S(1)} %get-tuple-element.83), channel_id=1, source_target_pairs={{0,24},{8,16},{16,8},{24,0},{1,25},{9,17},{17,9},{25,1},{2,26},{10... | collective-permute-start | bytes 786440 | tf_op jit(solution)/shard_map/ppermute | solution.py:377
  296.0 8.8 %collective-permute-start.32 = (bf16[512,256]{1,0:T(8,128)(2,1)S(1)}, bf16[512,256]{1,0:T(8,128)(2,1)S(1)}, u32[]{:S(2)}, u32[]{:S(2)}) collective-permute-start(bf16[512,256]{1,0:T(8,128)(2,1)S(1)} %get-tuple-element.84), channel_id=1, source_target_pairs={{0,16},{8,24},{16,0},{24,8},{1,17},{9,25},{17,1},{25,9},{2,18},{10... | collective-permute-start | bytes 786440 | tf_op jit(solution)/shard_map/ppermute | solution.py:377
  296.5 8.3 %collective-permute-start.31 = (bf16[512,256]{1,0:T(8,128)(2,1)S(1)}, bf16[512,256]{1,0:T(8,128)(2,1)S(1)}, u32[]{:S(2)}, u32[]{:S(2)}) collective-permute-start(bf16[512,256]{1,0:T(8,128)(2,1)S(1)} %get-tuple-element.85), channel_id=1, source_target_pairs={{0,8},{8,0},{16,24},{24,16},{1,9},{9,1},{17,25},{25,17},{2,10},{10... | collective-permute-start | bytes 786440 | tf_op jit(solution)/shard_map/ppermute | solution.py:377
Sparse Core Ops, SparseCore 0:
  11.2 60.0 all-gather.14
  75.2 67.2 all-gather.6
  148.2 52.8 all-gather.8
  223.9 80.8 all-gather.10
  306.5 80.3 all-gather.12
